TPU v7x, 32 devices: a whole 2x2x4 slice. The times are simulated.
32 devices in a mesh: rep: 2 (over x), dp: 2 (over core), tensor: 8 (over z, y).
Axes of the slice: x: 2, y: 2, z: 4, core: 2. Of those that a mesh axis runs over, the one named last changes fastest.
Arguments:
- hidden: bfloat16 [1024, 8192], P(('rep', 'dp'), 'tensor'), parts along dimension 0, may hold values from -6 to 6
- attn_gain: float32 [8192], replicated, may hold values from 0.25 to 1.75
- q_weight: bfloat16 [8192, 2048], P('dp', 'tensor'), may hold values from -0.0625 to 0.0625
- kv_weight: bfloat16 [8192, 256], P('tensor'), may hold values from -0.0625 to 0.0625
- kv_cache: bfloat16 [16, 256, 256], P(('rep', 'dp')), parts along dimension 0, may hold values from -200 to 200
- out_weight: bfloat16 [2048, 8192], P('tensor', 'dp'), may hold values from -0.5 to 0.5
- final_gain: float32 [8192], replicated, may hold values from 0.25 to 1.75
- vocab_weight: bfloat16 [8192, 4096], P('dp', 'tensor'), may hold values from -80 to 80
- resp_len: int32 [16], P('rep'), parts along dimension 0, may hold values from 1 to 128, as said below
- ctx_len: int32 [16], P(('rep', 'dp')), parts along dimension 0, may hold values from 1 to 256
- target_ids: int32 [1024], P('rep'), parts along dimension 0, may hold values from 0 to 4095
Outputs:
- layer_out: bfloat16 [1024, 8192], P(('rep', 'dp'), 'tensor'), parts along dimension 0
- token_logprob: float32 [1024], P(('rep', 'dp')), parts along dimension 0
There are 2 independent parts, one for each index of `rep`. A program takes and returns all parts, laid end to end along the dimension named above; an argument that names none is the same for every part. Nothing has to cross between parts.
Inputs may be any that keep to these rules, and one draw needn't show every extreme that they name: `resp_len`: within a data group the rollouts fill its first slots in order. The lengths of the two data groups of a part add up to exactly 256, so one group has more than 128 live slots and the other fewer; one rollout of the busier group has exactly 128 slots.
All inputs are finite; a program needn't handle non-finite values.
Results may differ from a plain program's by a relative error of at most 0.015.
The roundings to bfloat16 on the way count: a program that leaves them out, or rounds other values in their place, can miss the bound.
Values may be sent and summed in bfloat16 or wider, within the bound.
No kernel may reach another device: no remote copies, remote signals or barrier semaphores. Data moves between devices by JAX's collectives and lax.ppermute only.
A program may use at most 128 MiB of HBM per device.

v0:
```python
import jax
import jax.numpy as jnp
from jax import lax
from jax.sharding import PartitionSpec as P

HEAD = 128
QH_DEV = 2
GROUP = 16


EPS = 1e-05


def add_columns(left, piece):
    return jnp.dot(left, piece, preferred_element_type=jnp.float32)


def finish(attn_rows, resid_rows, targets, out_weight, final_gain, vocab_weight):
    count = attn_rows.shape[0]
    tensor_count = lax.axis_size("tensor")
    tensor_pos = lax.axis_index("tensor")
    partial_out = jnp.dot(
        attn_rows,
        lax.all_gather(out_weight, "dp", axis=1, tiled=True),
        preferred_element_type=jnp.float32,
    )
    full_width = partial_out.shape[1]
    shard = full_width // tensor_count
    branch = lax.psum(partial_out.astype(jnp.bfloat16), "tensor").astype(jnp.float32)
    mixed = resid_rows.astype(jnp.float32) + branch
    scale = lax.rsqrt(jnp.mean(mixed * mixed, axis=1, keepdims=True) + EPS)
    final_rows = (mixed * scale * final_gain).astype(jnp.bfloat16)
    mixed_shard = lax.dynamic_slice_in_dim(mixed, tensor_pos * shard, shard, 1)
    vocab_count = vocab_weight.shape[1]
    logits = add_columns(final_rows, lax.all_gather(vocab_weight, "dp", axis=0, tiled=True))
    column_ids = tensor_pos * vocab_count + lax.broadcasted_iota(jnp.int32, (count, vocab_count), 1)
    picked = jnp.sum(jnp.where(column_ids == targets[:, None], logits, 0.0), axis=1)
    top = lax.pmax(jnp.max(logits, axis=1), "tensor")
    total, picked_all = lax.psum(
        (jnp.sum(jnp.exp(logits - top[:, None]), axis=1), picked), "tensor"
    )
    logprob = picked_all - top - jnp.log(total)
    return (mixed_shard, logprob)


def per_device(
    hidden,
    attn_gain,
    q_weight,
    kv_weight,
    kv_cache,
    out_weight,
    final_gain,
    vocab_weight,
    resp_len,
    ctx_len,
    target_ids,
):
    rows_count = hidden.shape[0]
    tensor_count = lax.axis_size("tensor")
    tensor_pos = lax.axis_index("tensor")
    group = lax.axis_index("dp")
    shard = hidden.shape[1]
    full_width = shard * tensor_count
    seqs_count = ctx_len.shape[0]
    rows_f = hidden.astype(jnp.float32)
    square_sum = lax.psum(jnp.sum(rows_f * rows_f, axis=1), "tensor")
    scale = lax.rsqrt(square_sum / full_width + EPS)[:, None]
    gain_shard = lax.dynamic_slice_in_dim(attn_gain, tensor_pos * shard, shard, 0)
    normed = (rows_f * scale * gain_shard).astype(jnp.bfloat16)
    normed_full, resid = (
        lax.all_gather(normed, "tensor", axis=1, tiled=True),
        lax.all_gather(hidden, "tensor", axis=1, tiled=True),
    )
    kv_partial = jnp.dot(normed, kv_weight, preferred_element_type=jnp.float32)
    kv_all = lax.psum(kv_partial.astype(jnp.bfloat16), "tensor")
    kv_head = tensor_pos * QH_DEV // GROUP
    own_kv = lax.dynamic_slice_in_dim(kv_all, kv_head * 2 * HEAD, 2 * HEAD, 1)
    cache_own = lax.dynamic_slice_in_dim(kv_cache, kv_head * 2 * HEAD, 2 * HEAD, 2).reshape(
        -1, 2 * HEAD
    )
    keys = jnp.concatenate([cache_own[:, :HEAD], own_kv[:, :HEAD]], axis=0)
    vals = jnp.concatenate([cache_own[:, HEAD:], own_kv[:, HEAD:]], axis=0)
    query = add_columns(normed_full, lax.all_gather(q_weight, "dp", axis=0, tiled=True))
    query = query.astype(jnp.bfloat16).reshape(rows_count, QH_DEV, HEAD)
    own_lens = lax.dynamic_slice_in_dim(resp_len, group * seqs_count, seqs_count, 0)
    ends = jnp.cumsum(own_lens)
    own_live = ends[seqs_count - 1]
    row_ids = lax.broadcasted_iota(jnp.int32, (rows_count, 1), 0)
    seg = jnp.sum((row_ids >= ends[None, :]).astype(jnp.int32), axis=1)
    ctx_slots = kv_cache.shape[1]
    slot_seg = lax.broadcasted_iota(jnp.int32, (seqs_count, ctx_slots), 0).reshape(-1)
    slot_pos = lax.broadcasted_iota(jnp.int32, (seqs_count, ctx_slots), 1).reshape(-1)
    slot_len = jnp.broadcast_to(ctx_len[:, None], (seqs_count, ctx_slots)).reshape(-1)
    ctx_ok = (slot_seg[None, :] == seg[:, None]) & (slot_pos < slot_len)[None, :]
    own_ok = (seg[None, :] == seg[:, None]) & (row_ids[:, 0][None, :] <= row_ids)
    allowed = jnp.concatenate([ctx_ok, own_ok], axis=1)
    scores = jnp.einsum("rhe,ke->hrk", query, keys, preferred_element_type=jnp.float32) * HEAD ** (
        -0.5
    )
    scores = jnp.where(allowed[None], scores, -jnp.inf)
    top = jnp.max(scores, axis=2, keepdims=True)
    weights = jnp.exp(scores - top)
    probs = (weights / jnp.sum(weights, axis=2, keepdims=True)).astype(jnp.bfloat16)
    attn = jnp.einsum("hrk,ke->rhe", probs, vals, preferred_element_type=jnp.float32)
    attn = attn.astype(jnp.bfloat16).reshape(rows_count, QH_DEV * HEAD)
    own_targets = lax.dynamic_slice_in_dim(target_ids, group * rows_count, rows_count, 0)
    live = row_ids[:, 0] < own_live
    mixed_shard, logprob = finish(attn, resid, own_targets, out_weight, final_gain, vocab_weight)
    layer_out = jnp.where(live[:, None], mixed_shard, 0.0).astype(jnp.bfloat16)
    token_logprob = jnp.where(live, logprob, 0.0)
    return (layer_out, token_logprob)


def solution(mesh):
    placed = (
        P(("rep", "dp"), "tensor"),
        P(),
        P("dp", "tensor"),
        P("tensor", None),
        P(("rep", "dp"), None, None),
        P("tensor", "dp"),
        P(),
        P("dp", "tensor"),
        P("rep"),
        P(("rep", "dp")),
        P("rep"),
    )
    return jax.shard_map(
        per_device,
        mesh=mesh,
        in_specs=placed,
        out_specs=(P(("rep", "dp"), "tensor"), P(("rep", "dp"))),
        check_vma=False,
    )
```

profile of v0, /device:TPU:0, one launch (start us, length us, event | category | flops | bytes accessed | tf_op | source)
XLA Modules:
  0.0 399.1 jit_solution(1940676619454076744)
XLA Ops:
  8.0 0.0 copy-start
  8.0 0.0 copy-start.5
  8.0 0.0 copy-start.6
  8.0 0.0 all-reduce.4.cloned.1.call-start
  8.1 1.3 fusion.10
  9.4 23.1 %psum.35 = f32[256]{0:T(256)S(1)} all-reduce(f32[256]{0:T(256)S(1)} %fusion.10), channel_id=1, replica_groups=mesh['rep'=2,'dp'=2,'tensor'=8] {'tensor'}, use_global_device_ids=true, to_apply=%region_2.0 | all-reduce | flops 256 | bytes 2048 | tf_op jit(solution)/shard_map/psum | solution.py:67
  32.5 0.7 dynamic_slice.15
  33.2 0.0 copy-start.2
  33.2 1.3 fusion.12
  34.5 0.0 copy-start.1
  34.5 0.0 copy-done
  34.5 1.0 convolution_convert_fusion.1
  35.5 0.0 all-reduce.4.cloned.1.call-update
  35.5 0.0 all-gather.10.cloned.1.call-start
  35.5 0.5 all-gather.10.cloned.1.call-update
  36.1 0.0 all-gather.8.cloned.1.call-start
  36.1 0.0 copy-done.1
  36.1 0.5 all-gather.8.cloned.1.call-update
  36.6 0.0 all-gather.12.cloned.1.call-start
  36.7 0.5 all-gather.12.cloned.1.call-update
  37.2 0.0 all-gather.6.cloned.1.call-start
  37.3 0.7 all-gather.6.cloned.1.call-update
  38.0 0.0 all-reduce.6.cloned.1.call-start
  38.0 0.0 copy-done.5
  38.0 0.1 dynamic-slice_bitcast_fusion
  38.1 0.2 reduce-window.4
  38.3 0.0 copy-done.6
  38.3 0.1 iota_compare_fusion.1
  38.4 0.1 convert_reduce_fusion
  38.5 0.1 fusion.17
  38.6 0.3 compare_and_fusion
  38.9 0.1 pad_add_fusion
  39.0 0.0 copy-done.2
  39.1 90.6 %all-reduce.4.cloned.1.call-done = bf16[256,256]{1,0:T(8,128)(2,1)} async-done(((bf16[256,256]{1,0:T(8,128)(2,1)}), bf16[256,256]{1,0:T(8,128)(2,1)}) %all-reduce.4.cloned.1.call-update) | async-done | bytes 131088 | tf_op jit(solution)/shard_map/psum | solution.py:76
  129.7 0.9 fusion.32
  130.6 0.0 all-gather.10.cloned.1.call-done
  130.7 0.0 all-gather.8.cloned.1.call-done
  130.7 6.2 %convolution_convert_fusion.2 = bf16[256,256]{0,1:T(8,128)(2,1)S(1)} fusion(bf16[256,8192]{1,0:T(8,128)(2,1)} %all-gather.8.cloned.1.call-done, bf16[8192,256]{1,0:T(8,128)(2,1)} %all-gather.10.cloned.1.call-done), kind=kOutput, calls=%fused_computation.20 | convolution fusion | flops 1073807360 | bytes 8519680 | tf_op jit(solution)/shard_map/dot_general | solution.py:15
  136.9 1.0 fusion.33
  137.9 1.3 fusion.9
  139.2 0.5 all-gather.12.cloned.1.call-done
  139.7 5.4 %convolution_convert_fusion = bf16[256,8192]{1,0:T(8,128)(2,1)} fusion(bf16[256,256]{0,1:T(8,128)(2,1)S(1)} %bitcast.52, bf16[256,8192]{1,0:T(8,128)(2,1)} %all-gather.12.cloned.1.call-done), kind=kOutput, calls=%fused_computation.1 | convolution fusion | flops 1075838976 | bytes 8519680 | tf_op jit(solution)/shard_map/dot_general | solution.py:22
  145.1 0.0 copy-start.3
  145.1 0.0 all-reduce.6.cloned.1.call-update
  145.1 0.0 all-gather.14.cloned.1.call-start
  145.2 0.7 all-gather.14.cloned.1.call-update
  145.9 0.6 slice.16
  146.5 0.0 copy-done.3
  146.5 0.1 dynamic_slice.17
  146.5 0.6 iota_compare_fusion.3
  147.2 0.0 copy-start.4
  147.2 120.1 %all-gather.6.cloned.1.call-done = bf16[256,8192]{1,0:T(8,128)(2,1)} async-done(((bf16[256,1024]{1,0:T(8,128)(2,1)}), bf16[256,8192]{1,0:T(8,128)(2,1)}) %all-gather.6.cloned.1.call-update) | async-done | bytes 4194320 | tf_op jit(solution)/shard_map/all_gather | solution.py:73
  267.3 67.2 %all-reduce.6.cloned.1.call-done = bf16[256,8192]{1,0:T(8,128)(2,1)} async-done(((bf16[256,8192]{1,0:T(8,128)(2,1)}), bf16[256,8192]{1,0:T(8,128)(2,1)}) %all-reduce.6.cloned.1.call-update) | async-done | bytes 4194320 | tf_op jit(solution)/shard_map/psum | solution.py:29
  334.5 4.9 %multiply_reduce_fusion = f32[256]{0:T(256)S(1)} fusion(bf16[256,8192]{1,0:T(8,128)(2,1)} %all-reduce.6.cloned.1.call-done, bf16[256,8192]{1,0:T(8,128)(2,1)} %all-gather.6.cloned.1.call-done), kind=kLoop, calls=%fused_computation.3 | loop fusion | flops 10485504 | bytes 8389632 | tf_op jit(solution)/shard_map/reduce_sum | solution.py:31
  339.4 0.0 all-gather.14.cloned.1.call-done
  339.4 0.0 copy-done.4
  339.4 8.3 %fusion.34 = (f32[256]{0:T(256)S(1)}, f32[256,512]{1,0:T(8,128)S(1)}) fusion(bf16[8192,512]{1,0:T(8,128)(2,1)} %all-gather.14.cloned.1.call-done, f32[8192]{0:T(1024)S(1)} %copy-done.4, f32[256]{0:T(256)S(1)} %add_rsqrt_fusion, bf16[256,8192]{1,0:T(8,128)(2,1)} %all-reduce.6.cloned.1.call-done, bf16[256,8192]{1,0:T(8,128)(2,1)} %all-gather.6.cloned.1.call-done), kind=kOutput, calls=%fused_computation.57 | convolution fusion | flops 2160197376 | bytes 17336320 | tf_op jit(solution)/shard_map/dot_general | solution.py:15
  347.8 19.1 %pmax.7 = f32[256]{0:T(256)S(1)} all-reduce(f32[256]{0:T(256)S(1)} %get-tuple-element.10), channel_id=1, replica_groups=mesh['rep'=2,'dp'=2,'tensor'=8] {'tensor'}, use_global_device_ids=true, to_apply=%region_12.13 | all-reduce | flops 256 | bytes 2048 | tf_op jit(solution)/shard_map/pmax | solution.py:38
  366.9 0.3 select_reduce_fusion
  367.2 17.1 %all-reduce = (f32[256]{0:T(256)S(1)}, f32[256]{0:T(256)S(1)}) all-reduce(f32[256]{0:T(256)S(1)} %get-tuple-element.3, f32[256]{0:T(256)S(1)} %get-tuple-element.2), channel_id=1, replica_groups=mesh['rep'=2,'dp'=2,'tensor'=8] {'tensor'}, use_global_device_ids=true, to_apply=%region_14.15 | all-reduce | flops 512 | bytes 4096 | tf_op jit(solution)/shard_map/psum | solution.py:39
  384.3 1.2 subtract_select_fusion
  385.5 5.0 %convert_add_fusion = bf16[256,8192]{1,0:T(8,128)(2,1)S(1)} fusion(bf16[256,8192]{1,0:T(8,128)(2,1)} %all-reduce.6.cloned.1.call-done, bf16[256,8192]{1,0:T(8,128)(2,1)} %all-gather.6.cloned.1.call-done), kind=kLoop, calls=%fused_computation.4 | loop fusion | flops 8388608 | bytes 12582912 | tf_op jit(solution)/shard_map/add | solution.py:30
  390.6 1.0 select_convert_fusion
  (7 shorter events, 0.1 us)
Async XLA Ops:
  8.0 26.5 %copy-start = (bf16[1024,256]{1,0:T(8,128)(2,1)S(1)}, bf16[1024,256]{1,0:T(8,128)(2,1)}, u32[]{:S(2)}) copy-start(bf16[1024,256]{1,0:T(8,128)(2,1)} %param.14) | copy-start | bytes 1572868
  8.0 30.0 %copy-start.5 = (s32[8]{0:T(128)S(1)}, s32[8]{0:T(128)}, u32[]{:S(2)}) copy-start(s32[8]{0:T(128)} %param.19) | copy-start | bytes 100
  8.0 30.3 %copy-start.6 = (s32[4]{0:T(128)S(1)}, s32[4]{0:T(128)}, u32[]{:S(2)}) copy-start(s32[4]{0:T(128)} %param.20) | copy-start | bytes 52
  8.0 121.7 %all-reduce.4.cloned.1.call-start = ((), (), s32[]{:S(2)}) async-start(), calls=%async_computation.1 | async-start | bytes 262144 | tf_op jit(solution)/shard_map/psum | solution.py:76
  33.2 5.9 %copy-start.2 = (bf16[4,256,256]{2,1,0:T(8,128)(2,1)S(1)}, bf16[4,256,256]{2,1,0:T(8,128)(2,1)}, u32[]{:S(2)}) copy-start(bf16[4,256,256]{2,1,0:T(8,128)(2,1)} %param.15) | copy-start | bytes 1572868
  34.5 1.6 copy-start.1
  35.5 95.2 %all-gather.10.cloned.1.call-start = ((), (), s32[]{:S(2)}) async-start(), calls=%async_computation.3 | async-start | bytes 6291456 | tf_op jit(solution)/shard_map/all_gather | solution.py:84
  36.1 94.6 %all-gather.8.cloned.1.call-start = ((), (), s32[]{:S(2)}) async-start(), calls=%async_computation.2 | async-start | bytes 4718592 | tf_op jit(solution)/shard_map/all_gather | solution.py:72
  36.6 103.1 %all-gather.12.cloned.1.call-start = ((), (), s32[]{:S(2)}) async-start(), calls=%async_computation.4 | async-start | bytes 6291456 | tf_op jit(solution)/shard_map/all_gather | solution.py:24
  37.2 230.1 %all-gather.6.cloned.1.call-start = ((), (), s32[]{:S(2)}) async-start(), calls=%async_computation | async-start | bytes 4718592 | tf_op jit(solution)/shard_map/all_gather | solution.py:73
  38.0 296.5 %all-reduce.6.cloned.1.call-start = ((), (), s32[]{:S(2)}) async-start(), calls=%async_computation.5 | async-start | bytes 8388608 | tf_op jit(solution)/shard_map/psum | solution.py:29
  145.1 1.4 copy-start.3
  145.1 194.3 %all-gather.14.cloned.1.call-start = ((), (), s32[]{:S(2)}) async-start(), calls=%async_computation.6 | async-start | bytes 12582912 | tf_op jit(solution)/shard_map/all_gather | solution.py:35
  147.2 192.2 %copy-start.4 = (f32[8192]{0:T(1024)S(1)}, f32[8192]{0:T(1024)}, u32[]{:S(2)}) copy-start(f32[8192]{0:T(1024)} %param.17) | copy-start | bytes 98308
Sparse Core Ops, SparseCore 0:
  35.6 94.0 all-reduce.3
  145.2 189.1 all-reduce.5
Sparse Core Ops, SparseCore 1:
  37.6 10.8 all-gather.9
  51.3 74.5 all-gather.7
  127.4 12.3 all-gather.11
  142.2 125.1 all-gather.5
  269.0 18.9 all-gather.13
where the time goes:
time: 399 us
  waiting for transfers between devices  281 us (70%)
  blocking collectives  59.4 us (15%)
  matrix products  23.2 us (6%)
  other arithmetic  16.5 us (4%)
  between operations  15.9 us (4%)
    all_gather x1, waiting for transfers between devices, per_device(): lax.all_gather(hidden, 'tensor', axis=1, tiled=True)  120 us
    psum x1, waiting for transfers between devices, per_device(): kv_all = lax.psum(kv_partial.astype(jnp.bfloat16), 'tensor')  90.6 us
    psum x1, waiting for transfers between devices, finish(): lax.psum(partial_out.astype(jnp.bfloat16), 'tensor').astype(jnp.float32)  67.2 us
    psum x1, blocking collectives, per_device(): square_sum = lax.psum(jnp.sum(rows_f * rows_f, axis=1), 'tensor')  23.1 us
    pmax x1, blocking collectives, finish(): top = lax.pmax(jnp.max(logits, axis=1), 'tensor')  19.1 us
    psum x1, blocking collectives, finish(): lax.psum((jnp.sum(jnp.exp(logits - top[:, None]), axis=1), picked), 'tens...  17.1 us
    dot_general x2, matrix products, add_columns(): return jnp.dot(left, piece, preferred_element_type=jnp.float32)  14.6 us
  transfers between devices with their start and end apart: 7, of which 4 were waited for; matrix products, arithmetic and copies ran while one was open for 6% of the time, Pallas kernels for 0%

commit v1 on v0

v1 whole, which is shorter than its diff:
```python
import jax
import jax.numpy as jnp
from jax import lax
from jax.sharding import PartitionSpec as P

HEAD = 128
QH_DEV = 2
GROUP = 16
SIDE = 2


EPS = 1e-05


def product(left, right):
    return jnp.dot(left, right, preferred_element_type=jnp.float32)


def swap_dp(value):
    return lax.ppermute(value, "dp", [(0, 1), (1, 0)])


def swap_side(value):
    count = lax.axis_size("tensor")
    return lax.ppermute(value, "tensor", [(i, i ^ 1) for i in range(count)])


def ring_step(value):
    count = lax.axis_size("tensor")
    return lax.ppermute(value, "tensor", [(i, (i + SIDE) % count) for i in range(count)])


def doubling(value, combine):
    count = lax.axis_size("tensor")
    step = 1
    while step < count:
        other = lax.ppermute(value, "tensor", [(i, i ^ step) for i in range(count)])
        value = combine(value, other, step)
        step *= 2
    return value


def sum_tensor(value):
    return doubling(value, lambda a, b, step: a + b)


def gather_blocks(block):
    blocks = []
    for k in range(lax.axis_size("tensor") // SIDE):
        if k > 0:
            block = ring_step(block)
        blocks.append(block)
        blocks.append(swap_side(block))
    return blocks


def gathered_ids():
    count = lax.axis_size("tensor")
    pos = lax.axis_index("tensor")
    ids = []
    for k in range(count // SIDE):
        held = (pos - SIDE * k + count) % count
        ids += [held, held ^ 1]
    return ids


def scattered_ids():
    count = lax.axis_size("tensor")
    pos = lax.axis_index("tensor")
    ids = []
    for k in range(count // SIDE):
        held = (pos - SIDE * (k + 1) + count) % count
        ids += [held, held ^ 1]
    return ids


def pick_blocks(own, other, ids, axis):
    count = lax.axis_size("tensor")
    size = own.shape[axis] * 2 // count
    group = lax.axis_index("dp")
    picked = []
    for block in ids:
        place = (block % (count // 2)) * size
        here = lax.dynamic_slice_in_dim(own, place, size, axis)
        there = lax.dynamic_slice_in_dim(other, place, size, axis)
        picked.append(jnp.where(block // (count // 2) == group, here, there))
    return picked


def row_segment(rows, lens):
    ends = jnp.cumsum(lens)
    return jnp.sum((rows[:, None] >= ends[None, :]).astype(jnp.int32), axis=1)


def per_device(
    hidden,
    attn_gain,
    q_weight,
    kv_weight,
    kv_cache,
    out_weight,
    final_gain,
    vocab_weight,
    resp_len,
    ctx_len,
    target_ids,
):
    rows_count, shard = hidden.shape
    half = rows_count // 2
    tensor_count = lax.axis_size("tensor")
    tensor_pos = lax.axis_index("tensor")
    group = lax.axis_index("dp")
    full_width = shard * tensor_count
    seqs_count, ctx_slots = kv_cache.shape[:2]

    own_lens = lax.dynamic_slice_in_dim(resp_len, group * seqs_count, seqs_count, 0)
    other_lens = lax.dynamic_slice_in_dim(resp_len, (1 - group) * seqs_count, seqs_count, 0)
    busy = jnp.sum(own_lens) > half
    busy_lens = jnp.where(busy, own_lens, other_lens)
    light_total = jnp.sum(jnp.where(busy, other_lens, own_lens))
    is_long = busy_lens == half
    long_seq = jnp.sum(jnp.where(is_long, jnp.arange(seqs_count, dtype=jnp.int32), 0))
    long_start = jnp.sum(jnp.where(is_long, jnp.cumsum(busy_lens) - busy_lens, 0))
    slot = jnp.arange(half, dtype=jnp.int32)
    rest = slot - light_total
    rest_row = rest + jnp.where(rest >= long_start, half, 0)
    keep_src = jnp.where(busy, long_start + slot, jnp.where(rest < 0, slot, -1))
    send_src = jnp.where(busy & (rest >= 0), rest_row, -1)
    row_ids = jnp.arange(rows_count, dtype=jnp.int32)
    keep_pick = keep_src[:, None] == row_ids[None, :]
    send_pick = send_src[:, None] == row_ids[None, :]
    pick = jnp.concatenate([keep_pick, send_pick], axis=0).astype(jnp.bfloat16)
    moved = product(pick, hidden).astype(jnp.bfloat16)
    rows = moved[:half] + swap_dp(moved[half:])

    own_seg = row_segment(slot, own_lens)
    rest_seg = seqs_count + row_segment(rest_row, busy_lens)
    seg = jnp.where(busy, long_seq, jnp.where(rest < 0, own_seg, rest_seg))
    target_row = jnp.where(
        busy,
        group * rows_count + long_start + slot,
        jnp.where(rest < 0, group * rows_count + slot, (1 - group) * rows_count + rest_row),
    )
    all_rows = jnp.arange(target_ids.shape[0], dtype=jnp.int32)
    targets = jnp.sum(jnp.where(target_row[:, None] == all_rows[None, :], target_ids[None, :], 0), axis=1)

    q_blocks = pick_blocks(q_weight, swap_dp(q_weight), gathered_ids(), 0)
    out_blocks = pick_blocks(out_weight, swap_dp(out_weight), scattered_ids(), 1)
    vocab_blocks = pick_blocks(vocab_weight, swap_dp(vocab_weight), gathered_ids(), 0)

    rows_f = rows.astype(jnp.float32)
    square_sum = sum_tensor(jnp.sum(rows_f * rows_f, axis=1)[None, :])[0]
    scale = lax.rsqrt(square_sum / full_width + EPS)[:, None]

    def normed_block(block, index):
        gain = lax.dynamic_slice_in_dim(attn_gain, index * shard, shard, 0)
        return (block.astype(jnp.float32) * scale * gain).astype(jnp.bfloat16)

    kv_head = tensor_pos * QH_DEV // GROUP
    kv_partial = product(normed_block(rows, tensor_pos), kv_weight)
    kv_all = sum_tensor(kv_partial).astype(jnp.bfloat16)
    new_kv = lax.dynamic_slice_in_dim(kv_all, kv_head * 2 * HEAD, 2 * HEAD, 1)
    cache = lax.dynamic_slice_in_dim(kv_cache, kv_head * 2 * HEAD, 2 * HEAD, 2).reshape(-1, 2 * HEAD)
    both_cache = jnp.concatenate([cache, swap_dp(cache)], axis=0)
    both_ctx = jnp.concatenate([ctx_len, swap_dp(ctx_len)], axis=0)
    keys = jnp.concatenate([both_cache[:, :HEAD], new_kv[:, :HEAD]], axis=0)
    vals = jnp.concatenate([both_cache[:, HEAD:], new_kv[:, HEAD:]], axis=0)
    both_seqs = 2 * seqs_count
    slot_seg = lax.broadcasted_iota(jnp.int32, (both_seqs, ctx_slots), 0).reshape(-1)
    slot_pos = lax.broadcasted_iota(jnp.int32, (both_seqs, ctx_slots), 1).reshape(-1)
    slot_len = jnp.broadcast_to(both_ctx[:, None], (both_seqs, ctx_slots)).reshape(-1)
    ctx_ok = (slot_seg[None, :] == seg[:, None]) & (slot_pos < slot_len)[None, :]
    own_ok = (seg[None, :] == seg[:, None]) & (slot[None, :] <= slot[:, None])
    allowed = jnp.concatenate([ctx_ok, own_ok], axis=1)

    query = 0.0
    for block, index, weight in zip(gather_blocks(rows), gathered_ids(), q_blocks):
        query = query + product(normed_block(block, index), weight)
    query = query.astype(jnp.bfloat16).reshape(half, QH_DEV, HEAD)
    scores = jnp.einsum("rhe,ke->hrk", query, keys, preferred_element_type=jnp.float32) * HEAD ** (
        -0.5
    )
    scores = jnp.where(allowed[None], scores, -jnp.inf)
    top = jnp.max(scores, axis=2, keepdims=True)
    weights = jnp.exp(scores - top)
    probs = (weights / jnp.sum(weights, axis=2, keepdims=True)).astype(jnp.bfloat16)
    attn = jnp.einsum("hrk,ke->rhe", probs, vals, preferred_element_type=jnp.float32)
    attn = attn.astype(jnp.bfloat16).reshape(half, QH_DEV * HEAD)

    partial = None
    for k in range(tensor_count // SIDE):
        mine = product(attn, out_blocks[2 * k]).astype(jnp.bfloat16).astype(jnp.float32)
        theirs = product(attn, out_blocks[2 * k + 1]).astype(jnp.bfloat16)
        total = mine + swap_side(theirs).astype(jnp.float32)
        if partial is not None:
            total = total + ring_step(partial).astype(jnp.float32)
        partial = total.astype(jnp.bfloat16)
    mixed = rows_f + total

    square_sum = sum_tensor(jnp.sum(mixed * mixed, axis=1)[None, :])[0]
    scale = lax.rsqrt(square_sum / full_width + EPS)[:, None]
    gain = lax.dynamic_slice_in_dim(final_gain, tensor_pos * shard, shard, 0)
    final_rows = (mixed * scale * gain).astype(jnp.bfloat16)
    logits = 0.0
    for block, weight in zip(gather_blocks(final_rows), vocab_blocks):
        logits = logits + product(block, weight)
    vocab_count = vocab_weight.shape[1]
    column_ids = tensor_pos * vocab_count + lax.broadcasted_iota(jnp.int32, (half, vocab_count), 1)
    picked = jnp.sum(jnp.where(column_ids == targets[:, None], logits, 0.0), axis=1)
    top = jnp.max(logits, axis=1)
    total = jnp.sum(jnp.exp(logits - top[:, None]), axis=1)

    def join(a, b, step):
        first = (tensor_pos // step) % 2 == 0
        a, b = jnp.where(first, a, b), jnp.where(first, b, a)
        top = jnp.maximum(a[0], b[0])
        total = a[1] * jnp.exp(a[0] - top) + b[1] * jnp.exp(b[0] - top)
        return jnp.stack([top, total, a[2] + b[2]])

    top, total, picked = doubling(jnp.stack([top, total, picked]), join)
    logprob = (picked - top - jnp.log(total))[None, :]

    layer_rows = mixed.astype(jnp.bfloat16)
    layer_rows = jnp.concatenate([layer_rows, swap_dp(layer_rows)], axis=0)
    layer_out = lax.dot_general(
        pick, layer_rows, (((0,), (0,)), ((), ())), preferred_element_type=jnp.float32
    ).astype(jnp.bfloat16)
    both_logprob = jnp.concatenate([logprob, swap_dp(logprob)], axis=1)
    both_pick = jnp.concatenate([keep_pick, send_pick], axis=0)
    token_logprob = jnp.sum(jnp.where(both_pick, both_logprob.reshape(-1, 1), 0.0), axis=0)
    return (layer_out, token_logprob)


def solution(mesh):
    placed = (
        P(("rep", "dp"), "tensor"),
        P(),
        P("dp", "tensor"),
        P("tensor", None),
        P(("rep", "dp"), None, None),
        P("tensor", "dp"),
        P(),
        P("dp", "tensor"),
        P("rep"),
        P(("rep", "dp")),
        P("rep"),
    )
    return jax.shard_map(
        per_device,
        mesh=mesh,
        in_specs=placed,
        out_specs=(P(("rep", "dp"), "tensor"), P(("rep", "dp"))),
        check_vma=False,
    )
```

time: 399 us -> 199 us (0.50)
  waiting for transfers between devices: 281 us -> 104 us
  blocking collectives: 59.4 us -> 0 us
  starting transfers between devices: 0.29 us -> 31.5 us
  matrix products: 23.2 us -> 42.7 us
  between operations: 15.9 us -> 3.13 us
    psum x2 -> x0, waiting for transfers between devices: 158 us -> none  [the longest x1 90.6 us: per_device(): kv_all = lax.psum(kv_partial.astype(jnp.bfloat16), 'tensor')]
    all_gather x5 -> x0, waiting for transfers between devices: 121 us -> none  [the longest x1 120 us: per_device(): lax.all_gather(hidden, 'tensor', axis=1, tiled=True)]
    ppermute x0 -> x41, waiting for transfers between devices: none -> 104 us  [the longest x9 57.2 us: ring_step(): lax.ppermute(value, 'tensor', [(i, (i + SIDE) % count) for i in range(cou...]
    psum x2 -> x0, blocking collectives: 40.3 us -> none  [the longest x1 23.1 us: per_device(): square_sum = lax.psum(jnp.sum(rows_f * rows_f, axis=1), 'tensor')]
    ppermute x0 -> x41, starting transfers between devices: none -> 31.5 us  [the longest x12 14.7 us: doubling(): other = lax.ppermute(value, 'tensor', [(i, i ^ step) for i in range(count)])]
    pmax x1 -> x0, blocking collectives: 19.1 us -> none  [finish(): top = lax.pmax(jnp.max(logits, axis=1), 'tensor')]
    dot_general x4 -> x27, matrix products: 20.9 us -> 38.9 us  [the longest x26 37.7 us: product(): return jnp.dot(left, right, preferred_element_type=jnp.float32)]
    select_n x1 -> x7, other arithmetic: 1.22 us -> 5.37 us  [the longest x1 1.37 us: per_device(): busy_lens = jnp.where(busy, own_lens, other_lens)]
  transfers between devices with their start and end apart: 7 -> 41, of which waited for: 4 -> 23; matrix products, arithmetic and copies ran while one was open for 6% -> 25% of each run, Pallas kernels for 0% -> 0%
where the time goes in v1:
time: 199 us; the launch traced here: 198 us
  waiting for transfers between devices  104 us (52%)
  matrix products  42.7 us (21%)
  starting transfers between devices  31.5 us (16%)
  other arithmetic  14.5 us (7%)
  between operations  3.13 us (2%)
    ppermute x9, waiting for transfers between devices, ring_step(): lax.ppermute(value, 'tensor', [(i, (i + SIDE) % count) for i in range(cou...  57.2 us
    ppermute x12, waiting for transfers between devices, doubling(): other = lax.ppermute(value, 'tensor', [(i, i ^ step) for i in range(count)])  37.7 us
    dot_general x26, matrix products, product(): return jnp.dot(left, right, preferred_element_type=jnp.float32)  37.7 us
    ppermute x12, starting transfers between devices, doubling(): other = lax.ppermute(value, 'tensor', [(i, i ^ step) for i in range(count)])  14.7 us
    ppermute x12, starting transfers between devices, swap_side(): return lax.ppermute(value, 'tensor', [(i, i ^ 1) for i in range(count)])  13.2 us
    ppermute x12, waiting for transfers between devices, swap_side(): return lax.ppermute(value, 'tensor', [(i, i ^ 1) for i in range(count)])  9.28 us
  transfers between devices with their start and end apart: 41, of which 23 were waited for; matrix products, arithmetic and copies ran while one was open for 25% of the time, Pallas kernels for 0%

profile of v1, /device:TPU:0, one launch (start us, length us, event | category | flops | bytes accessed | tf_op | source)
XLA Modules:
  0.0 197.6 jit_solution(11711679016738698225)
XLA Ops:
  0.7 1.4 fusion.241
  2.8 1.4 broadcast_select_fusion.7
  5.0 1.3 and_select_fusion
  8.5 1.3 fusion.223
  10.1 1.3 broadcast_select_fusion.9
  13.8 2.7 %collective-permute-start.2 = (f32[1,128]{1,0:T(1,128)S(1)}, f32[1,128]{1,0:T(1,128)S(1)}, u32[]{:S(2)}, u32[]{:S(2)}) collective-permute-start(f32[1,128]{1,0:T(1,128)S(1)} %bitcast.113), channel_id=1, source_target_pairs={{0,1},{1,0},{2,3},{3,2},{4,5},{5,4},{6,7},{7,6},{8,9},{9,8},{10,11... | collective-permute-start | bytes 1544 | tf_op jit(solution)/shard_map/ppermute | solution.py:37
  16.5 1.5 collective-permute-done.2
  18.0 2.1 %collective-permute-start.3 = (f32[1,128]{1,0:T(1,128)S(1)}, f32[1,128]{1,0:T(1,128)S(1)}, u32[]{:S(2)}, u32[]{:S(2)}) collective-permute-start(f32[1,128]{1,0:T(1,128)S(1)} %bitcast_add_fusion.1), channel_id=1, source_target_pairs={{0,2},{1,3},{2,0},{3,1},{4,6},{5,7},{6,4},{7,5},{8,10},{9,11},{10,... | collective-permute-start | bytes 1544 | tf_op jit(solution)/shard_map/ppermute | solution.py:37
  20.1 1.4 collective-permute-done.3
  21.6 3.0 %collective-permute-start.4 = (f32[1,128]{1,0:T(1,128)S(1)}, f32[1,128]{1,0:T(1,128)S(1)}, u32[]{:S(2)}, u32[]{:S(2)}) collective-permute-start(f32[1,128]{1,0:T(1,128)S(1)} %add.454), channel_id=1, source_target_pairs={{0,4},{1,5},{2,6},{3,7},{4,0},{5,1},{6,2},{7,3},{8,12},{9,13},{10,... | collective-permute-start | bytes 1544 | tf_op jit(solution)/shard_map/ppermute | solution.py:37
  24.7 1.4 collective-permute-done.4
  26.4 1.9 collective-permute-start.5
  28.3 1.4 compare_and_fusion
  29.8 1.6 collective-permute-start.11
  31.5 2.0 collective-permute-start.6
  33.5 5.8 %collective-permute-done.6 = f32[128,256]{1,0:T(8,128)S(1)} collective-permute-done((f32[128,256]{1,0:T(8,128)S(1)}, f32[128,256]{1,0:T(8,128)S(1)}, u32[]{:S(2)}, u32[]{:S(2)}) %collective-permute-start.6) | collective-permute-done | bytes 131104 | tf_op jit(solution)/shard_map/ppermute | solution.py:37
  41.9 6.5 %collective-permute-done.7 = f32[128,256]{1,0:T(8,128)S(1)} collective-permute-done((f32[128,256]{1,0:T(8,128)S(1)}, f32[128,256]{1,0:T(8,128)S(1)}, u32[]{:S(2)}, u32[]{:S(2)}) %collective-permute-start.7) | collective-permute-done | bytes 131104 | tf_op jit(solution)/shard_map/ppermute | solution.py:37
  49.0 9.4 %collective-permute-done.13 = bf16[128,1024]{1,0:T(8,128)(2,1)S(1)} collective-permute-done((bf16[128,1024]{1,0:T(8,128)(2,1)S(1)}, bf16[128,1024]{1,0:T(8,128)(2,1)S(1)}, u32[]{:S(2)}, u32[]{:S(2)}) %collective-permute-start.13) | collective-permute-done | bytes 262176 | tf_op jit(solution)/shard_map/ppermute | solution.py:30
  59.2 1.4 fusion.127
  60.6 1.4 fusion.119
  62.0 6.2 %collective-permute-done.15 = bf16[128,1024]{1,0:T(8,128)(2,1)S(1)} collective-permute-done((bf16[128,1024]{1,0:T(8,128)(2,1)S(1)}, bf16[128,1024]{1,0:T(8,128)(2,1)S(1)}, u32[]{:S(2)}, u32[]{:S(2)}) %collective-permute-start.15) | collective-permute-done | bytes 262176 | tf_op jit(solution)/shard_map/ppermute | solution.py:30
  69.4 1.4 fusion.111
  71.6 1.4 fusion.131
  73.0 1.4 fusion.123
  74.4 2.8 %collective-permute-done.14 = bf16[128,1024]{1,0:T(8,128)(2,1)S(1)} collective-permute-done((bf16[128,1024]{1,0:T(8,128)(2,1)S(1)}, bf16[128,1024]{1,0:T(8,128)(2,1)S(1)}, u32[]{:S(2)}, u32[]{:S(2)}) %collective-permute-start.14) | collective-permute-done | bytes 262176 | tf_op jit(solution)/shard_map/ppermute | solution.py:25
  77.2 1.4 fusion.115
  78.6 1.4 collective-permute-done.16
  80.0 1.4 fusion.107
  81.4 1.4 fusion.30
  83.9 2.7 %convolution_convert_fusion.10 = bf16[128,2,128]{2,0,1:T(8,128)(2,1)S(1)} fusion(f32[2,128]{1,0:T(2,128)S(1)} %fusion.244, bf16[128,128]{1,0:T(8,128)(2,1)} %get-tuple-element.16, bf16[2048,128]{1,0:T(8,128)(2,1)} %fusion.79, pred[128,2176]{0,1:T(8,128)(4,1)} %copy-done.6, bf16[1024,256]{1,0:T(8,128)(2,1)} %copy-done.4, bf16[1024,256]{1,0:T(8,128)(2,1)S(1)} %bitcast.99, ...), kind=kOutput, calls=%fused_computation.47 | convolution fusion | flops 290818432 | bytes 2049024 | tf_op jit(solution)/shard_map/hrk,ke->rhe/dot_general | solution.py:187
  86.6 1.3 convolution_convert_fusion.2
  88.0 1.3 collective-permute-start.21
  89.3 1.3 convolution_convert_fusion.4
  91.5 4.7 %collective-permute-done.21 = bf16[128,1024]{1,0:T(8,128)(2,1)S(1)} collective-permute-done((bf16[128,1024]{1,0:T(8,128)(2,1)S(1)}, bf16[128,1024]{1,0:T(8,128)(2,1)S(1)}, u32[]{:S(2)}, u32[]{:S(2)}) %collective-permute-start.21) | collective-permute-done | bytes 262176 | tf_op jit(solution)/shard_map/ppermute | solution.py:25
  96.2 1.3 fusion.19
  97.6 2.1 %convolution_convert_fusion.6 = bf16[128,1024]{1,0:T(8,128)(2,1)} fusion(bf16[128,256]{0,1:T(8,128)(2,1)S(1)} %bitcast.91, bf16[256,4096]{1,0:T(8,128)(2,1)} %collective-permute-done.17, s32[]{:T(128)S(6)} %select_n.646, bf16[256,4096]{1,0:T(8,128)(2,1)S(1)} %copy-done.2, pred[]{:T(512)S(6)} %eq.196), kind=kOutput, calls=%fused_computation.19 | convolution fusion | flops 67502080 | bytes 1376261 | tf_op jit(solution)/shard_map/dot_general | solution.py:16
  101.2 5.6 %collective-permute-done.22 = bf16[128,1024]{1,0:T(8,128)(2,1)S(1)} collective-permute-done((bf16[128,1024]{1,0:T(8,128)(2,1)S(1)}, bf16[128,1024]{1,0:T(8,128)(2,1)S(1)}, u32[]{:S(2)}, u32[]{:S(2)}) %collective-permute-start.22) | collective-permute-done | bytes 262176 | tf_op jit(solution)/shard_map/ppermute | solution.py:30
  106.8 1.3 fusion.10
  108.3 2.1 %convolution_convert_fusion.8 = bf16[128,1024]{1,0:T(8,128)(2,1)} fusion(bf16[128,256]{0,1:T(8,128)(2,1)S(1)} %bitcast.93, bf16[256,4096]{1,0:T(8,128)(2,1)} %collective-permute-done.17, s32[]{:T(128)S(6)} %select_n.658, bf16[256,4096]{1,0:T(8,128)(2,1)S(1)} %copy-done.2, pred[]{:T(512)S(6)} %eq.198), kind=kOutput, calls=%fused_computation.25 | convolution fusion | flops 67502080 | bytes 1376261 | tf_op jit(solution)/shard_map/dot_general | solution.py:16
  111.7 6.9 %collective-permute-done.23 = bf16[128,1024]{1,0:T(8,128)(2,1)} collective-permute-done((bf16[128,1024]{1,0:T(8,128)(2,1)S(1)}, bf16[128,1024]{1,0:T(8,128)(2,1)}, u32[]{:S(2)}, u32[]{:S(2)}) %collective-permute-start.23) | collective-permute-done | bytes 262176 | tf_op jit(solution)/shard_map/ppermute | solution.py:30
  118.6 1.4 fusion.14
  120.1 8.1 %collective-permute-done.24 = bf16[128,1024]{1,0:T(8,128)(2,1)S(1)} collective-permute-done((bf16[128,1024]{1,0:T(8,128)(2,1)S(1)}, bf16[128,1024]{1,0:T(8,128)(2,1)S(1)}, u32[]{:S(2)}, u32[]{:S(2)}) %collective-permute-start.24) | collective-permute-done | bytes 262176 | tf_op jit(solution)/shard_map/ppermute | solution.py:30
  128.2 1.5 multiply_reduce_fusion
  129.8 1.4 collective-permute-start.26
  131.1 2.2 %collective-permute-done.26 = f32[1,128]{1,0:T(1,128)S(1)} collective-permute-done((f32[1,128]{1,0:T(1,128)S(1)}, f32[1,128]{1,0:T(1,128)S(1)}, u32[]{:S(2)}, u32[]{:S(2)}) %collective-permute-start.26) | collective-permute-done | bytes 544 | tf_op jit(solution)/shard_map/ppermute | solution.py:37
  133.4 3.5 %collective-permute-done.27 = f32[1,128]{1,0:T(1,128)S(1)} collective-permute-done((f32[1,128]{1,0:T(1,128)S(1)}, f32[1,128]{1,0:T(1,128)S(1)}, u32[]{:S(2)}, u32[]{:S(2)}) %collective-permute-start.27) | collective-permute-done | bytes 544 | tf_op jit(solution)/shard_map/ppermute | solution.py:37
  136.9 4.5 %collective-permute-done.28 = f32[1,128]{1,0:T(1,128)S(1)} collective-permute-done((f32[1,128]{1,0:T(1,128)S(1)}, f32[1,128]{1,0:T(1,128)S(1)}, u32[]{:S(2)}, u32[]{:S(2)}) %collective-permute-start.28) | collective-permute-done | bytes 544 | tf_op jit(solution)/shard_map/ppermute | solution.py:37
  141.6 10.3 %collective-permute-done.31 = bf16[128,1024]{1,0:T(8,128)(2,1)S(1)} collective-permute-done((bf16[128,1024]{1,0:T(8,128)(2,1)S(1)}, bf16[128,1024]{1,0:T(8,128)(2,1)S(1)}, u32[]{:S(2)}, u32[]{:S(2)}) %collective-permute-start.31) | collective-permute-done | bytes 262176 | tf_op jit(solution)/shard_map/ppermute | solution.py:30
  152.6 7.5 %collective-permute-done.33 = bf16[128,1024]{1,0:T(8,128)(2,1)S(1)} collective-permute-done((bf16[128,1024]{1,0:T(8,128)(2,1)S(1)}, bf16[128,1024]{1,0:T(8,128)(2,1)S(1)}, u32[]{:S(2)}, u32[]{:S(2)}) %collective-permute-start.33) | collective-permute-done | bytes 262176 | tf_op jit(solution)/shard_map/ppermute | solution.py:30
  160.1 1.3 broadcast_select_fusion.8
  161.6 1.4 collective-permute-start.30
  163.7 1.3 collective-permute-start.34
  165.0 3.2 %collective-permute-done.35 = bf16[128,1024]{1,0:T(8,128)(2,1)S(1)} collective-permute-done((bf16[128,1024]{1,0:T(8,128)(2,1)S(1)}, bf16[128,1024]{1,0:T(8,128)(2,1)S(1)}, u32[]{:S(2)}, u32[]{:S(2)}) %collective-permute-start.35) | collective-permute-done | bytes 262176 | tf_op jit(solution)/shard_map/ppermute | solution.py:30
  169.5 1.9 fusion.48
  171.5 1.9 fusion.41
  173.5 1.6 fusion.52
  175.1 1.6 fusion.22
  176.7 1.6 fusion.21
  178.4 1.6 fusion.34
  180.0 1.6 fusion.20
  181.7 1.7 fusion.249
  184.5 2.8 %collective-permute-done.37 = f32[3,128]{1,0:T(4,128)S(1)} collective-permute-done((f32[3,128]{1,0:T(4,128)S(1)}, f32[3,128]{1,0:T(4,128)S(1)}, u32[]{:S(2)}, u32[]{:S(2)}) %collective-permute-start.37) | collective-permute-done | bytes 1568 | tf_op jit(solution)/shard_map/ppermute | solution.py:37
  187.5 3.5 %collective-permute-done.38 = f32[3,128]{1,0:T(4,128)S(1)} collective-permute-done((f32[3,128]{1,0:T(4,128)S(1)}, f32[3,128]{1,0:T(4,128)S(1)}, u32[]{:S(2)}, u32[]{:S(2)}) %collective-permute-start.38) | collective-permute-done | bytes 1568 | tf_op jit(solution)/shard_map/ppermute | solution.py:37
  191.2 4.4 %collective-permute-done.39 = f32[3,128]{1,0:T(4,128)S(1)} collective-permute-done((f32[3,128]{1,0:T(4,128)S(1)}, f32[3,128]{1,0:T(4,128)S(1)}, u32[]{:S(2)}, u32[]{:S(2)}) %collective-permute-start.39) | collective-permute-done | bytes 1568 | tf_op jit(solution)/shard_map/ppermute | solution.py:37
  (122 shorter events, 22.5 us)
Async XLA Ops:
  0.6 5.9 %copy-start = (bf16[256,1024]{1,0:T(8,128)(2,1)S(1)}, bf16[256,1024]{1,0:T(8,128)(2,1)}, u32[]{:S(2)}) copy-start(bf16[256,1024]{1,0:T(8,128)(2,1)} %param.11) | copy-start | bytes 1572868
  0.6 19.4 %copy-start.11 = (s32[4]{0:T(128)S(1)}, s32[4]{0:T(128)}, u32[]{:S(2)}) copy-start(s32[4]{0:T(128)} %param.20) | copy-start | bytes 52
  0.7 25.5 %copy-start.5 = (bf16[1024,256]{1,0:T(8,128)(2,1)S(1)}, bf16[1024,256]{1,0:T(8,128)(2,1)}, u32[]{:S(2)}) copy-start(bf16[1024,256]{1,0:T(8,128)(2,1)} %param.14) | copy-start | bytes 1572868
  6.9 33.2 %copy-start.3 = (bf16[4,256,256]{2,1,0:T(8,128)(2,1)S(1)}, bf16[4,256,256]{2,1,0:T(8,128)(2,1)}, u32[]{:S(2)}) copy-start(bf16[4,256,256]{2,1,0:T(8,128)(2,1)} %param.15) | copy-start | bytes 1572868
  6.9 5.7 %collective-permute-start = (bf16[128,1024]{1,0:T(8,128)(2,1)S(1)}, bf16[128,1024]{1,0:T(8,128)(2,1)}, u32[]{:S(2)}, u32[]{:S(2)}) collective-permute-start(bf16[128,1024]{1,0:T(8,128)(2,1)S(1)} %slice.103), channel_id=1, source_target_pairs={{0,8},{8,0},{1,9},{9,1},{2,10},{10,2},{3,11},{11,3},{4,12},{12,4},... | collective-permute-start | bytes 786440 | tf_op jit(solution)/shard_map/ppermute | solution.py:20
  7.5 51.7 %collective-permute-start.9 = (bf16[4096,256]{1,0:T(8,128)(2,1)}, bf16[4096,256]{1,0:T(8,128)(2,1)}, u32[]{:S(2)}, u32[]{:S(2)}) collective-permute-start(bf16[4096,256]{1,0:T(8,128)(2,1)} %param.13), channel_id=1, source_target_pairs={{0,8},{8,0},{1,9},{9,1},{2,10},{10,2},{3,11},{11,3},{4,12},{12,4},... | collective-permute-start | bytes 6291464 | tf_op jit(solution)/shard_map/ppermute | solution.py:20
  7.5 12.5 %collective-permute-start.8 = (s32[4]{0:T(128)}, s32[4]{0:T(128)S(1)}, u32[]{:S(2)}, u32[]{:S(2)}) collective-permute-start(s32[4]{0:T(128)} %param.20), channel_id=1, source_target_pairs={{0,8},{8,0},{1,9},{9,1},{2,10},{10,2},{3,11},{11,3},{4,12},{12,4},... | collective-permute-start | bytes 56 | tf_op jit(solution)/shard_map/ppermute | solution.py:20
  8.0 31.4 %collective-permute-start.1 = (bf16[1024,256]{1,0:T(8,128)(2,1)}, bf16[1024,256]{1,0:T(8,128)(2,1)S(1)}, u32[]{:S(2)}, u32[]{:S(2)}) collective-permute-start(bf16[1024,256]{1,0:T(8,128)(2,1)} %bitcast.96), channel_id=1, source_target_pairs={{0,8},{8,0},{1,9},{9,1},{2,10},{10,2},{3,11},{11,3},{4,12},{12,4},... | collective-permute-start | bytes 1572872 | tf_op jit(solution)/shard_map/ppermute | solution.py:20
  8.1 78.6 %collective-permute-start.17 = (bf16[256,4096]{1,0:T(8,128)(2,1)}, bf16[256,4096]{1,0:T(8,128)(2,1)}, u32[]{:S(2)}, u32[]{:S(2)}) collective-permute-start(bf16[256,4096]{1,0:T(8,128)(2,1)} %param.16), channel_id=1, source_target_pairs={{0,8},{8,0},{1,9},{9,1},{2,10},{10,2},{3,11},{11,3},{4,12},{12,4},... | collective-permute-start | bytes 6291464 | tf_op jit(solution)/shard_map/ppermute | solution.py:20
  13.8 4.2 %collective-permute-start.2 = (f32[1,128]{1,0:T(1,128)S(1)}, f32[1,128]{1,0:T(1,128)S(1)}, u32[]{:S(2)}, u32[]{:S(2)}) collective-permute-start(f32[1,128]{1,0:T(1,128)S(1)} %bitcast.113), channel_id=1, source_target_pairs={{0,1},{1,0},{2,3},{3,2},{4,5},{5,4},{6,7},{7,6},{8,9},{9,8},{10,11... | collective-permute-start | bytes 1544 | tf_op jit(solution)/shard_map/ppermute | solution.py:37
  18.0 3.6 %collective-permute-start.3 = (f32[1,128]{1,0:T(1,128)S(1)}, f32[1,128]{1,0:T(1,128)S(1)}, u32[]{:S(2)}, u32[]{:S(2)}) collective-permute-start(f32[1,128]{1,0:T(1,128)S(1)} %bitcast_add_fusion.1), channel_id=1, source_target_pairs={{0,2},{1,3},{2,0},{3,1},{4,6},{5,7},{6,4},{7,5},{8,10},{9,11},{10,... | collective-permute-start | bytes 1544 | tf_op jit(solution)/shard_map/ppermute | solution.py:37
  21.6 4.6 %collective-permute-start.4 = (f32[1,128]{1,0:T(1,128)S(1)}, f32[1,128]{1,0:T(1,128)S(1)}, u32[]{:S(2)}, u32[]{:S(2)}) collective-permute-start(f32[1,128]{1,0:T(1,128)S(1)} %add.454), channel_id=1, source_target_pairs={{0,4},{1,5},{2,6},{3,7},{4,0},{5,1},{6,2},{7,3},{8,12},{9,13},{10,... | collective-permute-start | bytes 1544 | tf_op jit(solution)/shard_map/ppermute | solution.py:37
  26.1 33.1 %copy-start.7 = (bf16[4096,256]{1,0:T(8,128)(2,1)S(1)}, bf16[4096,256]{1,0:T(8,128)(2,1)}, u32[]{:S(2)}) copy-start(bf16[4096,256]{1,0:T(8,128)(2,1)} %param.13) | copy-start | bytes 6291460
  26.4 5.0 %collective-permute-start.5 = (f32[128,256]{1,0:T(8,128)S(1)}, f32[128,256]{1,0:T(8,128)S(1)}, u32[]{:S(2)}, u32[]{:S(2)}) collective-permute-start(f32[128,256]{1,0:T(8,128)S(1)} %fusion.155), channel_id=1, source_target_pairs={{0,1},{1,0},{2,3},{3,2},{4,5},{5,4},{6,7},{7,6},{8,9},{9,8},{10,11... | collective-permute-start | bytes 393224 | tf_op jit(solution)/shard_map/ppermute | solution.py:37
  29.8 11.2 %collective-permute-start.11 = (bf16[128,1024]{1,0:T(8,128)(2,1)S(1)}, bf16[128,1024]{1,0:T(8,128)(2,1)S(1)}, u32[]{:S(2)}, u32[]{:S(2)}) collective-permute-start(bf16[128,1024]{1,0:T(8,128)(2,1)S(1)} %get-tuple-element.11), channel_id=1, source_target_pairs={{0,2},{1,3},{2,4},{3,5},{4,6},{5,7},{6,0},{7,1},{8,10},{9,11},{10,... | collective-permute-start | bytes 786440 | tf_op jit(solution)/shard_map/ppermute | solution.py:30
  31.5 7.8 %collective-permute-start.6 = (f32[128,256]{1,0:T(8,128)S(1)}, f32[128,256]{1,0:T(8,128)S(1)}, u32[]{:S(2)}, u32[]{:S(2)}) collective-permute-start(f32[128,256]{1,0:T(8,128)S(1)} %add.458), channel_id=1, source_target_pairs={{0,2},{1,3},{2,0},{3,1},{4,6},{5,7},{6,4},{7,5},{8,10},{9,11},{10,... | collective-permute-start | bytes 393224 | tf_op jit(solution)/shard_map/ppermute | solution.py:37
  33.5 49.3 %copy-start.6 = (pred[128,2176]{0,1:T(8,128)(4,1)}, pred[128,2176]{0,1:T(8,128)(4,1)S(1)}, u32[]{:S(2)}) copy-start(pred[128,2176]{0,1:T(8,128)(4,1)S(1)} %pad_add_fusion) | copy-start | bytes 835588
  39.3 130.2 %collective-permute-start.29 = (bf16[4096,512]{1,0:T(8,128)(2,1)}, bf16[4096,512]{1,0:T(8,128)(2,1)}, u32[]{:S(2)}, u32[]{:S(2)}) collective-permute-start(bf16[4096,512]{1,0:T(8,128)(2,1)} %param.18), channel_id=1, source_target_pairs={{0,8},{8,0},{1,9},{9,1},{2,10},{10,2},{3,11},{11,3},{4,12},{12,4},... | collective-permute-start | bytes 12582920 | tf_op jit(solution)/shard_map/ppermute | solution.py:20
  39.4 43.4 %copy-start.4 = (bf16[1024,256]{1,0:T(8,128)(2,1)}, bf16[1024,256]{1,0:T(8,128)(2,1)S(1)}, u32[]{:S(2)}) copy-start(bf16[1024,256]{1,0:T(8,128)(2,1)S(1)} %collective-permute-done.1) | copy-start | bytes 1572868
  39.4 9.0 %collective-permute-start.7 = (f32[128,256]{1,0:T(8,128)S(1)}, f32[128,256]{1,0:T(8,128)S(1)}, u32[]{:S(2)}, u32[]{:S(2)}) collective-permute-start(f32[128,256]{1,0:T(8,128)S(1)} %add.459), channel_id=1, source_target_pairs={{0,4},{1,5},{2,6},{3,7},{4,0},{5,1},{6,2},{7,3},{8,12},{9,13},{10,... | collective-permute-start | bytes 393224 | tf_op jit(solution)/shard_map/ppermute | solution.py:37
  41.0 29.9 %collective-permute-start.10 = (bf16[128,1024]{1,0:T(8,128)(2,1)S(1)}, bf16[128,1024]{1,0:T(8,128)(2,1)S(1)}, u32[]{:S(2)}, u32[]{:S(2)}) collective-permute-start(bf16[128,1024]{1,0:T(8,128)(2,1)S(1)} %get-tuple-element.11), channel_id=1, source_target_pairs={{0,1},{1,0},{2,3},{3,2},{4,5},{5,4},{6,7},{7,6},{8,9},{9,8},{10,11... | collective-permute-start | bytes 786440 | tf_op jit(solution)/shard_map/ppermute | solution.py:25
  48.4 10.1 %collective-permute-start.13 = (bf16[128,1024]{1,0:T(8,128)(2,1)S(1)}, bf16[128,1024]{1,0:T(8,128)(2,1)S(1)}, u32[]{:S(2)}, u32[]{:S(2)}) collective-permute-start(bf16[128,1024]{1,0:T(8,128)(2,1)S(1)} %collective-permute-done.11), channel_id=1, source_target_pairs={{0,2},{1,3},{2,4},{3,5},{4,6},{5,7},{6,0},{7,1},{8,10},{9,11},{10,... | collective-permute-start | bytes 786440 | tf_op jit(solution)/shard_map/ppermute | solution.py:30
  49.0 33.8 %copy-start.9 = (bf16[128,128]{1,0:T(8,128)(2,1)}, bf16[128,128]{1,0:T(8,128)(2,1)S(1)}, u32[]{:S(2)}) copy-start(bf16[128,128]{1,0:T(8,128)(2,1)S(1)} %get-tuple-element.17) | copy-start | bytes 98308
  58.4 14.6 %collective-permute-start.12 = (bf16[128,1024]{1,0:T(8,128)(2,1)S(1)}, bf16[128,1024]{1,0:T(8,128)(2,1)S(1)}, u32[]{:S(2)}, u32[]{:S(2)}) collective-permute-start(bf16[128,1024]{1,0:T(8,128)(2,1)S(1)} %collective-permute-done.11), channel_id=1, source_target_pairs={{0,1},{1,0},{2,3},{3,2},{4,5},{5,4},{6,7},{7,6},{8,9},{9,8},{10,11... | collective-permute-start | bytes 786440 | tf_op jit(solution)/shard_map/ppermute | solution.py:25
  59.2 9.0 %collective-permute-start.15 = (bf16[128,1024]{1,0:T(8,128)(2,1)S(1)}, bf16[128,1024]{1,0:T(8,128)(2,1)S(1)}, u32[]{:S(2)}, u32[]{:S(2)}) collective-permute-start(bf16[128,1024]{1,0:T(8,128)(2,1)S(1)} %collective-permute-done.13), channel_id=1, source_target_pairs={{0,2},{1,3},{2,4},{3,5},{4,6},{5,7},{6,0},{7,1},{8,10},{9,11},{10,... | collective-permute-start | bytes 786440 | tf_op jit(solution)/shard_map/ppermute | solution.py:30
  68.2 9.1 %collective-permute-start.14 = (bf16[128,1024]{1,0:T(8,128)(2,1)S(1)}, bf16[128,1024]{1,0:T(8,128)(2,1)S(1)}, u32[]{:S(2)}, u32[]{:S(2)}) collective-permute-start(bf16[128,1024]{1,0:T(8,128)(2,1)S(1)} %collective-permute-done.13), channel_id=1, source_target_pairs={{0,1},{1,0},{2,3},{3,2},{4,5},{5,4},{6,7},{7,6},{8,9},{9,8},{10,11... | collective-permute-start | bytes 786440 | tf_op jit(solution)/shard_map/ppermute | solution.py:25
  70.8 9.2 %collective-permute-start.16 = (bf16[128,1024]{1,0:T(8,128)(2,1)S(1)}, bf16[128,1024]{1,0:T(8,128)(2,1)S(1)}, u32[]{:S(2)}, u32[]{:S(2)}) collective-permute-start(bf16[128,1024]{1,0:T(8,128)(2,1)S(1)} %collective-permute-done.15), channel_id=1, source_target_pairs={{0,1},{1,0},{2,3},{3,2},{4,5},{5,4},{6,7},{7,6},{8,9},{9,8},{10,11... | collective-permute-start | bytes 786440 | tf_op jit(solution)/shard_map/ppermute | solution.py:25
  82.8 1.1 copy-start.8
  83.8 2.8 %copy-start.2 = (bf16[256,4096]{1,0:T(8,128)(2,1)S(1)}, bf16[256,4096]{1,0:T(8,128)(2,1)}, u32[]{:S(2)}) copy-start(bf16[256,4096]{1,0:T(8,128)(2,1)} %param.16) | copy-start | bytes 6291460
  88.0 8.2 %collective-permute-start.21 = (bf16[128,1024]{1,0:T(8,128)(2,1)S(1)}, bf16[128,1024]{1,0:T(8,128)(2,1)S(1)}, u32[]{:S(2)}, u32[]{:S(2)}) collective-permute-start(bf16[128,1024]{1,0:T(8,128)(2,1)S(1)} %convolution_convert_fusion.2), channel_id=1, source_target_pairs={{0,1},{1,0},{2,3},{3,2},{4,5},{5,4},{6,7},{7,6},{8,9},{9,8},{10,11... | collective-permute-start | bytes 786440 | tf_op jit(solution)/shard_map/ppermute | solution.py:25
  90.7 10.6 %collective-permute-start.20 = (bf16[128,1024]{1,0:T(8,128)(2,1)S(1)}, bf16[128,1024]{1,0:T(8,128)(2,1)S(1)}, u32[]{:S(2)}, u32[]{:S(2)}) collective-permute-start(bf16[128,1024]{1,0:T(8,128)(2,1)S(1)} %convolution_convert_fusion.4), channel_id=1, source_target_pairs={{0,1},{1,0},{2,3},{3,2},{4,5},{5,4},{6,7},{7,6},{8,9},{9,8},{10,11... | collective-permute-start | bytes 786440 | tf_op jit(solution)/shard_map/ppermute | solution.py:25
  97.5 9.3 %collective-permute-start.22 = (bf16[128,1024]{1,0:T(8,128)(2,1)S(1)}, bf16[128,1024]{1,0:T(8,128)(2,1)S(1)}, u32[]{:S(2)}, u32[]{:S(2)}) collective-permute-start(bf16[128,1024]{1,0:T(8,128)(2,1)S(1)} %fusion.19), channel_id=1, source_target_pairs={{0,2},{1,3},{2,4},{3,5},{4,6},{5,7},{6,0},{7,1},{8,10},{9,11},{10,... | collective-permute-start | bytes 786440 | tf_op jit(solution)/shard_map/ppermute | solution.py:30
  99.6 12.0 %collective-permute-start.19 = (bf16[128,1024]{1,0:T(8,128)(2,1)}, bf16[128,1024]{1,0:T(8,128)(2,1)S(1)}, u32[]{:S(2)}, u32[]{:S(2)}) collective-permute-start(bf16[128,1024]{1,0:T(8,128)(2,1)} %convolution_convert_fusion.6), channel_id=1, source_target_pairs={{0,1},{1,0},{2,3},{3,2},{4,5},{5,4},{6,7},{7,6},{8,9},{9,8},{10,11... | collective-permute-start | bytes 786440 | tf_op jit(solution)/shard_map/ppermute | solution.py:25
  108.2 10.4 %collective-permute-start.23 = (bf16[128,1024]{1,0:T(8,128)(2,1)S(1)}, bf16[128,1024]{1,0:T(8,128)(2,1)}, u32[]{:S(2)}, u32[]{:S(2)}) collective-permute-start(bf16[128,1024]{1,0:T(8,128)(2,1)S(1)} %fusion.10), channel_id=1, source_target_pairs={{0,2},{1,3},{2,4},{3,5},{4,6},{5,7},{6,0},{7,1},{8,10},{9,11},{10,... | collective-permute-start | bytes 786440 | tf_op jit(solution)/shard_map/ppermute | solution.py:30
  110.4 31.1 %dynamic-slice-start = ((f32[8192]{0:T(1024)}, s32[]{:T(128)}), f32[1024]{0:T(1024)S(1)}, s32[]{:S(2)}) async-start(f32[8192]{0:T(1024)} %param.17, s32[]{:T(128)} %select_n.592), calls=%async_computation | async-start | bytes 8704 | tf_op jit(solution)/shard_map/dynamic_slice | solution.py:202
  110.4 9.8 %collective-permute-start.18 = (bf16[128,1024]{1,0:T(8,128)(2,1)}, bf16[128,1024]{1,0:T(8,128)(2,1)}, u32[]{:S(2)}, u32[]{:S(2)}) collective-permute-start(bf16[128,1024]{1,0:T(8,128)(2,1)} %convolution_convert_fusion.8), channel_id=1, source_target_pairs={{0,1},{1,0},{2,3},{3,2},{4,5},{5,4},{6,7},{7,6},{8,9},{9,8},{10,11... | collective-permute-start | bytes 786440 | tf_op jit(solution)/shard_map/ppermute | solution.py:25
  120.0 41.4 %copy-start.10 = (s32[512]{0:T(512)S(1)}, s32[512]{0:T(512)}, u32[]{:S(2)}) copy-start(s32[512]{0:T(512)} %param.21) | copy-start | bytes 6148
  120.0 8.2 %collective-permute-start.24 = (bf16[128,1024]{1,0:T(8,128)(2,1)S(1)}, bf16[128,1024]{1,0:T(8,128)(2,1)S(1)}, u32[]{:S(2)}, u32[]{:S(2)}) collective-permute-start(bf16[128,1024]{1,0:T(8,128)(2,1)S(1)} %fusion.14), channel_id=1, source_target_pairs={{0,2},{1,3},{2,4},{3,5},{4,6},{5,7},{6,0},{7,1},{8,10},{9,11},{10,... | collective-permute-start | bytes 786440 | tf_op jit(solution)/shard_map/ppermute | solution.py:30
  129.8 3.6 %collective-permute-start.26 = (f32[1,128]{1,0:T(1,128)S(1)}, f32[1,128]{1,0:T(1,128)S(1)}, u32[]{:S(2)}, u32[]{:S(2)}) collective-permute-start(f32[1,128]{1,0:T(1,128)S(1)} %bitcast.111), channel_id=1, source_target_pairs={{0,1},{1,0},{2,3},{3,2},{4,5},{5,4},{6,7},{7,6},{8,9},{9,8},{10,11... | collective-permute-start | bytes 1544 | tf_op jit(solution)/shard_map/ppermute | solution.py:37
  133.4 3.5 %collective-permute-start.27 = (f32[1,128]{1,0:T(1,128)S(1)}, f32[1,128]{1,0:T(1,128)S(1)}, u32[]{:S(2)}, u32[]{:S(2)}) collective-permute-start(f32[1,128]{1,0:T(1,128)S(1)} %bitcast_add_fusion), channel_id=1, source_target_pairs={{0,2},{1,3},{2,0},{3,1},{4,6},{5,7},{6,4},{7,5},{8,10},{9,11},{10,... | collective-permute-start | bytes 1544 | tf_op jit(solution)/shard_map/ppermute | solution.py:37
  136.9 4.5 %collective-permute-start.28 = (f32[1,128]{1,0:T(1,128)S(1)}, f32[1,128]{1,0:T(1,128)S(1)}, u32[]{:S(2)}, u32[]{:S(2)}) collective-permute-start(f32[1,128]{1,0:T(1,128)S(1)} %add.519), channel_id=1, source_target_pairs={{0,4},{1,5},{2,6},{3,7},{4,0},{5,1},{6,2},{7,3},{8,12},{9,13},{10,... | collective-permute-start | bytes 1544 | tf_op jit(solution)/shard_map/ppermute | solution.py:37
  141.5 10.3 %collective-permute-start.31 = (bf16[128,1024]{1,0:T(8,128)(2,1)S(1)}, bf16[128,1024]{1,0:T(8,128)(2,1)S(1)}, u32[]{:S(2)}, u32[]{:S(2)}) collective-permute-start(bf16[128,1024]{1,0:T(8,128)(2,1)S(1)} %get-tuple-element.14), channel_id=1, source_target_pairs={{0,2},{1,3},{2,4},{3,5},{4,6},{5,7},{6,0},{7,1},{8,10},{9,11},{10,... | collective-permute-start | bytes 786440 | tf_op jit(solution)/shard_map/ppermute | solution.py:30
  151.9 8.2 %collective-permute-start.33 = (bf16[128,1024]{1,0:T(8,128)(2,1)S(1)}, bf16[128,1024]{1,0:T(8,128)(2,1)S(1)}, u32[]{:S(2)}, u32[]{:S(2)}) collective-permute-start(bf16[128,1024]{1,0:T(8,128)(2,1)S(1)} %collective-permute-done.31), channel_id=1, source_target_pairs={{0,2},{1,3},{2,4},{3,5},{4,6},{5,7},{6,0},{7,1},{8,10},{9,11},{10,... | collective-permute-start | bytes 786440 | tf_op jit(solution)/shard_map/ppermute | solution.py:30
  160.1 8.2 %collective-permute-start.35 = (bf16[128,1024]{1,0:T(8,128)(2,1)S(1)}, bf16[128,1024]{1,0:T(8,128)(2,1)S(1)}, u32[]{:S(2)}, u32[]{:S(2)}) collective-permute-start(bf16[128,1024]{1,0:T(8,128)(2,1)S(1)} %collective-permute-done.33), channel_id=1, source_target_pairs={{0,2},{1,3},{2,4},{3,5},{4,6},{5,7},{6,0},{7,1},{8,10},{9,11},{10,... | collective-permute-start | bytes 786440 | tf_op jit(solution)/shard_map/ppermute | solution.py:30
  161.6 11.8 %copy-start.1 = (bf16[4096,512]{1,0:T(8,128)(2,1)S(1)}, bf16[4096,512]{1,0:T(8,128)(2,1)}, u32[]{:S(2)}) copy-start(bf16[4096,512]{1,0:T(8,128)(2,1)} %param.18) | copy-start | bytes 12582916
  161.6 11.8 %collective-permute-start.30 = (bf16[128,1024]{1,0:T(8,128)(2,1)S(1)}, bf16[128,1024]{1,0:T(8,128)(2,1)S(1)}, u32[]{:S(2)}, u32[]{:S(2)}) collective-permute-start(bf16[128,1024]{1,0:T(8,128)(2,1)S(1)} %get-tuple-element.14), channel_id=1, source_target_pairs={{0,1},{1,0},{2,3},{3,2},{4,5},{5,4},{6,7},{7,6},{8,9},{9,8},{10,11... | collective-permute-start | bytes 786440 | tf_op jit(solution)/shard_map/ppermute | solution.py:25
  163.0 13.8 %collective-permute-start.32 = (bf16[128,1024]{1,0:T(8,128)(2,1)S(1)}, bf16[128,1024]{1,0:T(8,128)(2,1)S(1)}, u32[]{:S(2)}, u32[]{:S(2)}) collective-permute-start(bf16[128,1024]{1,0:T(8,128)(2,1)S(1)} %collective-permute-done.31), channel_id=1, source_target_pairs={{0,1},{1,0},{2,3},{3,2},{4,5},{5,4},{6,7},{7,6},{8,9},{9,8},{10,11... | collective-permute-start | bytes 786440 | tf_op jit(solution)/shard_map/ppermute | solution.py:25
  163.7 16.3 %collective-permute-start.34 = (bf16[128,1024]{1,0:T(8,128)(2,1)S(1)}, bf16[128,1024]{1,0:T(8,128)(2,1)S(1)}, u32[]{:S(2)}, u32[]{:S(2)}) collective-permute-start(bf16[128,1024]{1,0:T(8,128)(2,1)S(1)} %collective-permute-done.33), channel_id=1, source_target_pairs={{0,1},{1,0},{2,3},{3,2},{4,5},{5,4},{6,7},{7,6},{8,9},{9,8},{10,11... | collective-permute-start | bytes 786440 | tf_op jit(solution)/shard_map/ppermute | solution.py:25
  168.2 13.5 %collective-permute-start.36 = (bf16[128,1024]{1,0:T(8,128)(2,1)S(1)}, bf16[128,1024]{1,0:T(8,128)(2,1)S(1)}, u32[]{:S(2)}, u32[]{:S(2)}) collective-permute-start(bf16[128,1024]{1,0:T(8,128)(2,1)S(1)} %collective-permute-done.35), channel_id=1, source_target_pairs={{0,1},{1,0},{2,3},{3,2},{4,5},{5,4},{6,7},{7,6},{8,9},{9,8},{10,11... | collective-permute-start | bytes 786440 | tf_op jit(solution)/shard_map/ppermute | solution.py:25
  183.7 3.7 %collective-permute-start.37 = (f32[3,128]{1,0:T(4,128)S(1)}, f32[3,128]{1,0:T(4,128)S(1)}, u32[]{:S(2)}, u32[]{:S(2)}) collective-permute-start(f32[3,128]{1,0:T(4,128)S(1)} %pad_maximum_fusion.1), channel_id=1, source_target_pairs={{0,1},{1,0},{2,3},{3,2},{4,5},{5,4},{6,7},{7,6},{8,9},{9,8},{10,11... | collective-permute-start | bytes 4616 | tf_op jit(solution)/shard_map/ppermute | solution.py:37
  187.4 3.7 %collective-permute-start.38 = (f32[3,128]{1,0:T(4,128)S(1)}, f32[3,128]{1,0:T(4,128)S(1)}, u32[]{:S(2)}, u32[]{:S(2)}) collective-permute-start(f32[3,128]{1,0:T(4,128)S(1)} %pad_maximum_fusion.2), channel_id=1, source_target_pairs={{0,2},{1,3},{2,0},{3,1},{4,6},{5,7},{6,4},{7,5},{8,10},{9,11},{10,... | collective-permute-start | bytes 4616 | tf_op jit(solution)/shard_map/ppermute | solution.py:37
  191.1 4.5 %collective-permute-start.39 = (f32[3,128]{1,0:T(4,128)S(1)}, f32[3,128]{1,0:T(4,128)S(1)}, u32[]{:S(2)}, u32[]{:S(2)}) collective-permute-start(f32[3,128]{1,0:T(4,128)S(1)} %pad_maximum_fusion.3), channel_id=1, source_target_pairs={{0,4},{1,5},{2,6},{3,7},{4,0},{5,1},{6,2},{7,3},{8,12},{9,13},{10,... | collective-permute-start | bytes 4616 | tf_op jit(solution)/shard_map/ppermute | solution.py:37
  191.2 4.6 %collective-permute-start.25 = (bf16[128,1024]{1,0:T(8,128)(2,1)S(1)}, bf16[128,1024]{1,0:T(8,128)(2,1)S(1)}, u32[]{:S(2)}, u32[]{:S(2)}) collective-permute-start(bf16[128,1024]{1,0:T(8,128)(2,1)S(1)} %get-tuple-element.15), channel_id=1, source_target_pairs={{0,8},{8,0},{1,9},{9,1},{2,10},{10,2},{3,11},{11,3},{4,12},{12,4},... | collective-permute-start | bytes 786440 | tf_op jit(solution)/shard_map/ppermute | solution.py:20
  195.6 1.2 collective-permute-start.40

commit v2 on v1

v2 whole, which is shorter than its diff:
```python
import functools

import jax
import jax.numpy as jnp
from jax import lax
from jax.experimental import pallas as pl
from jax.experimental.pallas import tpu as pltpu
from jax.sharding import PartitionSpec as P

HEAD = 128
QH_DEV = 2
GROUP = 16
SIDE = 2


EPS = 1e-05
VMEM_LIMIT = 48 * 1024 * 1024


def product(left, right):
    return jnp.dot(left, right, preferred_element_type=jnp.float32)


def swap_dp(value):
    return lax.ppermute(value, "dp", [(0, 1), (1, 0)])


def swap_side(value):
    count = lax.axis_size("tensor")
    return lax.ppermute(value, "tensor", [(i, i ^ 1) for i in range(count)])


def ring_step(value):
    count = lax.axis_size("tensor")
    return lax.ppermute(value, "tensor", [(i, (i + SIDE) % count) for i in range(count)])


def doubling(value, combine):
    count = lax.axis_size("tensor")
    step = 1
    while step < count:
        other = lax.ppermute(value, "tensor", [(i, i ^ step) for i in range(count)])
        value = combine(value, other, step)
        step *= 2
    return value


def sum_tensor(value):
    return doubling(value, lambda a, b, step: a + b)


def gather_blocks(block):
    blocks = []
    for k in range(lax.axis_size("tensor") // SIDE):
        if k > 0:
            block = ring_step(block)
        blocks.append(block)
        blocks.append(swap_side(block))
    return blocks


def gathered_ids():
    count = lax.axis_size("tensor")
    pos = lax.axis_index("tensor")
    ids = []
    for k in range(count // SIDE):
        held = (pos - SIDE * k + count) % count
        ids += [held, held ^ 1]
    return ids


def scattered_ids():
    count = lax.axis_size("tensor")
    pos = lax.axis_index("tensor")
    ids = []
    for k in range(count // SIDE):
        held = (pos - SIDE * (k + 1) + count) % count
        ids += [held, held ^ 1]
    return ids


def row_plan(lens_ref, seqs_count, half):
    group = lax.axis_index("dp")
    own = [lens_ref[group * seqs_count + i] for i in range(seqs_count)]
    other = [lens_ref[(1 - group) * seqs_count + i] for i in range(seqs_count)]
    busy = sum(own) > half
    light_total = jnp.where(busy, sum(other), sum(own))
    own_ends, busy_ends = [], []
    long_seq, long_start = jnp.int32(0), jnp.int32(0)
    own_end, busy_end = jnp.int32(0), jnp.int32(0)
    for i in range(seqs_count):
        length = jnp.where(busy, own[i], other[i])
        long_seq = jnp.where(length == half, i, long_seq)
        long_start = jnp.where(length == half, busy_end, long_start)
        own_end, busy_end = own_end + own[i], busy_end + length
        own_ends.append(own_end)
        busy_ends.append(busy_end)
    return busy, light_total, long_seq, long_start, own_ends, busy_ends


def rest_rows(slot, light_total, long_start, half):
    rest = slot - light_total
    return rest, rest + jnp.where(rest >= long_start, half, 0)


def pack_kernel(seqs_count, lens_ref, hidden_ref, keep_ref, send_ref, pick_ref):
    rows_count = hidden_ref.shape[0]
    half = rows_count // 2
    busy, light_total, _, long_start, _, _ = row_plan(lens_ref, seqs_count, half)
    slot = lax.broadcasted_iota(jnp.int32, (half, rows_count), 0)
    row = lax.broadcasted_iota(jnp.int32, (half, rows_count), 1)
    rest, rest_row = rest_rows(slot, light_total, long_start, half)
    keep_src = jnp.where(busy, long_start + slot, jnp.where(rest < 0, slot, -1))
    send_src = jnp.where(busy & (rest >= 0), rest_row, -1)
    keep_pick = jnp.where(keep_src == row, 1.0, 0.0).astype(jnp.bfloat16)
    send_pick = jnp.where(send_src == row, 1.0, 0.0).astype(jnp.bfloat16)
    pick_ref[:half] = keep_pick
    pick_ref[half:] = send_pick
    hidden = hidden_ref[...]
    send_ref[...] = product(send_pick, hidden).astype(jnp.bfloat16)
    keep_ref[...] = product(keep_pick, hidden).astype(jnp.bfloat16)


def pack(resp_len, hidden, seqs_count):
    rows_count, shard = hidden.shape
    half = rows_count // 2
    vmem = pl.BlockSpec(memory_space=pltpu.VMEM)
    return pl.pallas_call(
        functools.partial(pack_kernel, seqs_count),
        out_shape=[
            jax.ShapeDtypeStruct((half, shard), jnp.bfloat16),
            jax.ShapeDtypeStruct((half, shard), jnp.bfloat16),
            jax.ShapeDtypeStruct((rows_count, rows_count), jnp.bfloat16),
        ],
        in_specs=[pl.BlockSpec(memory_space=pltpu.SMEM), vmem],
        out_specs=[vmem] * 3,
        compiler_params=pltpu.CompilerParams(vmem_limit_bytes=VMEM_LIMIT),
        name="pack_rows",
    )(resp_len, hidden)


def block_copies(ids, axis, own_ref, other_ref, held, sems):
    count = lax.axis_size("tensor")
    group = lax.axis_index("dp")
    size = own_ref.shape[axis] * 2 // count
    copies = []
    for j, block in enumerate(ids):
        place = pl.ds(pl.multiple_of((block % (count // 2)) * size, size), size)
        at = (place, slice(None)) if axis == 0 else (slice(None), place)
        here = pltpu.make_async_copy(own_ref.at[at], held.at[j], sems.at[j])
        there = pltpu.make_async_copy(other_ref.at[at], held.at[j], sems.at[j])
        copies.append((block // (count // 2) == group, here, there))
    return copies


def start_copies(copies):
    for is_here, here, there in copies:
        pl.when(is_here)(here.start)
        pl.when(jnp.logical_not(is_here))(there.start)


def attention_kernel(
    seqs_count,
    count,
    lens_ref,
    ctx_ref,
    gain_ref,
    kv_ref,
    q_own,
    q_other,
    cache_own,
    cache_other,
    out_own,
    out_other,
    *refs,
):
    blocks, outs = refs[:count], refs[count : 2 * count]
    q_held, cache_held, out_held, q_sems, cache_sems, out_sems = refs[2 * count :]
    half, shard = blocks[0].shape
    ctx_slots = cache_own.shape[1]
    ids = gathered_ids()
    q_copies = block_copies(ids, 0, q_own, q_other, q_held, q_sems)
    out_copies = block_copies(scattered_ids(), 1, out_own, out_other, out_held, out_sems)
    cache_copies = [
        pltpu.make_async_copy(cache_own, cache_held.at[0], cache_sems.at[0]),
        pltpu.make_async_copy(cache_other, cache_held.at[1], cache_sems.at[1]),
    ]
    start_copies(q_copies)
    for copy in cache_copies:
        copy.start()
    start_copies(out_copies)

    squares = jnp.zeros((half, 1), jnp.float32)
    for block in blocks:
        values = block[...].astype(jnp.float32)
        squares += jnp.sum(values * values, axis=1, keepdims=True)
    scale = lax.rsqrt(squares / (shard * count) + EPS)
    query = jnp.zeros((half, q_own.shape[1]), jnp.float32)
    for j, block in enumerate(blocks):
        gain = gain_ref[pl.ds(ids[j], 1), :]
        normed = (block[...].astype(jnp.float32) * scale * gain).astype(jnp.bfloat16)
        q_copies[j][1].wait()
        query += product(normed, q_held[j])
    query = query.astype(jnp.bfloat16)
    new_kv = (kv_ref[...] * scale).astype(jnp.bfloat16)

    busy, light_total, long_seq, long_start, own_ends, busy_ends = row_plan(
        lens_ref, seqs_count, half
    )
    slot = lax.broadcasted_iota(jnp.int32, (half, 1), 0)
    rest, rest_row = rest_rows(slot, light_total, long_start, half)
    own_seg, rest_seg = jnp.zeros_like(slot), jnp.full_like(slot, seqs_count)
    for i in range(seqs_count):
        own_seg += jnp.where(slot >= own_ends[i], 1, 0)
        rest_seg += jnp.where(rest_row >= busy_ends[i], 1, 0)
    seg = jnp.where(busy, long_seq, jnp.where(rest < 0, own_seg, rest_seg))
    position = lax.broadcasted_iota(jnp.int32, (half, ctx_slots), 1)
    ctx_ok = jnp.concatenate(
        [(seg == i) & (position < ctx_ref[i]) for i in range(2 * seqs_count)], axis=1
    )
    slot_b = lax.broadcasted_iota(jnp.int32, (half, half), 1)
    rest_b, rest_row_b = rest_rows(slot_b, light_total, long_start, half)
    own_seg_b, rest_seg_b = jnp.zeros_like(slot_b), jnp.full_like(slot_b, seqs_count)
    for i in range(seqs_count):
        own_seg_b += jnp.where(slot_b >= own_ends[i], 1, 0)
        rest_seg_b += jnp.where(rest_row_b >= busy_ends[i], 1, 0)
    seg_b = jnp.where(busy, long_seq, jnp.where(rest_b < 0, own_seg_b, rest_seg_b))
    own_ok = (seg_b == seg) & (slot_b <= slot)

    for copy in cache_copies:
        copy.wait()
    keys = cache_held[:, :, :, :HEAD].reshape(-1, HEAD)
    vals = cache_held[:, :, :, HEAD:].reshape(-1, HEAD)
    heads = []
    for h in range(QH_DEV):
        own_query = query[:, h * HEAD : (h + 1) * HEAD]
        contract = (((1,), (1,)), ((), ()))
        ctx_scores = lax.dot_general(own_query, keys, contract, preferred_element_type=jnp.float32)
        own_scores = lax.dot_general(
            own_query, new_kv[:, :HEAD], contract, preferred_element_type=jnp.float32
        )
        ctx_scores = jnp.where(ctx_ok, ctx_scores * HEAD ** (-0.5), -jnp.inf)
        own_scores = jnp.where(own_ok, own_scores * HEAD ** (-0.5), -jnp.inf)
        top = jnp.maximum(
            jnp.max(ctx_scores, axis=1, keepdims=True), jnp.max(own_scores, axis=1, keepdims=True)
        )
        ctx_weights, own_weights = jnp.exp(ctx_scores - top), jnp.exp(own_scores - top)
        total = jnp.sum(ctx_weights, axis=1, keepdims=True) + jnp.sum(
            own_weights, axis=1, keepdims=True
        )
        heads.append(
            product((ctx_weights / total).astype(jnp.bfloat16), vals)
            + product((own_weights / total).astype(jnp.bfloat16), new_kv[:, HEAD:])
        )
    attn = jnp.concatenate(heads, axis=1).astype(jnp.bfloat16)
    for j, out in enumerate(outs):
        out_copies[j][1].wait()
        out[...] = product(attn, out_held[j]).astype(jnp.bfloat16)


def attend(resp_len, both_ctx, attn_gain, kv_sum, q_pair, cache_pair, out_pair, blocks):
    count = len(blocks)
    half, shard = blocks[0].shape
    seqs_count, ctx_slots, width = cache_pair[0].shape
    q_width, attn_width = q_pair[0].shape[1], out_pair[0].shape[0]
    vmem = pl.BlockSpec(memory_space=pltpu.VMEM)
    smem = pl.BlockSpec(memory_space=pltpu.SMEM)
    anywhere = pl.BlockSpec(memory_space=pl.ANY)
    return pl.pallas_call(
        functools.partial(attention_kernel, seqs_count, count),
        out_shape=[jax.ShapeDtypeStruct((half, shard), jnp.bfloat16)] * count,
        in_specs=[smem] * 2 + [vmem] * 2 + [anywhere] * 6 + [vmem] * count,
        out_specs=[vmem] * count,
        scratch_shapes=[
            pltpu.VMEM((count, shard, q_width), jnp.bfloat16),
            pltpu.VMEM((2, seqs_count, ctx_slots, width), jnp.bfloat16),
            pltpu.VMEM((count, attn_width, shard), jnp.bfloat16),
            pltpu.SemaphoreType.DMA((count,)),
            pltpu.SemaphoreType.DMA((2,)),
            pltpu.SemaphoreType.DMA((count,)),
        ],
        compiler_params=pltpu.CompilerParams(vmem_limit_bytes=VMEM_LIMIT),
        name="attend",
    )(resp_len, both_ctx, attn_gain.reshape(count, shard), kv_sum, *q_pair, *cache_pair, *out_pair, *blocks)


def vocab_kernel(count, targets_ref, squares_ref, own_ref, other_ref, *refs):
    blocks, (stats_ref, held, sems) = refs[:count], refs[count:]
    half, shard = blocks[0].shape
    copies = block_copies(gathered_ids(), 0, own_ref, other_ref, held, sems)
    start_copies(copies)
    scale = lax.rsqrt(squares_ref[...] / (shard * count) + EPS)
    vocab_count = own_ref.shape[1]
    logits = jnp.zeros((half, vocab_count), jnp.float32)
    for j, block in enumerate(blocks):
        copies[j][1].wait()
        logits += product(block[...], held[j])
    logits = logits * scale
    column_ids = lax.axis_index("tensor") * vocab_count + lax.broadcasted_iota(
        jnp.int32, (half, vocab_count), 1
    )
    picked = jnp.sum(
        jnp.where(column_ids == targets_ref[...], logits, 0.0), axis=1, keepdims=True
    )
    top = jnp.max(logits, axis=1, keepdims=True)
    total = jnp.sum(jnp.exp(logits - top), axis=1, keepdims=True)
    lane = lax.broadcasted_iota(jnp.int32, (half, half), 1)
    stats = jnp.where(lane == 0, top, jnp.where(lane == 1, total, picked))
    stats_ref[...] = jnp.transpose(stats)[:8]


def vocab_stats(targets, square_sum, vocab_pair, blocks):
    count = len(blocks)
    half, shard = blocks[0].shape
    vocab_count = vocab_pair[0].shape[1]
    vmem = pl.BlockSpec(memory_space=pltpu.VMEM)
    anywhere = pl.BlockSpec(memory_space=pl.ANY)
    return pl.pallas_call(
        functools.partial(vocab_kernel, count),
        out_shape=jax.ShapeDtypeStruct((8, half), jnp.float32),
        in_specs=[vmem] * 2 + [anywhere] * 2 + [vmem] * count,
        out_specs=vmem,
        scratch_shapes=[
            pltpu.VMEM((count, shard, vocab_count), jnp.bfloat16),
            pltpu.SemaphoreType.DMA((count,)),
        ],
        compiler_params=pltpu.CompilerParams(vmem_limit_bytes=VMEM_LIMIT),
        name="vocab_stats",
    )(targets.reshape(half, 1), square_sum.reshape(half, 1), *vocab_pair, *blocks)


def per_device(
    hidden,
    attn_gain,
    q_weight,
    kv_weight,
    kv_cache,
    out_weight,
    final_gain,
    vocab_weight,
    resp_len,
    ctx_len,
    target_ids,
):
    rows_count, shard = hidden.shape
    half = rows_count // 2
    tensor_count = lax.axis_size("tensor")
    tensor_pos = lax.axis_index("tensor")
    group = lax.axis_index("dp")
    seqs_count = kv_cache.shape[0]

    keep, send, pick = pack(resp_len, hidden, seqs_count)
    rows = keep + swap_dp(send)
    rows_f = rows.astype(jnp.float32)
    blocks = gather_blocks(rows)

    gain = lax.dynamic_slice_in_dim(attn_gain, tensor_pos * shard, shard, 0)
    kv_head = tensor_pos * QH_DEV // GROUP
    kv_partial = product((rows_f * gain).astype(jnp.bfloat16), kv_weight)
    kv_sum = lax.dynamic_slice_in_dim(sum_tensor(kv_partial), kv_head * 2 * HEAD, 2 * HEAD, 1)
    cache = lax.dynamic_slice_in_dim(kv_cache, kv_head * 2 * HEAD, 2 * HEAD, 2)
    both_ctx = jnp.concatenate([ctx_len, swap_dp(ctx_len)], axis=0)
    products = attend(
        resp_len,
        both_ctx,
        attn_gain,
        kv_sum,
        (q_weight, swap_dp(q_weight)),
        (cache, swap_dp(cache)),
        (out_weight, swap_dp(out_weight)),
        blocks,
    )

    partial = None
    for k in range(tensor_count // SIDE):
        total = products[2 * k].astype(jnp.float32) + swap_side(products[2 * k + 1]).astype(jnp.float32)
        if partial is not None:
            total = total + ring_step(partial).astype(jnp.float32)
        partial = total.astype(jnp.bfloat16)
    mixed = rows_f + total

    gain = lax.dynamic_slice_in_dim(final_gain, tensor_pos * shard, shard, 0)
    blocks = gather_blocks((mixed * gain).astype(jnp.bfloat16))
    square_sum = sum_tensor(jnp.sum(mixed * mixed, axis=1)[None, :])[0]
    layer_rows = mixed.astype(jnp.bfloat16)
    layer_rows = jnp.concatenate([layer_rows, swap_dp(layer_rows)], axis=0)
    layer_out = lax.dot_general(
        pick, layer_rows, (((0,), (0,)), ((), ())), preferred_element_type=jnp.float32
    ).astype(jnp.bfloat16)

    own_targets = lax.dynamic_slice_in_dim(target_ids, group * rows_count, rows_count, 0)
    sent_targets = jnp.sum(jnp.where(pick > 0, own_targets[None, :], 0), axis=1)
    targets = sent_targets[:half] + swap_dp(sent_targets[None, half:])[0]
    stats = vocab_stats(targets, square_sum, (vocab_weight, swap_dp(vocab_weight)), blocks)

    def join(a, b, step):
        first = (tensor_pos // step) % 2 == 0
        a, b = jnp.where(first, a, b), jnp.where(first, b, a)
        top = jnp.maximum(a[0], b[0])
        total = a[1] * jnp.exp(a[0] - top) + b[1] * jnp.exp(b[0] - top)
        return jnp.stack([top, total, a[2] + b[2]])

    top, total, picked = doubling(stats[:3], join)
    logprob = (picked - top - jnp.log(total))[None, :]
    both_logprob = jnp.concatenate([logprob, swap_dp(logprob)], axis=1)
    token_logprob = jnp.sum(jnp.where(pick > 0, both_logprob.reshape(-1, 1), 0.0), axis=0)
    return (layer_out, token_logprob)


def solution(mesh):
    placed = (
        P(("rep", "dp"), "tensor"),
        P(),
        P("dp", "tensor"),
        P("tensor", None),
        P(("rep", "dp"), None, None),
        P("tensor", "dp"),
        P(),
        P("dp", "tensor"),
        P("rep"),
        P(("rep", "dp")),
        P("rep"),
    )
    return jax.shard_map(
        per_device,
        mesh=mesh,
        in_specs=placed,
        out_specs=(P(("rep", "dp"), "tensor"), P(("rep", "dp"))),
        check_vma=False,
    )
```

time: 199 us -> 180 us (0.905)
  matrix products: 42.7 us -> 1.35 us
  waiting for transfers between devices: 104 us -> 125 us
  Pallas kernels: 0 us -> 13.1 us
  other arithmetic: 14.5 us -> 2.67 us
  local copies, waits for them, and re-layouts: 1.56 us -> 4.85 us
  between operations: 3.13 us -> 0.93 us
    dot_general x26 -> x1, matrix products: 37.7 us -> 0.23 us  [product(): return jnp.dot(left, right, preferred_element_type=jnp.float32)]
    ppermute x12, waiting for transfers between devices: 9.28 us -> 41.7 us  [swap_side(): return lax.ppermute(value, 'tensor', [(i, i ^ 1) for i in range(count)])]
    pallas_call x0 -> x3, Pallas kernels: none -> 13.1 us  [the longest x1 8.18 us: attend(): pl.pallas_call(functools.partial(attention_kernel, seqs_count, count), ou...]
    ppermute x9, waiting for transfers between devices: 57.2 us -> 46.9 us  [ring_step(): lax.ppermute(value, 'tensor', [(i, (i + SIDE) % count) for i in range(cou...]
    ppermute x12 -> x9, waiting for transfers between devices: 37.7 us -> 32.3 us  [doubling(): other = lax.ppermute(value, 'tensor', [(i, i ^ step) for i in range(count)])]
    select_n x4 -> x0, other arithmetic: 5.34 us -> none  [the longest x1 1.37 us: per_device(): busy_lens = jnp.where(busy, own_lens, other_lens)]
    ppermute x8 -> x9, waiting for transfers between devices: 0.02 us -> 4.46 us  [swap_dp(): return lax.ppermute(value, 'dp', [(0, 1), (1, 0)])]
    reduce_sum x7 -> x2, other arithmetic: 4.45 us -> 0.8 us  [the longest x1 0.68 us: per_device(): jnp.sum(jnp.where(pick > 0, both_logprob.reshape(-1, 1), 0.0), axis=0)]
  transfers between devices with their start and end apart: 41 -> 39, of which waited for: 23 -> 25; matrix products, arithmetic and copies ran while one was open for 25% -> 3% of each run, Pallas kernels for 0% -> 5%
where the time goes in v2:
time: 180 us
  waiting for transfers between devices  125 us (69%)
  starting transfers between devices  31.4 us (17%)
  Pallas kernels  13.1 us (7%)
  local copies, waits for them, and re-layouts  4.85 us (3%)
  other arithmetic  2.67 us (1%)
    ppermute x9, waiting for transfers between devices, ring_step(): lax.ppermute(value, 'tensor', [(i, (i + SIDE) % count) for i in range(cou...  46.9 us
    ppermute x12, waiting for transfers between devices, swap_side(): return lax.ppermute(value, 'tensor', [(i, i ^ 1) for i in range(count)])  41.7 us
    ppermute x9, waiting for transfers between devices, doubling(): other = lax.ppermute(value, 'tensor', [(i, i ^ step) for i in range(count)])  32.3 us
    ppermute x9, starting transfers between devices, doubling(): other = lax.ppermute(value, 'tensor', [(i, i ^ step) for i in range(count)])  15.2 us
    ppermute x12, starting transfers between devices, swap_side(): return lax.ppermute(value, 'tensor', [(i, i ^ 1) for i in range(count)])  14.5 us
    pallas_call x1, Pallas kernels, attend(): pl.pallas_call(functools.partial(attention_kernel, seqs_count, count), ou...  8.18 us
    ppermute x9, waiting for transfers between devices, swap_dp(): return lax.ppermute(value, 'dp', [(0, 1), (1, 0)])  4.46 us
    pallas_call x1, Pallas kernels, vocab_stats(): pl.pallas_call(functools.partial(vocab_kernel, count), out_shape=jax.Shap...  4.06 us
  transfers between devices with their start and end apart: 39, of which 25 were waited for; matrix products, arithmetic and copies ran while one was open for 3% of the time, Pallas kernels for 5%

profile of v2, /device:TPU:0, one launch (start us, length us, event | category | flops | bytes accessed | tf_op | source)
XLA Modules:
  0.0 179.8 jit_solution(5561353226783413693)
XLA Ops:
  0.7 0.5 collective-permute-start.5
  1.3 1.0 copy-done.2
  2.3 0.7 copy-done.4
  3.0 0.9 pack_rows.1
  3.8 0.5 collective-permute-start
  4.3 0.7 dynamic_slice.11
  5.0 3.3 %collective-permute-done = bf16[128,1024]{1,0:T(8,128)(2,1)S(1)} collective-permute-done((bf16[128,1024]{1,0:T(8,128)(2,1)S(1)}, bf16[128,1024]{1,0:T(8,128)(2,1)S(1)}, u32[]{:S(2)}, u32[]{:S(2)}) %collective-permute-start) | collective-permute-done | bytes 262176 | tf_op jit(solution)/shard_map/ppermute | solution.py:25
  8.4 0.2 fusion.4
  8.7 3.0 %collective-permute-start.2 = (f32[128,256]{1,0:T(8,128)S(1)}, f32[128,256]{1,0:T(8,128)S(1)}, u32[]{:S(2)}, u32[]{:S(2)}) collective-permute-start(f32[128,256]{1,0:T(8,128)S(1)} %fusion.4), channel_id=1, source_target_pairs={{0,1},{1,0},{2,3},{3,2},{4,5},{5,4},{6,7},{7,6},{8,9},{9,8},{10,11... | collective-permute-start | bytes 393224 | tf_op jit(solution)/shard_map/ppermute | solution.py:42
  11.6 3.8 %collective-permute-done.2 = f32[128,256]{1,0:T(8,128)S(1)} collective-permute-done((f32[128,256]{1,0:T(8,128)S(1)}, f32[128,256]{1,0:T(8,128)S(1)}, u32[]{:S(2)}, u32[]{:S(2)}) %collective-permute-start.2) | collective-permute-done | bytes 131104 | tf_op jit(solution)/shard_map/ppermute | solution.py:42
  15.4 1.9 %collective-permute-start.3 = (f32[128,256]{1,0:T(8,128)S(1)}, f32[128,256]{1,0:T(8,128)S(1)}, u32[]{:S(2)}, u32[]{:S(2)}) collective-permute-start(f32[128,256]{1,0:T(8,128)S(1)} %add.97), channel_id=1, source_target_pairs={{0,2},{1,3},{2,0},{3,1},{4,6},{5,7},{6,4},{7,5},{8,10},{9,11},{10,... | collective-permute-start | bytes 393224 | tf_op jit(solution)/shard_map/ppermute | solution.py:42
  17.3 1.1 collective-permute-done.1
  18.4 0.2 collective-permute-start.9
  18.6 1.9 %collective-permute-done.3 = f32[128,256]{1,0:T(8,128)S(1)} collective-permute-done((f32[128,256]{1,0:T(8,128)S(1)}, f32[128,256]{1,0:T(8,128)S(1)}, u32[]{:S(2)}, u32[]{:S(2)}) %collective-permute-start.3) | collective-permute-done | bytes 131104 | tf_op jit(solution)/shard_map/ppermute | solution.py:42
  20.6 1.6 collective-permute-start.8
  22.2 6.4 %collective-permute-done.9.refs_2_ = bf16[128,1024]{1,0:T(8,128)(2,1)S(1)} collective-permute-done((bf16[128,1024]{1,0:T(8,128)(2,1)S(1)}, bf16[128,1024]{1,0:T(8,128)(2,1)S(1)}, u32[]{:S(2)}, u32[]{:S(2)}) %collective-permute-start.9) | collective-permute-done | bytes 262176 | tf_op jit(solution)/shard_map/ppermute | solution.py:35
  28.7 1.9 %collective-permute-start.4 = (f32[128,256]{1,0:T(8,128)S(1)}, f32[128,256]{1,0:T(8,128)}, u32[]{:S(2)}, u32[]{:S(2)}) collective-permute-start(f32[128,256]{1,0:T(8,128)S(1)} %add.98), channel_id=1, source_target_pairs={{0,4},{1,5},{2,6},{3,7},{4,0},{5,1},{6,2},{7,3},{8,12},{9,13},{10,... | collective-permute-start | bytes 393224 | tf_op jit(solution)/shard_map/ppermute | solution.py:42
  30.6 13.2 %collective-permute-done.4 = f32[128,256]{1,0:T(8,128)} collective-permute-done((f32[128,256]{1,0:T(8,128)S(1)}, f32[128,256]{1,0:T(8,128)}, u32[]{:S(2)}, u32[]{:S(2)}) %collective-permute-start.4) | collective-permute-done | bytes 131104 | tf_op jit(solution)/shard_map/ppermute | solution.py:42
  43.8 1.5 collective-permute-start.10
  45.3 6.8 %collective-permute-done.10.refs_3_ = bf16[128,1024]{1,0:T(8,128)(2,1)S(1)} collective-permute-done((bf16[128,1024]{1,0:T(8,128)(2,1)S(1)}, bf16[128,1024]{1,0:T(8,128)(2,1)S(1)}, u32[]{:S(2)}, u32[]{:S(2)}) %collective-permute-start.10) | collective-permute-done | bytes 262176 | tf_op jit(solution)/shard_map/ppermute | solution.py:30
  52.0 1.5 collective-permute-start.12
  53.6 1.5 collective-permute-done.13.refs_6_
  55.1 0.5 collective-permute-start.14
  55.6 1.4 reshape.15.gain_ref
  57.0 1.0 add.99.kv_ref
  58.0 3.3 %collective-permute-done.12.refs_5_ = bf16[128,1024]{1,0:T(8,128)(2,1)S(1)} collective-permute-done((bf16[128,1024]{1,0:T(8,128)(2,1)S(1)}, bf16[128,1024]{1,0:T(8,128)(2,1)S(1)}, u32[]{:S(2)}, u32[]{:S(2)}) %collective-permute-start.12) | collective-permute-done | bytes 262176 | tf_op jit(solution)/shard_map/ppermute | solution.py:30
  61.3 3.9 %collective-permute-done.14.refs_7_ = bf16[128,1024]{1,0:T(8,128)(2,1)} collective-permute-done((bf16[128,1024]{1,0:T(8,128)(2,1)S(1)}, bf16[128,1024]{1,0:T(8,128)(2,1)}, u32[]{:S(2)}, u32[]{:S(2)}) %collective-permute-start.14) | collective-permute-done | bytes 262176 | tf_op jit(solution)/shard_map/ppermute | solution.py:30
  65.2 0.7 copy-done.3
  66.0 8.2 %attend.1 = (bf16[128,1024]{1,0:T(8,128)(2,1)S(1)}, bf16[128,1024]{1,0:T(8,128)(2,1)S(1)}, bf16[128,1024]{1,0:T(8,128)(2,1)S(1)}, bf16[128,1024]{1,0:T(8,128)(2,...) custom-call(s32[8]{0:T(128)S(1)} %copy-done.5, ...), custom_call_target="tpu_custom_call" | custom-call | tf_op jit(solution)/shard_map/attend/pallas_call | solution.py:269
  74.2 1.6 collective-permute-start.18
  75.8 0.5 collective-permute-start.17
  76.3 7.2 %collective-permute-done.18 = bf16[128,1024]{1,0:T(8,128)(2,1)S(1)} collective-permute-done((bf16[128,1024]{1,0:T(8,128)(2,1)S(1)}, bf16[128,1024]{1,0:T(8,128)(2,1)S(1)}, u32[]{:S(2)}, u32[]{:S(2)}) %collective-permute-start.18) | collective-permute-done | bytes 262176 | tf_op jit(solution)/shard_map/ppermute | solution.py:30
  83.6 1.6 collective-permute-start.16
  85.2 3.9 %collective-permute-done.17 = bf16[128,1024]{1,0:T(8,128)(2,1)S(1)} collective-permute-done((bf16[128,1024]{1,0:T(8,128)(2,1)S(1)}, bf16[128,1024]{1,0:T(8,128)(2,1)S(1)}, u32[]{:S(2)}, u32[]{:S(2)}) %collective-permute-start.17) | collective-permute-done | bytes 262176 | tf_op jit(solution)/shard_map/ppermute | solution.py:30
  89.1 4.6 %collective-permute-done.19 = bf16[128,1024]{1,0:T(8,128)(2,1)S(1)} collective-permute-done((bf16[128,1024]{1,0:T(8,128)(2,1)S(1)}, bf16[128,1024]{1,0:T(8,128)(2,1)S(1)}, u32[]{:S(2)}, u32[]{:S(2)}) %collective-permute-start.19) | collective-permute-done | bytes 262176 | tf_op jit(solution)/shard_map/ppermute | solution.py:35
  93.7 0.1 add_convert_fusion.1
  93.9 1.6 collective-permute-start.15
  95.5 9.1 %collective-permute-done.20 = bf16[128,1024]{1,0:T(8,128)(2,1)S(1)} collective-permute-done((bf16[128,1024]{1,0:T(8,128)(2,1)S(1)}, bf16[128,1024]{1,0:T(8,128)(2,1)S(1)}, u32[]{:S(2)}, u32[]{:S(2)}) %collective-permute-start.20) | collective-permute-done | bytes 262176 | tf_op jit(solution)/shard_map/ppermute | solution.py:35
  104.6 0.1 add_convert_fusion
  104.8 10.0 %collective-permute-done.21 = bf16[128,1024]{1,0:T(8,128)(2,1)S(1)} collective-permute-done((bf16[128,1024]{1,0:T(8,128)(2,1)S(1)}, bf16[128,1024]{1,0:T(8,128)(2,1)S(1)}, u32[]{:S(2)}, u32[]{:S(2)}) %collective-permute-start.21) | collective-permute-done | bytes 262176 | tf_op jit(solution)/shard_map/ppermute | solution.py:35
  114.8 0.3 multiply_convert_fusion
  115.2 8.8 %collective-permute-done.29.refs_2_ = bf16[128,1024]{1,0:T(8,128)(2,1)S(1)} collective-permute-done((bf16[128,1024]{1,0:T(8,128)(2,1)S(1)}, bf16[128,1024]{1,0:T(8,128)(2,1)S(1)}, u32[]{:S(2)}, u32[]{:S(2)}) %collective-permute-start.29) | collective-permute-done | bytes 262176 | tf_op jit(solution)/shard_map/ppermute | solution.py:35
  124.1 1.5 collective-permute-start.24
  125.7 6.4 %collective-permute-done.31.refs_4_ = bf16[128,1024]{1,0:T(8,128)(2,1)S(1)} collective-permute-done((bf16[128,1024]{1,0:T(8,128)(2,1)S(1)}, bf16[128,1024]{1,0:T(8,128)(2,1)S(1)}, u32[]{:S(2)}, u32[]{:S(2)}) %collective-permute-start.31) | collective-permute-done | bytes 262176 | tf_op jit(solution)/shard_map/ppermute | solution.py:35
  132.3 3.8 %collective-permute-done.25 = f32[1,128]{1,0:T(1,128)S(1)} collective-permute-done((f32[1,128]{1,0:T(1,128)S(1)}, f32[1,128]{1,0:T(1,128)S(1)}, u32[]{:S(2)}, u32[]{:S(2)}) %collective-permute-start.25) | collective-permute-done | bytes 544 | tf_op jit(solution)/shard_map/ppermute | solution.py:42
  136.1 4.8 %collective-permute-start.26 = (f32[1,128]{1,0:T(1,128)S(1)}, f32[1,128]{1,0:T(1,128)S(1)}, u32[]{:S(2)}, u32[]{:S(2)}) collective-permute-start(f32[1,128]{1,0:T(1,128)S(1)} %add.114), channel_id=1, source_target_pairs={{0,4},{1,5},{2,6},{3,7},{4,0},{5,1},{6,2},{7,3},{8,12},{9,13},{10,... | collective-permute-start | bytes 1544 | tf_op jit(solution)/shard_map/ppermute | solution.py:42
  140.9 1.5 collective-permute-start.28
  142.4 0.5 collective-permute-start.30
  142.9 1.5 collective-permute-start.32
  144.4 0.5 collective-permute-start.34
  145.0 0.1 copy.13.targets_ref
  145.2 4.9 %collective-permute-done.28.refs_1_ = bf16[128,1024]{1,0:T(8,128)(2,1)S(1)} collective-permute-done((bf16[128,1024]{1,0:T(8,128)(2,1)S(1)}, bf16[128,1024]{1,0:T(8,128)(2,1)S(1)}, u32[]{:S(2)}, u32[]{:S(2)}) %collective-permute-start.28) | collective-permute-done | bytes 262176 | tf_op jit(solution)/shard_map/ppermute | solution.py:30
  150.1 5.6 %collective-permute-done.30.refs_3_ = bf16[128,1024]{1,0:T(8,128)(2,1)S(1)} collective-permute-done((bf16[128,1024]{1,0:T(8,128)(2,1)S(1)}, bf16[128,1024]{1,0:T(8,128)(2,1)S(1)}, u32[]{:S(2)}, u32[]{:S(2)}) %collective-permute-start.30) | collective-permute-done | bytes 262176 | tf_op jit(solution)/shard_map/ppermute | solution.py:30
  155.7 3.3 %collective-permute-done.32.refs_5_ = bf16[128,1024]{1,0:T(8,128)(2,1)S(1)} collective-permute-done((bf16[128,1024]{1,0:T(8,128)(2,1)S(1)}, bf16[128,1024]{1,0:T(8,128)(2,1)S(1)}, u32[]{:S(2)}, u32[]{:S(2)}) %collective-permute-start.32) | collective-permute-done | bytes 262176 | tf_op jit(solution)/shard_map/ppermute | solution.py:30
  159.1 2.8 %collective-permute-done.34.refs_7_ = bf16[128,1024]{1,0:T(8,128)(2,1)S(1)} collective-permute-done((bf16[128,1024]{1,0:T(8,128)(2,1)S(1)}, bf16[128,1024]{1,0:T(8,128)(2,1)S(1)}, u32[]{:S(2)}, u32[]{:S(2)}) %collective-permute-start.34) | collective-permute-done | bytes 262176 | tf_op jit(solution)/shard_map/ppermute | solution.py:30
  161.9 4.1 %vocab_stats.1 = f32[8,128]{1,0:T(8,128)S(1)} custom-call(s32[128,1]{1,0:T(8,128)S(1)} %copy.13.targets_ref, f32[128,1]{1,0:T(8,128)S(1)} %copy.14.squares_ref, bf16[4096,512]{1,0:T(8,128)(2,1)} %own_ref.1, bf16[4096,512]{1,0:T(8,128)(2,1)} %collective-permute-done.27.other_ref, bf16[128,1024]{1,0:T(8,128)(2,1)S(1)} %get-tuple-element.28.refs_0_, ...), custom_call_target="tpu_custom_call" | custom-call | tf_op jit(solution)/shard_map/vocab_stats/pallas_call | solution.py:318
  165.9 1.6 collective-permute-start.35
  167.5 2.1 %collective-permute-done.35 = f32[3,128]{1,0:T(4,128)S(1)} collective-permute-done((f32[3,128]{1,0:T(4,128)S(1)}, f32[3,128]{1,0:T(4,128)S(1)}, u32[]{:S(2)}, u32[]{:S(2)}) %collective-permute-start.35) | collective-permute-done | bytes 1568 | tf_op jit(solution)/shard_map/ppermute | solution.py:42
  169.6 0.1 collective-permute-start.36
  169.8 3.5 %collective-permute-done.36 = f32[3,128]{1,0:T(4,128)S(1)} collective-permute-done((f32[3,128]{1,0:T(4,128)S(1)}, f32[3,128]{1,0:T(4,128)S(1)}, u32[]{:S(2)}, u32[]{:S(2)}) %collective-permute-start.36) | collective-permute-done | bytes 1568 | tf_op jit(solution)/shard_map/ppermute | solution.py:42
  173.3 0.4 collective-permute-start.37
  173.8 4.1 %collective-permute-done.37 = f32[3,128]{1,0:T(4,128)S(1)} collective-permute-done((f32[3,128]{1,0:T(4,128)S(1)}, f32[3,128]{1,0:T(4,128)S(1)}, u32[]{:S(2)}, u32[]{:S(2)}) %collective-permute-start.37) | collective-permute-done | bytes 1568 | tf_op jit(solution)/shard_map/ppermute | solution.py:42
  178.0 1.1 convolution_convert_fusion
  179.1 0.7 select_reduce_fusion
  (70 shorter events, 1.3 us)
Async XLA Ops:
  0.6 7.8 %copy-start = (bf16[1024,256]{1,0:T(8,128)(2,1)S(1)}, bf16[1024,256]{1,0:T(8,128)(2,1)}, u32[]{:S(2)}) copy-start(bf16[1024,256]{1,0:T(8,128)(2,1)} %param.14) | copy-start | bytes 1572868
  0.6 11.0 %copy-start.1 = (bf16[4,256,256]{2,1,0:T(8,128)(2,1)S(1)}, bf16[4,256,256]{2,1,0:T(8,128)(2,1)}, u32[]{:S(2)}) copy-start(bf16[4,256,256]{2,1,0:T(8,128)(2,1)} %cache_own) | copy-start | bytes 1572868
  0.7 64.5 %collective-permute-start.5 = (bf16[4096,256]{1,0:T(8,128)(2,1)}, bf16[4096,256]{1,0:T(8,128)(2,1)}, u32[]{:S(2)}, u32[]{:S(2)}) collective-permute-start(bf16[4096,256]{1,0:T(8,128)(2,1)} %q_own.1), channel_id=1, source_target_pairs={{0,8},{8,0},{1,9},{9,1},{2,10},{10,2},{3,11},{11,3},{4,12},{12,4},... | collective-permute-start | bytes 6291464 | tf_op jit(solution)/shard_map/ppermute | solution.py:25
  1.2 64.0 %collective-permute-start.7 = (bf16[256,4096]{1,0:T(8,128)(2,1)}, bf16[256,4096]{1,0:T(8,128)(2,1)}, u32[]{:S(2)}, u32[]{:S(2)}) collective-permute-start(bf16[256,4096]{1,0:T(8,128)(2,1)} %out_own.1), channel_id=1, source_target_pairs={{0,8},{8,0},{1,9},{9,1},{2,10},{10,2},{3,11},{11,3},{4,12},{12,4},... | collective-permute-start | bytes 6291464 | tf_op jit(solution)/shard_map/ppermute | solution.py:25
  1.3 1.0 copy-start.2
  2.3 0.7 copy-start.4
  3.0 14.3 %copy-start.8 = (s32[4]{0:T(128)S(1)}, s32[4]{0:T(128)}, u32[]{:S(2)}) copy-start(s32[4]{0:T(128)} %param.20) | copy-start | bytes 52
  3.0 62.3 %copy-start.5 = (s32[8]{0:T(128)S(1)}, s32[8]{0:T(128)}, u32[]{:S(2)}) copy-start(s32[8]{0:T(128)} %lens_ref.3) | copy-start | bytes 100
  3.8 4.5 %collective-permute-start = (bf16[128,1024]{1,0:T(8,128)(2,1)S(1)}, bf16[128,1024]{1,0:T(8,128)(2,1)S(1)}, u32[]{:S(2)}, u32[]{:S(2)}) collective-permute-start(bf16[128,1024]{1,0:T(8,128)(2,1)S(1)} %get-tuple-element.15), channel_id=1, source_target_pairs={{0,8},{8,0},{1,9},{9,1},{2,10},{10,2},{3,11},{11,3},{4,12},{12,4},... | collective-permute-start | bytes 786440 | tf_op jit(solution)/shard_map/ppermute | solution.py:25
  8.7 6.8 %collective-permute-start.2 = (f32[128,256]{1,0:T(8,128)S(1)}, f32[128,256]{1,0:T(8,128)S(1)}, u32[]{:S(2)}, u32[]{:S(2)}) collective-permute-start(f32[128,256]{1,0:T(8,128)S(1)} %fusion.4), channel_id=1, source_target_pairs={{0,1},{1,0},{2,3},{3,2},{4,5},{5,4},{6,7},{7,6},{8,9},{9,8},{10,11... | collective-permute-start | bytes 393224 | tf_op jit(solution)/shard_map/ppermute | solution.py:42
  11.6 17.1 %collective-permute-start.6 = (bf16[4,256,256]{2,1,0:T(8,128)(2,1)S(1)}, bf16[4,256,256]{2,1,0:T(8,128)(2,1)S(1)}, u32[]{:S(2)}, u32[]{:S(2)}) collective-permute-start(bf16[4,256,256]{2,1,0:T(8,128)(2,1)S(1)} %copy-done.1), channel_id=1, source_target_pairs={{0,8},{8,0},{1,9},{9,1},{2,10},{10,2},{3,11},{11,3},{4,12},{12,4},... | collective-permute-start | bytes 1572872 | tf_op jit(solution)/shard_map/ppermute | solution.py:25
  15.4 5.2 %collective-permute-start.3 = (f32[128,256]{1,0:T(8,128)S(1)}, f32[128,256]{1,0:T(8,128)S(1)}, u32[]{:S(2)}, u32[]{:S(2)}) collective-permute-start(f32[128,256]{1,0:T(8,128)S(1)} %add.97), channel_id=1, source_target_pairs={{0,2},{1,3},{2,0},{3,1},{4,6},{5,7},{6,4},{7,5},{8,10},{9,11},{10,... | collective-permute-start | bytes 393224 | tf_op jit(solution)/shard_map/ppermute | solution.py:42
  17.3 1.1 collective-permute-start.1
  18.4 10.2 %collective-permute-start.9 = (bf16[128,1024]{1,0:T(8,128)(2,1)S(1)}, bf16[128,1024]{1,0:T(8,128)(2,1)S(1)}, u32[]{:S(2)}, u32[]{:S(2)}) collective-permute-start(bf16[128,1024]{1,0:T(8,128)(2,1)S(1)} %add.95.refs_0_), channel_id=1, source_target_pairs={{0,2},{1,3},{2,4},{3,5},{4,6},{5,7},{6,0},{7,1},{8,10},{9,11},{10,... | collective-permute-start | bytes 786440 | tf_op jit(solution)/shard_map/ppermute | solution.py:35
  20.6 8.1 %collective-permute-start.8 = (bf16[128,1024]{1,0:T(8,128)(2,1)S(1)}, bf16[128,1024]{1,0:T(8,128)(2,1)S(1)}, u32[]{:S(2)}, u32[]{:S(2)}) collective-permute-start(bf16[128,1024]{1,0:T(8,128)(2,1)S(1)} %add.95.refs_0_), channel_id=1, source_target_pairs={{0,1},{1,0},{2,3},{3,2},{4,5},{5,4},{6,7},{7,6},{8,9},{9,8},{10,11... | collective-permute-start | bytes 786440 | tf_op jit(solution)/shard_map/ppermute | solution.py:30
  28.6 16.6 %collective-permute-start.11 = (bf16[128,1024]{1,0:T(8,128)(2,1)S(1)}, bf16[128,1024]{1,0:T(8,128)(2,1)S(1)}, u32[]{:S(2)}, u32[]{:S(2)}) collective-permute-start(bf16[128,1024]{1,0:T(8,128)(2,1)S(1)} %collective-permute-done.9.refs_2_), channel_id=1, source_target_pairs={{0,2},{1,3},{2,4},{3,5},{4,6},{5,7},{6,0},{7,1},{8,10},{9,11},{10,... | collective-permute-start | bytes 786440 | tf_op jit(solution)/shard_map/ppermute | solution.py:35
  28.6 133.2 %collective-permute-start.27 = (bf16[4096,512]{1,0:T(8,128)(2,1)}, bf16[4096,512]{1,0:T(8,128)(2,1)}, u32[]{:S(2)}, u32[]{:S(2)}) collective-permute-start(bf16[4096,512]{1,0:T(8,128)(2,1)} %own_ref.1), channel_id=1, source_target_pairs={{0,8},{8,0},{1,9},{9,1},{2,10},{10,2},{3,11},{11,3},{4,12},{12,4},... | collective-permute-start | bytes 12582920 | tf_op jit(solution)/shard_map/ppermute | solution.py:25
  28.7 26.4 %copy-start.6 = (f32[128,256]{1,0:T(8,128)}, f32[128,256]{1,0:T(8,128)S(1)}, u32[]{:S(2)}) copy-start(f32[128,256]{1,0:T(8,128)S(1)} %add.98) | copy-start | bytes 393220
  28.7 15.1 %collective-permute-start.4 = (f32[128,256]{1,0:T(8,128)S(1)}, f32[128,256]{1,0:T(8,128)}, u32[]{:S(2)}, u32[]{:S(2)}) collective-permute-start(f32[128,256]{1,0:T(8,128)S(1)} %add.98), channel_id=1, source_target_pairs={{0,4},{1,5},{2,6},{3,7},{4,0},{5,1},{6,2},{7,3},{8,12},{9,13},{10,... | collective-permute-start | bytes 393224 | tf_op jit(solution)/shard_map/ppermute | solution.py:42
  43.8 8.3 %collective-permute-start.10 = (bf16[128,1024]{1,0:T(8,128)(2,1)S(1)}, bf16[128,1024]{1,0:T(8,128)(2,1)S(1)}, u32[]{:S(2)}, u32[]{:S(2)}) collective-permute-start(bf16[128,1024]{1,0:T(8,128)(2,1)S(1)} %collective-permute-done.9.refs_2_), channel_id=1, source_target_pairs={{0,1},{1,0},{2,3},{3,2},{4,5},{5,4},{6,7},{7,6},{8,9},{9,8},{10,11... | collective-permute-start | bytes 786440 | tf_op jit(solution)/shard_map/ppermute | solution.py:30
  45.3 9.8 %collective-permute-start.13 = (bf16[128,1024]{1,0:T(8,128)(2,1)S(1)}, bf16[128,1024]{1,0:T(8,128)(2,1)S(1)}, u32[]{:S(2)}, u32[]{:S(2)}) collective-permute-start(bf16[128,1024]{1,0:T(8,128)(2,1)S(1)} %collective-permute-done.11.refs_4_), channel_id=1, source_target_pairs={{0,2},{1,3},{2,4},{3,5},{4,6},{5,7},{6,0},{7,1},{8,10},{9,11},{10,... | collective-permute-start | bytes 786440 | tf_op jit(solution)/shard_map/ppermute | solution.py:35
  52.0 9.2 %collective-permute-start.12 = (bf16[128,1024]{1,0:T(8,128)(2,1)S(1)}, bf16[128,1024]{1,0:T(8,128)(2,1)S(1)}, u32[]{:S(2)}, u32[]{:S(2)}) collective-permute-start(bf16[128,1024]{1,0:T(8,128)(2,1)S(1)} %collective-permute-done.11.refs_4_), channel_id=1, source_target_pairs={{0,1},{1,0},{2,3},{3,2},{4,5},{5,4},{6,7},{7,6},{8,9},{9,8},{10,11... | collective-permute-start | bytes 786440 | tf_op jit(solution)/shard_map/ppermute | solution.py:30
  55.1 10.1 %collective-permute-start.14 = (bf16[128,1024]{1,0:T(8,128)(2,1)S(1)}, bf16[128,1024]{1,0:T(8,128)(2,1)}, u32[]{:S(2)}, u32[]{:S(2)}) collective-permute-start(bf16[128,1024]{1,0:T(8,128)(2,1)S(1)} %collective-permute-done.13.refs_6_), channel_id=1, source_target_pairs={{0,1},{1,0},{2,3},{3,2},{4,5},{5,4},{6,7},{7,6},{8,9},{9,8},{10,11... | collective-permute-start | bytes 786440 | tf_op jit(solution)/shard_map/ppermute | solution.py:30
  65.2 0.8 copy-start.3
  74.2 40.7 %dynamic-slice-start = ((f32[8192]{0:T(1024)}, s32[]{:T(128)}), f32[1024]{0:T(1024)S(1)}, s32[]{:S(2)}) async-start(f32[8192]{0:T(1024)} %param.17, s32[]{:T(128)} %select_n.73), calls=%async_computation | async-start | bytes 8704 | tf_op jit(solution)/shard_map/dynamic_slice | solution.py:382
  74.2 9.3 %collective-permute-start.18 = (bf16[128,1024]{1,0:T(8,128)(2,1)S(1)}, bf16[128,1024]{1,0:T(8,128)(2,1)S(1)}, u32[]{:S(2)}, u32[]{:S(2)}) collective-permute-start(bf16[128,1024]{1,0:T(8,128)(2,1)S(1)} %get-tuple-element.23), channel_id=1, source_target_pairs={{0,1},{1,0},{2,3},{3,2},{4,5},{5,4},{6,7},{7,6},{8,9},{9,8},{10,11... | collective-permute-start | bytes 786440 | tf_op jit(solution)/shard_map/ppermute | solution.py:30
  75.8 13.3 %collective-permute-start.17 = (bf16[128,1024]{1,0:T(8,128)(2,1)S(1)}, bf16[128,1024]{1,0:T(8,128)(2,1)S(1)}, u32[]{:S(2)}, u32[]{:S(2)}) collective-permute-start(bf16[128,1024]{1,0:T(8,128)(2,1)S(1)} %get-tuple-element.21), channel_id=1, source_target_pairs={{0,1},{1,0},{2,3},{3,2},{4,5},{5,4},{6,7},{7,6},{8,9},{9,8},{10,11... | collective-permute-start | bytes 786440 | tf_op jit(solution)/shard_map/ppermute | solution.py:30
  83.5 40.5 %copy-start.7 = (s32[512]{0:T(512)S(1)}, s32[512]{0:T(512)}, u32[]{:S(2)}) copy-start(s32[512]{0:T(512)} %param.21) | copy-start | bytes 6148
  83.6 10.1 %collective-permute-start.19 = (bf16[128,1024]{1,0:T(8,128)(2,1)S(1)}, bf16[128,1024]{1,0:T(8,128)(2,1)S(1)}, u32[]{:S(2)}, u32[]{:S(2)}) collective-permute-start(bf16[128,1024]{1,0:T(8,128)(2,1)S(1)} %add_convert_fusion.2), channel_id=1, source_target_pairs={{0,2},{1,3},{2,4},{3,5},{4,6},{5,7},{6,0},{7,1},{8,10},{9,11},{10,... | collective-permute-start | bytes 786440 | tf_op jit(solution)/shard_map/ppermute | solution.py:35
  83.6 11.9 %collective-permute-start.16 = (bf16[128,1024]{1,0:T(8,128)(2,1)S(1)}, bf16[128,1024]{1,0:T(8,128)(2,1)S(1)}, u32[]{:S(2)}, u32[]{:S(2)}) collective-permute-start(bf16[128,1024]{1,0:T(8,128)(2,1)S(1)} %get-tuple-element.19), channel_id=1, source_target_pairs={{0,1},{1,0},{2,3},{3,2},{4,5},{5,4},{6,7},{7,6},{8,9},{9,8},{10,11... | collective-permute-start | bytes 786440 | tf_op jit(solution)/shard_map/ppermute | solution.py:30
  93.8 10.8 %collective-permute-start.20 = (bf16[128,1024]{1,0:T(8,128)(2,1)S(1)}, bf16[128,1024]{1,0:T(8,128)(2,1)S(1)}, u32[]{:S(2)}, u32[]{:S(2)}) collective-permute-start(bf16[128,1024]{1,0:T(8,128)(2,1)S(1)} %add_convert_fusion.1), channel_id=1, source_target_pairs={{0,2},{1,3},{2,4},{3,5},{4,6},{5,7},{6,0},{7,1},{8,10},{9,11},{10,... | collective-permute-start | bytes 786440 | tf_op jit(solution)/shard_map/ppermute | solution.py:35
  93.9 10.9 %collective-permute-start.15 = (bf16[128,1024]{1,0:T(8,128)(2,1)S(1)}, bf16[128,1024]{1,0:T(8,128)(2,1)S(1)}, u32[]{:S(2)}, u32[]{:S(2)}) collective-permute-start(bf16[128,1024]{1,0:T(8,128)(2,1)S(1)} %get-tuple-element.17), channel_id=1, source_target_pairs={{0,1},{1,0},{2,3},{3,2},{4,5},{5,4},{6,7},{7,6},{8,9},{9,8},{10,11... | collective-permute-start | bytes 786440 | tf_op jit(solution)/shard_map/ppermute | solution.py:30
  104.7 10.1 %collective-permute-start.21 = (bf16[128,1024]{1,0:T(8,128)(2,1)S(1)}, bf16[128,1024]{1,0:T(8,128)(2,1)S(1)}, u32[]{:S(2)}, u32[]{:S(2)}) collective-permute-start(bf16[128,1024]{1,0:T(8,128)(2,1)S(1)} %add_convert_fusion), channel_id=1, source_target_pairs={{0,2},{1,3},{2,4},{3,5},{4,6},{5,7},{6,0},{7,1},{8,10},{9,11},{10,... | collective-permute-start | bytes 786440 | tf_op jit(solution)/shard_map/ppermute | solution.py:35
  115.1 8.9 %collective-permute-start.29 = (bf16[128,1024]{1,0:T(8,128)(2,1)S(1)}, bf16[128,1024]{1,0:T(8,128)(2,1)S(1)}, u32[]{:S(2)}, u32[]{:S(2)}) collective-permute-start(bf16[128,1024]{1,0:T(8,128)(2,1)S(1)} %get-tuple-element.28.refs_0_), channel_id=1, source_target_pairs={{0,2},{1,3},{2,4},{3,5},{4,6},{5,7},{6,0},{7,1},{8,10},{9,11},{10,... | collective-permute-start | bytes 786440 | tf_op jit(solution)/shard_map/ppermute | solution.py:35
  124.0 8.2 %collective-permute-start.31 = (bf16[128,1024]{1,0:T(8,128)(2,1)S(1)}, bf16[128,1024]{1,0:T(8,128)(2,1)S(1)}, u32[]{:S(2)}, u32[]{:S(2)}) collective-permute-start(bf16[128,1024]{1,0:T(8,128)(2,1)S(1)} %collective-permute-done.29.refs_2_), channel_id=1, source_target_pairs={{0,2},{1,3},{2,4},{3,5},{4,6},{5,7},{6,0},{7,1},{8,10},{9,11},{10,... | collective-permute-start | bytes 786440 | tf_op jit(solution)/shard_map/ppermute | solution.py:35
  124.1 8.1 %collective-permute-start.24 = (f32[1,128]{1,0:T(1,128)S(1)}, f32[1,128]{1,0:T(1,128)S(1)}, u32[]{:S(2)}, u32[]{:S(2)}) collective-permute-start(f32[1,128]{1,0:T(1,128)S(1)} %bitcast.16), channel_id=1, source_target_pairs={{0,1},{1,0},{2,3},{3,2},{4,5},{5,4},{6,7},{7,6},{8,9},{9,8},{10,11... | collective-permute-start | bytes 1544 | tf_op jit(solution)/shard_map/ppermute | solution.py:42
  132.2 12.3 %collective-permute-start.33 = (bf16[128,1024]{1,0:T(8,128)(2,1)S(1)}, bf16[128,1024]{1,0:T(8,128)(2,1)S(1)}, u32[]{:S(2)}, u32[]{:S(2)}) collective-permute-start(bf16[128,1024]{1,0:T(8,128)(2,1)S(1)} %collective-permute-done.31.refs_4_), channel_id=1, source_target_pairs={{0,2},{1,3},{2,4},{3,5},{4,6},{5,7},{6,0},{7,1},{8,10},{9,11},{10,... | collective-permute-start | bytes 786440 | tf_op jit(solution)/shard_map/ppermute | solution.py:35
  132.2 3.9 %collective-permute-start.25 = (f32[1,128]{1,0:T(1,128)S(1)}, f32[1,128]{1,0:T(1,128)S(1)}, u32[]{:S(2)}, u32[]{:S(2)}) collective-permute-start(f32[1,128]{1,0:T(1,128)S(1)} %bitcast_add_fusion.1), channel_id=1, source_target_pairs={{0,2},{1,3},{2,0},{3,1},{4,6},{5,7},{6,4},{7,5},{8,10},{9,11},{10,... | collective-permute-start | bytes 1544 | tf_op jit(solution)/shard_map/ppermute | solution.py:42
  132.3 10.1 %collective-permute-start.23 = (s32[1,128]{1,0:T(1,128)S(1)}, s32[1,128]{1,0:T(1,128)S(1)}, u32[]{:S(2)}, u32[]{:S(2)}) collective-permute-start(s32[1,128]{1,0:T(1,128)S(1)} %slice_bitcast_fusion), channel_id=1, source_target_pairs={{0,8},{8,0},{1,9},{9,1},{2,10},{10,2},{3,11},{11,3},{4,12},{12,4},... | collective-permute-start | bytes 1544 | tf_op jit(solution)/shard_map/ppermute | solution.py:25
  136.1 6.8 %collective-permute-start.26 = (f32[1,128]{1,0:T(1,128)S(1)}, f32[1,128]{1,0:T(1,128)S(1)}, u32[]{:S(2)}, u32[]{:S(2)}) collective-permute-start(f32[1,128]{1,0:T(1,128)S(1)} %add.114), channel_id=1, source_target_pairs={{0,4},{1,5},{2,6},{3,7},{4,0},{5,1},{6,2},{7,3},{8,12},{9,13},{10,... | collective-permute-start | bytes 1544 | tf_op jit(solution)/shard_map/ppermute | solution.py:42
  140.9 9.2 %collective-permute-start.28 = (bf16[128,1024]{1,0:T(8,128)(2,1)S(1)}, bf16[128,1024]{1,0:T(8,128)(2,1)S(1)}, u32[]{:S(2)}, u32[]{:S(2)}) collective-permute-start(bf16[128,1024]{1,0:T(8,128)(2,1)S(1)} %get-tuple-element.28.refs_0_), channel_id=1, source_target_pairs={{0,1},{1,0},{2,3},{3,2},{4,5},{5,4},{6,7},{7,6},{8,9},{9,8},{10,11... | collective-permute-start | bytes 786440 | tf_op jit(solution)/shard_map/ppermute | solution.py:30
  142.4 13.3 %collective-permute-start.30 = (bf16[128,1024]{1,0:T(8,128)(2,1)S(1)}, bf16[128,1024]{1,0:T(8,128)(2,1)S(1)}, u32[]{:S(2)}, u32[]{:S(2)}) collective-permute-start(bf16[128,1024]{1,0:T(8,128)(2,1)S(1)} %collective-permute-done.29.refs_2_), channel_id=1, source_target_pairs={{0,1},{1,0},{2,3},{3,2},{4,5},{5,4},{6,7},{7,6},{8,9},{9,8},{10,11... | collective-permute-start | bytes 786440 | tf_op jit(solution)/shard_map/ppermute | solution.py:30
  142.9 16.1 %collective-permute-start.32 = (bf16[128,1024]{1,0:T(8,128)(2,1)S(1)}, bf16[128,1024]{1,0:T(8,128)(2,1)S(1)}, u32[]{:S(2)}, u32[]{:S(2)}) collective-permute-start(bf16[128,1024]{1,0:T(8,128)(2,1)S(1)} %collective-permute-done.31.refs_4_), channel_id=1, source_target_pairs={{0,1},{1,0},{2,3},{3,2},{4,5},{5,4},{6,7},{7,6},{8,9},{9,8},{10,11... | collective-permute-start | bytes 786440 | tf_op jit(solution)/shard_map/ppermute | solution.py:30
  144.4 17.4 %collective-permute-start.34 = (bf16[128,1024]{1,0:T(8,128)(2,1)S(1)}, bf16[128,1024]{1,0:T(8,128)(2,1)S(1)}, u32[]{:S(2)}, u32[]{:S(2)}) collective-permute-start(bf16[128,1024]{1,0:T(8,128)(2,1)S(1)} %collective-permute-done.33.refs_6_), channel_id=1, source_target_pairs={{0,1},{1,0},{2,3},{3,2},{4,5},{5,4},{6,7},{7,6},{8,9},{9,8},{10,11... | collective-permute-start | bytes 786440 | tf_op jit(solution)/shard_map/ppermute | solution.py:30
  165.9 3.7 %collective-permute-start.35 = (f32[3,128]{1,0:T(4,128)S(1)}, f32[3,128]{1,0:T(4,128)S(1)}, u32[]{:S(2)}, u32[]{:S(2)}) collective-permute-start(f32[3,128]{1,0:T(4,128)S(1)} %slice.71), channel_id=1, source_target_pairs={{0,1},{1,0},{2,3},{3,2},{4,5},{5,4},{6,7},{7,6},{8,9},{9,8},{10,11... | collective-permute-start | bytes 4616 | tf_op jit(solution)/shard_map/ppermute | solution.py:42
  169.6 3.7 %collective-permute-start.36 = (f32[3,128]{1,0:T(4,128)S(1)}, f32[3,128]{1,0:T(4,128)S(1)}, u32[]{:S(2)}, u32[]{:S(2)}) collective-permute-start(f32[3,128]{1,0:T(4,128)S(1)} %pad_maximum_fusion), channel_id=1, source_target_pairs={{0,2},{1,3},{2,0},{3,1},{4,6},{5,7},{6,4},{7,5},{8,10},{9,11},{10,... | collective-permute-start | bytes 4616 | tf_op jit(solution)/shard_map/ppermute | solution.py:42
  173.3 4.5 %collective-permute-start.37 = (f32[3,128]{1,0:T(4,128)S(1)}, f32[3,128]{1,0:T(4,128)S(1)}, u32[]{:S(2)}, u32[]{:S(2)}) collective-permute-start(f32[3,128]{1,0:T(4,128)S(1)} %pad_maximum_fusion.1), channel_id=1, source_target_pairs={{0,4},{1,5},{2,6},{3,7},{4,0},{5,1},{6,2},{7,3},{8,12},{9,13},{10,... | collective-permute-start | bytes 4616 | tf_op jit(solution)/shard_map/ppermute | solution.py:42
  173.8 4.2 %collective-permute-start.22 = (bf16[128,1024]{1,0:T(8,128)(2,1)S(1)}, bf16[128,1024]{1,0:T(8,128)(2,1)S(1)}, u32[]{:S(2)}, u32[]{:S(2)}) collective-permute-start(bf16[128,1024]{1,0:T(8,128)(2,1)S(1)} %get-tuple-element.30), channel_id=1, source_target_pairs={{0,8},{8,0},{1,9},{9,1},{2,10},{10,2},{3,11},{11,3},{4,12},{12,4},... | collective-permute-start | bytes 786440 | tf_op jit(solution)/shard_map/ppermute | solution.py:25
  177.9 1.2 collective-permute-start.38

commit v3 on v2

--- a/solution.py
+++ b/solution.py
@@ -49,14 +49,21 @@
     return doubling(value, lambda a, b, step: a + b)
 
 
-def gather_blocks(block):
-    blocks = []
-    for k in range(lax.axis_size("tensor") // SIDE):
-        if k > 0:
-            block = ring_step(block)
-        blocks.append(block)
-        blocks.append(swap_side(block))
-    return blocks
+def after(value, *others):
+    return lax.optimization_barrier((value, *others))[0]
+
+
+def gather_blocks(block, beside=()):
+    count = lax.axis_size("tensor") // SIDE
+    blocks, values = [], []
+    for k in range(count):
+        crossed = swap_side(block)
+        blocks += [block, crossed]
+        ready = beside[k](block) if k < len(beside) else []
+        values += ready
+        if k + 1 < count:
+            block = after(ring_step(block), crossed, *ready)
+    return blocks, values
 
 
 def gathered_ids():
@@ -165,7 +172,6 @@
     lens_ref,
     ctx_ref,
     gain_ref,
-    kv_ref,
     q_own,
     q_other,
     cache_own,
@@ -176,7 +182,7 @@
 ):
     blocks, outs = refs[:count], refs[count : 2 * count]
     q_held, cache_held, out_held, q_sems, cache_sems, out_sems = refs[2 * count :]
-    half, shard = blocks[0].shape
+    half, shard = outs[0].shape
     ctx_slots = cache_own.shape[1]
     ids = gathered_ids()
     q_copies = block_copies(ids, 0, q_own, q_other, q_held, q_sems)
@@ -192,17 +198,22 @@
 
     squares = jnp.zeros((half, 1), jnp.float32)
     for block in blocks:
-        values = block[...].astype(jnp.float32)
+        values = block[:, :shard].astype(jnp.float32)
         squares += jnp.sum(values * values, axis=1, keepdims=True)
     scale = lax.rsqrt(squares / (shard * count) + EPS)
     query = jnp.zeros((half, q_own.shape[1]), jnp.float32)
     for j, block in enumerate(blocks):
         gain = gain_ref[pl.ds(ids[j], 1), :]
-        normed = (block[...].astype(jnp.float32) * scale * gain).astype(jnp.bfloat16)
+        normed = (block[:, :shard].astype(jnp.float32) * scale * gain).astype(jnp.bfloat16)
         q_copies[j][1].wait()
         query += product(normed, q_held[j])
     query = query.astype(jnp.bfloat16)
-    new_kv = (kv_ref[...] * scale).astype(jnp.bfloat16)
+    kv_head = lax.axis_index("tensor") * QH_DEV // GROUP
+    kv_place = pl.ds(pl.multiple_of(shard + kv_head * 2 * HEAD, 2 * HEAD), 2 * HEAD)
+    kv_sum = jnp.zeros((half, 2 * HEAD), jnp.float32)
+    for block in blocks:
+        kv_sum += block[:, kv_place].astype(jnp.float32)
+    new_kv = (kv_sum * scale).astype(jnp.bfloat16)
 
     busy, light_total, long_seq, long_start, own_ends, busy_ends = row_plan(
         lens_ref, seqs_count, half
@@ -258,9 +269,9 @@
         out[...] = product(attn, out_held[j]).astype(jnp.bfloat16)
 
 
-def attend(resp_len, both_ctx, attn_gain, kv_sum, q_pair, cache_pair, out_pair, blocks):
+def attend(resp_len, both_ctx, attn_gain, q_pair, cache_pair, out_pair, blocks):
     count = len(blocks)
-    half, shard = blocks[0].shape
+    half, shard = blocks[0].shape[0], attn_gain.shape[0] // count
     seqs_count, ctx_slots, width = cache_pair[0].shape
     q_width, attn_width = q_pair[0].shape[1], out_pair[0].shape[0]
     vmem = pl.BlockSpec(memory_space=pltpu.VMEM)
@@ -269,7 +280,7 @@
     return pl.pallas_call(
         functools.partial(attention_kernel, seqs_count, count),
         out_shape=[jax.ShapeDtypeStruct((half, shard), jnp.bfloat16)] * count,
-        in_specs=[smem] * 2 + [vmem] * 2 + [anywhere] * 6 + [vmem] * count,
+        in_specs=[smem] * 2 + [vmem] + [anywhere] * 6 + [vmem] * count,
         out_specs=[vmem] * count,
         scratch_shapes=[
             pltpu.VMEM((count, shard, q_width), jnp.bfloat16),
@@ -281,20 +292,25 @@
         ],
         compiler_params=pltpu.CompilerParams(vmem_limit_bytes=VMEM_LIMIT),
         name="attend",
-    )(resp_len, both_ctx, attn_gain.reshape(count, shard), kv_sum, *q_pair, *cache_pair, *out_pair, *blocks)
-
-
-def vocab_kernel(count, targets_ref, squares_ref, own_ref, other_ref, *refs):
+    )(resp_len, both_ctx, attn_gain.reshape(count, shard), *q_pair, *cache_pair, *out_pair, *blocks)
+
+
+def vocab_kernel(count, targets_ref, gain_ref, own_ref, other_ref, *refs):
     blocks, (stats_ref, held, sems) = refs[:count], refs[count:]
     half, shard = blocks[0].shape
-    copies = block_copies(gathered_ids(), 0, own_ref, other_ref, held, sems)
+    ids = gathered_ids()
+    copies = block_copies(ids, 0, own_ref, other_ref, held, sems)
     start_copies(copies)
-    scale = lax.rsqrt(squares_ref[...] / (shard * count) + EPS)
     vocab_count = own_ref.shape[1]
     logits = jnp.zeros((half, vocab_count), jnp.float32)
+    squares = jnp.zeros((half, 1), jnp.float32)
     for j, block in enumerate(blocks):
         copies[j][1].wait()
-        logits += product(block[...], held[j])
+        values = block[...]
+        logits += product(values, held[j])
+        mixed = values.astype(jnp.float32) / gain_ref[pl.ds(ids[j], 1), :]
+        squares += jnp.sum(mixed * mixed, axis=1, keepdims=True)
+    scale = lax.rsqrt(squares / (shard * count) + EPS)
     logits = logits * scale
     column_ids = lax.axis_index("tensor") * vocab_count + lax.broadcasted_iota(
         jnp.int32, (half, vocab_count), 1
@@ -309,7 +325,7 @@
     stats_ref[...] = jnp.transpose(stats)[:8]
 
 
-def vocab_stats(targets, square_sum, vocab_pair, blocks):
+def vocab_stats(targets, final_gain, vocab_pair, blocks):
     count = len(blocks)
     half, shard = blocks[0].shape
     vocab_count = vocab_pair[0].shape[1]
@@ -326,7 +342,7 @@
         ],
         compiler_params=pltpu.CompilerParams(vmem_limit_bytes=VMEM_LIMIT),
         name="vocab_stats",
-    )(targets.reshape(half, 1), square_sum.reshape(half, 1), *vocab_pair, *blocks)
+    )(targets.reshape(half, 1), final_gain.reshape(count, shard), *vocab_pair, *blocks)
 
 
 def per_device(
@@ -352,22 +368,41 @@
     keep, send, pick = pack(resp_len, hidden, seqs_count)
     rows = keep + swap_dp(send)
     rows_f = rows.astype(jnp.float32)
-    blocks = gather_blocks(rows)
 
     gain = lax.dynamic_slice_in_dim(attn_gain, tensor_pos * shard, shard, 0)
-    kv_head = tensor_pos * QH_DEV // GROUP
     kv_partial = product((rows_f * gain).astype(jnp.bfloat16), kv_weight)
-    kv_sum = lax.dynamic_slice_in_dim(sum_tensor(kv_partial), kv_head * 2 * HEAD, 2 * HEAD, 1)
-    cache = lax.dynamic_slice_in_dim(kv_cache, kv_head * 2 * HEAD, 2 * HEAD, 2)
-    both_ctx = jnp.concatenate([ctx_len, swap_dp(ctx_len)], axis=0)
+    cache = kv_cache
+    if kv_cache.shape[2] != 2 * HEAD:
+        kv_head = tensor_pos * QH_DEV // GROUP
+        cache = lax.dynamic_slice_in_dim(kv_cache, kv_head * 2 * HEAD, 2 * HEAD, 2)
+    def swap_rest(block):
+        context = after(ctx_len, block)
+        own_targets = lax.dynamic_slice_in_dim(
+            after(target_ids, block), group * rows_count, rows_count, 0
+        )
+        sent_targets = jnp.sum(jnp.where(pick > 0, own_targets[None, :], 0), axis=1)
+        return [
+            swap_dp(after(cache, block)),
+            jnp.concatenate([ctx_len, swap_dp(context)], axis=0),
+            sent_targets[:half] + swap_dp(sent_targets[None, half:])[0],
+        ]
+
+    blocks, values = gather_blocks(
+        jnp.concatenate([rows, kv_partial.astype(jnp.bfloat16)], axis=1),
+        [
+            lambda block: [swap_dp(after(q_weight, block))],
+            lambda block: [swap_dp(after(out_weight, block))],
+            swap_rest,
+        ],
+    )
+    q_other, out_other, cache_other, both_ctx, targets = values
     products = attend(
         resp_len,
         both_ctx,
         attn_gain,
-        kv_sum,
-        (q_weight, swap_dp(q_weight)),
-        (cache, swap_dp(cache)),
-        (out_weight, swap_dp(out_weight)),
+        (q_weight, q_other),
+        (cache, cache_other),
+        (out_weight, out_other),
         blocks,
     )
 
@@ -380,18 +415,21 @@
     mixed = rows_f + total
 
     gain = lax.dynamic_slice_in_dim(final_gain, tensor_pos * shard, shard, 0)
-    blocks = gather_blocks((mixed * gain).astype(jnp.bfloat16))
-    square_sum = sum_tensor(jnp.sum(mixed * mixed, axis=1)[None, :])[0]
-    layer_rows = mixed.astype(jnp.bfloat16)
-    layer_rows = jnp.concatenate([layer_rows, swap_dp(layer_rows)], axis=0)
-    layer_out = lax.dot_general(
-        pick, layer_rows, (((0,), (0,)), ((), ())), preferred_element_type=jnp.float32
-    ).astype(jnp.bfloat16)
-
-    own_targets = lax.dynamic_slice_in_dim(target_ids, group * rows_count, rows_count, 0)
-    sent_targets = jnp.sum(jnp.where(pick > 0, own_targets[None, :], 0), axis=1)
-    targets = sent_targets[:half] + swap_dp(sent_targets[None, half:])[0]
-    stats = vocab_stats(targets, square_sum, (vocab_weight, swap_dp(vocab_weight)), blocks)
+
+    def place_rows(block):
+        layer_rows = mixed.astype(jnp.bfloat16)
+        layer_rows = jnp.concatenate([layer_rows, swap_dp(layer_rows)], axis=0)
+        return [
+            lax.dot_general(
+                pick, layer_rows, (((0,), (0,)), ((), ())), preferred_element_type=jnp.float32
+            ).astype(jnp.bfloat16)
+        ]
+
+    blocks, (layer_out, vocab_other) = gather_blocks(
+        (mixed * gain).astype(jnp.bfloat16),
+        [place_rows, lambda block: [swap_dp(after(vocab_weight, block))]],
+    )
+    stats = vocab_stats(targets, final_gain, (vocab_weight, vocab_other), blocks)
 
     def join(a, b, step):
         first = (tensor_pos // step) % 2 == 0

time: 180 us -> 153 us (0.85)
  starting transfers between devices: 31.4 us -> 17 us
  waiting for transfers between devices: 125 us -> 112 us
    ppermute x9 -> x3, waiting for transfers between devices: 32.3 us -> 11 us  [doubling(): other = lax.ppermute(value, 'tensor', [(i, i ^ step) for i in range(count)])]
    ppermute x9 -> x3, starting transfers between devices: 15.2 us -> 0.73 us  [doubling(): other = lax.ppermute(value, 'tensor', [(i, i ^ step) for i in range(count)])]
    ppermute x12, waiting for transfers between devices: 41.7 us -> 52.3 us  [swap_side(): return lax.ppermute(value, 'tensor', [(i, i ^ 1) for i in range(count)])]
    unnamed x18 -> x34, local copies, waits for them, and re-layouts: 2.48 us -> 4.95 us
  transfers between devices with their start and end apart: 39 -> 33, of which waited for: 25 -> 24; matrix products, arithmetic and copies ran while one was open for 3% -> 2% of each run, Pallas kernels for 5% -> 0%
where the time goes in v3:
time: 153 us; the launch traced here: 152 us
  waiting for transfers between devices  112 us (73%)
  starting transfers between devices  17 us (11%)
  Pallas kernels  13.3 us (9%)
  local copies, waits for them, and re-layouts  6.02 us (4%)
  other arithmetic  1.56 us (1%)
    ppermute x12, waiting for transfers between devices, swap_side(): return lax.ppermute(value, 'tensor', [(i, i ^ 1) for i in range(count)])  52.3 us
    ppermute x9, waiting for transfers between devices, ring_step(): lax.ppermute(value, 'tensor', [(i, (i + SIDE) % count) for i in range(cou...  45.5 us
    ppermute x12, starting transfers between devices, swap_side(): return lax.ppermute(value, 'tensor', [(i, i ^ 1) for i in range(count)])  12.8 us
    ppermute x3, waiting for transfers between devices, doubling(): other = lax.ppermute(value, 'tensor', [(i, i ^ step) for i in range(count)])  11 us
    pallas_call x1, Pallas kernels, attend(): pl.pallas_call(functools.partial(attention_kernel, seqs_count, count), ou...  8.32 us
    unnamed x34, local copies, waits for them, and re-layouts  4.95 us
    pallas_call x1, Pallas kernels, vocab_stats(): pl.pallas_call(functools.partial(vocab_kernel, count), out_shape=jax.Shap...  4.08 us
    ppermute x9, waiting for transfers between devices, swap_dp(): return lax.ppermute(value, 'dp', [(0, 1), (1, 0)])  3.33 us
  transfers between devices with their start and end apart: 33, of which 24 were waited for; matrix products, arithmetic and copies ran while one was open for 2% of the time, Pallas kernels for 0%

profile of v3, /device:TPU:0, one launch (start us, length us, event | category | flops | bytes accessed | tf_op | source)
XLA Modules:
  0.0 152.4 jit_solution(1774596110560404545)
XLA Ops:
  0.7 1.1 copy-done.2
  1.8 0.7 copy-done.5
  2.5 0.9 pack_rows.1
  3.3 0.5 collective-permute-start
  3.9 0.8 dynamic_slice.9
  4.7 0.3 collective-permute-done
  5.1 0.2 convolution_convert_fusion.1
  5.4 0.1 copy-done.11
  5.5 0.4 collective-permute-start.3
  5.8 2.7 %collective-permute-start.2 = (bf16[128,1280]{1,0:T(8,128)(2,1)S(1)}, bf16[128,1280]{1,0:T(8,128)(2,1)S(1)}, u32[]{:S(2)}, u32[]{:S(2)}) collective-permute-start(bf16[128,1280]{1,0:T(8,128)(2,1)S(1)} %pad_maximum_fusion.refs_0_), channel_id=1, source_target_pairs={{0,1},{1,0},{2,3},{3,2},{4,5},{5,4},{6,7},{7,6},{8,9},{9,8},{10,11... | collective-permute-start | bytes 983048 | tf_op jit(solution)/shard_map/ppermute | solution.py:30
  8.5 1.6 %collective-permute-start.1 = (bf16[128,1280]{1,0:T(8,128)(2,1)S(1)}, bf16[128,1280]{1,0:T(8,128)(2,1)S(1)}, u32[]{:S(2)}, u32[]{:S(2)}) collective-permute-start(bf16[128,1280]{1,0:T(8,128)(2,1)S(1)} %pad_maximum_fusion.refs_0_), channel_id=1, source_target_pairs={{0,2},{1,3},{2,4},{3,5},{4,6},{5,7},{6,0},{7,1},{8,10},{9,11},{10,... | collective-permute-start | bytes 983048 | tf_op jit(solution)/shard_map/ppermute | solution.py:35
  10.1 6.6 %collective-permute-done.2.refs_1_ = bf16[128,1280]{1,0:T(8,128)(2,1)S(1)} collective-permute-done((bf16[128,1280]{1,0:T(8,128)(2,1)S(1)}, bf16[128,1280]{1,0:T(8,128)(2,1)S(1)}, u32[]{:S(2)}, u32[]{:S(2)}) %collective-permute-start.2) | collective-permute-done | bytes 327712 | tf_op jit(solution)/shard_map/ppermute | solution.py:30
  16.7 3.3 %collective-permute-done.1.refs_2_ = bf16[128,1280]{1,0:T(8,128)(2,1)S(1)} collective-permute-done((bf16[128,1280]{1,0:T(8,128)(2,1)S(1)}, bf16[128,1280]{1,0:T(8,128)(2,1)S(1)}, u32[]{:S(2)}, u32[]{:S(2)}) %collective-permute-start.1) | collective-permute-done | bytes 327712 | tf_op jit(solution)/shard_map/ppermute | solution.py:35
  20.1 1.3 copy-done.12
  21.4 0.5 collective-permute-start.5
  21.9 8.4 %collective-permute-done.5.refs_3_ = bf16[128,1280]{1,0:T(8,128)(2,1)S(1)} collective-permute-done((bf16[128,1280]{1,0:T(8,128)(2,1)S(1)}, bf16[128,1280]{1,0:T(8,128)(2,1)S(1)}, u32[]{:S(2)}, u32[]{:S(2)}) %collective-permute-start.5) | collective-permute-done | bytes 327712 | tf_op jit(solution)/shard_map/ppermute | solution.py:30
  30.3 2.3 %collective-permute-done.4.refs_4_ = bf16[128,1280]{1,0:T(8,128)(2,1)S(1)} collective-permute-done((bf16[128,1280]{1,0:T(8,128)(2,1)S(1)}, bf16[128,1280]{1,0:T(8,128)(2,1)S(1)}, u32[]{:S(2)}, u32[]{:S(2)}) %collective-permute-start.4) | collective-permute-done | bytes 327712 | tf_op jit(solution)/shard_map/ppermute | solution.py:35
  32.6 1.3 collective-permute-start.9
  33.9 0.1 dynamic_slice.10
  34.0 0.1 select_reduce_fusion.1
  34.2 0.6 collective-permute-start.11
  34.7 0.1 collective-permute-start.7
  34.8 1.0 collective-permute-done.7
  35.8 0.1 pad_add_fusion.ctx_ref
  35.9 6.5 %collective-permute-done.10.refs_6_ = bf16[128,1280]{1,0:T(8,128)(2,1)} collective-permute-done((bf16[128,1280]{1,0:T(8,128)(2,1)S(1)}, bf16[128,1280]{1,0:T(8,128)(2,1)}, u32[]{:S(2)}, u32[]{:S(2)}) %collective-permute-start.10) | collective-permute-done | bytes 327712 | tf_op jit(solution)/shard_map/ppermute | solution.py:35
  42.5 0.7 copy-done.3
  43.2 1.0 collective-permute-start.12
  44.2 6.3 %collective-permute-done.12.refs_7_ = bf16[128,1280]{1,0:T(8,128)(2,1)} collective-permute-done((bf16[128,1280]{1,0:T(8,128)(2,1)}, bf16[128,1280]{1,0:T(8,128)(2,1)}, u32[]{:S(2)}, u32[]{:S(2)}) %collective-permute-start.12) | collective-permute-done | bytes 327712 | tf_op jit(solution)/shard_map/ppermute | solution.py:30
  50.6 1.0 copy-done.4
  51.6 8.3 %attend.1 = (bf16[128,1024]{1,0:T(8,128)(2,1)S(1)}, bf16[128,1024]{1,0:T(8,128)(2,1)S(1)}, bf16[128,1024]{1,0:T(8,128)(2,1)S(1)}, bf16[128,1024]{1,0:T(8,128)(2,...) custom-call(s32[8]{0:T(128)S(1)} %copy-done.6, ...), custom_call_target="tpu_custom_call" | custom-call | tf_op jit(solution)/shard_map/attend/pallas_call | solution.py:280
  59.9 1.1 collective-permute-start.16
  61.0 1.0 collective-permute-start.15
  62.0 7.2 %collective-permute-done.16 = bf16[128,1024]{1,0:T(8,128)(2,1)S(1)} collective-permute-done((bf16[128,1024]{1,0:T(8,128)(2,1)S(1)}, bf16[128,1024]{1,0:T(8,128)(2,1)S(1)}, u32[]{:S(2)}, u32[]{:S(2)}) %collective-permute-start.16) | collective-permute-done | bytes 262176 | tf_op jit(solution)/shard_map/ppermute | solution.py:30
  69.4 1.1 collective-permute-start.14
  70.4 3.8 %collective-permute-done.15 = bf16[128,1024]{1,0:T(8,128)(2,1)S(1)} collective-permute-done((bf16[128,1024]{1,0:T(8,128)(2,1)S(1)}, bf16[128,1024]{1,0:T(8,128)(2,1)S(1)}, u32[]{:S(2)}, u32[]{:S(2)}) %collective-permute-start.15) | collective-permute-done | bytes 262176 | tf_op jit(solution)/shard_map/ppermute | solution.py:30
  74.2 4.6 %collective-permute-done.17 = bf16[128,1024]{1,0:T(8,128)(2,1)S(1)} collective-permute-done((bf16[128,1024]{1,0:T(8,128)(2,1)S(1)}, bf16[128,1024]{1,0:T(8,128)(2,1)S(1)}, u32[]{:S(2)}, u32[]{:S(2)}) %collective-permute-start.17) | collective-permute-done | bytes 262176 | tf_op jit(solution)/shard_map/ppermute | solution.py:35
  78.8 0.1 add_convert_fusion.1
  79.0 0.8 collective-permute-start.13
  79.9 7.7 %collective-permute-done.18 = bf16[128,1024]{1,0:T(8,128)(2,1)S(1)} collective-permute-done((bf16[128,1024]{1,0:T(8,128)(2,1)S(1)}, bf16[128,1024]{1,0:T(8,128)(2,1)S(1)}, u32[]{:S(2)}, u32[]{:S(2)}) %collective-permute-start.18) | collective-permute-done | bytes 262176 | tf_op jit(solution)/shard_map/ppermute | solution.py:35
  87.6 0.1 add_convert_fusion
  87.8 8.1 %collective-permute-done.19 = bf16[128,1024]{1,0:T(8,128)(2,1)S(1)} collective-permute-done((bf16[128,1024]{1,0:T(8,128)(2,1)S(1)}, bf16[128,1024]{1,0:T(8,128)(2,1)S(1)}, u32[]{:S(2)}, u32[]{:S(2)}) %collective-permute-start.19) | collective-permute-done | bytes 262176 | tf_op jit(solution)/shard_map/ppermute | solution.py:35
  95.9 0.2 multiply_convert_fusion
  96.1 0.1 collective-permute-start.20
  96.3 0.6 collective-permute-start.22
  96.9 0.9 collective-permute-done.20
  97.7 1.1 convolution_convert_fusion
  98.8 7.9 %collective-permute-done.21.refs_2_ = bf16[128,1024]{1,0:T(8,128)(2,1)S(1)} collective-permute-done((bf16[128,1024]{1,0:T(8,128)(2,1)S(1)}, bf16[128,1024]{1,0:T(8,128)(2,1)S(1)}, u32[]{:S(2)}, u32[]{:S(2)}) %collective-permute-start.21) | collective-permute-done | bytes 262176 | tf_op jit(solution)/shard_map/ppermute | solution.py:35
  106.7 0.6 collective-permute-start.24
  107.3 8.1 %collective-permute-done.24.refs_3_ = bf16[128,1024]{1,0:T(8,128)(2,1)S(1)} collective-permute-done((bf16[128,1024]{1,0:T(8,128)(2,1)S(1)}, bf16[128,1024]{1,0:T(8,128)(2,1)S(1)}, u32[]{:S(2)}, u32[]{:S(2)}) %collective-permute-start.24) | collective-permute-done | bytes 262176 | tf_op jit(solution)/shard_map/ppermute | solution.py:30
  115.4 2.0 %collective-permute-done.25.refs_4_ = bf16[128,1024]{1,0:T(8,128)(2,1)S(1)} collective-permute-done((bf16[128,1024]{1,0:T(8,128)(2,1)S(1)}, bf16[128,1024]{1,0:T(8,128)(2,1)S(1)}, u32[]{:S(2)}, u32[]{:S(2)}) %collective-permute-start.25) | collective-permute-done | bytes 262176 | tf_op jit(solution)/shard_map/ppermute | solution.py:35
  117.5 1.5 collective-permute-start.26
  119.0 6.0 %collective-permute-done.26.refs_5_ = bf16[128,1024]{1,0:T(8,128)(2,1)S(1)} collective-permute-done((bf16[128,1024]{1,0:T(8,128)(2,1)S(1)}, bf16[128,1024]{1,0:T(8,128)(2,1)S(1)}, u32[]{:S(2)}, u32[]{:S(2)}) %collective-permute-start.26) | collective-permute-done | bytes 262176 | tf_op jit(solution)/shard_map/ppermute | solution.py:30
  125.0 3.0 %collective-permute-done.27.refs_6_ = bf16[128,1024]{1,0:T(8,128)(2,1)S(1)} collective-permute-done((bf16[128,1024]{1,0:T(8,128)(2,1)S(1)}, bf16[128,1024]{1,0:T(8,128)(2,1)S(1)}, u32[]{:S(2)}, u32[]{:S(2)}) %collective-permute-start.27) | collective-permute-done | bytes 262176 | tf_op jit(solution)/shard_map/ppermute | solution.py:35
  128.0 0.5 collective-permute-start.28
  128.6 0.1 copy.13.targets_ref
  128.7 5.7 %collective-permute-done.28.refs_7_ = bf16[128,1024]{1,0:T(8,128)(2,1)S(1)} collective-permute-done((bf16[128,1024]{1,0:T(8,128)(2,1)S(1)}, bf16[128,1024]{1,0:T(8,128)(2,1)S(1)}, u32[]{:S(2)}, u32[]{:S(2)}) %collective-permute-start.28) | collective-permute-done | bytes 262176 | tf_op jit(solution)/shard_map/ppermute | solution.py:30
  134.4 4.1 %vocab_stats.1 = f32[8,128]{1,0:T(8,128)S(1)} custom-call(s32[128,1]{1,0:T(8,128)S(1)} %copy.13.targets_ref, f32[8,1024]{1,0:T(8,128)S(1)} %reshape.20.gain_ref, bf16[4096,512]{1,0:T(8,128)(2,1)} %own_ref.1, bf16[4096,512]{1,0:T(8,128)(2,1)} %copy-done.8, bf16[128,1024]{1,0:T(8,128)(2,1)S(1)} %get-tuple-element.52.refs_0_, ...), custom_call_target="tpu_custom_call" | custom-call | tf_op jit(solution)/shard_map/vocab_stats/pallas_call | solution.py:334
  138.5 0.6 collective-permute-start.29
  139.1 3.1 %collective-permute-done.29 = f32[3,128]{1,0:T(4,128)S(1)} collective-permute-done((f32[3,128]{1,0:T(4,128)S(1)}, f32[3,128]{1,0:T(4,128)S(1)}, u32[]{:S(2)}, u32[]{:S(2)}) %collective-permute-start.29) | collective-permute-done | bytes 1568 | tf_op jit(solution)/shard_map/ppermute | solution.py:42
  142.3 3.5 %collective-permute-done.30 = f32[3,128]{1,0:T(4,128)S(1)} collective-permute-done((f32[3,128]{1,0:T(4,128)S(1)}, f32[3,128]{1,0:T(4,128)S(1)}, u32[]{:S(2)}, u32[]{:S(2)}) %collective-permute-start.30) | collective-permute-done | bytes 1568 | tf_op jit(solution)/shard_map/ppermute | solution.py:42
  146.0 4.4 %collective-permute-done.31 = f32[3,128]{1,0:T(4,128)S(1)} collective-permute-done((f32[3,128]{1,0:T(4,128)S(1)}, f32[3,128]{1,0:T(4,128)S(1)}, u32[]{:S(2)}, u32[]{:S(2)}) %collective-permute-start.31) | collective-permute-done | bytes 1568 | tf_op jit(solution)/shard_map/ppermute | solution.py:42
  150.5 0.1 collective-permute-start.32
  150.6 1.1 collective-permute-done.32
  151.7 0.7 select_reduce_fusion
  (69 shorter events, 0.8 us)
Async XLA Ops:
  0.6 4.5 %copy-start = (bf16[1024,256]{1,0:T(8,128)(2,1)S(1)}, bf16[1024,256]{1,0:T(8,128)(2,1)}, u32[]{:S(2)}) copy-start(bf16[1024,256]{1,0:T(8,128)(2,1)} %param.14) | copy-start | bytes 1572868
  0.6 33.3 %copy-start.1 = (bf16[4,256,256]{2,1,0:T(8,128)(2,1)S(1)}, bf16[4,256,256]{2,1,0:T(8,128)(2,1)}, u32[]{:S(2)}) copy-start(bf16[4,256,256]{2,1,0:T(8,128)(2,1)} %cache_own.1) | copy-start | bytes 1572868
  0.7 1.1 copy-start.2
  1.8 0.7 copy-start.5
  2.4 31.5 %copy-start.15 = (s32[512]{0:T(512)S(1)}, s32[512]{0:T(512)}, u32[]{:S(2)}) copy-start(s32[512]{0:T(512)} %param.21) | copy-start | bytes 6148
  2.4 32.3 %copy-start.16 = (s32[4]{0:T(128)S(1)}, s32[4]{0:T(128)}, u32[]{:S(2)}) copy-start(s32[4]{0:T(128)} %param.20) | copy-start | bytes 52
  2.4 41.8 %copy-start.13 = (f32[8192]{0:T(1024)S(1)}, f32[8192]{0:T(1024)}, u32[]{:S(2)}) copy-start(f32[8192]{0:T(1024)} %param.12) | copy-start | bytes 98308
  2.4 48.1 %copy-start.6 = (s32[8]{0:T(128)S(1)}, s32[8]{0:T(128)}, u32[]{:S(2)}) copy-start(s32[8]{0:T(128)} %lens_ref.3) | copy-start | bytes 100
  3.3 1.7 %collective-permute-start = (bf16[128,1024]{1,0:T(8,128)(2,1)S(1)}, bf16[128,1024]{1,0:T(8,128)(2,1)S(1)}, u32[]{:S(2)}, u32[]{:S(2)}) collective-permute-start(bf16[128,1024]{1,0:T(8,128)(2,1)S(1)} %get-tuple-element.27), channel_id=1, source_target_pairs={{0,8},{8,0},{1,9},{9,1},{2,10},{10,2},{3,11},{11,3},{4,12},{12,4},... | collective-permute-start | bytes 786440 | tf_op jit(solution)/shard_map/ppermute | solution.py:25
  3.8 1.6 %copy-start.11 = (bf16[4096,256]{1,0:T(8,128)(2,1)S(1)}, bf16[4096,256]{1,0:T(8,128)(2,1)}, u32[]{:S(2)}) copy-start(bf16[4096,256]{1,0:T(8,128)(2,1)} %q_own.1) | copy-start | bytes 6291460
  5.1 27.5 %copy-start.9 = (bf16[128,1024]{1,0:T(8,128)(2,1)}, bf16[128,1024]{1,0:T(8,128)(2,1)S(1)}, u32[]{:S(2)}) copy-start(bf16[128,1024]{1,0:T(8,128)(2,1)S(1)} %add.74) | copy-start | bytes 786436
  5.5 14.6 %collective-permute-start.3 = (bf16[4096,256]{1,0:T(8,128)(2,1)S(1)}, bf16[4096,256]{1,0:T(8,128)(2,1)S(1)}, u32[]{:S(2)}, u32[]{:S(2)}) collective-permute-start(bf16[4096,256]{1,0:T(8,128)(2,1)S(1)} %copy-done.11), channel_id=1, source_target_pairs={{0,8},{8,0},{1,9},{9,1},{2,10},{10,2},{3,11},{11,3},{4,12},{12,4},... | collective-permute-start | bytes 6291464 | tf_op jit(solution)/shard_map/ppermute | solution.py:25
  5.8 10.9 %collective-permute-start.2 = (bf16[128,1280]{1,0:T(8,128)(2,1)S(1)}, bf16[128,1280]{1,0:T(8,128)(2,1)S(1)}, u32[]{:S(2)}, u32[]{:S(2)}) collective-permute-start(bf16[128,1280]{1,0:T(8,128)(2,1)S(1)} %pad_maximum_fusion.refs_0_), channel_id=1, source_target_pairs={{0,1},{1,0},{2,3},{3,2},{4,5},{5,4},{6,7},{7,6},{8,9},{9,8},{10,11... | collective-permute-start | bytes 983048 | tf_op jit(solution)/shard_map/ppermute | solution.py:30
  8.5 11.5 %collective-permute-start.1 = (bf16[128,1280]{1,0:T(8,128)(2,1)S(1)}, bf16[128,1280]{1,0:T(8,128)(2,1)S(1)}, u32[]{:S(2)}, u32[]{:S(2)}) collective-permute-start(bf16[128,1280]{1,0:T(8,128)(2,1)S(1)} %pad_maximum_fusion.refs_0_), channel_id=1, source_target_pairs={{0,2},{1,3},{2,4},{3,5},{4,6},{5,7},{6,0},{7,1},{8,10},{9,11},{10,... | collective-permute-start | bytes 983048 | tf_op jit(solution)/shard_map/ppermute | solution.py:35
  20.0 1.3 copy-start.12
  20.0 12.5 %collective-permute-start.6 = (bf16[256,4096]{1,0:T(8,128)(2,1)}, bf16[256,4096]{1,0:T(8,128)(2,1)}, u32[]{:S(2)}, u32[]{:S(2)}) collective-permute-start(bf16[256,4096]{1,0:T(8,128)(2,1)} %out_own.1), channel_id=1, source_target_pairs={{0,8},{8,0},{1,9},{9,1},{2,10},{10,2},{3,11},{11,3},{4,12},{12,4},... | collective-permute-start | bytes 6291464 | tf_op jit(solution)/shard_map/ppermute | solution.py:25
  21.4 8.9 %collective-permute-start.5 = (bf16[128,1280]{1,0:T(8,128)(2,1)S(1)}, bf16[128,1280]{1,0:T(8,128)(2,1)S(1)}, u32[]{:S(2)}, u32[]{:S(2)}) collective-permute-start(bf16[128,1280]{1,0:T(8,128)(2,1)S(1)} %collective-permute-done.1.refs_2_), channel_id=1, source_target_pairs={{0,1},{1,0},{2,3},{3,2},{4,5},{5,4},{6,7},{7,6},{8,9},{9,8},{10,11... | collective-permute-start | bytes 983048 | tf_op jit(solution)/shard_map/ppermute | solution.py:30
  21.9 10.7 %collective-permute-start.4 = (bf16[128,1280]{1,0:T(8,128)(2,1)S(1)}, bf16[128,1280]{1,0:T(8,128)(2,1)S(1)}, u32[]{:S(2)}, u32[]{:S(2)}) collective-permute-start(bf16[128,1280]{1,0:T(8,128)(2,1)S(1)} %collective-permute-done.1.refs_2_), channel_id=1, source_target_pairs={{0,2},{1,3},{2,4},{3,5},{4,6},{5,7},{6,0},{7,1},{8,10},{9,11},{10,... | collective-permute-start | bytes 983048 | tf_op jit(solution)/shard_map/ppermute | solution.py:35
  32.6 9.9 %collective-permute-start.10 = (bf16[128,1280]{1,0:T(8,128)(2,1)S(1)}, bf16[128,1280]{1,0:T(8,128)(2,1)}, u32[]{:S(2)}, u32[]{:S(2)}) collective-permute-start(bf16[128,1280]{1,0:T(8,128)(2,1)S(1)} %collective-permute-done.4.refs_4_), channel_id=1, source_target_pairs={{0,2},{1,3},{2,4},{3,5},{4,6},{5,7},{6,0},{7,1},{8,10},{9,11},{10,... | collective-permute-start | bytes 983048 | tf_op jit(solution)/shard_map/ppermute | solution.py:35
  32.6 9.9 %collective-permute-start.9 = (bf16[128,1280]{1,0:T(8,128)(2,1)S(1)}, bf16[128,1280]{1,0:T(8,128)(2,1)S(1)}, u32[]{:S(2)}, u32[]{:S(2)}) collective-permute-start(bf16[128,1280]{1,0:T(8,128)(2,1)S(1)} %collective-permute-done.4.refs_4_), channel_id=1, source_target_pairs={{0,1},{1,0},{2,3},{3,2},{4,5},{5,4},{6,7},{7,6},{8,9},{9,8},{10,11... | collective-permute-start | bytes 983048 | tf_op jit(solution)/shard_map/ppermute | solution.py:30
  33.9 9.3 %collective-permute-start.8 = (bf16[4,256,256]{2,1,0:T(8,128)(2,1)S(1)}, bf16[4,256,256]{2,1,0:T(8,128)(2,1)S(1)}, u32[]{:S(2)}, u32[]{:S(2)}) collective-permute-start(bf16[4,256,256]{2,1,0:T(8,128)(2,1)S(1)} %copy-done.1), channel_id=1, source_target_pairs={{0,8},{8,0},{1,9},{9,1},{2,10},{10,2},{3,11},{11,3},{4,12},{12,4},... | collective-permute-start | bytes 1572872 | tf_op jit(solution)/shard_map/ppermute | solution.py:25
  34.2 1.8 %collective-permute-start.11 = (s32[1,128]{1,0:T(1,128)S(1)}, s32[1,128]{1,0:T(1,128)S(1)}, u32[]{:S(2)}, u32[]{:S(2)}) collective-permute-start(s32[1,128]{1,0:T(1,128)S(1)} %slice_bitcast_fusion), channel_id=1, source_target_pairs={{0,8},{8,0},{1,9},{9,1},{2,10},{10,2},{3,11},{11,3},{4,12},{12,4},... | collective-permute-start | bytes 1544 | tf_op jit(solution)/shard_map/ppermute | solution.py:25
  34.7 1.1 collective-permute-start.7
  42.5 0.7 copy-start.3
  43.2 7.4 %collective-permute-start.12 = (bf16[128,1280]{1,0:T(8,128)(2,1)}, bf16[128,1280]{1,0:T(8,128)(2,1)}, u32[]{:S(2)}, u32[]{:S(2)}) collective-permute-start(bf16[128,1280]{1,0:T(8,128)(2,1)} %collective-permute-done.10.refs_6_), channel_id=1, source_target_pairs={{0,1},{1,0},{2,3},{3,2},{4,5},{5,4},{6,7},{7,6},{8,9},{9,8},{10,11... | collective-permute-start | bytes 983048 | tf_op jit(solution)/shard_map/ppermute | solution.py:30
  50.6 1.0 copy-start.4
  59.9 36.0 %copy-start.10 = (bf16[128,1024]{1,0:T(8,128)(2,1)S(1)}, bf16[128,1024]{1,0:T(8,128)(2,1)}, u32[]{:S(2)}) copy-start(bf16[128,1024]{1,0:T(8,128)(2,1)} %copy-done.9) | copy-start | bytes 786436
  59.9 36.0 %dynamic-slice-start = ((f32[8192]{0:T(1024)}, s32[]{:T(128)}), f32[1024]{0:T(1024)S(1)}, s32[]{:S(2)}) async-start(f32[8192]{0:T(1024)} %param.17, s32[]{:T(128)} %select_n.70), calls=%async_computation | async-start | bytes 8704 | tf_op jit(solution)/shard_map/dynamic_slice | solution.py:417
  59.9 9.3 %collective-permute-start.16 = (bf16[128,1024]{1,0:T(8,128)(2,1)S(1)}, bf16[128,1024]{1,0:T(8,128)(2,1)S(1)}, u32[]{:S(2)}, u32[]{:S(2)}) collective-permute-start(bf16[128,1024]{1,0:T(8,128)(2,1)S(1)} %get-tuple-element.43), channel_id=1, source_target_pairs={{0,1},{1,0},{2,3},{3,2},{4,5},{5,4},{6,7},{7,6},{8,9},{9,8},{10,11... | collective-permute-start | bytes 786440 | tf_op jit(solution)/shard_map/ppermute | solution.py:30
  61.0 13.2 %collective-permute-start.15 = (bf16[128,1024]{1,0:T(8,128)(2,1)S(1)}, bf16[128,1024]{1,0:T(8,128)(2,1)S(1)}, u32[]{:S(2)}, u32[]{:S(2)}) collective-permute-start(bf16[128,1024]{1,0:T(8,128)(2,1)S(1)} %get-tuple-element.41), channel_id=1, source_target_pairs={{0,1},{1,0},{2,3},{3,2},{4,5},{5,4},{6,7},{7,6},{8,9},{9,8},{10,11... | collective-permute-start | bytes 786440 | tf_op jit(solution)/shard_map/ppermute | solution.py:30
  69.3 9.5 %collective-permute-start.17 = (bf16[128,1024]{1,0:T(8,128)(2,1)S(1)}, bf16[128,1024]{1,0:T(8,128)(2,1)S(1)}, u32[]{:S(2)}, u32[]{:S(2)}) collective-permute-start(bf16[128,1024]{1,0:T(8,128)(2,1)S(1)} %add_convert_fusion.2), channel_id=1, source_target_pairs={{0,2},{1,3},{2,4},{3,5},{4,6},{5,7},{6,0},{7,1},{8,10},{9,11},{10,... | collective-permute-start | bytes 786440 | tf_op jit(solution)/shard_map/ppermute | solution.py:35
  69.4 10.5 %collective-permute-start.14 = (bf16[128,1024]{1,0:T(8,128)(2,1)S(1)}, bf16[128,1024]{1,0:T(8,128)(2,1)S(1)}, u32[]{:S(2)}, u32[]{:S(2)}) collective-permute-start(bf16[128,1024]{1,0:T(8,128)(2,1)S(1)} %get-tuple-element.39), channel_id=1, source_target_pairs={{0,1},{1,0},{2,3},{3,2},{4,5},{5,4},{6,7},{7,6},{8,9},{9,8},{10,11... | collective-permute-start | bytes 786440 | tf_op jit(solution)/shard_map/ppermute | solution.py:30
  78.8 27.9 %copy-start.7 = (bf16[4096,512]{1,0:T(8,128)(2,1)S(1)}, bf16[4096,512]{1,0:T(8,128)(2,1)}, u32[]{:S(2)}) copy-start(bf16[4096,512]{1,0:T(8,128)(2,1)} %own_ref.1) | copy-start | bytes 12582916
  79.0 49.6 %copy-start.14 = (f32[8192]{0:T(1024)S(1)}, f32[8192]{0:T(1024)}, u32[]{:S(2)}) copy-start(f32[8192]{0:T(1024)} %param.17) | copy-start | bytes 98308
  79.0 8.6 %collective-permute-start.18 = (bf16[128,1024]{1,0:T(8,128)(2,1)S(1)}, bf16[128,1024]{1,0:T(8,128)(2,1)S(1)}, u32[]{:S(2)}, u32[]{:S(2)}) collective-permute-start(bf16[128,1024]{1,0:T(8,128)(2,1)S(1)} %add_convert_fusion.1), channel_id=1, source_target_pairs={{0,2},{1,3},{2,4},{3,5},{4,6},{5,7},{6,0},{7,1},{8,10},{9,11},{10,... | collective-permute-start | bytes 786440 | tf_op jit(solution)/shard_map/ppermute | solution.py:35
  79.0 8.7 %collective-permute-start.13 = (bf16[128,1024]{1,0:T(8,128)(2,1)S(1)}, bf16[128,1024]{1,0:T(8,128)(2,1)S(1)}, u32[]{:S(2)}, u32[]{:S(2)}) collective-permute-start(bf16[128,1024]{1,0:T(8,128)(2,1)S(1)} %get-tuple-element.37), channel_id=1, source_target_pairs={{0,1},{1,0},{2,3},{3,2},{4,5},{5,4},{6,7},{7,6},{8,9},{9,8},{10,11... | collective-permute-start | bytes 786440 | tf_op jit(solution)/shard_map/ppermute | solution.py:30
  87.7 8.2 %collective-permute-start.19 = (bf16[128,1024]{1,0:T(8,128)(2,1)S(1)}, bf16[128,1024]{1,0:T(8,128)(2,1)S(1)}, u32[]{:S(2)}, u32[]{:S(2)}) collective-permute-start(bf16[128,1024]{1,0:T(8,128)(2,1)S(1)} %add_convert_fusion), channel_id=1, source_target_pairs={{0,2},{1,3},{2,4},{3,5},{4,6},{5,7},{6,0},{7,1},{8,10},{9,11},{10,... | collective-permute-start | bytes 786440 | tf_op jit(solution)/shard_map/ppermute | solution.py:35
  96.1 1.6 %collective-permute-start.20 = (bf16[128,1024]{1,0:T(8,128)(2,1)S(1)}, bf16[128,1024]{1,0:T(8,128)(2,1)S(1)}, u32[]{:S(2)}, u32[]{:S(2)}) collective-permute-start(bf16[128,1024]{1,0:T(8,128)(2,1)S(1)} %get-tuple-element.53), channel_id=1, source_target_pairs={{0,8},{8,0},{1,9},{9,1},{2,10},{10,2},{3,11},{11,3},{4,12},{12,4},... | collective-permute-start | bytes 786440 | tf_op jit(solution)/shard_map/ppermute | solution.py:25
  96.2 10.5 %collective-permute-start.21 = (bf16[128,1024]{1,0:T(8,128)(2,1)S(1)}, bf16[128,1024]{1,0:T(8,128)(2,1)S(1)}, u32[]{:S(2)}, u32[]{:S(2)}) collective-permute-start(bf16[128,1024]{1,0:T(8,128)(2,1)S(1)} %get-tuple-element.52.refs_0_), channel_id=1, source_target_pairs={{0,2},{1,3},{2,4},{3,5},{4,6},{5,7},{6,0},{7,1},{8,10},{9,11},{10,... | collective-permute-start | bytes 786440 | tf_op jit(solution)/shard_map/ppermute | solution.py:35
  96.3 10.4 %collective-permute-start.22 = (bf16[128,1024]{1,0:T(8,128)(2,1)S(1)}, bf16[128,1024]{1,0:T(8,128)(2,1)S(1)}, u32[]{:S(2)}, u32[]{:S(2)}) collective-permute-start(bf16[128,1024]{1,0:T(8,128)(2,1)S(1)} %get-tuple-element.52.refs_0_), channel_id=1, source_target_pairs={{0,1},{1,0},{2,3},{3,2},{4,5},{5,4},{6,7},{7,6},{8,9},{9,8},{10,11... | collective-permute-start | bytes 786440 | tf_op jit(solution)/shard_map/ppermute | solution.py:30
  106.7 10.8 %collective-permute-start.23 = (bf16[4096,512]{1,0:T(8,128)(2,1)S(1)}, bf16[4096,512]{1,0:T(8,128)(2,1)S(1)}, u32[]{:S(2)}, u32[]{:S(2)}) collective-permute-start(bf16[4096,512]{1,0:T(8,128)(2,1)S(1)} %copy-done.7), channel_id=1, source_target_pairs={{0,8},{8,0},{1,9},{9,1},{2,10},{10,2},{3,11},{11,3},{4,12},{12,4},... | collective-permute-start | bytes 12582920 | tf_op jit(solution)/shard_map/ppermute | solution.py:25
  106.7 8.7 %collective-permute-start.24 = (bf16[128,1024]{1,0:T(8,128)(2,1)S(1)}, bf16[128,1024]{1,0:T(8,128)(2,1)S(1)}, u32[]{:S(2)}, u32[]{:S(2)}) collective-permute-start(bf16[128,1024]{1,0:T(8,128)(2,1)S(1)} %collective-permute-done.21.refs_2_), channel_id=1, source_target_pairs={{0,1},{1,0},{2,3},{3,2},{4,5},{5,4},{6,7},{7,6},{8,9},{9,8},{10,11... | collective-permute-start | bytes 786440 | tf_op jit(solution)/shard_map/ppermute | solution.py:30
  107.3 10.2 %collective-permute-start.25 = (bf16[128,1024]{1,0:T(8,128)(2,1)S(1)}, bf16[128,1024]{1,0:T(8,128)(2,1)S(1)}, u32[]{:S(2)}, u32[]{:S(2)}) collective-permute-start(bf16[128,1024]{1,0:T(8,128)(2,1)S(1)} %collective-permute-done.21.refs_2_), channel_id=1, source_target_pairs={{0,2},{1,3},{2,4},{3,5},{4,6},{5,7},{6,0},{7,1},{8,10},{9,11},{10,... | collective-permute-start | bytes 786440 | tf_op jit(solution)/shard_map/ppermute | solution.py:35
  117.5 10.6 %copy-start.8 = (bf16[4096,512]{1,0:T(8,128)(2,1)}, bf16[4096,512]{1,0:T(8,128)(2,1)S(1)}, u32[]{:S(2)}) copy-start(bf16[4096,512]{1,0:T(8,128)(2,1)S(1)} %collective-permute-done.23.other_ref) | copy-start | bytes 12582916
  117.5 7.5 %collective-permute-start.26 = (bf16[128,1024]{1,0:T(8,128)(2,1)S(1)}, bf16[128,1024]{1,0:T(8,128)(2,1)S(1)}, u32[]{:S(2)}, u32[]{:S(2)}) collective-permute-start(bf16[128,1024]{1,0:T(8,128)(2,1)S(1)} %collective-permute-done.25.refs_4_), channel_id=1, source_target_pairs={{0,1},{1,0},{2,3},{3,2},{4,5},{5,4},{6,7},{7,6},{8,9},{9,8},{10,11... | collective-permute-start | bytes 786440 | tf_op jit(solution)/shard_map/ppermute | solution.py:30
  119.0 9.1 %collective-permute-start.27 = (bf16[128,1024]{1,0:T(8,128)(2,1)S(1)}, bf16[128,1024]{1,0:T(8,128)(2,1)S(1)}, u32[]{:S(2)}, u32[]{:S(2)}) collective-permute-start(bf16[128,1024]{1,0:T(8,128)(2,1)S(1)} %collective-permute-done.25.refs_4_), channel_id=1, source_target_pairs={{0,2},{1,3},{2,4},{3,5},{4,6},{5,7},{6,0},{7,1},{8,10},{9,11},{10,... | collective-permute-start | bytes 786440 | tf_op jit(solution)/shard_map/ppermute | solution.py:35
  128.0 6.4 %collective-permute-start.28 = (bf16[128,1024]{1,0:T(8,128)(2,1)S(1)}, bf16[128,1024]{1,0:T(8,128)(2,1)S(1)}, u32[]{:S(2)}, u32[]{:S(2)}) collective-permute-start(bf16[128,1024]{1,0:T(8,128)(2,1)S(1)} %collective-permute-done.27.refs_6_), channel_id=1, source_target_pairs={{0,1},{1,0},{2,3},{3,2},{4,5},{5,4},{6,7},{7,6},{8,9},{9,8},{10,11... | collective-permute-start | bytes 786440 | tf_op jit(solution)/shard_map/ppermute | solution.py:30
  138.5 3.7 %collective-permute-start.29 = (f32[3,128]{1,0:T(4,128)S(1)}, f32[3,128]{1,0:T(4,128)S(1)}, u32[]{:S(2)}, u32[]{:S(2)}) collective-permute-start(f32[3,128]{1,0:T(4,128)S(1)} %slice.71), channel_id=1, source_target_pairs={{0,1},{1,0},{2,3},{3,2},{4,5},{5,4},{6,7},{7,6},{8,9},{9,8},{10,11... | collective-permute-start | bytes 4616 | tf_op jit(solution)/shard_map/ppermute | solution.py:42
  142.2 3.7 %collective-permute-start.30 = (f32[3,128]{1,0:T(4,128)S(1)}, f32[3,128]{1,0:T(4,128)S(1)}, u32[]{:S(2)}, u32[]{:S(2)}) collective-permute-start(f32[3,128]{1,0:T(4,128)S(1)} %pad_maximum_fusion.1), channel_id=1, source_target_pairs={{0,2},{1,3},{2,0},{3,1},{4,6},{5,7},{6,4},{7,5},{8,10},{9,11},{10,... | collective-permute-start | bytes 4616 | tf_op jit(solution)/shard_map/ppermute | solution.py:42
  145.9 4.5 %collective-permute-start.31 = (f32[3,128]{1,0:T(4,128)S(1)}, f32[3,128]{1,0:T(4,128)S(1)}, u32[]{:S(2)}, u32[]{:S(2)}) collective-permute-start(f32[3,128]{1,0:T(4,128)S(1)} %pad_maximum_fusion.2), channel_id=1, source_target_pairs={{0,4},{1,5},{2,6},{3,7},{4,0},{5,1},{6,2},{7,3},{8,12},{9,13},{10,... | collective-permute-start | bytes 4616 | tf_op jit(solution)/shard_map/ppermute | solution.py:42
  150.5 1.2 collective-permute-start.32

commit v4 on v3

--- a/solution.py
+++ b/solution.py
@@ -166,27 +166,92 @@
         pl.when(jnp.logical_not(is_here))(there.start)
 
 
+def query_blocks(blocks, shard, ids, copies, held, gain_ref, query, new_kv, squares):
+    kv_head = lax.axis_index("tensor") * QH_DEV // GROUP
+    kv_place = pl.ds(pl.multiple_of(shard + kv_head * 2 * HEAD, 2 * HEAD), 2 * HEAD)
+    for j, block in enumerate(blocks):
+        values = block[:, :shard].astype(jnp.float32)
+        squares += jnp.sum(values * values, axis=1, keepdims=True)
+        gained = (values * gain_ref[pl.ds(ids[j], 1), :]).astype(jnp.bfloat16)
+        new_kv += block[:, kv_place].astype(jnp.float32)
+        copies[j][1].wait()
+        query += product(gained, held[j])
+    return query, new_kv, squares
+
+
+def query_kernel(shard, gain_ref, q_own, q_other, *refs):
+    blocks, (query_ref, kv_ref, squares_ref, held, sems) = refs[:-5], refs[-5:]
+    ids = gathered_ids()[: len(blocks)]
+    copies = block_copies(ids, 0, q_own, q_other, held, sems)
+    start_copies(copies)
+    query, new_kv = jnp.zeros(query_ref.shape, jnp.float32), jnp.zeros(kv_ref.shape, jnp.float32)
+    squares = jnp.zeros((query.shape[0], 1), jnp.float32)
+    query, new_kv, squares = query_blocks(
+        blocks, shard, ids, copies, held, gain_ref, query, new_kv, squares
+    )
+    query_ref[...] = query
+    kv_ref[...] = new_kv
+    squares_ref[...] = jnp.broadcast_to(squares, squares_ref.shape)
+
+
+def query_part(gains, q_pair, blocks):
+    shard, used, half = gains.shape[1], len(blocks), blocks[0].shape[0]
+    q_width = q_pair[0].shape[1]
+    vmem = pl.BlockSpec(memory_space=pltpu.VMEM)
+    anywhere = pl.BlockSpec(memory_space=pl.ANY)
+    return pl.pallas_call(
+        functools.partial(query_kernel, shard),
+        out_shape=[
+            jax.ShapeDtypeStruct((half, q_width), jnp.float32),
+            jax.ShapeDtypeStruct((half, 2 * HEAD), jnp.float32),
+            jax.ShapeDtypeStruct((half, 128), jnp.float32),
+        ],
+        in_specs=[vmem] + [anywhere] * 2 + [vmem] * used,
+        out_specs=[vmem] * 3,
+        scratch_shapes=[
+            pltpu.VMEM((used, shard, q_width), jnp.bfloat16),
+            pltpu.SemaphoreType.DMA((used,)),
+        ],
+        compiler_params=pltpu.CompilerParams(vmem_limit_bytes=VMEM_LIMIT),
+        cost_estimate=pl.CostEstimate(
+            flops=2 * half * used * shard * q_width,
+            bytes_accessed=2 * used * shard * (half + q_width),
+            transcendentals=0,
+        ),
+        name="query_part",
+    )(gains, *q_pair, *blocks)
+
+
 def attention_kernel(
     seqs_count,
-    count,
     lens_ref,
     ctx_ref,
     gain_ref,
+    query_ref,
+    kv_ref,
+    squares_ref,
+    block_ref,
     q_own,
     q_other,
     cache_own,
     cache_other,
     out_own,
     out_other,
-    *refs,
+    attn_ref,
+    first_ref,
+    q_held,
+    cache_held,
+    out_held,
+    q_sems,
+    cache_sems,
+    out_sems,
 ):
-    blocks, outs = refs[:count], refs[count : 2 * count]
-    q_held, cache_held, out_held, q_sems, cache_sems, out_sems = refs[2 * count :]
-    half, shard = outs[0].shape
+    half, shard = first_ref.shape
+    count = lax.axis_size("tensor")
     ctx_slots = cache_own.shape[1]
-    ids = gathered_ids()
+    ids = gathered_ids()[-1:]
     q_copies = block_copies(ids, 0, q_own, q_other, q_held, q_sems)
-    out_copies = block_copies(scattered_ids(), 1, out_own, out_other, out_held, out_sems)
+    out_copies = block_copies(scattered_ids()[1:2], 1, out_own, out_other, out_held, out_sems)
     cache_copies = [
         pltpu.make_async_copy(cache_own, cache_held.at[0], cache_sems.at[0]),
         pltpu.make_async_copy(cache_other, cache_held.at[1], cache_sems.at[1]),
@@ -196,153 +261,238 @@
         copy.start()
     start_copies(out_copies)
 
-    squares = jnp.zeros((half, 1), jnp.float32)
-    for block in blocks:
-        values = block[:, :shard].astype(jnp.float32)
-        squares += jnp.sum(values * values, axis=1, keepdims=True)
+    query, new_kv, squares = query_blocks(
+        [block_ref],
+        shard,
+        ids,
+        q_copies,
+        q_held,
+        gain_ref,
+        query_ref[...],
+        kv_ref[...],
+        squares_ref[:, :1],
+    )
     scale = lax.rsqrt(squares / (shard * count) + EPS)
-    query = jnp.zeros((half, q_own.shape[1]), jnp.float32)
-    for j, block in enumerate(blocks):
-        gain = gain_ref[pl.ds(ids[j], 1), :]
-        normed = (block[:, :shard].astype(jnp.float32) * scale * gain).astype(jnp.bfloat16)
-        q_copies[j][1].wait()
-        query += product(normed, q_held[j])
-    query = query.astype(jnp.bfloat16)
-    kv_head = lax.axis_index("tensor") * QH_DEV // GROUP
-    kv_place = pl.ds(pl.multiple_of(shard + kv_head * 2 * HEAD, 2 * HEAD), 2 * HEAD)
-    kv_sum = jnp.zeros((half, 2 * HEAD), jnp.float32)
-    for block in blocks:
-        kv_sum += block[:, kv_place].astype(jnp.float32)
-    new_kv = (kv_sum * scale).astype(jnp.bfloat16)
+    query = (query * scale).astype(jnp.bfloat16)
+    new_kv = (new_kv * scale).astype(jnp.bfloat16)
 
     busy, light_total, long_seq, long_start, own_ends, busy_ends = row_plan(
         lens_ref, seqs_count, half
     )
+
+    def segments(slot):
+        rest, rest_row = rest_rows(slot, light_total, long_start, half)
+        own_seg, rest_seg = jnp.zeros_like(slot), jnp.full_like(slot, seqs_count)
+        for i in range(seqs_count):
+            own_seg += jnp.where(slot >= own_ends[i], 1, 0)
+            rest_seg += jnp.where(rest_row >= busy_ends[i], 1, 0)
+        return jnp.where(busy, long_seq, jnp.where(rest < 0, own_seg, rest_seg))
+
     slot = lax.broadcasted_iota(jnp.int32, (half, 1), 0)
-    rest, rest_row = rest_rows(slot, light_total, long_start, half)
-    own_seg, rest_seg = jnp.zeros_like(slot), jnp.full_like(slot, seqs_count)
-    for i in range(seqs_count):
-        own_seg += jnp.where(slot >= own_ends[i], 1, 0)
-        rest_seg += jnp.where(rest_row >= busy_ends[i], 1, 0)
-    seg = jnp.where(busy, long_seq, jnp.where(rest < 0, own_seg, rest_seg))
+    key_slot = lax.broadcasted_iota(jnp.int32, (1, half), 1)
+    seg = segments(slot)
+    own_ok = (segments(key_slot) == seg) & (key_slot <= slot)
     position = lax.broadcasted_iota(jnp.int32, (half, ctx_slots), 1)
-    ctx_ok = jnp.concatenate(
-        [(seg == i) & (position < ctx_ref[i]) for i in range(2 * seqs_count)], axis=1
-    )
-    slot_b = lax.broadcasted_iota(jnp.int32, (half, half), 1)
-    rest_b, rest_row_b = rest_rows(slot_b, light_total, long_start, half)
-    own_seg_b, rest_seg_b = jnp.zeros_like(slot_b), jnp.full_like(slot_b, seqs_count)
-    for i in range(seqs_count):
-        own_seg_b += jnp.where(slot_b >= own_ends[i], 1, 0)
-        rest_seg_b += jnp.where(rest_row_b >= busy_ends[i], 1, 0)
-    seg_b = jnp.where(busy, long_seq, jnp.where(rest_b < 0, own_seg_b, rest_seg_b))
-    own_ok = (seg_b == seg) & (slot_b <= slot)
 
     for copy in cache_copies:
         copy.wait()
     keys = cache_held[:, :, :, :HEAD].reshape(-1, HEAD)
     vals = cache_held[:, :, :, HEAD:].reshape(-1, HEAD)
-    heads = []
+    stacked = jnp.concatenate(
+        [query[:, h * HEAD : (h + 1) * HEAD] for h in range(QH_DEV)], axis=0
+    )
+    contract = (((1,), (1,)), ((), ()))
+    ctx_scores = lax.dot_general(stacked, keys, contract, preferred_element_type=jnp.float32)
+    own_scores = lax.dot_general(
+        stacked, new_kv[:, :HEAD], contract, preferred_element_type=jnp.float32
+    )
+    ctx_scores = ctx_scores * HEAD ** (-0.5)
+    own_scores = own_scores * HEAD ** (-0.5)
+    heads_ctx, heads_own = [], []
     for h in range(QH_DEV):
-        own_query = query[:, h * HEAD : (h + 1) * HEAD]
-        contract = (((1,), (1,)), ((), ()))
-        ctx_scores = lax.dot_general(own_query, keys, contract, preferred_element_type=jnp.float32)
-        own_scores = lax.dot_general(
-            own_query, new_kv[:, :HEAD], contract, preferred_element_type=jnp.float32
+        rows = slice(h * half, (h + 1) * half)
+        pieces = []
+        for i in range(2 * seqs_count):
+            allowed = (seg == i) & (position < ctx_ref[i])
+            piece = ctx_scores[rows, i * ctx_slots : (i + 1) * ctx_slots]
+            pieces.append(jnp.where(allowed, piece, -jnp.inf))
+        scores = jnp.concatenate(pieces, axis=1)
+        own = jnp.where(own_ok, own_scores[rows], -jnp.inf)
+        top = jnp.maximum(
+            jnp.max(scores, axis=1, keepdims=True), jnp.max(own, axis=1, keepdims=True)
         )
-        ctx_scores = jnp.where(ctx_ok, ctx_scores * HEAD ** (-0.5), -jnp.inf)
-        own_scores = jnp.where(own_ok, own_scores * HEAD ** (-0.5), -jnp.inf)
-        top = jnp.maximum(
-            jnp.max(ctx_scores, axis=1, keepdims=True), jnp.max(own_scores, axis=1, keepdims=True)
-        )
-        ctx_weights, own_weights = jnp.exp(ctx_scores - top), jnp.exp(own_scores - top)
-        total = jnp.sum(ctx_weights, axis=1, keepdims=True) + jnp.sum(
+        weights, own_weights = jnp.exp(scores - top), jnp.exp(own - top)
+        total = jnp.sum(weights, axis=1, keepdims=True) + jnp.sum(
             own_weights, axis=1, keepdims=True
         )
-        heads.append(
-            product((ctx_weights / total).astype(jnp.bfloat16), vals)
-            + product((own_weights / total).astype(jnp.bfloat16), new_kv[:, HEAD:])
-        )
-    attn = jnp.concatenate(heads, axis=1).astype(jnp.bfloat16)
-    for j, out in enumerate(outs):
-        out_copies[j][1].wait()
-        out[...] = product(attn, out_held[j]).astype(jnp.bfloat16)
-
-
-def attend(resp_len, both_ctx, attn_gain, q_pair, cache_pair, out_pair, blocks):
-    count = len(blocks)
-    half, shard = blocks[0].shape[0], attn_gain.shape[0] // count
+        heads_ctx.append((weights / total).astype(jnp.bfloat16))
+        heads_own.append((own_weights / total).astype(jnp.bfloat16))
+    mixed_vals = product(jnp.concatenate(heads_ctx, axis=0), vals) + product(
+        jnp.concatenate(heads_own, axis=0), new_kv[:, HEAD:]
+    )
+    attn = jnp.concatenate(
+        [mixed_vals[h * half : (h + 1) * half] for h in range(QH_DEV)], axis=1
+    ).astype(jnp.bfloat16)
+    attn_ref[...] = attn
+    out_copies[0][1].wait()
+    first_ref[...] = product(attn, out_held[0]).astype(jnp.bfloat16)
+
+
+def attend(resp_len, both_ctx, gains, parts, block, q_pair, cache_pair, out_pair):
+    half, shard = block.shape[0], gains.shape[1]
     seqs_count, ctx_slots, width = cache_pair[0].shape
     q_width, attn_width = q_pair[0].shape[1], out_pair[0].shape[0]
     vmem = pl.BlockSpec(memory_space=pltpu.VMEM)
     smem = pl.BlockSpec(memory_space=pltpu.SMEM)
     anywhere = pl.BlockSpec(memory_space=pl.ANY)
     return pl.pallas_call(
-        functools.partial(attention_kernel, seqs_count, count),
-        out_shape=[jax.ShapeDtypeStruct((half, shard), jnp.bfloat16)] * count,
-        in_specs=[smem] * 2 + [vmem] + [anywhere] * 6 + [vmem] * count,
-        out_specs=[vmem] * count,
+        functools.partial(attention_kernel, seqs_count),
+        out_shape=[
+            jax.ShapeDtypeStruct((half, attn_width), jnp.bfloat16),
+            jax.ShapeDtypeStruct((half, shard), jnp.bfloat16),
+        ],
+        in_specs=[smem] * 2 + [vmem] * 5 + [anywhere] * 6,
+        out_specs=[vmem] * 2,
         scratch_shapes=[
-            pltpu.VMEM((count, shard, q_width), jnp.bfloat16),
+            pltpu.VMEM((1, shard, q_width), jnp.bfloat16),
             pltpu.VMEM((2, seqs_count, ctx_slots, width), jnp.bfloat16),
-            pltpu.VMEM((count, attn_width, shard), jnp.bfloat16),
-            pltpu.SemaphoreType.DMA((count,)),
+            pltpu.VMEM((1, attn_width, shard), jnp.bfloat16),
+            pltpu.SemaphoreType.DMA((1,)),
             pltpu.SemaphoreType.DMA((2,)),
-            pltpu.SemaphoreType.DMA((count,)),
+            pltpu.SemaphoreType.DMA((1,)),
         ],
         compiler_params=pltpu.CompilerParams(vmem_limit_bytes=VMEM_LIMIT),
         name="attend",
-    )(resp_len, both_ctx, attn_gain.reshape(count, shard), *q_pair, *cache_pair, *out_pair, *blocks)
-
-
-def vocab_kernel(count, targets_ref, gain_ref, own_ref, other_ref, *refs):
-    blocks, (stats_ref, held, sems) = refs[:count], refs[count:]
-    half, shard = blocks[0].shape
-    ids = gathered_ids()
+    )(resp_len, both_ctx, gains, *parts, block, *q_pair, *cache_pair, *out_pair)
+
+
+def out_kernel(attn_ref, out_own, out_other, *refs):
+    outs, (held, sems) = refs[:-2], refs[-2:]
+    ids = scattered_ids()
+    copies = block_copies(ids[:1] + ids[2:], 1, out_own, out_other, held, sems)
+    start_copies(copies)
+    attn = attn_ref[...]
+    for j, out in enumerate(outs):
+        copies[j][1].wait()
+        out[...] = product(attn, held[j]).astype(jnp.bfloat16)
+
+
+def out_products(attn, out_pair):
+    half, attn_width = attn.shape
+    count = lax.axis_size("tensor")
+    shard = out_pair[0].shape[1] * 2 // count
+    vmem = pl.BlockSpec(memory_space=pltpu.VMEM)
+    anywhere = pl.BlockSpec(memory_space=pl.ANY)
+    return pl.pallas_call(
+        out_kernel,
+        out_shape=[jax.ShapeDtypeStruct((half, shard), jnp.bfloat16)] * (count - 1),
+        in_specs=[vmem] + [anywhere] * 2,
+        out_specs=[vmem] * (count - 1),
+        scratch_shapes=[
+            pltpu.VMEM((count - 1, attn_width, shard), jnp.bfloat16),
+            pltpu.SemaphoreType.DMA((count - 1,)),
+        ],
+        compiler_params=pltpu.CompilerParams(vmem_limit_bytes=VMEM_LIMIT),
+        cost_estimate=pl.CostEstimate(
+            flops=2 * half * (count - 1) * shard * attn_width,
+            bytes_accessed=2 * (count - 1) * shard * (half + attn_width),
+            transcendentals=0,
+        ),
+        name="out_products",
+    )(attn, *out_pair)
+
+
+def logit_blocks(blocks, ids, copies, held, gain_ref, logits, squares):
+    for j, block in enumerate(blocks):
+        values = block[...]
+        mixed = values.astype(jnp.float32) / gain_ref[pl.ds(ids[j], 1), :]
+        squares += jnp.sum(mixed * mixed, axis=1, keepdims=True)
+        copies[j][1].wait()
+        logits += product(values, held[j])
+    return logits, squares
+
+
+def logit_kernel(gain_ref, own_ref, other_ref, *refs):
+    blocks, (logits_ref, squares_ref, held, sems) = refs[:-4], refs[-4:]
+    ids = gathered_ids()[: len(blocks)]
     copies = block_copies(ids, 0, own_ref, other_ref, held, sems)
     start_copies(copies)
-    vocab_count = own_ref.shape[1]
-    logits = jnp.zeros((half, vocab_count), jnp.float32)
-    squares = jnp.zeros((half, 1), jnp.float32)
-    for j, block in enumerate(blocks):
-        copies[j][1].wait()
-        values = block[...]
-        logits += product(values, held[j])
-        mixed = values.astype(jnp.float32) / gain_ref[pl.ds(ids[j], 1), :]
-        squares += jnp.sum(mixed * mixed, axis=1, keepdims=True)
-    scale = lax.rsqrt(squares / (shard * count) + EPS)
-    logits = logits * scale
-    column_ids = lax.axis_index("tensor") * vocab_count + lax.broadcasted_iota(
-        jnp.int32, (half, vocab_count), 1
-    )
-    picked = jnp.sum(
-        jnp.where(column_ids == targets_ref[...], logits, 0.0), axis=1, keepdims=True
-    )
-    top = jnp.max(logits, axis=1, keepdims=True)
-    total = jnp.sum(jnp.exp(logits - top), axis=1, keepdims=True)
-    lane = lax.broadcasted_iota(jnp.int32, (half, half), 1)
-    stats = jnp.where(lane == 0, top, jnp.where(lane == 1, total, picked))
-    stats_ref[...] = jnp.transpose(stats)[:8]
-
-
-def vocab_stats(targets, final_gain, vocab_pair, blocks):
-    count = len(blocks)
-    half, shard = blocks[0].shape
+    logits = jnp.zeros(logits_ref.shape, jnp.float32)
+    squares = jnp.zeros((logits.shape[0], 1), jnp.float32)
+    logits, squares = logit_blocks(blocks, ids, copies, held, gain_ref, logits, squares)
+    logits_ref[...] = logits
+    squares_ref[...] = jnp.broadcast_to(squares, squares_ref.shape)
+
+
+def logit_part(gains, vocab_pair, blocks):
+    used, (half, shard) = len(blocks), blocks[0].shape
     vocab_count = vocab_pair[0].shape[1]
     vmem = pl.BlockSpec(memory_space=pltpu.VMEM)
     anywhere = pl.BlockSpec(memory_space=pl.ANY)
     return pl.pallas_call(
-        functools.partial(vocab_kernel, count),
+        logit_kernel,
+        out_shape=[
+            jax.ShapeDtypeStruct((half, vocab_count), jnp.float32),
+            jax.ShapeDtypeStruct((half, 128), jnp.float32),
+        ],
+        in_specs=[vmem] + [anywhere] * 2 + [vmem] * used,
+        out_specs=[vmem] * 2,
+        scratch_shapes=[
+            pltpu.VMEM((used, shard, vocab_count), jnp.bfloat16),
+            pltpu.SemaphoreType.DMA((used,)),
+        ],
+        compiler_params=pltpu.CompilerParams(vmem_limit_bytes=VMEM_LIMIT),
+        cost_estimate=pl.CostEstimate(
+            flops=2 * half * used * shard * vocab_count,
+            bytes_accessed=2 * used * shard * (half + vocab_count),
+            transcendentals=0,
+        ),
+        name="logit_part",
+    )(gains, *vocab_pair, *blocks)
+
+
+def stats_kernel(
+    targets_ref, gain_ref, logits_ref, squares_ref, block_ref, own_ref, other_ref, stats_ref, held, sems
+):
+    half, shard = block_ref.shape
+    ids = gathered_ids()[-1:]
+    copies = block_copies(ids, 0, own_ref, other_ref, held, sems)
+    start_copies(copies)
+    logits, squares = logit_blocks(
+        [block_ref], ids, copies, held, gain_ref, logits_ref[...], squares_ref[:, :1]
+    )
+    logits = logits * lax.rsqrt(squares / (shard * lax.axis_size("tensor")) + EPS)
+    vocab_count = logits.shape[1]
+    column_ids = lax.axis_index("tensor") * vocab_count + lax.broadcasted_iota(
+        jnp.int32, (half, vocab_count), 1
+    )
+    picked = jnp.sum(
+        jnp.where(column_ids == targets_ref[...], logits, 0.0), axis=1, keepdims=True
+    )
+    top = jnp.max(logits, axis=1, keepdims=True)
+    total = jnp.sum(jnp.exp(logits - top), axis=1, keepdims=True)
+    lane = lax.broadcasted_iota(jnp.int32, (half, 128), 1)
+    stats = jnp.where(lane == 0, top, jnp.where(lane == 1, total, picked))
+    stats_ref[...] = jnp.transpose(stats)[:8]
+
+
+def vocab_stats(targets, gains, parts, block, vocab_pair):
+    half, shard = block.shape
+    vocab_count = vocab_pair[0].shape[1]
+    vmem = pl.BlockSpec(memory_space=pltpu.VMEM)
+    anywhere = pl.BlockSpec(memory_space=pl.ANY)
+    return pl.pallas_call(
+        stats_kernel,
         out_shape=jax.ShapeDtypeStruct((8, half), jnp.float32),
-        in_specs=[vmem] * 2 + [anywhere] * 2 + [vmem] * count,
+        in_specs=[vmem] * 5 + [anywhere] * 2,
         out_specs=vmem,
         scratch_shapes=[
-            pltpu.VMEM((count, shard, vocab_count), jnp.bfloat16),
-            pltpu.SemaphoreType.DMA((count,)),
+            pltpu.VMEM((1, shard, vocab_count), jnp.bfloat16),
+            pltpu.SemaphoreType.DMA((1,)),
         ],
         compiler_params=pltpu.CompilerParams(vmem_limit_bytes=VMEM_LIMIT),
         name="vocab_stats",
-    )(targets.reshape(half, 1), final_gain.reshape(count, shard), *vocab_pair, *blocks)
+    )(targets.reshape(half, 1), gains, *parts, block, *vocab_pair)
 
 
 def per_device(
@@ -396,15 +546,14 @@
         ],
     )
     q_other, out_other, cache_other, both_ctx, targets = values
-    products = attend(
-        resp_len,
-        both_ctx,
-        attn_gain,
-        (q_weight, q_other),
-        (cache, cache_other),
-        (out_weight, out_other),
-        blocks,
-    )
+    q_pair, out_pair = (q_weight, q_other), (out_weight, out_other)
+    gains = attn_gain.reshape(tensor_count, shard)
+    parts = query_part(gains, q_pair, blocks[:-1])
+    attn, first = attend(
+        resp_len, both_ctx, gains, parts, blocks[-1], q_pair, (cache, cache_other), out_pair
+    )
+    products = out_products(attn, out_pair)
+    products = [products[0], first, *products[1:]]
 
     partial = None
     for k in range(tensor_count // SIDE):
@@ -429,17 +578,39 @@
         (mixed * gain).astype(jnp.bfloat16),
         [place_rows, lambda block: [swap_dp(after(vocab_weight, block))]],
     )
-    stats = vocab_stats(targets, final_gain, (vocab_weight, vocab_other), blocks)
-
-    def join(a, b, step):
-        first = (tensor_pos // step) % 2 == 0
-        a, b = jnp.where(first, a, b), jnp.where(first, b, a)
-        top = jnp.maximum(a[0], b[0])
-        total = a[1] * jnp.exp(a[0] - top) + b[1] * jnp.exp(b[0] - top)
-        return jnp.stack([top, total, a[2] + b[2]])
-
-    top, total, picked = doubling(stats[:3], join)
-    logprob = (picked - top - jnp.log(total))[None, :]
+    gains = final_gain.reshape(tensor_count, shard)
+    vocab_pair = (vocab_weight, vocab_other)
+    parts = logit_part(gains, vocab_pair, blocks[:-1])
+    stats = vocab_stats(targets, gains, parts, blocks[-1], vocab_pair)[:3]
+
+    def join(parts):
+        top = functools.reduce(jnp.maximum, [part[0] for part in parts])
+        total = sum(part[1] * jnp.exp(part[0] - top) for part in parts)
+        return jnp.stack([top, total, sum(part[2] for part in parts)])
+
+    def in_order(part, others, place):
+        held = [part, *others]
+        return [
+            functools.reduce(
+                lambda a, c: jnp.where(place(c) == p, held[c], a), range(1, len(held)), held[0]
+            )
+            for p in range(len(held))
+        ]
+
+    side = tensor_pos % SIDE
+    stats = join(in_order(stats, [swap_side(stats)], lambda c: side ^ c))
+    ring_count = tensor_count // SIDE
+    ring_pos = tensor_pos // SIDE
+    others = [
+        lax.ppermute(
+            stats, "tensor", [(i, (i + SIDE * c) % tensor_count) for i in range(tensor_count)]
+        )
+        for c in range(1, ring_count)
+    ]
+    stats = join(
+        in_order(stats, others, lambda c: (ring_pos - c + ring_count) % ring_count)
+    )
+    logprob = (stats[2] - stats[0] - jnp.log(stats[1]))[None, :]
     both_logprob = jnp.concatenate([logprob, swap_dp(logprob)], axis=1)
     token_logprob = jnp.sum(jnp.where(pick > 0, both_logprob.reshape(-1, 1), 0.0), axis=0)
     return (layer_out, token_logprob)

time: 153 us -> 146 us (0.954)
  waiting for transfers between devices: 112 us -> 95.5 us
  starting transfers between devices: 17 us -> 22.2 us
  local copies, waits for them, and re-layouts: 6.02 us -> 9.14 us
  Pallas kernels: 13.3 us -> 15.1 us
    ppermute x12 -> x13, waiting for transfers between devices: 52.3 us -> 32.7 us  [swap_side(): return lax.ppermute(value, 'tensor', [(i, i ^ 1) for i in range(count)])]
    ppermute x9, waiting for transfers between devices: 45.5 us -> 55 us  [ring_step(): lax.ppermute(value, 'tensor', [(i, (i + SIDE) % count) for i in range(cou...]
    ppermute x3, waiting for transfers between devices: 11 us -> 4.61 us  [per_device(): lax.ppermute(stats, 'tensor', [(i, (i + SIDE * c) % tensor_count) for i i...]
    unnamed x34 -> x44, local copies, waits for them, and re-layouts: 4.95 us -> 7.47 us
    ppermute x9, starting transfers between devices: 1.82 us -> 4.09 us  [ring_step(): lax.ppermute(value, 'tensor', [(i, (i + SIDE) % count) for i in range(cou...]
    pallas_call x2 -> x5, Pallas kernels: 12.4 us -> 14.2 us  [the longest x1 3.7 us: logit_part(): pl.pallas_call(logit_kernel, out_shape=[jax.ShapeDtypeStruct((half, vocab...]
    ppermute x12 -> x13, starting transfers between devices: 12.8 us -> 14.4 us  [swap_side(): return lax.ppermute(value, 'tensor', [(i, i ^ 1) for i in range(count)])]
  transfers between devices with their start and end apart: 33 -> 34, of which waited for: 24 -> 25; matrix products, arithmetic and copies ran while one was open for 2% -> 2% of each run, Pallas kernels for 0% -> 7%
where the time goes in v4:
time: 146 us
  waiting for transfers between devices  95.5 us (65%)
  starting transfers between devices  22.2 us (15%)
  Pallas kernels  15.1 us (10%)
  local copies, waits for them, and re-layouts  9.14 us (6%)
  other arithmetic  1.55 us (1%)
    ppermute x9, waiting for transfers between devices, ring_step(): lax.ppermute(value, 'tensor', [(i, (i + SIDE) % count) for i in range(cou...  55 us
    ppermute x13, waiting for transfers between devices, swap_side(): return lax.ppermute(value, 'tensor', [(i, i ^ 1) for i in range(count)])  32.7 us
    ppermute x13, starting transfers between devices, swap_side(): return lax.ppermute(value, 'tensor', [(i, i ^ 1) for i in range(count)])  14.4 us
    unnamed x44, local copies, waits for them, and re-layouts  7.47 us
    ppermute x3, waiting for transfers between devices, per_device(): lax.ppermute(stats, 'tensor', [(i, (i + SIDE * c) % tensor_count) for i i...  4.61 us
    ppermute x9, starting transfers between devices, ring_step(): lax.ppermute(value, 'tensor', [(i, (i + SIDE) % count) for i in range(cou...  4.09 us
    pallas_call x1, Pallas kernels, logit_part(): pl.pallas_call(logit_kernel, out_shape=[jax.ShapeDtypeStruct((half, vocab...  3.7 us
    pallas_call x1, Pallas kernels, query_part(): pl.pallas_call(functools.partial(query_kernel, shard), out_shape=[jax.Sha...  3.55 us
  transfers between devices with their start and end apart: 34, of which 25 were waited for; matrix products, arithmetic and copies ran while one was open for 2% of the time, Pallas kernels for 7%

profile of v4, /device:TPU:0, one launch (start us, length us, event | category | flops | bytes accessed | tf_op | source)
XLA Modules:
  0.0 145.9 jit_solution(5661035632850952799)
XLA Ops:
  0.7 1.2 copy-done.5
  1.9 0.7 copy-done.13
  2.5 0.9 pack_rows.1
  3.4 0.5 collective-permute-start
  3.9 0.7 dynamic_slice.9
  4.6 0.5 collective-permute-done
  5.2 0.2 convolution_convert_fusion.1
  5.4 0.4 collective-permute-start.3
  5.9 2.7 %collective-permute-start.1 = (bf16[128,1280]{1,0:T(8,128)(2,1)S(1)}, bf16[128,1280]{1,0:T(8,128)(2,1)S(1)}, u32[]{:S(2)}, u32[]{:S(2)}) collective-permute-start(bf16[128,1280]{1,0:T(8,128)(2,1)S(1)} %pad_maximum_fusion.refs_0_), channel_id=1, source_target_pairs={{0,2},{1,3},{2,4},{3,5},{4,6},{5,7},{6,0},{7,1},{8,10},{9,11},{10,... | collective-permute-start | bytes 983048 | tf_op jit(solution)/shard_map/ppermute | solution.py:35
  8.6 1.5 %collective-permute-start.2 = (bf16[128,1280]{1,0:T(8,128)(2,1)S(1)}, bf16[128,1280]{1,0:T(8,128)(2,1)S(1)}, u32[]{:S(2)}, u32[]{:S(2)}) collective-permute-start(bf16[128,1280]{1,0:T(8,128)(2,1)S(1)} %pad_maximum_fusion.refs_0_), channel_id=1, source_target_pairs={{0,1},{1,0},{2,3},{3,2},{4,5},{5,4},{6,7},{7,6},{8,9},{9,8},{10,11... | collective-permute-start | bytes 983048 | tf_op jit(solution)/shard_map/ppermute | solution.py:30
  10.1 8.7 %collective-permute-done.1.refs_2_ = bf16[128,1280]{1,0:T(8,128)(2,1)S(1)} collective-permute-done((bf16[128,1280]{1,0:T(8,128)(2,1)S(1)}, bf16[128,1280]{1,0:T(8,128)(2,1)S(1)}, u32[]{:S(2)}, u32[]{:S(2)}) %collective-permute-start.1) | collective-permute-done | bytes 327712 | tf_op jit(solution)/shard_map/ppermute | solution.py:35
  18.9 0.7 copy-done.9
  19.6 1.4 copy-done.16
  21.0 1.0 collective-permute-start.4
  22.0 1.5 %collective-permute-start.5 = (bf16[128,1280]{1,0:T(8,128)(2,1)S(1)}, bf16[128,1280]{1,0:T(8,128)(2,1)}, u32[]{:S(2)}, u32[]{:S(2)}) collective-permute-start(bf16[128,1280]{1,0:T(8,128)(2,1)S(1)} %collective-permute-done.1.refs_2_), channel_id=1, source_target_pairs={{0,1},{1,0},{2,3},{3,2},{4,5},{5,4},{6,7},{7,6},{8,9},{9,8},{10,11... | collective-permute-start | bytes 983048 | tf_op jit(solution)/shard_map/ppermute | solution.py:30
  23.5 8.8 %collective-permute-done.4.refs_4_ = bf16[128,1280]{1,0:T(8,128)(2,1)} collective-permute-done((bf16[128,1280]{1,0:T(8,128)(2,1)S(1)}, bf16[128,1280]{1,0:T(8,128)(2,1)}, u32[]{:S(2)}, u32[]{:S(2)}) %collective-permute-start.4) | collective-permute-done | bytes 327712 | tf_op jit(solution)/shard_map/ppermute | solution.py:35
  32.3 1.4 collective-permute-start.8
  33.8 0.5 collective-permute-start.10
  34.6 0.3 collective-permute-done.7
  35.0 0.9 collective-permute-done.11
  35.8 5.2 %collective-permute-done.8.refs_5_ = bf16[128,1280]{1,0:T(8,128)(2,1)S(1)} collective-permute-done((bf16[128,1280]{1,0:T(8,128)(2,1)}, bf16[128,1280]{1,0:T(8,128)(2,1)S(1)}, u32[]{:S(2)}, u32[]{:S(2)}) %collective-permute-start.8) | collective-permute-done | bytes 327712 | tf_op jit(solution)/shard_map/ppermute | solution.py:30
  41.1 0.7 copy-done.11
  41.8 2.1 %collective-permute-done.9.refs_6_ = bf16[128,1280]{1,0:T(8,128)(2,1)} collective-permute-done((bf16[128,1280]{1,0:T(8,128)(2,1)}, bf16[128,1280]{1,0:T(8,128)(2,1)}, u32[]{:S(2)}, u32[]{:S(2)}) %collective-permute-start.9) | collective-permute-done | bytes 327712 | tf_op jit(solution)/shard_map/ppermute | solution.py:35
  43.8 0.8 copy-done.7
  44.6 0.9 collective-permute-start.12
  45.5 0.8 reshape.18.gain_ref
  46.3 1.0 copy-done.10
  47.2 1.0 copy-done.12
  48.2 3.6 %query_part.1 = (f32[128,256]{1,0:T(8,128)S(1)}, f32[128,256]{1,0:T(8,128)S(1)}, f32[128,128]{1,0:T(8,128)S(1)}) custom-call(f32[8,1024]{1,0:T(8,128)S(1)} %reshape.18.gain_ref, bf16[4096,256]{1,0:T(8,128)(2,1)S(1)} %copy-done.3, bf16[4096,256]{1,0:T(8,128)(2,1)} %copy-done.16, bf16[128,1280]{1,0:T(8,128)(2,1)S(1)} %pad_maximum_fusion.refs_0_, ...), custom_call_target="tpu_custom_call" | custom-call | flops 469762048 | bytes 5505024 | tf_op jit(solution)/shard_map/query_part/pallas_call | solution.py:202
  51.8 0.3 collective-permute-done.12.block_ref
  52.1 3.4 %attend.1 = (bf16[128,256]{1,0:T(8,128)(2,1)S(1)}, bf16[128,1024]{1,0:T(8,128)(2,1)S(1)}) custom-call(s32[8]{0:T(128)S(1)} %copy-done.14, s32[8]{0:T(128)S(1)} %pad_add_fusion.ctx_ref, f32[8,1024]{1,0:T(8,128)S(1)} %reshape.18.gain_ref, f32[128,256]{1,0:T(8,128)S(1)} %get-tuple-element.42.query_ref, f32[128,256]{1,0:T(8,128)S(1)} %get-tuple-element.43.kv_ref, ...), custom_call_target="tpu_custom_call" | custom-call | tf_op jit(solution)/shard_map/attend/pallas_call | solution.py:348
  55.6 1.1 collective-permute-start.16
  56.7 2.8 %out_products.1 = (bf16[128,1024]{1,0:T(8,128)(2,1)S(1)}, bf16[128,1024]{1,0:T(8,128)(2,1)S(1)}, bf16[128,1024]{1,0:T(8,128)(2,1)S(1)}, bf16[128,1024]{1,0:T(8,1...) custom-call(bf16[128,256]{1,0:T(8,128)(2,1)S(1)} %get-tuple-element.45.att, ...), custom_call_target="tpu_custom_call" | custom-call | flops 469762048 | bytes 5505024 | tf_op jit(solution)/shard_map/out_products/pallas_call | solution.py:386
  59.5 1.1 collective-permute-start.15
  60.5 4.3 %collective-permute-done.16 = bf16[128,1024]{1,0:T(8,128)(2,1)S(1)} collective-permute-done((bf16[128,1024]{1,0:T(8,128)(2,1)S(1)}, bf16[128,1024]{1,0:T(8,128)(2,1)S(1)}, u32[]{:S(2)}, u32[]{:S(2)}) %collective-permute-start.16) | collective-permute-done | bytes 262176 | tf_op jit(solution)/shard_map/ppermute | solution.py:30
  65.0 1.0 collective-permute-start.14
  66.0 4.5 %collective-permute-done.15 = bf16[128,1024]{1,0:T(8,128)(2,1)S(1)} collective-permute-done((bf16[128,1024]{1,0:T(8,128)(2,1)S(1)}, bf16[128,1024]{1,0:T(8,128)(2,1)S(1)}, u32[]{:S(2)}, u32[]{:S(2)}) %collective-permute-start.15) | collective-permute-done | bytes 262176 | tf_op jit(solution)/shard_map/ppermute | solution.py:30
  70.4 4.4 %collective-permute-done.17 = bf16[128,1024]{1,0:T(8,128)(2,1)S(1)} collective-permute-done((bf16[128,1024]{1,0:T(8,128)(2,1)S(1)}, bf16[128,1024]{1,0:T(8,128)(2,1)S(1)}, u32[]{:S(2)}, u32[]{:S(2)}) %collective-permute-start.17) | collective-permute-done | bytes 262176 | tf_op jit(solution)/shard_map/ppermute | solution.py:35
  75.1 1.0 collective-permute-start.13
  76.1 9.9 %collective-permute-done.18 = bf16[128,1024]{1,0:T(8,128)(2,1)S(1)} collective-permute-done((bf16[128,1024]{1,0:T(8,128)(2,1)S(1)}, bf16[128,1024]{1,0:T(8,128)(2,1)S(1)}, u32[]{:S(2)}, u32[]{:S(2)}) %collective-permute-start.18) | collective-permute-done | bytes 262176 | tf_op jit(solution)/shard_map/ppermute | solution.py:35
  86.2 8.1 %collective-permute-done.19 = bf16[128,1024]{1,0:T(8,128)(2,1)S(1)} collective-permute-done((bf16[128,1024]{1,0:T(8,128)(2,1)S(1)}, bf16[128,1024]{1,0:T(8,128)(2,1)S(1)}, u32[]{:S(2)}, u32[]{:S(2)}) %collective-permute-start.19) | collective-permute-done | bytes 262176 | tf_op jit(solution)/shard_map/ppermute | solution.py:35
  94.7 1.0 collective-permute-start.22
  95.7 0.5 collective-permute-done.20
  96.1 1.1 convolution_convert_fusion
  97.2 7.9 %collective-permute-done.21.refs_2_ = bf16[128,1024]{1,0:T(8,128)(2,1)S(1)} collective-permute-done((bf16[128,1024]{1,0:T(8,128)(2,1)S(1)}, bf16[128,1024]{1,0:T(8,128)(2,1)S(1)}, u32[]{:S(2)}, u32[]{:S(2)}) %collective-permute-start.21) | collective-permute-done | bytes 262176 | tf_op jit(solution)/shard_map/ppermute | solution.py:35
  105.1 1.0 collective-permute-start.24
  106.1 7.7 %collective-permute-done.24.refs_3_ = bf16[128,1024]{1,0:T(8,128)(2,1)S(1)} collective-permute-done((bf16[128,1024]{1,0:T(8,128)(2,1)S(1)}, bf16[128,1024]{1,0:T(8,128)(2,1)S(1)}, u32[]{:S(2)}, u32[]{:S(2)}) %collective-permute-start.24) | collective-permute-done | bytes 262176 | tf_op jit(solution)/shard_map/ppermute | solution.py:30
  113.8 2.4 %collective-permute-done.25.refs_4_ = bf16[128,1024]{1,0:T(8,128)(2,1)S(1)} collective-permute-done((bf16[128,1024]{1,0:T(8,128)(2,1)S(1)}, bf16[128,1024]{1,0:T(8,128)(2,1)S(1)}, u32[]{:S(2)}, u32[]{:S(2)}) %collective-permute-start.25) | collective-permute-done | bytes 262176 | tf_op jit(solution)/shard_map/ppermute | solution.py:35
  116.3 1.1 collective-permute-start.26
  117.4 6.4 %collective-permute-done.26.refs_5_ = bf16[128,1024]{1,0:T(8,128)(2,1)S(1)} collective-permute-done((bf16[128,1024]{1,0:T(8,128)(2,1)S(1)}, bf16[128,1024]{1,0:T(8,128)(2,1)S(1)}, u32[]{:S(2)}, u32[]{:S(2)}) %collective-permute-start.26) | collective-permute-done | bytes 262176 | tf_op jit(solution)/shard_map/ppermute | solution.py:30
  123.8 2.6 %collective-permute-done.27.refs_6_ = bf16[128,1024]{1,0:T(8,128)(2,1)S(1)} collective-permute-done((bf16[128,1024]{1,0:T(8,128)(2,1)S(1)}, bf16[128,1024]{1,0:T(8,128)(2,1)S(1)}, u32[]{:S(2)}, u32[]{:S(2)}) %collective-permute-start.27) | collective-permute-done | bytes 262176 | tf_op jit(solution)/shard_map/ppermute | solution.py:35
  126.4 0.9 collective-permute-start.28
  127.5 3.7 %logit_part.1 = (f32[128,512]{1,0:T(8,128)S(1)}, f32[128,128]{1,0:T(8,128)S(1)}) custom-call(f32[8,1024]{1,0:T(8,128)S(1)} %reshape.20.gain_ref, bf16[4096,512]{1,0:T(8,128)(2,1)} %own_ref.3, bf16[4096,512]{1,0:T(8,128)(2,1)} %copy-done.15, bf16[128,1024]{1,0:T(8,128)(2,1)S(1)} %get-tuple-element.62.refs_0_, ...), custom_call_target="tpu_custom_call" | custom-call | flops 939524096 | bytes 9175040 | tf_op jit(solution)/shard_map/logit_part/pallas_call | solution.py:432
  131.2 1.6 %collective-permute-done.28.block_ref = bf16[128,1024]{1,0:T(8,128)(2,1)S(1)} collective-permute-done((bf16[128,1024]{1,0:T(8,128)(2,1)S(1)}, bf16[128,1024]{1,0:T(8,128)(2,1)S(1)}, u32[]{:S(2)}, u32[]{:S(2)}) %collective-permute-start.28) | collective-permute-done | bytes 262176 | tf_op jit(solution)/shard_map/ppermute | solution.py:30
  132.8 0.8 vocab_stats.1
  133.6 1.0 collective-permute-start.29
  134.6 2.7 %collective-permute-done.29 = f32[3,128]{1,0:T(4,128)S(1)} collective-permute-done((f32[3,128]{1,0:T(4,128)S(1)}, f32[3,128]{1,0:T(4,128)S(1)}, u32[]{:S(2)}, u32[]{:S(2)}) %collective-permute-start.29) | collective-permute-done | bytes 1568 | tf_op jit(solution)/shard_map/ppermute | solution.py:30
  137.4 1.2 collective-permute-start.31
  138.6 0.8 collective-permute-start.32
  139.4 1.6 %collective-permute-done.30 = f32[3,128]{1,0:T(4,128)S(1)} collective-permute-done((f32[3,128]{1,0:T(4,128)S(1)}, f32[3,128]{1,0:T(4,128)S(1)}, u32[]{:S(2)}, u32[]{:S(2)}) %collective-permute-start.30) | collective-permute-done | bytes 1568 | tf_op jit(solution)/shard_map/ppermute | solution.py:605
  140.9 1.0 collective-permute-done.31
  141.9 2.1 %collective-permute-done.32 = f32[3,128]{1,0:T(4,128)S(1)} collective-permute-done((f32[3,128]{1,0:T(4,128)S(1)}, f32[3,128]{1,0:T(4,128)S(1)}, u32[]{:S(2)}, u32[]{:S(2)}) %collective-permute-start.32) | collective-permute-done | bytes 1568 | tf_op jit(solution)/shard_map/ppermute | solution.py:605
  144.1 1.1 collective-permute-done.33
  145.2 0.7 select_reduce_fusion
  (82 shorter events, 1.8 us)
Async XLA Ops:
  0.6 4.5 %copy-start = (bf16[1024,256]{1,0:T(8,128)(2,1)S(1)}, bf16[1024,256]{1,0:T(8,128)(2,1)}, u32[]{:S(2)}) copy-start(bf16[1024,256]{1,0:T(8,128)(2,1)} %param.14) | copy-start | bytes 1572868
  0.6 4.8 %copy-start.3 = (bf16[4096,256]{1,0:T(8,128)(2,1)S(1)}, bf16[4096,256]{1,0:T(8,128)(2,1)}, u32[]{:S(2)}) copy-start(bf16[4096,256]{1,0:T(8,128)(2,1)} %q_own.3) | copy-start | bytes 6291460
  0.7 1.2 copy-start.5
  1.8 0.7 copy-start.13
  2.5 31.3 %copy-start.21 = (s32[4]{0:T(128)S(1)}, s32[4]{0:T(128)}, u32[]{:S(2)}) copy-start(s32[4]{0:T(128)} %param.20) | copy-start | bytes 52
  2.5 31.8 %copy-start.20 = (s32[512]{0:T(512)S(1)}, s32[512]{0:T(512)}, u32[]{:S(2)}) copy-start(s32[512]{0:T(512)} %param.21) | copy-start | bytes 6148
  3.4 1.7 %collective-permute-start = (bf16[128,1024]{1,0:T(8,128)(2,1)S(1)}, bf16[128,1024]{1,0:T(8,128)(2,1)S(1)}, u32[]{:S(2)}, u32[]{:S(2)}) collective-permute-start(bf16[128,1024]{1,0:T(8,128)(2,1)S(1)} %get-tuple-element.33), channel_id=1, source_target_pairs={{0,8},{8,0},{1,9},{9,1},{2,10},{10,2},{3,11},{11,3},{4,12},{12,4},... | collective-permute-start | bytes 786440 | tf_op jit(solution)/shard_map/ppermute | solution.py:25
  5.1 16.8 %copy-start.17 = (bf16[128,1024]{1,0:T(8,128)(2,1)}, bf16[128,1024]{1,0:T(8,128)(2,1)S(1)}, u32[]{:S(2)}) copy-start(bf16[128,1024]{1,0:T(8,128)(2,1)S(1)} %add.119) | copy-start | bytes 786436
  5.4 14.2 %collective-permute-start.3 = (bf16[4096,256]{1,0:T(8,128)(2,1)S(1)}, bf16[4096,256]{1,0:T(8,128)(2,1)S(1)}, u32[]{:S(2)}, u32[]{:S(2)}) collective-permute-start(bf16[4096,256]{1,0:T(8,128)(2,1)S(1)} %copy-done.3), channel_id=1, source_target_pairs={{0,8},{8,0},{1,9},{9,1},{2,10},{10,2},{3,11},{11,3},{4,12},{12,4},... | collective-permute-start | bytes 6291464 | tf_op jit(solution)/shard_map/ppermute | solution.py:25
  5.9 13.0 %collective-permute-start.1 = (bf16[128,1280]{1,0:T(8,128)(2,1)S(1)}, bf16[128,1280]{1,0:T(8,128)(2,1)S(1)}, u32[]{:S(2)}, u32[]{:S(2)}) collective-permute-start(bf16[128,1280]{1,0:T(8,128)(2,1)S(1)} %pad_maximum_fusion.refs_0_), channel_id=1, source_target_pairs={{0,2},{1,3},{2,4},{3,5},{4,6},{5,7},{6,0},{7,1},{8,10},{9,11},{10,... | collective-permute-start | bytes 983048 | tf_op jit(solution)/shard_map/ppermute | solution.py:35
  8.6 10.3 %collective-permute-start.2 = (bf16[128,1280]{1,0:T(8,128)(2,1)S(1)}, bf16[128,1280]{1,0:T(8,128)(2,1)S(1)}, u32[]{:S(2)}, u32[]{:S(2)}) collective-permute-start(bf16[128,1280]{1,0:T(8,128)(2,1)S(1)} %pad_maximum_fusion.refs_0_), channel_id=1, source_target_pairs={{0,1},{1,0},{2,3},{3,2},{4,5},{5,4},{6,7},{7,6},{8,9},{9,8},{10,11... | collective-permute-start | bytes 983048 | tf_op jit(solution)/shard_map/ppermute | solution.py:30
  18.9 0.7 copy-start.9
  19.6 1.4 copy-start.16
  19.6 12.7 %collective-permute-start.6 = (bf16[256,4096]{1,0:T(8,128)(2,1)}, bf16[256,4096]{1,0:T(8,128)(2,1)}, u32[]{:S(2)}, u32[]{:S(2)}) collective-permute-start(bf16[256,4096]{1,0:T(8,128)(2,1)} %out_own.3), channel_id=1, source_target_pairs={{0,8},{8,0},{1,9},{9,1},{2,10},{10,2},{3,11},{11,3},{4,12},{12,4},... | collective-permute-start | bytes 6291464 | tf_op jit(solution)/shard_map/ppermute | solution.py:25
  21.0 11.3 %collective-permute-start.4 = (bf16[128,1280]{1,0:T(8,128)(2,1)S(1)}, bf16[128,1280]{1,0:T(8,128)(2,1)}, u32[]{:S(2)}, u32[]{:S(2)}) collective-permute-start(bf16[128,1280]{1,0:T(8,128)(2,1)S(1)} %collective-permute-done.1.refs_2_), channel_id=1, source_target_pairs={{0,2},{1,3},{2,4},{3,5},{4,6},{5,7},{6,0},{7,1},{8,10},{9,11},{10,... | collective-permute-start | bytes 983048 | tf_op jit(solution)/shard_map/ppermute | solution.py:35
  22.0 10.3 %collective-permute-start.5 = (bf16[128,1280]{1,0:T(8,128)(2,1)S(1)}, bf16[128,1280]{1,0:T(8,128)(2,1)}, u32[]{:S(2)}, u32[]{:S(2)}) collective-permute-start(bf16[128,1280]{1,0:T(8,128)(2,1)S(1)} %collective-permute-done.1.refs_2_), channel_id=1, source_target_pairs={{0,1},{1,0},{2,3},{3,2},{4,5},{5,4},{6,7},{7,6},{8,9},{9,8},{10,11... | collective-permute-start | bytes 983048 | tf_op jit(solution)/shard_map/ppermute | solution.py:30
  32.3 8.7 %collective-permute-start.8 = (bf16[128,1280]{1,0:T(8,128)(2,1)}, bf16[128,1280]{1,0:T(8,128)(2,1)S(1)}, u32[]{:S(2)}, u32[]{:S(2)}) collective-permute-start(bf16[128,1280]{1,0:T(8,128)(2,1)} %collective-permute-done.4.refs_4_), channel_id=1, source_target_pairs={{0,1},{1,0},{2,3},{3,2},{4,5},{5,4},{6,7},{7,6},{8,9},{9,8},{10,11... | collective-permute-start | bytes 983048 | tf_op jit(solution)/shard_map/ppermute | solution.py:30
  33.7 10.2 %collective-permute-start.9 = (bf16[128,1280]{1,0:T(8,128)(2,1)}, bf16[128,1280]{1,0:T(8,128)(2,1)}, u32[]{:S(2)}, u32[]{:S(2)}) collective-permute-start(bf16[128,1280]{1,0:T(8,128)(2,1)} %collective-permute-done.4.refs_4_), channel_id=1, source_target_pairs={{0,2},{1,3},{2,4},{3,5},{4,6},{5,7},{6,0},{7,1},{8,10},{9,11},{10,... | collective-permute-start | bytes 983048 | tf_op jit(solution)/shard_map/ppermute | solution.py:35
  33.8 1.1 collective-permute-start.7
  33.8 10.1 %collective-permute-start.10 = (bf16[4,256,256]{2,1,0:T(8,128)(2,1)}, bf16[4,256,256]{2,1,0:T(8,128)(2,1)S(1)}, u32[]{:S(2)}, u32[]{:S(2)}) collective-permute-start(bf16[4,256,256]{2,1,0:T(8,128)(2,1)} %cache_own.1), channel_id=1, source_target_pairs={{0,8},{8,0},{1,9},{9,1},{2,10},{10,2},{3,11},{11,3},{4,12},{12,4},... | collective-permute-start | bytes 1572872 | tf_op jit(solution)/shard_map/ppermute | solution.py:25
  34.5 1.3 collective-permute-start.11
  41.0 0.7 copy-start.11
  43.8 0.8 copy-start.7
  44.6 7.5 %collective-permute-start.12 = (bf16[128,1280]{1,0:T(8,128)(2,1)}, bf16[128,1280]{1,0:T(8,128)(2,1)}, u32[]{:S(2)}, u32[]{:S(2)}) collective-permute-start(bf16[128,1280]{1,0:T(8,128)(2,1)} %collective-permute-done.9.refs_6_), channel_id=1, source_target_pairs={{0,1},{1,0},{2,3},{3,2},{4,5},{5,4},{6,7},{7,6},{8,9},{9,8},{10,11... | collective-permute-start | bytes 983048 | tf_op jit(solution)/shard_map/ppermute | solution.py:30
  46.3 1.0 copy-start.10
  47.2 1.0 copy-start.12
  48.2 3.9 %copy-start.6 = (bf16[4,256,256]{2,1,0:T(8,128)(2,1)S(1)}, bf16[4,256,256]{2,1,0:T(8,128)(2,1)}, u32[]{:S(2)}) copy-start(bf16[4,256,256]{2,1,0:T(8,128)(2,1)} %cache_own.1) | copy-start | bytes 1572868
  48.2 3.9 %copy-start.8 = (bf16[4,256,256]{2,1,0:T(8,128)(2,1)S(1)}, bf16[4,256,256]{2,1,0:T(8,128)(2,1)}, u32[]{:S(2)}) copy-start(bf16[4,256,256]{2,1,0:T(8,128)(2,1)} %copy-done.7) | copy-start | bytes 1572868
  48.2 3.9 %copy-start.14 = (s32[8]{0:T(128)S(1)}, s32[8]{0:T(128)}, u32[]{:S(2)}) copy-start(s32[8]{0:T(128)} %lens_ref.3) | copy-start | bytes 100
  52.1 4.6 %copy-start.4 = (bf16[256,4096]{1,0:T(8,128)(2,1)S(1)}, bf16[256,4096]{1,0:T(8,128)(2,1)}, u32[]{:S(2)}) copy-start(bf16[256,4096]{1,0:T(8,128)(2,1)} %out_own.3) | copy-start | bytes 6291460
  55.6 9.2 %collective-permute-start.16 = (bf16[128,1024]{1,0:T(8,128)(2,1)S(1)}, bf16[128,1024]{1,0:T(8,128)(2,1)S(1)}, u32[]{:S(2)}, u32[]{:S(2)}) collective-permute-start(bf16[128,1024]{1,0:T(8,128)(2,1)S(1)} %get-tuple-element.53), channel_id=1, source_target_pairs={{0,1},{1,0},{2,3},{3,2},{4,5},{5,4},{6,7},{7,6},{8,9},{9,8},{10,11... | collective-permute-start | bytes 786440 | tf_op jit(solution)/shard_map/ppermute | solution.py:30
  59.5 34.8 %copy-start.18 = (bf16[128,1024]{1,0:T(8,128)(2,1)S(1)}, bf16[128,1024]{1,0:T(8,128)(2,1)}, u32[]{:S(2)}) copy-start(bf16[128,1024]{1,0:T(8,128)(2,1)} %copy-done.17) | copy-start | bytes 786436
  59.5 34.8 %dynamic-slice-start = ((f32[8192]{0:T(1024)}, s32[]{:T(128)}), f32[1024]{0:T(1024)S(1)}, s32[]{:S(2)}) async-start(f32[8192]{0:T(1024)} %param.17, s32[]{:T(128)} %select_n.142), calls=%async_computation | async-start | bytes 8704 | tf_op jit(solution)/shard_map/dynamic_slice | solution.py:566
  59.5 11.0 %collective-permute-start.15 = (bf16[128,1024]{1,0:T(8,128)(2,1)S(1)}, bf16[128,1024]{1,0:T(8,128)(2,1)S(1)}, u32[]{:S(2)}, u32[]{:S(2)}) collective-permute-start(bf16[128,1024]{1,0:T(8,128)(2,1)S(1)} %get-tuple-element.51), channel_id=1, source_target_pairs={{0,1},{1,0},{2,3},{3,2},{4,5},{5,4},{6,7},{7,6},{8,9},{9,8},{10,11... | collective-permute-start | bytes 786440 | tf_op jit(solution)/shard_map/ppermute | solution.py:30
  64.9 10.0 %collective-permute-start.17 = (bf16[128,1024]{1,0:T(8,128)(2,1)S(1)}, bf16[128,1024]{1,0:T(8,128)(2,1)S(1)}, u32[]{:S(2)}, u32[]{:S(2)}) collective-permute-start(bf16[128,1024]{1,0:T(8,128)(2,1)S(1)} %add_convert_fusion.2), channel_id=1, source_target_pairs={{0,2},{1,3},{2,4},{3,5},{4,6},{5,7},{6,0},{7,1},{8,10},{9,11},{10,... | collective-permute-start | bytes 786440 | tf_op jit(solution)/shard_map/ppermute | solution.py:35
  65.0 11.1 %collective-permute-start.14 = (bf16[128,1024]{1,0:T(8,128)(2,1)S(1)}, bf16[128,1024]{1,0:T(8,128)(2,1)S(1)}, u32[]{:S(2)}, u32[]{:S(2)}) collective-permute-start(bf16[128,1024]{1,0:T(8,128)(2,1)S(1)} %get-tuple-element.49), channel_id=1, source_target_pairs={{0,1},{1,0},{2,3},{3,2},{4,5},{5,4},{6,7},{7,6},{8,9},{9,8},{10,11... | collective-permute-start | bytes 786440 | tf_op jit(solution)/shard_map/ppermute | solution.py:30
  74.9 30.2 %copy-start.1 = (bf16[4096,512]{1,0:T(8,128)(2,1)S(1)}, bf16[4096,512]{1,0:T(8,128)(2,1)}, u32[]{:S(2)}) copy-start(bf16[4096,512]{1,0:T(8,128)(2,1)} %own_ref.3) | copy-start | bytes 12582916
  75.0 52.4 %copy-start.19 = (f32[8192]{0:T(1024)S(1)}, f32[8192]{0:T(1024)}, u32[]{:S(2)}) copy-start(f32[8192]{0:T(1024)} %param.17) | copy-start | bytes 98308
  75.0 10.9 %collective-permute-start.18 = (bf16[128,1024]{1,0:T(8,128)(2,1)S(1)}, bf16[128,1024]{1,0:T(8,128)(2,1)S(1)}, u32[]{:S(2)}, u32[]{:S(2)}) collective-permute-start(bf16[128,1024]{1,0:T(8,128)(2,1)S(1)} %add_convert_fusion.1), channel_id=1, source_target_pairs={{0,2},{1,3},{2,4},{3,5},{4,6},{5,7},{6,0},{7,1},{8,10},{9,11},{10,... | collective-permute-start | bytes 786440 | tf_op jit(solution)/shard_map/ppermute | solution.py:35
  75.1 11.1 %collective-permute-start.13 = (bf16[128,1024]{1,0:T(8,128)(2,1)S(1)}, bf16[128,1024]{1,0:T(8,128)(2,1)S(1)}, u32[]{:S(2)}, u32[]{:S(2)}) collective-permute-start(bf16[128,1024]{1,0:T(8,128)(2,1)S(1)} %get-tuple-element.47), channel_id=1, source_target_pairs={{0,1},{1,0},{2,3},{3,2},{4,5},{5,4},{6,7},{7,6},{8,9},{9,8},{10,11... | collective-permute-start | bytes 786440 | tf_op jit(solution)/shard_map/ppermute | solution.py:30
  86.1 8.2 %collective-permute-start.19 = (bf16[128,1024]{1,0:T(8,128)(2,1)S(1)}, bf16[128,1024]{1,0:T(8,128)(2,1)S(1)}, u32[]{:S(2)}, u32[]{:S(2)}) collective-permute-start(bf16[128,1024]{1,0:T(8,128)(2,1)S(1)} %add_convert_fusion), channel_id=1, source_target_pairs={{0,2},{1,3},{2,4},{3,5},{4,6},{5,7},{6,0},{7,1},{8,10},{9,11},{10,... | collective-permute-start | bytes 786440 | tf_op jit(solution)/shard_map/ppermute | solution.py:35
  94.5 1.6 %collective-permute-start.20 = (bf16[128,1024]{1,0:T(8,128)(2,1)S(1)}, bf16[128,1024]{1,0:T(8,128)(2,1)S(1)}, u32[]{:S(2)}, u32[]{:S(2)}) collective-permute-start(bf16[128,1024]{1,0:T(8,128)(2,1)S(1)} %get-tuple-element.63), channel_id=1, source_target_pairs={{0,8},{8,0},{1,9},{9,1},{2,10},{10,2},{3,11},{11,3},{4,12},{12,4},... | collective-permute-start | bytes 786440 | tf_op jit(solution)/shard_map/ppermute | solution.py:25
  94.6 10.5 %collective-permute-start.21 = (bf16[128,1024]{1,0:T(8,128)(2,1)S(1)}, bf16[128,1024]{1,0:T(8,128)(2,1)S(1)}, u32[]{:S(2)}, u32[]{:S(2)}) collective-permute-start(bf16[128,1024]{1,0:T(8,128)(2,1)S(1)} %get-tuple-element.62.refs_0_), channel_id=1, source_target_pairs={{0,2},{1,3},{2,4},{3,5},{4,6},{5,7},{6,0},{7,1},{8,10},{9,11},{10,... | collective-permute-start | bytes 786440 | tf_op jit(solution)/shard_map/ppermute | solution.py:35
  94.7 10.4 %collective-permute-start.22 = (bf16[128,1024]{1,0:T(8,128)(2,1)S(1)}, bf16[128,1024]{1,0:T(8,128)(2,1)S(1)}, u32[]{:S(2)}, u32[]{:S(2)}) collective-permute-start(bf16[128,1024]{1,0:T(8,128)(2,1)S(1)} %get-tuple-element.62.refs_0_), channel_id=1, source_target_pairs={{0,1},{1,0},{2,3},{3,2},{4,5},{5,4},{6,7},{7,6},{8,9},{9,8},{10,11... | collective-permute-start | bytes 786440 | tf_op jit(solution)/shard_map/ppermute | solution.py:30
  105.1 11.2 %collective-permute-start.23 = (bf16[4096,512]{1,0:T(8,128)(2,1)S(1)}, bf16[4096,512]{1,0:T(8,128)(2,1)S(1)}, u32[]{:S(2)}, u32[]{:S(2)}) collective-permute-start(bf16[4096,512]{1,0:T(8,128)(2,1)S(1)} %copy-done.1), channel_id=1, source_target_pairs={{0,8},{8,0},{1,9},{9,1},{2,10},{10,2},{3,11},{11,3},{4,12},{12,4},... | collective-permute-start | bytes 12582920 | tf_op jit(solution)/shard_map/ppermute | solution.py:25
  105.1 8.7 %collective-permute-start.24 = (bf16[128,1024]{1,0:T(8,128)(2,1)S(1)}, bf16[128,1024]{1,0:T(8,128)(2,1)S(1)}, u32[]{:S(2)}, u32[]{:S(2)}) collective-permute-start(bf16[128,1024]{1,0:T(8,128)(2,1)S(1)} %collective-permute-done.21.refs_2_), channel_id=1, source_target_pairs={{0,1},{1,0},{2,3},{3,2},{4,5},{5,4},{6,7},{7,6},{8,9},{9,8},{10,11... | collective-permute-start | bytes 786440 | tf_op jit(solution)/shard_map/ppermute | solution.py:30
  106.1 10.2 %collective-permute-start.25 = (bf16[128,1024]{1,0:T(8,128)(2,1)S(1)}, bf16[128,1024]{1,0:T(8,128)(2,1)S(1)}, u32[]{:S(2)}, u32[]{:S(2)}) collective-permute-start(bf16[128,1024]{1,0:T(8,128)(2,1)S(1)} %collective-permute-done.21.refs_2_), channel_id=1, source_target_pairs={{0,2},{1,3},{2,4},{3,5},{4,6},{5,7},{6,0},{7,1},{8,10},{9,11},{10,... | collective-permute-start | bytes 786440 | tf_op jit(solution)/shard_map/ppermute | solution.py:35
  116.3 10.2 %copy-start.15 = (bf16[4096,512]{1,0:T(8,128)(2,1)}, bf16[4096,512]{1,0:T(8,128)(2,1)S(1)}, u32[]{:S(2)}) copy-start(bf16[4096,512]{1,0:T(8,128)(2,1)S(1)} %collective-permute-done.23.other_ref) | copy-start | bytes 12582916
  116.3 7.5 %collective-permute-start.26 = (bf16[128,1024]{1,0:T(8,128)(2,1)S(1)}, bf16[128,1024]{1,0:T(8,128)(2,1)S(1)}, u32[]{:S(2)}, u32[]{:S(2)}) collective-permute-start(bf16[128,1024]{1,0:T(8,128)(2,1)S(1)} %collective-permute-done.25.refs_4_), channel_id=1, source_target_pairs={{0,1},{1,0},{2,3},{3,2},{4,5},{5,4},{6,7},{7,6},{8,9},{9,8},{10,11... | collective-permute-start | bytes 786440 | tf_op jit(solution)/shard_map/ppermute | solution.py:30
  117.4 9.1 %collective-permute-start.27 = (bf16[128,1024]{1,0:T(8,128)(2,1)S(1)}, bf16[128,1024]{1,0:T(8,128)(2,1)S(1)}, u32[]{:S(2)}, u32[]{:S(2)}) collective-permute-start(bf16[128,1024]{1,0:T(8,128)(2,1)S(1)} %collective-permute-done.25.refs_4_), channel_id=1, source_target_pairs={{0,2},{1,3},{2,4},{3,5},{4,6},{5,7},{6,0},{7,1},{8,10},{9,11},{10,... | collective-permute-start | bytes 786440 | tf_op jit(solution)/shard_map/ppermute | solution.py:35
  126.4 6.4 %collective-permute-start.28 = (bf16[128,1024]{1,0:T(8,128)(2,1)S(1)}, bf16[128,1024]{1,0:T(8,128)(2,1)S(1)}, u32[]{:S(2)}, u32[]{:S(2)}) collective-permute-start(bf16[128,1024]{1,0:T(8,128)(2,1)S(1)} %collective-permute-done.27.refs_6_), channel_id=1, source_target_pairs={{0,1},{1,0},{2,3},{3,2},{4,5},{5,4},{6,7},{7,6},{8,9},{9,8},{10,11... | collective-permute-start | bytes 786440 | tf_op jit(solution)/shard_map/ppermute | solution.py:30
  127.5 5.3 %copy-start.2 = (bf16[4096,512]{1,0:T(8,128)(2,1)S(1)}, bf16[4096,512]{1,0:T(8,128)(2,1)}, u32[]{:S(2)}) copy-start(bf16[4096,512]{1,0:T(8,128)(2,1)} %own_ref.3) | copy-start | bytes 12582916
  133.6 3.7 %collective-permute-start.29 = (f32[3,128]{1,0:T(4,128)S(1)}, f32[3,128]{1,0:T(4,128)S(1)}, u32[]{:S(2)}, u32[]{:S(2)}) collective-permute-start(f32[3,128]{1,0:T(4,128)S(1)} %slice.71), channel_id=1, source_target_pairs={{0,1},{1,0},{2,3},{3,2},{4,5},{5,4},{6,7},{7,6},{8,9},{9,8},{10,11... | collective-permute-start | bytes 4616 | tf_op jit(solution)/shard_map/ppermute | solution.py:30
  137.3 3.6 %collective-permute-start.30 = (f32[3,128]{1,0:T(4,128)S(1)}, f32[3,128]{1,0:T(4,128)S(1)}, u32[]{:S(2)}, u32[]{:S(2)}) collective-permute-start(f32[3,128]{1,0:T(4,128)S(1)} %pad_maximum_fusion.1), channel_id=1, source_target_pairs={{0,6},{1,7},{2,0},{3,1},{4,2},{5,3},{6,4},{7,5},{8,14},{9,15},{10,... | collective-permute-start | bytes 4616 | tf_op jit(solution)/shard_map/ppermute | solution.py:605
  137.4 4.5 %collective-permute-start.31 = (f32[3,128]{1,0:T(4,128)S(1)}, f32[3,128]{1,0:T(4,128)S(1)}, u32[]{:S(2)}, u32[]{:S(2)}) collective-permute-start(f32[3,128]{1,0:T(4,128)S(1)} %pad_maximum_fusion.1), channel_id=1, source_target_pairs={{0,4},{1,5},{2,6},{3,7},{4,0},{5,1},{6,2},{7,3},{8,12},{9,13},{10,... | collective-permute-start | bytes 4616 | tf_op jit(solution)/shard_map/ppermute | solution.py:605
  138.6 5.4 %collective-permute-start.32 = (f32[3,128]{1,0:T(4,128)S(1)}, f32[3,128]{1,0:T(4,128)S(1)}, u32[]{:S(2)}, u32[]{:S(2)}) collective-permute-start(f32[3,128]{1,0:T(4,128)S(1)} %pad_maximum_fusion.1), channel_id=1, source_target_pairs={{0,2},{1,3},{2,4},{3,5},{4,6},{5,7},{6,0},{7,1},{8,10},{9,11},{10,... | collective-permute-start | bytes 4616 | tf_op jit(solution)/shard_map/ppermute | solution.py:605
  144.0 1.2 collective-permute-start.33

commit v5 on v4

--- a/solution.py
+++ b/solution.py
@@ -14,7 +14,7 @@
 
 
 EPS = 1e-05
-VMEM_LIMIT = 48 * 1024 * 1024
+VMEM_LIMIT = 52 * 1024 * 1024
 
 
 def product(left, right):
@@ -30,23 +30,20 @@
     return lax.ppermute(value, "tensor", [(i, i ^ 1) for i in range(count)])
 
 
+def ring_seat(seat, count):
+    return jnp.where(seat == 0, 0, jnp.where(seat <= count // 2, 2 * seat - 1, 2 * (count - seat)))
+
+
+def seat_of(place, count):
+    return jnp.where(place % 2 == 1, (place + 1) // 2, (count - place // 2) % count)
+
+
 def ring_step(value):
     count = lax.axis_size("tensor")
-    return lax.ppermute(value, "tensor", [(i, (i + SIDE) % count) for i in range(count)])
-
-
-def doubling(value, combine):
-    count = lax.axis_size("tensor")
-    step = 1
-    while step < count:
-        other = lax.ppermute(value, "tensor", [(i, i ^ step) for i in range(count)])
-        value = combine(value, other, step)
-        step *= 2
-    return value
-
-
-def sum_tensor(value):
-    return doubling(value, lambda a, b, step: a + b)
+    ring = [0, *range(1, count // SIDE, 2), *range(count // SIDE - 2, 0, -2)]
+    following = dict(zip(ring, ring[1:] + ring[:1]))
+    pairs = [(i, following[i // SIDE] * SIDE + i % SIDE) for i in range(count)]
+    return lax.ppermute(value, "tensor", pairs)
 
 
 def after(value, *others):
@@ -66,24 +63,24 @@
     return blocks, values
 
 
-def gathered_ids():
+def ring_ids(first):
     count = lax.axis_size("tensor")
     pos = lax.axis_index("tensor")
+    ring_count = count // SIDE
+    seat = seat_of(pos // SIDE, ring_count)
     ids = []
-    for k in range(count // SIDE):
-        held = (pos - SIDE * k + count) % count
+    for k in range(first, first + ring_count):
+        held = ring_seat((seat - k + 2 * ring_count) % ring_count, ring_count) * SIDE + pos % SIDE
         ids += [held, held ^ 1]
     return ids
 
 
+def gathered_ids():
+    return ring_ids(0)
+
+
 def scattered_ids():
-    count = lax.axis_size("tensor")
-    pos = lax.axis_index("tensor")
-    ids = []
-    for k in range(count // SIDE):
-        held = (pos - SIDE * (k + 1) + count) % count
-        ids += [held, held ^ 1]
-    return ids
+    return ring_ids(1)
 
 
 def row_plan(lens_ref, seqs_count, half):
@@ -198,7 +195,7 @@
     shard, used, half = gains.shape[1], len(blocks), blocks[0].shape[0]
     q_width = q_pair[0].shape[1]
     vmem = pl.BlockSpec(memory_space=pltpu.VMEM)
-    anywhere = pl.BlockSpec(memory_space=pl.ANY)
+    anywhere = pl.BlockSpec(memory_space=pltpu.HBM)
     return pl.pallas_call(
         functools.partial(query_kernel, shard),
         out_shape=[
@@ -344,7 +341,7 @@
     q_width, attn_width = q_pair[0].shape[1], out_pair[0].shape[0]
     vmem = pl.BlockSpec(memory_space=pltpu.VMEM)
     smem = pl.BlockSpec(memory_space=pltpu.SMEM)
-    anywhere = pl.BlockSpec(memory_space=pl.ANY)
+    anywhere = pl.BlockSpec(memory_space=pltpu.HBM)
     return pl.pallas_call(
         functools.partial(attention_kernel, seqs_count),
         out_shape=[
@@ -382,7 +379,7 @@
     count = lax.axis_size("tensor")
     shard = out_pair[0].shape[1] * 2 // count
     vmem = pl.BlockSpec(memory_space=pltpu.VMEM)
-    anywhere = pl.BlockSpec(memory_space=pl.ANY)
+    anywhere = pl.BlockSpec(memory_space=pltpu.HBM)
     return pl.pallas_call(
         out_kernel,
         out_shape=[jax.ShapeDtypeStruct((half, shard), jnp.bfloat16)] * (count - 1),
@@ -428,7 +425,7 @@
     used, (half, shard) = len(blocks), blocks[0].shape
     vocab_count = vocab_pair[0].shape[1]
     vmem = pl.BlockSpec(memory_space=pltpu.VMEM)
-    anywhere = pl.BlockSpec(memory_space=pl.ANY)
+    anywhere = pl.BlockSpec(memory_space=pltpu.HBM)
     return pl.pallas_call(
         logit_kernel,
         out_shape=[
@@ -480,7 +477,7 @@
     half, shard = block.shape
     vocab_count = vocab_pair[0].shape[1]
     vmem = pl.BlockSpec(memory_space=pltpu.VMEM)
-    anywhere = pl.BlockSpec(memory_space=pl.ANY)
+    anywhere = pl.BlockSpec(memory_space=pltpu.HBM)
     return pl.pallas_call(
         stats_kernel,
         out_shape=jax.ShapeDtypeStruct((8, half), jnp.float32),

time: 146 us -> 136 us (0.932)
  waiting for transfers between devices: 95.5 us -> 77.1 us
  starting transfers between devices: 22.2 us -> 32.3 us
  local copies, waits for them, and re-layouts: 9.14 us -> 5.09 us
  Pallas kernels: 15.1 us -> 17.6 us
    ppermute x9, waiting for transfers between devices: 55 us -> 40.7 us  [ring_step(): return lax.ppermute(value, 'tensor', pairs)]
    ppermute x9, starting transfers between devices: 4.09 us -> 13.3 us  [ring_step(): return lax.ppermute(value, 'tensor', pairs)]
    ppermute x13, waiting for transfers between devices: 32.7 us -> 28.9 us  [swap_side(): return lax.ppermute(value, 'tensor', [(i, i ^ 1) for i in range(count)])]
    unnamed x44 -> x32, local copies, waits for them, and re-layouts: 7.47 us -> 4.03 us
    ppermute x3, starting transfers between devices: 2.07 us -> 3.84 us  [per_device(): lax.ppermute(stats, 'tensor', [(i, (i + SIDE * c) % tensor_count) for i i...]
  transfers between devices with their start and end apart: 34 -> 34, of which waited for: 25 -> 28; matrix products, arithmetic and copies ran while one was open for 2% -> 2% of each run, Pallas kernels for 7% -> 8%
where the time goes in v5:
time: 136 us
  waiting for transfers between devices  77.1 us (57%)
  starting transfers between devices  32.3 us (24%)
  Pallas kernels  17.6 us (13%)
  local copies, waits for them, and re-layouts  5.09 us (4%)
  other arithmetic  1.55 us (1%)
    ppermute x9, waiting for transfers between devices, ring_step(): return lax.ppermute(value, 'tensor', pairs)  40.7 us
    ppermute x13, waiting for transfers between devices, swap_side(): return lax.ppermute(value, 'tensor', [(i, i ^ 1) for i in range(count)])  28.9 us
    ppermute x13, starting transfers between devices, swap_side(): return lax.ppermute(value, 'tensor', [(i, i ^ 1) for i in range(count)])  13.4 us
    ppermute x9, starting transfers between devices, ring_step(): return lax.ppermute(value, 'tensor', pairs)  13.3 us
    ppermute x3, waiting for transfers between devices, per_device(): lax.ppermute(stats, 'tensor', [(i, (i + SIDE * c) % tensor_count) for i i...  4.74 us
    pallas_call x1, Pallas kernels, logit_part(): pl.pallas_call(logit_kernel, out_shape=[jax.ShapeDtypeStruct((half, vocab...  4.55 us
    unnamed x32, local copies, waits for them, and re-layouts  4.03 us
    ppermute x3, starting transfers between devices, per_device(): lax.ppermute(stats, 'tensor', [(i, (i + SIDE * c) % tensor_count) for i i...  3.84 us
  transfers between devices with their start and end apart: 34, of which 28 were waited for; matrix products, arithmetic and copies ran while one was open for 2% of the time, Pallas kernels for 8%

profile of v5, /device:TPU:0, one launch (start us, length us, event | category | flops | bytes accessed | tf_op | source)
XLA Modules:
  0.0 135.9 jit_solution(12623906791117632141)
XLA Ops:
  0.7 1.1 copy-done.1
  1.7 0.7 copy-done.3
  2.4 0.9 pack_rows.1
  3.3 0.5 collective-permute-start
  3.8 0.8 dynamic_slice.9
  5.4 0.4 collective-permute-start.3
  5.8 2.7 %collective-permute-start.1 = (bf16[128,1280]{1,0:T(8,128)(2,1)S(1)}, bf16[128,1280]{1,0:T(8,128)(2,1)S(1)}, u32[]{:S(2)}, u32[]{:S(2)}) collective-permute-start(bf16[128,1280]{1,0:T(8,128)(2,1)S(1)} %pad_maximum_fusion.refs_0_), channel_id=1, source_target_pairs={{0,2},{1,3},{2,6},{3,7},{4,0},{5,1},{6,4},{7,5},{8,10},{9,11},{10,... | collective-permute-start | bytes 983048 | tf_op jit(solution)/shard_map/ppermute | solution.py:46
  8.5 1.5 %collective-permute-start.2 = (bf16[128,1280]{1,0:T(8,128)(2,1)S(1)}, bf16[128,1280]{1,0:T(8,128)(2,1)S(1)}, u32[]{:S(2)}, u32[]{:S(2)}) collective-permute-start(bf16[128,1280]{1,0:T(8,128)(2,1)S(1)} %pad_maximum_fusion.refs_0_), channel_id=1, source_target_pairs={{0,1},{1,0},{2,3},{3,2},{4,5},{5,4},{6,7},{7,6},{8,9},{9,8},{10,11... | collective-permute-start | bytes 983048 | tf_op jit(solution)/shard_map/ppermute | solution.py:30
  10.0 7.7 %collective-permute-done.1.refs_2_ = bf16[128,1280]{1,0:T(8,128)(2,1)S(1)} collective-permute-done((bf16[128,1280]{1,0:T(8,128)(2,1)S(1)}, bf16[128,1280]{1,0:T(8,128)(2,1)S(1)}, u32[]{:S(2)}, u32[]{:S(2)}) %collective-permute-start.1) | collective-permute-done | bytes 327712 | tf_op jit(solution)/shard_map/ppermute | solution.py:46
  17.7 0.5 collective-permute-done.2.refs_1_
  18.2 1.3 copy-done.8
  19.6 2.6 %collective-permute-start.4 = (bf16[128,1280]{1,0:T(8,128)(2,1)S(1)}, bf16[128,1280]{1,0:T(8,128)(2,1)S(1)}, u32[]{:S(2)}, u32[]{:S(2)}) collective-permute-start(bf16[128,1280]{1,0:T(8,128)(2,1)S(1)} %collective-permute-done.1.refs_2_), channel_id=1, source_target_pairs={{0,2},{1,3},{2,6},{3,7},{4,0},{5,1},{6,4},{7,5},{8,10},{9,11},{10,... | collective-permute-start | bytes 983048 | tf_op jit(solution)/shard_map/ppermute | solution.py:46
  22.1 1.5 %collective-permute-start.5 = (bf16[128,1280]{1,0:T(8,128)(2,1)S(1)}, bf16[128,1280]{1,0:T(8,128)(2,1)S(1)}, u32[]{:S(2)}, u32[]{:S(2)}) collective-permute-start(bf16[128,1280]{1,0:T(8,128)(2,1)S(1)} %collective-permute-done.1.refs_2_), channel_id=1, source_target_pairs={{0,1},{1,0},{2,3},{3,2},{4,5},{5,4},{6,7},{7,6},{8,9},{9,8},{10,11... | collective-permute-start | bytes 983048 | tf_op jit(solution)/shard_map/ppermute | solution.py:30
  23.7 5.7 %collective-permute-done.4.refs_4_ = bf16[128,1280]{1,0:T(8,128)(2,1)S(1)} collective-permute-done((bf16[128,1280]{1,0:T(8,128)(2,1)S(1)}, bf16[128,1280]{1,0:T(8,128)(2,1)S(1)}, u32[]{:S(2)}, u32[]{:S(2)}) %collective-permute-start.4) | collective-permute-done | bytes 327712 | tf_op jit(solution)/shard_map/ppermute | solution.py:46
  29.4 1.3 collective-permute-done.5.refs_3_
  30.7 1.5 %collective-permute-start.8 = (bf16[128,1280]{1,0:T(8,128)(2,1)S(1)}, bf16[128,1280]{1,0:T(8,128)(2,1)S(1)}, u32[]{:S(2)}, u32[]{:S(2)}) collective-permute-start(bf16[128,1280]{1,0:T(8,128)(2,1)S(1)} %collective-permute-done.4.refs_4_), channel_id=1, source_target_pairs={{0,1},{1,0},{2,3},{3,2},{4,5},{5,4},{6,7},{7,6},{8,9},{9,8},{10,11... | collective-permute-start | bytes 983048 | tf_op jit(solution)/shard_map/ppermute | solution.py:30
  32.2 1.5 %collective-permute-start.9 = (bf16[128,1280]{1,0:T(8,128)(2,1)S(1)}, bf16[128,1280]{1,0:T(8,128)(2,1)}, u32[]{:S(2)}, u32[]{:S(2)}) collective-permute-start(bf16[128,1280]{1,0:T(8,128)(2,1)S(1)} %collective-permute-done.4.refs_4_), channel_id=1, source_target_pairs={{0,2},{1,3},{2,6},{3,7},{4,0},{5,1},{6,4},{7,5},{8,10},{9,11},{10,... | collective-permute-start | bytes 983048 | tf_op jit(solution)/shard_map/ppermute | solution.py:46
  33.7 0.5 collective-permute-start.10
  34.9 0.9 collective-permute-done.11
  35.8 2.5 %collective-permute-done.8.refs_5_ = bf16[128,1280]{1,0:T(8,128)(2,1)S(1)} collective-permute-done((bf16[128,1280]{1,0:T(8,128)(2,1)S(1)}, bf16[128,1280]{1,0:T(8,128)(2,1)S(1)}, u32[]{:S(2)}, u32[]{:S(2)}) %collective-permute-start.8) | collective-permute-done | bytes 327712 | tf_op jit(solution)/shard_map/ppermute | solution.py:30
  38.3 2.2 %collective-permute-done.9.refs_6_ = bf16[128,1280]{1,0:T(8,128)(2,1)} collective-permute-done((bf16[128,1280]{1,0:T(8,128)(2,1)S(1)}, bf16[128,1280]{1,0:T(8,128)(2,1)}, u32[]{:S(2)}, u32[]{:S(2)}) %collective-permute-start.9) | collective-permute-done | bytes 327712 | tf_op jit(solution)/shard_map/ppermute | solution.py:46
  40.6 0.8 copy-done.9
  41.4 0.5 collective-permute-start.12
  41.9 3.8 %query_part.1 = (f32[128,256]{1,0:T(8,128)S(1)}, f32[128,256]{1,0:T(8,128)S(1)}, f32[128,128]{1,0:T(8,128)S(1)}) custom-call(f32[8,1024]{1,0:T(8,128)S(1)} %reshape.18.gain_ref, bf16[4096,256]{1,0:T(8,128)(2,1)} %q_own.3, bf16[4096,256]{1,0:T(8,128)(2,1)} %copy-done.8, bf16[128,1280]{1,0:T(8,128)(2,1)S(1)} %pad_maximum_fusion.refs_0_, ...), custom_call_target="tpu_custom_call" | custom-call | flops 469762048 | bytes 5505024 | tf_op jit(solution)/shard_map/query_part/pallas_call | solution.py:199
  45.8 2.9 %collective-permute-done.12.block_ref = bf16[128,1280]{1,0:T(8,128)(2,1)S(1)} collective-permute-done((bf16[128,1280]{1,0:T(8,128)(2,1)}, bf16[128,1280]{1,0:T(8,128)(2,1)S(1)}, u32[]{:S(2)}, u32[]{:S(2)}) %collective-permute-start.12) | collective-permute-done | bytes 327712 | tf_op jit(solution)/shard_map/ppermute | solution.py:30
  48.7 3.6 %attend.1 = (bf16[128,256]{1,0:T(8,128)(2,1)S(1)}, bf16[128,1024]{1,0:T(8,128)(2,1)S(1)}) custom-call(s32[8]{0:T(128)S(1)} %copy-done.4, s32[8]{0:T(128)S(1)} %pad_add_fusion.ctx_ref, f32[8,1024]{1,0:T(8,128)S(1)} %reshape.18.gain_ref, f32[128,256]{1,0:T(8,128)S(1)} %get-tuple-element.42.query_ref, f32[128,256]{1,0:T(8,128)S(1)} %get-tuple-element.43.kv_ref, ...), custom_call_target="tpu_custom_call" | custom-call | tf_op jit(solution)/shard_map/attend/pallas_call | solution.py:345
  52.3 0.6 collective-permute-start.16
  52.9 2.8 %out_products.1 = (bf16[128,1024]{1,0:T(8,128)(2,1)S(1)}, bf16[128,1024]{1,0:T(8,128)(2,1)S(1)}, bf16[128,1024]{1,0:T(8,128)(2,1)S(1)}, bf16[128,1024]{1,0:T(8,1...) custom-call(bf16[128,256]{1,0:T(8,128)(2,1)S(1)} %get-tuple-element.45.att, ...), custom_call_target="tpu_custom_call" | custom-call | flops 469762048 | bytes 5505024 | tf_op jit(solution)/shard_map/out_products/pallas_call | solution.py:383
  55.7 1.6 %collective-permute-start.15 = (bf16[128,1024]{1,0:T(8,128)(2,1)S(1)}, bf16[128,1024]{1,0:T(8,128)(2,1)S(1)}, u32[]{:S(2)}, u32[]{:S(2)}) collective-permute-start(bf16[128,1024]{1,0:T(8,128)(2,1)S(1)} %get-tuple-element.51), channel_id=1, source_target_pairs={{0,1},{1,0},{2,3},{3,2},{4,5},{5,4},{6,7},{7,6},{8,9},{9,8},{10,11... | collective-permute-start | bytes 786440 | tf_op jit(solution)/shard_map/ppermute | solution.py:30
  57.3 4.4 %collective-permute-done.16 = bf16[128,1024]{1,0:T(8,128)(2,1)S(1)} collective-permute-done((bf16[128,1024]{1,0:T(8,128)(2,1)S(1)}, bf16[128,1024]{1,0:T(8,128)(2,1)S(1)}, u32[]{:S(2)}, u32[]{:S(2)}) %collective-permute-start.16) | collective-permute-done | bytes 262176 | tf_op jit(solution)/shard_map/ppermute | solution.py:30
  61.7 1.0 collective-permute-start.17
  62.7 1.0 collective-permute-start.14
  63.7 3.4 %collective-permute-done.15 = bf16[128,1024]{1,0:T(8,128)(2,1)S(1)} collective-permute-done((bf16[128,1024]{1,0:T(8,128)(2,1)S(1)}, bf16[128,1024]{1,0:T(8,128)(2,1)S(1)}, u32[]{:S(2)}, u32[]{:S(2)}) %collective-permute-start.15) | collective-permute-done | bytes 262176 | tf_op jit(solution)/shard_map/ppermute | solution.py:30
  67.1 2.0 %collective-permute-done.17 = bf16[128,1024]{1,0:T(8,128)(2,1)S(1)} collective-permute-done((bf16[128,1024]{1,0:T(8,128)(2,1)S(1)}, bf16[128,1024]{1,0:T(8,128)(2,1)S(1)}, u32[]{:S(2)}, u32[]{:S(2)}) %collective-permute-start.17) | collective-permute-done | bytes 262176 | tf_op jit(solution)/shard_map/ppermute | solution.py:46
  69.2 0.4 collective-permute-start.18
  69.6 0.9 collective-permute-start.13
  70.6 5.9 %collective-permute-done.18 = bf16[128,1024]{1,0:T(8,128)(2,1)S(1)} collective-permute-done((bf16[128,1024]{1,0:T(8,128)(2,1)S(1)}, bf16[128,1024]{1,0:T(8,128)(2,1)S(1)}, u32[]{:S(2)}, u32[]{:S(2)}) %collective-permute-start.18) | collective-permute-done | bytes 262176 | tf_op jit(solution)/shard_map/ppermute | solution.py:46
  76.6 0.4 collective-permute-start.19
  77.0 6.9 %collective-permute-done.19 = bf16[128,1024]{1,0:T(8,128)(2,1)S(1)} collective-permute-done((bf16[128,1024]{1,0:T(8,128)(2,1)S(1)}, bf16[128,1024]{1,0:T(8,128)(2,1)S(1)}, u32[]{:S(2)}, u32[]{:S(2)}) %collective-permute-start.19) | collective-permute-done | bytes 262176 | tf_op jit(solution)/shard_map/ppermute | solution.py:46
  84.2 0.4 collective-permute-start.21
  84.6 0.9 collective-permute-start.22
  85.8 1.1 convolution_convert_fusion
  86.9 7.0 %collective-permute-done.21.refs_2_ = bf16[128,1024]{1,0:T(8,128)(2,1)S(1)} collective-permute-done((bf16[128,1024]{1,0:T(8,128)(2,1)S(1)}, bf16[128,1024]{1,0:T(8,128)(2,1)S(1)}, u32[]{:S(2)}, u32[]{:S(2)}) %collective-permute-start.21) | collective-permute-done | bytes 262176 | tf_op jit(solution)/shard_map/ppermute | solution.py:46
  93.9 0.7 collective-permute-start.24
  94.6 2.7 %collective-permute-start.25 = (bf16[128,1024]{1,0:T(8,128)(2,1)S(1)}, bf16[128,1024]{1,0:T(8,128)(2,1)S(1)}, u32[]{:S(2)}, u32[]{:S(2)}) collective-permute-start(bf16[128,1024]{1,0:T(8,128)(2,1)S(1)} %collective-permute-done.21.refs_2_), channel_id=1, source_target_pairs={{0,2},{1,3},{2,6},{3,7},{4,0},{5,1},{6,4},{7,5},{8,10},{9,11},{10,... | collective-permute-start | bytes 786440 | tf_op jit(solution)/shard_map/ppermute | solution.py:46
  97.3 5.3 %collective-permute-done.24.refs_3_ = bf16[128,1024]{1,0:T(8,128)(2,1)S(1)} collective-permute-done((bf16[128,1024]{1,0:T(8,128)(2,1)S(1)}, bf16[128,1024]{1,0:T(8,128)(2,1)S(1)}, u32[]{:S(2)}, u32[]{:S(2)}) %collective-permute-start.24) | collective-permute-done | bytes 262176 | tf_op jit(solution)/shard_map/ppermute | solution.py:30
  102.6 1.3 collective-permute-done.25.refs_4_
  103.8 1.4 %collective-permute-start.26 = (bf16[128,1024]{1,0:T(8,128)(2,1)S(1)}, bf16[128,1024]{1,0:T(8,128)(2,1)S(1)}, u32[]{:S(2)}, u32[]{:S(2)}) collective-permute-start(bf16[128,1024]{1,0:T(8,128)(2,1)S(1)} %collective-permute-done.25.refs_4_), channel_id=1, source_target_pairs={{0,1},{1,0},{2,3},{3,2},{4,5},{5,4},{6,7},{7,6},{8,9},{9,8},{10,11... | collective-permute-start | bytes 786440 | tf_op jit(solution)/shard_map/ppermute | solution.py:30
  105.2 1.6 %collective-permute-start.27 = (bf16[128,1024]{1,0:T(8,128)(2,1)S(1)}, bf16[128,1024]{1,0:T(8,128)(2,1)S(1)}, u32[]{:S(2)}, u32[]{:S(2)}) collective-permute-start(bf16[128,1024]{1,0:T(8,128)(2,1)S(1)} %collective-permute-done.25.refs_4_), channel_id=1, source_target_pairs={{0,2},{1,3},{2,6},{3,7},{4,0},{5,1},{6,4},{7,5},{8,10},{9,11},{10,... | collective-permute-start | bytes 786440 | tf_op jit(solution)/shard_map/ppermute | solution.py:46
  106.9 4.5 %collective-permute-done.26.refs_5_ = bf16[128,1024]{1,0:T(8,128)(2,1)S(1)} collective-permute-done((bf16[128,1024]{1,0:T(8,128)(2,1)S(1)}, bf16[128,1024]{1,0:T(8,128)(2,1)S(1)}, u32[]{:S(2)}, u32[]{:S(2)}) %collective-permute-start.26) | collective-permute-done | bytes 262176 | tf_op jit(solution)/shard_map/ppermute | solution.py:30
  111.4 2.0 %collective-permute-done.27.refs_6_ = bf16[128,1024]{1,0:T(8,128)(2,1)S(1)} collective-permute-done((bf16[128,1024]{1,0:T(8,128)(2,1)S(1)}, bf16[128,1024]{1,0:T(8,128)(2,1)S(1)}, u32[]{:S(2)}, u32[]{:S(2)}) %collective-permute-start.27) | collective-permute-done | bytes 262176 | tf_op jit(solution)/shard_map/ppermute | solution.py:46
  113.4 0.6 collective-permute-start.28
  114.2 4.5 %logit_part.1 = (f32[128,512]{1,0:T(8,128)S(1)}, f32[128,128]{1,0:T(8,128)S(1)}) custom-call(f32[8,1024]{1,0:T(8,128)S(1)} %reshape.20.gain_ref, bf16[4096,512]{1,0:T(8,128)(2,1)} %own_ref.3, bf16[4096,512]{1,0:T(8,128)(2,1)} %copy-done.6, bf16[128,1024]{1,0:T(8,128)(2,1)S(1)} %get-tuple-element.62.refs_0_, ...), custom_call_target="tpu_custom_call" | custom-call | flops 939524096 | bytes 9175040 | tf_op jit(solution)/shard_map/logit_part/pallas_call | solution.py:429
  118.7 1.0 collective-permute-done.28.block_ref
  119.8 1.9 %vocab_stats.1 = f32[8,128]{1,0:T(8,128)S(1)} custom-call(s32[128,1]{1,0:T(8,128)S(1)} %copy.13.targets_ref, f32[8,1024]{1,0:T(8,128)S(1)} %reshape.20.gain_ref, f32[128,512]{1,0:T(8,128)S(1)} %get-tuple-element.58.logits_ref, f32[128,128]{1,0:T(8,128)S(1)} %get-tuple-element.59.squares_ref, bf16[128,1024]{1,0:T(8,128)(2,1)S(1)} %collective-permute-done.28.block_ref, ...), custom_call_target="tpu_custom_call" | custom-call | tf_op jit(solution)/shard_map/vocab_stats/pallas_call | solution.py:481
  121.7 0.7 collective-permute-start.29
  122.4 2.9 %collective-permute-done.29 = f32[3,128]{1,0:T(4,128)S(1)} collective-permute-done((f32[3,128]{1,0:T(4,128)S(1)}, f32[3,128]{1,0:T(4,128)S(1)}, u32[]{:S(2)}, u32[]{:S(2)}) %collective-permute-start.29) | collective-permute-done | bytes 1568 | tf_op jit(solution)/shard_map/ppermute | solution.py:30
  125.3 3.2 %collective-permute-start.30 = (f32[3,128]{1,0:T(4,128)S(1)}, f32[3,128]{1,0:T(4,128)S(1)}, u32[]{:S(2)}, u32[]{:S(2)}) collective-permute-start(f32[3,128]{1,0:T(4,128)S(1)} %pad_maximum_fusion.1), channel_id=1, source_target_pairs={{0,6},{1,7},{2,0},{3,1},{4,2},{5,3},{6,4},{7,5},{8,14},{9,15},{10,... | collective-permute-start | bytes 4616 | tf_op jit(solution)/shard_map/ppermute | solution.py:602
  128.5 0.6 collective-permute-start.32
  129.2 0.7 collective-permute-done.30
  129.9 3.2 %collective-permute-done.31 = f32[3,128]{1,0:T(4,128)S(1)} collective-permute-done((f32[3,128]{1,0:T(4,128)S(1)}, f32[3,128]{1,0:T(4,128)S(1)}, u32[]{:S(2)}, u32[]{:S(2)}) %collective-permute-start.31) | collective-permute-done | bytes 1568 | tf_op jit(solution)/shard_map/ppermute | solution.py:602
  133.0 0.9 collective-permute-done.32
  134.1 1.1 collective-permute-done.33
  135.2 0.7 select_reduce_fusion
  (70 shorter events, 2.8 us)
Async XLA Ops:
  0.6 4.4 %copy-start = (bf16[1024,256]{1,0:T(8,128)(2,1)S(1)}, bf16[1024,256]{1,0:T(8,128)(2,1)}, u32[]{:S(2)}) copy-start(bf16[1024,256]{1,0:T(8,128)(2,1)} %param.14) | copy-start | bytes 1572868
  0.6 1.1 copy-start.1
  1.7 0.7 copy-start.3
  2.4 31.3 %copy-start.15 = (s32[4]{0:T(128)S(1)}, s32[4]{0:T(128)}, u32[]{:S(2)}) copy-start(s32[4]{0:T(128)} %param.20) | copy-start | bytes 52
  2.4 31.3 %copy-start.2 = (bf16[4,256,256]{2,1,0:T(8,128)(2,1)S(1)}, bf16[4,256,256]{2,1,0:T(8,128)(2,1)}, u32[]{:S(2)}) copy-start(bf16[4,256,256]{2,1,0:T(8,128)(2,1)} %cache_own.1) | copy-start | bytes 1572868
  2.4 31.8 %copy-start.14 = (s32[512]{0:T(512)S(1)}, s32[512]{0:T(512)}, u32[]{:S(2)}) copy-start(s32[512]{0:T(512)} %param.21) | copy-start | bytes 6148
  2.4 39.5 %copy-start.12 = (f32[8192]{0:T(1024)S(1)}, f32[8192]{0:T(1024)}, u32[]{:S(2)}) copy-start(f32[8192]{0:T(1024)} %param.12) | copy-start | bytes 98308
  3.3 1.7 %collective-permute-start = (bf16[128,1024]{1,0:T(8,128)(2,1)S(1)}, bf16[128,1024]{1,0:T(8,128)(2,1)S(1)}, u32[]{:S(2)}, u32[]{:S(2)}) collective-permute-start(bf16[128,1024]{1,0:T(8,128)(2,1)S(1)} %get-tuple-element.33), channel_id=1, source_target_pairs={{0,8},{8,0},{1,9},{9,1},{2,10},{10,2},{3,11},{11,3},{4,12},{12,4},... | collective-permute-start | bytes 786440 | tf_op jit(solution)/shard_map/ppermute | solution.py:25
  3.8 1.6 %copy-start.7 = (bf16[4096,256]{1,0:T(8,128)(2,1)S(1)}, bf16[4096,256]{1,0:T(8,128)(2,1)}, u32[]{:S(2)}) copy-start(bf16[4096,256]{1,0:T(8,128)(2,1)} %q_own.3) | copy-start | bytes 6291460
  5.4 12.8 %collective-permute-start.3 = (bf16[4096,256]{1,0:T(8,128)(2,1)S(1)}, bf16[4096,256]{1,0:T(8,128)(2,1)S(1)}, u32[]{:S(2)}, u32[]{:S(2)}) collective-permute-start(bf16[4096,256]{1,0:T(8,128)(2,1)S(1)} %copy-done.7), channel_id=1, source_target_pairs={{0,8},{8,0},{1,9},{9,1},{2,10},{10,2},{3,11},{11,3},{4,12},{12,4},... | collective-permute-start | bytes 6291464 | tf_op jit(solution)/shard_map/ppermute | solution.py:25
  5.8 12.0 %collective-permute-start.1 = (bf16[128,1280]{1,0:T(8,128)(2,1)S(1)}, bf16[128,1280]{1,0:T(8,128)(2,1)S(1)}, u32[]{:S(2)}, u32[]{:S(2)}) collective-permute-start(bf16[128,1280]{1,0:T(8,128)(2,1)S(1)} %pad_maximum_fusion.refs_0_), channel_id=1, source_target_pairs={{0,2},{1,3},{2,6},{3,7},{4,0},{5,1},{6,4},{7,5},{8,10},{9,11},{10,... | collective-permute-start | bytes 983048 | tf_op jit(solution)/shard_map/ppermute | solution.py:46
  8.5 9.7 %collective-permute-start.2 = (bf16[128,1280]{1,0:T(8,128)(2,1)S(1)}, bf16[128,1280]{1,0:T(8,128)(2,1)S(1)}, u32[]{:S(2)}, u32[]{:S(2)}) collective-permute-start(bf16[128,1280]{1,0:T(8,128)(2,1)S(1)} %pad_maximum_fusion.refs_0_), channel_id=1, source_target_pairs={{0,1},{1,0},{2,3},{3,2},{4,5},{5,4},{6,7},{7,6},{8,9},{9,8},{10,11... | collective-permute-start | bytes 983048 | tf_op jit(solution)/shard_map/ppermute | solution.py:30
  18.2 1.4 copy-start.8
  18.2 12.5 %collective-permute-start.6 = (bf16[256,4096]{1,0:T(8,128)(2,1)}, bf16[256,4096]{1,0:T(8,128)(2,1)}, u32[]{:S(2)}, u32[]{:S(2)}) collective-permute-start(bf16[256,4096]{1,0:T(8,128)(2,1)} %out_own.3), channel_id=1, source_target_pairs={{0,8},{8,0},{1,9},{9,1},{2,10},{10,2},{3,11},{11,3},{4,12},{12,4},... | collective-permute-start | bytes 6291464 | tf_op jit(solution)/shard_map/ppermute | solution.py:25
  19.6 9.8 %collective-permute-start.4 = (bf16[128,1280]{1,0:T(8,128)(2,1)S(1)}, bf16[128,1280]{1,0:T(8,128)(2,1)S(1)}, u32[]{:S(2)}, u32[]{:S(2)}) collective-permute-start(bf16[128,1280]{1,0:T(8,128)(2,1)S(1)} %collective-permute-done.1.refs_2_), channel_id=1, source_target_pairs={{0,2},{1,3},{2,6},{3,7},{4,0},{5,1},{6,4},{7,5},{8,10},{9,11},{10,... | collective-permute-start | bytes 983048 | tf_op jit(solution)/shard_map/ppermute | solution.py:46
  22.1 8.6 %collective-permute-start.5 = (bf16[128,1280]{1,0:T(8,128)(2,1)S(1)}, bf16[128,1280]{1,0:T(8,128)(2,1)S(1)}, u32[]{:S(2)}, u32[]{:S(2)}) collective-permute-start(bf16[128,1280]{1,0:T(8,128)(2,1)S(1)} %collective-permute-done.1.refs_2_), channel_id=1, source_target_pairs={{0,1},{1,0},{2,3},{3,2},{4,5},{5,4},{6,7},{7,6},{8,9},{9,8},{10,11... | collective-permute-start | bytes 983048 | tf_op jit(solution)/shard_map/ppermute | solution.py:30
  30.7 7.6 %collective-permute-start.8 = (bf16[128,1280]{1,0:T(8,128)(2,1)S(1)}, bf16[128,1280]{1,0:T(8,128)(2,1)S(1)}, u32[]{:S(2)}, u32[]{:S(2)}) collective-permute-start(bf16[128,1280]{1,0:T(8,128)(2,1)S(1)} %collective-permute-done.4.refs_4_), channel_id=1, source_target_pairs={{0,1},{1,0},{2,3},{3,2},{4,5},{5,4},{6,7},{7,6},{8,9},{9,8},{10,11... | collective-permute-start | bytes 983048 | tf_op jit(solution)/shard_map/ppermute | solution.py:30
  32.2 8.4 %collective-permute-start.9 = (bf16[128,1280]{1,0:T(8,128)(2,1)S(1)}, bf16[128,1280]{1,0:T(8,128)(2,1)}, u32[]{:S(2)}, u32[]{:S(2)}) collective-permute-start(bf16[128,1280]{1,0:T(8,128)(2,1)S(1)} %collective-permute-done.4.refs_4_), channel_id=1, source_target_pairs={{0,2},{1,3},{2,6},{3,7},{4,0},{5,1},{6,4},{7,5},{8,10},{9,11},{10,... | collective-permute-start | bytes 983048 | tf_op jit(solution)/shard_map/ppermute | solution.py:46
  33.7 1.1 collective-permute-start.7
  33.7 6.8 %collective-permute-start.10 = (bf16[4,256,256]{2,1,0:T(8,128)(2,1)S(1)}, bf16[4,256,256]{2,1,0:T(8,128)(2,1)S(1)}, u32[]{:S(2)}, u32[]{:S(2)}) collective-permute-start(bf16[4,256,256]{2,1,0:T(8,128)(2,1)S(1)} %copy-done.2), channel_id=1, source_target_pairs={{0,8},{8,0},{1,9},{9,1},{2,10},{10,2},{3,11},{11,3},{4,12},{12,4},... | collective-permute-start | bytes 1572872 | tf_op jit(solution)/shard_map/ppermute | solution.py:25
  34.5 1.3 collective-permute-start.11
  38.3 2.2 %copy-start.10 = (bf16[128,1280]{1,0:T(8,128)(2,1)}, bf16[128,1280]{1,0:T(8,128)(2,1)S(1)}, u32[]{:S(2)}) copy-start(bf16[128,1280]{1,0:T(8,128)(2,1)S(1)} %collective-permute-done.8.refs_5_) | copy-start | bytes 983044
  40.6 0.8 copy-start.9
  41.4 7.3 %collective-permute-start.12 = (bf16[128,1280]{1,0:T(8,128)(2,1)}, bf16[128,1280]{1,0:T(8,128)(2,1)S(1)}, u32[]{:S(2)}, u32[]{:S(2)}) collective-permute-start(bf16[128,1280]{1,0:T(8,128)(2,1)} %collective-permute-done.9.refs_6_), channel_id=1, source_target_pairs={{0,1},{1,0},{2,3},{3,2},{4,5},{5,4},{6,7},{7,6},{8,9},{9,8},{10,11... | collective-permute-start | bytes 983048 | tf_op jit(solution)/shard_map/ppermute | solution.py:30
  41.9 6.8 %copy-start.4 = (s32[8]{0:T(128)S(1)}, s32[8]{0:T(128)}, u32[]{:S(2)}) copy-start(s32[8]{0:T(128)} %lens_ref.3) | copy-start | bytes 100
  52.3 9.3 %collective-permute-start.16 = (bf16[128,1024]{1,0:T(8,128)(2,1)S(1)}, bf16[128,1024]{1,0:T(8,128)(2,1)S(1)}, u32[]{:S(2)}, u32[]{:S(2)}) collective-permute-start(bf16[128,1024]{1,0:T(8,128)(2,1)S(1)} %get-tuple-element.53), channel_id=1, source_target_pairs={{0,1},{1,0},{2,3},{3,2},{4,5},{5,4},{6,7},{7,6},{8,9},{9,8},{10,11... | collective-permute-start | bytes 786440 | tf_op jit(solution)/shard_map/ppermute | solution.py:30
  55.7 28.3 %dynamic-slice-start = ((f32[8192]{0:T(1024)}, s32[]{:T(128)}), f32[1024]{0:T(1024)S(1)}, s32[]{:S(2)}) async-start(f32[8192]{0:T(1024)} %param.17, s32[]{:T(128)} %select_n.142), calls=%async_computation | async-start | bytes 8704 | tf_op jit(solution)/shard_map/dynamic_slice | solution.py:563
  55.7 11.4 %collective-permute-start.15 = (bf16[128,1024]{1,0:T(8,128)(2,1)S(1)}, bf16[128,1024]{1,0:T(8,128)(2,1)S(1)}, u32[]{:S(2)}, u32[]{:S(2)}) collective-permute-start(bf16[128,1024]{1,0:T(8,128)(2,1)S(1)} %get-tuple-element.51), channel_id=1, source_target_pairs={{0,1},{1,0},{2,3},{3,2},{4,5},{5,4},{6,7},{7,6},{8,9},{9,8},{10,11... | collective-permute-start | bytes 786440 | tf_op jit(solution)/shard_map/ppermute | solution.py:30
  61.7 7.3 %collective-permute-start.17 = (bf16[128,1024]{1,0:T(8,128)(2,1)S(1)}, bf16[128,1024]{1,0:T(8,128)(2,1)S(1)}, u32[]{:S(2)}, u32[]{:S(2)}) collective-permute-start(bf16[128,1024]{1,0:T(8,128)(2,1)S(1)} %add_convert_fusion.2), channel_id=1, source_target_pairs={{0,2},{1,3},{2,6},{3,7},{4,0},{5,1},{6,4},{7,5},{8,10},{9,11},{10,... | collective-permute-start | bytes 786440 | tf_op jit(solution)/shard_map/ppermute | solution.py:46
  62.7 7.9 %collective-permute-start.14 = (bf16[128,1024]{1,0:T(8,128)(2,1)S(1)}, bf16[128,1024]{1,0:T(8,128)(2,1)S(1)}, u32[]{:S(2)}, u32[]{:S(2)}) collective-permute-start(bf16[128,1024]{1,0:T(8,128)(2,1)S(1)} %get-tuple-element.49), channel_id=1, source_target_pairs={{0,1},{1,0},{2,3},{3,2},{4,5},{5,4},{6,7},{7,6},{8,9},{9,8},{10,11... | collective-permute-start | bytes 786440 | tf_op jit(solution)/shard_map/ppermute | solution.py:30
  69.0 24.8 %copy-start.5 = (bf16[4096,512]{1,0:T(8,128)(2,1)S(1)}, bf16[4096,512]{1,0:T(8,128)(2,1)}, u32[]{:S(2)}) copy-start(bf16[4096,512]{1,0:T(8,128)(2,1)} %own_ref.3) | copy-start | bytes 12582916
  69.2 44.9 %copy-start.13 = (f32[8192]{0:T(1024)S(1)}, f32[8192]{0:T(1024)}, u32[]{:S(2)}) copy-start(f32[8192]{0:T(1024)} %param.17) | copy-start | bytes 98308
  69.2 7.3 %collective-permute-start.18 = (bf16[128,1024]{1,0:T(8,128)(2,1)S(1)}, bf16[128,1024]{1,0:T(8,128)(2,1)S(1)}, u32[]{:S(2)}, u32[]{:S(2)}) collective-permute-start(bf16[128,1024]{1,0:T(8,128)(2,1)S(1)} %add_convert_fusion.1), channel_id=1, source_target_pairs={{0,2},{1,3},{2,6},{3,7},{4,0},{5,1},{6,4},{7,5},{8,10},{9,11},{10,... | collective-permute-start | bytes 786440 | tf_op jit(solution)/shard_map/ppermute | solution.py:46
  69.6 7.5 %collective-permute-start.13 = (bf16[128,1024]{1,0:T(8,128)(2,1)S(1)}, bf16[128,1024]{1,0:T(8,128)(2,1)S(1)}, u32[]{:S(2)}, u32[]{:S(2)}) collective-permute-start(bf16[128,1024]{1,0:T(8,128)(2,1)S(1)} %get-tuple-element.47), channel_id=1, source_target_pairs={{0,1},{1,0},{2,3},{3,2},{4,5},{5,4},{6,7},{7,6},{8,9},{9,8},{10,11... | collective-permute-start | bytes 786440 | tf_op jit(solution)/shard_map/ppermute | solution.py:30
  76.6 7.3 %collective-permute-start.19 = (bf16[128,1024]{1,0:T(8,128)(2,1)S(1)}, bf16[128,1024]{1,0:T(8,128)(2,1)S(1)}, u32[]{:S(2)}, u32[]{:S(2)}) collective-permute-start(bf16[128,1024]{1,0:T(8,128)(2,1)S(1)} %add_convert_fusion), channel_id=1, source_target_pairs={{0,2},{1,3},{2,6},{3,7},{4,0},{5,1},{6,4},{7,5},{8,10},{9,11},{10,... | collective-permute-start | bytes 786440 | tf_op jit(solution)/shard_map/ppermute | solution.py:46
  84.2 1.6 %collective-permute-start.20 = (bf16[128,1024]{1,0:T(8,128)(2,1)S(1)}, bf16[128,1024]{1,0:T(8,128)(2,1)S(1)}, u32[]{:S(2)}, u32[]{:S(2)}) collective-permute-start(bf16[128,1024]{1,0:T(8,128)(2,1)S(1)} %get-tuple-element.63), channel_id=1, source_target_pairs={{0,8},{8,0},{1,9},{9,1},{2,10},{10,2},{3,11},{11,3},{4,12},{12,4},... | collective-permute-start | bytes 786440 | tf_op jit(solution)/shard_map/ppermute | solution.py:25
  84.2 9.6 %collective-permute-start.21 = (bf16[128,1024]{1,0:T(8,128)(2,1)S(1)}, bf16[128,1024]{1,0:T(8,128)(2,1)S(1)}, u32[]{:S(2)}, u32[]{:S(2)}) collective-permute-start(bf16[128,1024]{1,0:T(8,128)(2,1)S(1)} %get-tuple-element.62.refs_0_), channel_id=1, source_target_pairs={{0,2},{1,3},{2,6},{3,7},{4,0},{5,1},{6,4},{7,5},{8,10},{9,11},{10,... | collective-permute-start | bytes 786440 | tf_op jit(solution)/shard_map/ppermute | solution.py:46
  84.6 9.2 %collective-permute-start.22 = (bf16[128,1024]{1,0:T(8,128)(2,1)S(1)}, bf16[128,1024]{1,0:T(8,128)(2,1)S(1)}, u32[]{:S(2)}, u32[]{:S(2)}) collective-permute-start(bf16[128,1024]{1,0:T(8,128)(2,1)S(1)} %get-tuple-element.62.refs_0_), channel_id=1, source_target_pairs={{0,1},{1,0},{2,3},{3,2},{4,5},{5,4},{6,7},{7,6},{8,9},{9,8},{10,11... | collective-permute-start | bytes 786440 | tf_op jit(solution)/shard_map/ppermute | solution.py:30
  93.8 10.0 %collective-permute-start.23 = (bf16[4096,512]{1,0:T(8,128)(2,1)S(1)}, bf16[4096,512]{1,0:T(8,128)(2,1)S(1)}, u32[]{:S(2)}, u32[]{:S(2)}) collective-permute-start(bf16[4096,512]{1,0:T(8,128)(2,1)S(1)} %copy-done.5), channel_id=1, source_target_pairs={{0,8},{8,0},{1,9},{9,1},{2,10},{10,2},{3,11},{11,3},{4,12},{12,4},... | collective-permute-start | bytes 12582920 | tf_op jit(solution)/shard_map/ppermute | solution.py:25
  93.9 8.7 %collective-permute-start.24 = (bf16[128,1024]{1,0:T(8,128)(2,1)S(1)}, bf16[128,1024]{1,0:T(8,128)(2,1)S(1)}, u32[]{:S(2)}, u32[]{:S(2)}) collective-permute-start(bf16[128,1024]{1,0:T(8,128)(2,1)S(1)} %collective-permute-done.21.refs_2_), channel_id=1, source_target_pairs={{0,1},{1,0},{2,3},{3,2},{4,5},{5,4},{6,7},{7,6},{8,9},{9,8},{10,11... | collective-permute-start | bytes 786440 | tf_op jit(solution)/shard_map/ppermute | solution.py:30
  94.6 9.3 %collective-permute-start.25 = (bf16[128,1024]{1,0:T(8,128)(2,1)S(1)}, bf16[128,1024]{1,0:T(8,128)(2,1)S(1)}, u32[]{:S(2)}, u32[]{:S(2)}) collective-permute-start(bf16[128,1024]{1,0:T(8,128)(2,1)S(1)} %collective-permute-done.21.refs_2_), channel_id=1, source_target_pairs={{0,2},{1,3},{2,6},{3,7},{4,0},{5,1},{6,4},{7,5},{8,10},{9,11},{10,... | collective-permute-start | bytes 786440 | tf_op jit(solution)/shard_map/ppermute | solution.py:46
  103.8 9.5 %copy-start.6 = (bf16[4096,512]{1,0:T(8,128)(2,1)}, bf16[4096,512]{1,0:T(8,128)(2,1)S(1)}, u32[]{:S(2)}) copy-start(bf16[4096,512]{1,0:T(8,128)(2,1)S(1)} %collective-permute-done.23.other_ref) | copy-start | bytes 12582916
  103.8 7.5 %collective-permute-start.26 = (bf16[128,1024]{1,0:T(8,128)(2,1)S(1)}, bf16[128,1024]{1,0:T(8,128)(2,1)S(1)}, u32[]{:S(2)}, u32[]{:S(2)}) collective-permute-start(bf16[128,1024]{1,0:T(8,128)(2,1)S(1)} %collective-permute-done.25.refs_4_), channel_id=1, source_target_pairs={{0,1},{1,0},{2,3},{3,2},{4,5},{5,4},{6,7},{7,6},{8,9},{9,8},{10,11... | collective-permute-start | bytes 786440 | tf_op jit(solution)/shard_map/ppermute | solution.py:30
  105.2 8.2 %collective-permute-start.27 = (bf16[128,1024]{1,0:T(8,128)(2,1)S(1)}, bf16[128,1024]{1,0:T(8,128)(2,1)S(1)}, u32[]{:S(2)}, u32[]{:S(2)}) collective-permute-start(bf16[128,1024]{1,0:T(8,128)(2,1)S(1)} %collective-permute-done.25.refs_4_), channel_id=1, source_target_pairs={{0,2},{1,3},{2,6},{3,7},{4,0},{5,1},{6,4},{7,5},{8,10},{9,11},{10,... | collective-permute-start | bytes 786440 | tf_op jit(solution)/shard_map/ppermute | solution.py:46
  113.4 0.8 copy-start.11
  113.4 6.4 %collective-permute-start.28 = (bf16[128,1024]{1,0:T(8,128)(2,1)S(1)}, bf16[128,1024]{1,0:T(8,128)(2,1)S(1)}, u32[]{:S(2)}, u32[]{:S(2)}) collective-permute-start(bf16[128,1024]{1,0:T(8,128)(2,1)S(1)} %collective-permute-done.27.refs_6_), channel_id=1, source_target_pairs={{0,1},{1,0},{2,3},{3,2},{4,5},{5,4},{6,7},{7,6},{8,9},{9,8},{10,11... | collective-permute-start | bytes 786440 | tf_op jit(solution)/shard_map/ppermute | solution.py:30
  121.7 3.7 %collective-permute-start.29 = (f32[3,128]{1,0:T(4,128)S(1)}, f32[3,128]{1,0:T(4,128)S(1)}, u32[]{:S(2)}, u32[]{:S(2)}) collective-permute-start(f32[3,128]{1,0:T(4,128)S(1)} %slice.71), channel_id=1, source_target_pairs={{0,1},{1,0},{2,3},{3,2},{4,5},{5,4},{6,7},{7,6},{8,9},{9,8},{10,11... | collective-permute-start | bytes 4616 | tf_op jit(solution)/shard_map/ppermute | solution.py:30
  125.3 4.5 %collective-permute-start.30 = (f32[3,128]{1,0:T(4,128)S(1)}, f32[3,128]{1,0:T(4,128)S(1)}, u32[]{:S(2)}, u32[]{:S(2)}) collective-permute-start(f32[3,128]{1,0:T(4,128)S(1)} %pad_maximum_fusion.1), channel_id=1, source_target_pairs={{0,6},{1,7},{2,0},{3,1},{4,2},{5,3},{6,4},{7,5},{8,14},{9,15},{10,... | collective-permute-start | bytes 4616 | tf_op jit(solution)/shard_map/ppermute | solution.py:602
  128.5 4.5 %collective-permute-start.31 = (f32[3,128]{1,0:T(4,128)S(1)}, f32[3,128]{1,0:T(4,128)S(1)}, u32[]{:S(2)}, u32[]{:S(2)}) collective-permute-start(f32[3,128]{1,0:T(4,128)S(1)} %pad_maximum_fusion.1), channel_id=1, source_target_pairs={{0,4},{1,5},{2,6},{3,7},{4,0},{5,1},{6,2},{7,3},{8,12},{9,13},{10,... | collective-permute-start | bytes 4616 | tf_op jit(solution)/shard_map/ppermute | solution.py:602
  128.5 5.4 %collective-permute-start.32 = (f32[3,128]{1,0:T(4,128)S(1)}, f32[3,128]{1,0:T(4,128)S(1)}, u32[]{:S(2)}, u32[]{:S(2)}) collective-permute-start(f32[3,128]{1,0:T(4,128)S(1)} %pad_maximum_fusion.1), channel_id=1, source_target_pairs={{0,2},{1,3},{2,4},{3,5},{4,6},{5,7},{6,0},{7,1},{8,10},{9,11},{10,... | collective-permute-start | bytes 4616 | tf_op jit(solution)/shard_map/ppermute | solution.py:602
  134.0 1.2 collective-permute-start.33

commit v6 on v5

--- a/solution.py
+++ b/solution.py
@@ -11,6 +11,7 @@
 QH_DEV = 2
 GROUP = 16
 SIDE = 2
+SWAP_STEP = {"q": 0, "out": 1, "cache": 1, "ctx": 2, "targets": 2, "layer": 5, "vocab": 5}
 
 
 EPS = 1e-05
@@ -148,11 +149,12 @@
     group = lax.axis_index("dp")
     size = own_ref.shape[axis] * 2 // count
     copies = []
+    places = held if isinstance(held, list) else [held.at[j] for j in range(len(ids))]
     for j, block in enumerate(ids):
         place = pl.ds(pl.multiple_of((block % (count // 2)) * size, size), size)
         at = (place, slice(None)) if axis == 0 else (slice(None), place)
-        here = pltpu.make_async_copy(own_ref.at[at], held.at[j], sems.at[j])
-        there = pltpu.make_async_copy(other_ref.at[at], held.at[j], sems.at[j])
+        here = pltpu.make_async_copy(own_ref.at[at], places[j], sems.at[j])
+        there = pltpu.make_async_copy(other_ref.at[at], places[j], sems.at[j])
         copies.append((block // (count // 2) == group, here, there))
     return copies
 
@@ -522,27 +524,42 @@
     if kv_cache.shape[2] != 2 * HEAD:
         kv_head = tensor_pos * QH_DEV // GROUP
         cache = lax.dynamic_slice_in_dim(kv_cache, kv_head * 2 * HEAD, 2 * HEAD, 2)
-    def swap_rest(block):
-        context = after(ctx_len, block)
+    moved = {}
+
+    def swap_rows(value):
+        return lambda block: swap_dp(after(value, block))
+
+    def swap_targets(block):
         own_targets = lax.dynamic_slice_in_dim(
             after(target_ids, block), group * rows_count, rows_count, 0
         )
         sent_targets = jnp.sum(jnp.where(pick > 0, own_targets[None, :], 0), axis=1)
-        return [
-            swap_dp(after(cache, block)),
-            jnp.concatenate([ctx_len, swap_dp(context)], axis=0),
-            sent_targets[:half] + swap_dp(sent_targets[None, half:])[0],
-        ]
-
-    blocks, values = gather_blocks(
+        return sent_targets[:half] + swap_dp(sent_targets[None, half:])[0]
+
+    moves = {
+        "q": swap_rows(q_weight),
+        "out": swap_rows(out_weight),
+        "cache": swap_rows(cache),
+        "ctx": lambda block: jnp.concatenate([ctx_len, swap_dp(after(ctx_len, block))], axis=0),
+        "targets": swap_targets,
+        "vocab": swap_rows(vocab_weight),
+    }
+
+    def moves_at(step):
+        def run(block):
+            for name in moves:
+                if SWAP_STEP[name] == step:
+                    moved[name] = moves[name](block)
+            return [moved[name] for name in moves if SWAP_STEP[name] == step]
+
+        return run
+
+    blocks, _ = gather_blocks(
         jnp.concatenate([rows, kv_partial.astype(jnp.bfloat16)], axis=1),
-        [
-            lambda block: [swap_dp(after(q_weight, block))],
-            lambda block: [swap_dp(after(out_weight, block))],
-            swap_rest,
-        ],
-    )
-    q_other, out_other, cache_other, both_ctx, targets = values
+        [moves_at(step) for step in range(4)],
+    )
+    q_other, out_other, cache_other = moved["q"], moved["out"], moved["cache"]
+    both_ctx = moved["ctx"]
     q_pair, out_pair = (q_weight, q_other), (out_weight, out_other)
     gains = attn_gain.reshape(tensor_count, shard)
     parts = query_part(gains, q_pair, blocks[:-1])
@@ -564,17 +581,18 @@
 
     def place_rows(block):
         layer_rows = mixed.astype(jnp.bfloat16)
+        if SWAP_STEP["layer"] > 4:
+            layer_rows = after(layer_rows, block)
         layer_rows = jnp.concatenate([layer_rows, swap_dp(layer_rows)], axis=0)
-        return [
-            lax.dot_general(
-                pick, layer_rows, (((0,), (0,)), ((), ())), preferred_element_type=jnp.float32
-            ).astype(jnp.bfloat16)
-        ]
-
-    blocks, (layer_out, vocab_other) = gather_blocks(
-        (mixed * gain).astype(jnp.bfloat16),
-        [place_rows, lambda block: [swap_dp(after(vocab_weight, block))]],
-    )
+        return lax.dot_general(
+            pick, layer_rows, (((0,), (0,)), ((), ())), preferred_element_type=jnp.float32
+        ).astype(jnp.bfloat16)
+
+    moves["layer"] = place_rows
+    blocks, _ = gather_blocks(
+        (mixed * gain).astype(jnp.bfloat16), [moves_at(step) for step in range(4, 8)]
+    )
+    layer_out, vocab_other, targets = moved["layer"], moved["vocab"], moved["targets"]
     gains = final_gain.reshape(tensor_count, shard)
     vocab_pair = (vocab_weight, vocab_other)
     parts = logit_part(gains, vocab_pair, blocks[:-1])

time: 136 us -> 133 us (0.978)
  waiting for transfers between devices: 77.1 us -> 74.8 us
    ppermute x13, waiting for transfers between devices: 28.9 us -> 24.2 us  [swap_side(): return lax.ppermute(value, 'tensor', [(i, i ^ 1) for i in range(count)])]
    ppermute x9, waiting for transfers between devices: 2.8 us -> 5.94 us  [swap_dp(): return lax.ppermute(value, 'dp', [(0, 1), (1, 0)])]
    unnamed x32 -> x30, local copies, waits for them, and re-layouts: 4.03 us -> 3.46 us
where the time goes in v6:
time: 133 us; the launch traced here: 132 us
  waiting for transfers between devices  74.8 us (56%)
  starting transfers between devices  31.7 us (24%)
  Pallas kernels  17.5 us (13%)
  local copies, waits for them, and re-layouts  4.53 us (3%)
  other arithmetic  1.55 us (1%)
  matrix products  1.35 us (1%)
    ppermute x9, waiting for transfers between devices, ring_step(): return lax.ppermute(value, 'tensor', pairs)  40 us
    ppermute x13, waiting for transfers between devices, swap_side(): return lax.ppermute(value, 'tensor', [(i, i ^ 1) for i in range(count)])  24.2 us
    ppermute x13, starting transfers between devices, swap_side(): return lax.ppermute(value, 'tensor', [(i, i ^ 1) for i in range(count)])  13 us
    ppermute x9, starting transfers between devices, ring_step(): return lax.ppermute(value, 'tensor', pairs)  12.8 us
    ppermute x9, waiting for transfers between devices, swap_dp(): return lax.ppermute(value, 'dp', [(0, 1), (1, 0)])  5.94 us
    ppermute x3, waiting for transfers between devices, per_device(): lax.ppermute(stats, 'tensor', [(i, (i + SIDE * c) % tensor_count) for i i...  4.74 us
    pallas_call x1, Pallas kernels, logit_part(): pl.pallas_call(logit_kernel, out_shape=[jax.ShapeDtypeStruct((half, vocab...  4.54 us
    pallas_call x1, Pallas kernels, query_part(): pl.pallas_call(functools.partial(query_kernel, shard), out_shape=[jax.Sha...  3.84 us
  transfers between devices with their start and end apart: 34, of which 28 were waited for; matrix products, arithmetic and copies ran while one was open for 2% of the time, Pallas kernels for 8%

profile of v6, /device:TPU:0, one launch (start us, length us, event | category | flops | bytes accessed | tf_op | source)
XLA Modules:
  0.0 132.4 jit_solution(16890052906318908302)
XLA Ops:
  0.7 1.1 copy-done.1
  1.7 0.7 copy-done.3
  2.4 0.9 pack_rows.1
  3.3 0.5 collective-permute-start
  3.8 0.8 dynamic_slice.9
  5.4 0.4 collective-permute-start.3
  5.8 2.7 %collective-permute-start.1 = (bf16[128,1280]{1,0:T(8,128)(2,1)S(1)}, bf16[128,1280]{1,0:T(8,128)(2,1)S(1)}, u32[]{:S(2)}, u32[]{:S(2)}) collective-permute-start(bf16[128,1280]{1,0:T(8,128)(2,1)S(1)} %pad_maximum_fusion.refs_0_), channel_id=1, source_target_pairs={{0,2},{1,3},{2,6},{3,7},{4,0},{5,1},{6,4},{7,5},{8,10},{9,11},{10,... | collective-permute-start | bytes 983048 | tf_op jit(solution)/shard_map/ppermute | solution.py:47
  8.5 1.5 %collective-permute-start.2 = (bf16[128,1280]{1,0:T(8,128)(2,1)S(1)}, bf16[128,1280]{1,0:T(8,128)(2,1)S(1)}, u32[]{:S(2)}, u32[]{:S(2)}) collective-permute-start(bf16[128,1280]{1,0:T(8,128)(2,1)S(1)} %pad_maximum_fusion.refs_0_), channel_id=1, source_target_pairs={{0,1},{1,0},{2,3},{3,2},{4,5},{5,4},{6,7},{7,6},{8,9},{9,8},{10,11... | collective-permute-start | bytes 983048 | tf_op jit(solution)/shard_map/ppermute | solution.py:31
  10.0 7.7 %collective-permute-done.1.refs_2_ = bf16[128,1280]{1,0:T(8,128)(2,1)S(1)} collective-permute-done((bf16[128,1280]{1,0:T(8,128)(2,1)S(1)}, bf16[128,1280]{1,0:T(8,128)(2,1)S(1)}, u32[]{:S(2)}, u32[]{:S(2)}) %collective-permute-start.1) | collective-permute-done | bytes 327712 | tf_op jit(solution)/shard_map/ppermute | solution.py:47
  17.7 0.5 collective-permute-done.2.refs_1_
  18.2 0.5 collective-permute-start.7
  18.7 0.8 copy-done.8
  19.6 2.6 %collective-permute-start.4 = (bf16[128,1280]{1,0:T(8,128)(2,1)S(1)}, bf16[128,1280]{1,0:T(8,128)(2,1)S(1)}, u32[]{:S(2)}, u32[]{:S(2)}) collective-permute-start(bf16[128,1280]{1,0:T(8,128)(2,1)S(1)} %collective-permute-done.1.refs_2_), channel_id=1, source_target_pairs={{0,2},{1,3},{2,6},{3,7},{4,0},{5,1},{6,4},{7,5},{8,10},{9,11},{10,... | collective-permute-start | bytes 983048 | tf_op jit(solution)/shard_map/ppermute | solution.py:47
  22.1 1.5 %collective-permute-start.5 = (bf16[128,1280]{1,0:T(8,128)(2,1)S(1)}, bf16[128,1280]{1,0:T(8,128)(2,1)S(1)}, u32[]{:S(2)}, u32[]{:S(2)}) collective-permute-start(bf16[128,1280]{1,0:T(8,128)(2,1)S(1)} %collective-permute-done.1.refs_2_), channel_id=1, source_target_pairs={{0,1},{1,0},{2,3},{3,2},{4,5},{5,4},{6,7},{7,6},{8,9},{9,8},{10,11... | collective-permute-start | bytes 983048 | tf_op jit(solution)/shard_map/ppermute | solution.py:31
  23.7 5.7 %collective-permute-done.4.refs_4_ = bf16[128,1280]{1,0:T(8,128)(2,1)S(1)} collective-permute-done((bf16[128,1280]{1,0:T(8,128)(2,1)S(1)}, bf16[128,1280]{1,0:T(8,128)(2,1)S(1)}, u32[]{:S(2)}, u32[]{:S(2)}) %collective-permute-start.4) | collective-permute-done | bytes 327712 | tf_op jit(solution)/shard_map/ppermute | solution.py:47
  29.4 1.3 collective-permute-done.5.refs_3_
  30.7 1.5 %collective-permute-start.9 = (bf16[128,1280]{1,0:T(8,128)(2,1)S(1)}, bf16[128,1280]{1,0:T(8,128)(2,1)S(1)}, u32[]{:S(2)}, u32[]{:S(2)}) collective-permute-start(bf16[128,1280]{1,0:T(8,128)(2,1)S(1)} %collective-permute-done.4.refs_4_), channel_id=1, source_target_pairs={{0,1},{1,0},{2,3},{3,2},{4,5},{5,4},{6,7},{7,6},{8,9},{9,8},{10,11... | collective-permute-start | bytes 983048 | tf_op jit(solution)/shard_map/ppermute | solution.py:31
  32.2 1.5 %collective-permute-start.10 = (bf16[128,1280]{1,0:T(8,128)(2,1)S(1)}, bf16[128,1280]{1,0:T(8,128)(2,1)}, u32[]{:S(2)}, u32[]{:S(2)}) collective-permute-start(bf16[128,1280]{1,0:T(8,128)(2,1)S(1)} %collective-permute-done.4.refs_4_), channel_id=1, source_target_pairs={{0,2},{1,3},{2,6},{3,7},{4,0},{5,1},{6,4},{7,5},{8,10},{9,11},{10,... | collective-permute-start | bytes 983048 | tf_op jit(solution)/shard_map/ppermute | solution.py:47
  34.0 0.6 collective-permute-start.11
  34.5 0.3 collective-permute-done.8
  34.9 0.4 collective-permute-done.11
  35.4 3.0 %collective-permute-done.9.refs_5_ = bf16[128,1280]{1,0:T(8,128)(2,1)S(1)} collective-permute-done((bf16[128,1280]{1,0:T(8,128)(2,1)S(1)}, bf16[128,1280]{1,0:T(8,128)(2,1)S(1)}, u32[]{:S(2)}, u32[]{:S(2)}) %collective-permute-start.9) | collective-permute-done | bytes 327712 | tf_op jit(solution)/shard_map/ppermute | solution.py:31
  38.4 0.7 copy-done.9
  39.1 1.5 %collective-permute-done.10.refs_6_ = bf16[128,1280]{1,0:T(8,128)(2,1)} collective-permute-done((bf16[128,1280]{1,0:T(8,128)(2,1)S(1)}, bf16[128,1280]{1,0:T(8,128)(2,1)}, u32[]{:S(2)}, u32[]{:S(2)}) %collective-permute-start.10) | collective-permute-done | bytes 327712 | tf_op jit(solution)/shard_map/ppermute | solution.py:47
  40.6 0.5 collective-permute-start.12
  41.2 3.8 %query_part.1 = (f32[128,256]{1,0:T(8,128)S(1)}, f32[128,256]{1,0:T(8,128)S(1)}, f32[128,128]{1,0:T(8,128)S(1)}) custom-call(f32[8,1024]{1,0:T(8,128)S(1)} %reshape.18.gain_ref, bf16[4096,256]{1,0:T(8,128)(2,1)} %q_own.3, bf16[4096,256]{1,0:T(8,128)(2,1)} %copy-done.8, bf16[128,1280]{1,0:T(8,128)(2,1)S(1)} %pad_maximum_fusion.refs_0_, ...), custom_call_target="tpu_custom_call" | custom-call | flops 469762048 | bytes 5505024 | tf_op jit(solution)/shard_map/query_part/pallas_call | solution.py:201
  45.0 2.9 %collective-permute-done.12.block_ref = bf16[128,1280]{1,0:T(8,128)(2,1)S(1)} collective-permute-done((bf16[128,1280]{1,0:T(8,128)(2,1)}, bf16[128,1280]{1,0:T(8,128)(2,1)S(1)}, u32[]{:S(2)}, u32[]{:S(2)}) %collective-permute-start.12) | collective-permute-done | bytes 327712 | tf_op jit(solution)/shard_map/ppermute | solution.py:31
  47.9 3.6 %attend.1 = (bf16[128,256]{1,0:T(8,128)(2,1)S(1)}, bf16[128,1024]{1,0:T(8,128)(2,1)S(1)}) custom-call(s32[8]{0:T(128)S(1)} %copy-done.4, s32[8]{0:T(128)S(1)} %pad_add_fusion.ctx_ref, f32[8,1024]{1,0:T(8,128)S(1)} %reshape.18.gain_ref, f32[128,256]{1,0:T(8,128)S(1)} %get-tuple-element.43.query_ref, f32[128,256]{1,0:T(8,128)S(1)} %get-tuple-element.44.kv_ref, ...), custom_call_target="tpu_custom_call" | custom-call | tf_op jit(solution)/shard_map/attend/pallas_call | solution.py:347
  51.6 0.6 collective-permute-start.16
  52.1 2.8 %out_products.1 = (bf16[128,1024]{1,0:T(8,128)(2,1)S(1)}, bf16[128,1024]{1,0:T(8,128)(2,1)S(1)}, bf16[128,1024]{1,0:T(8,128)(2,1)S(1)}, bf16[128,1024]{1,0:T(8,1...) custom-call(bf16[128,256]{1,0:T(8,128)(2,1)S(1)} %get-tuple-element.46.att, ...), custom_call_target="tpu_custom_call" | custom-call | flops 469762048 | bytes 5505024 | tf_op jit(solution)/shard_map/out_products/pallas_call | solution.py:385
  54.9 1.6 %collective-permute-start.15 = (bf16[128,1024]{1,0:T(8,128)(2,1)S(1)}, bf16[128,1024]{1,0:T(8,128)(2,1)S(1)}, u32[]{:S(2)}, u32[]{:S(2)}) collective-permute-start(bf16[128,1024]{1,0:T(8,128)(2,1)S(1)} %get-tuple-element.52), channel_id=1, source_target_pairs={{0,1},{1,0},{2,3},{3,2},{4,5},{5,4},{6,7},{7,6},{8,9},{9,8},{10,11... | collective-permute-start | bytes 786440 | tf_op jit(solution)/shard_map/ppermute | solution.py:31
  56.5 4.4 %collective-permute-done.16 = bf16[128,1024]{1,0:T(8,128)(2,1)S(1)} collective-permute-done((bf16[128,1024]{1,0:T(8,128)(2,1)S(1)}, bf16[128,1024]{1,0:T(8,128)(2,1)S(1)}, u32[]{:S(2)}, u32[]{:S(2)}) %collective-permute-start.16) | collective-permute-done | bytes 262176 | tf_op jit(solution)/shard_map/ppermute | solution.py:31
  60.9 0.9 collective-permute-start.17
  61.9 1.0 collective-permute-start.14
  62.9 3.4 %collective-permute-done.15 = bf16[128,1024]{1,0:T(8,128)(2,1)S(1)} collective-permute-done((bf16[128,1024]{1,0:T(8,128)(2,1)S(1)}, bf16[128,1024]{1,0:T(8,128)(2,1)S(1)}, u32[]{:S(2)}, u32[]{:S(2)}) %collective-permute-start.15) | collective-permute-done | bytes 262176 | tf_op jit(solution)/shard_map/ppermute | solution.py:31
  66.3 2.0 %collective-permute-done.17 = bf16[128,1024]{1,0:T(8,128)(2,1)S(1)} collective-permute-done((bf16[128,1024]{1,0:T(8,128)(2,1)S(1)}, bf16[128,1024]{1,0:T(8,128)(2,1)S(1)}, u32[]{:S(2)}, u32[]{:S(2)}) %collective-permute-start.17) | collective-permute-done | bytes 262176 | tf_op jit(solution)/shard_map/ppermute | solution.py:47
  68.4 0.4 collective-permute-start.18
  68.8 0.9 collective-permute-start.13
  69.9 6.3 %collective-permute-done.18 = bf16[128,1024]{1,0:T(8,128)(2,1)S(1)} collective-permute-done((bf16[128,1024]{1,0:T(8,128)(2,1)S(1)}, bf16[128,1024]{1,0:T(8,128)(2,1)S(1)}, u32[]{:S(2)}, u32[]{:S(2)}) %collective-permute-start.18) | collective-permute-done | bytes 262176 | tf_op jit(solution)/shard_map/ppermute | solution.py:47
  76.4 7.2 %collective-permute-done.19 = bf16[128,1024]{1,0:T(8,128)(2,1)S(1)} collective-permute-done((bf16[128,1024]{1,0:T(8,128)(2,1)S(1)}, bf16[128,1024]{1,0:T(8,128)(2,1)S(1)}, u32[]{:S(2)}, u32[]{:S(2)}) %collective-permute-start.19) | collective-permute-done | bytes 262176 | tf_op jit(solution)/shard_map/ppermute | solution.py:47
  83.9 0.8 collective-permute-start.21
  84.7 6.5 %collective-permute-done.20.refs_2_ = bf16[128,1024]{1,0:T(8,128)(2,1)S(1)} collective-permute-done((bf16[128,1024]{1,0:T(8,128)(2,1)S(1)}, bf16[128,1024]{1,0:T(8,128)(2,1)S(1)}, u32[]{:S(2)}, u32[]{:S(2)}) %collective-permute-start.20) | collective-permute-done | bytes 262176 | tf_op jit(solution)/shard_map/ppermute | solution.py:47
  91.2 0.5 collective-permute-start.22
  91.9 3.1 %collective-permute-start.25 = (bf16[128,1024]{1,0:T(8,128)(2,1)S(1)}, bf16[128,1024]{1,0:T(8,128)(2,1)S(1)}, u32[]{:S(2)}, u32[]{:S(2)}) collective-permute-start(bf16[128,1024]{1,0:T(8,128)(2,1)S(1)} %collective-permute-done.20.refs_2_), channel_id=1, source_target_pairs={{0,2},{1,3},{2,6},{3,7},{4,0},{5,1},{6,4},{7,5},{8,10},{9,11},{10,... | collective-permute-start | bytes 786440 | tf_op jit(solution)/shard_map/ppermute | solution.py:47
  95.0 3.8 %collective-permute-done.22 = bf16[128,1024]{1,0:T(8,128)(2,1)S(1)} collective-permute-done((bf16[128,1024]{1,0:T(8,128)(2,1)S(1)}, bf16[128,1024]{1,0:T(8,128)(2,1)S(1)}, u32[]{:S(2)}, u32[]{:S(2)}) %collective-permute-start.22) | collective-permute-done | bytes 262176 | tf_op jit(solution)/shard_map/ppermute | solution.py:26
  98.7 1.1 convolution_convert_fusion
  100.0 0.9 collective-permute-done.25.refs_4_
  100.9 1.7 %collective-permute-start.26 = (bf16[128,1024]{1,0:T(8,128)(2,1)S(1)}, bf16[128,1024]{1,0:T(8,128)(2,1)S(1)}, u32[]{:S(2)}, u32[]{:S(2)}) collective-permute-start(bf16[128,1024]{1,0:T(8,128)(2,1)S(1)} %collective-permute-done.25.refs_4_), channel_id=1, source_target_pairs={{0,1},{1,0},{2,3},{3,2},{4,5},{5,4},{6,7},{7,6},{8,9},{9,8},{10,11... | collective-permute-start | bytes 786440 | tf_op jit(solution)/shard_map/ppermute | solution.py:31
  102.6 1.4 %collective-permute-start.27 = (bf16[128,1024]{1,0:T(8,128)(2,1)S(1)}, bf16[128,1024]{1,0:T(8,128)(2,1)S(1)}, u32[]{:S(2)}, u32[]{:S(2)}) collective-permute-start(bf16[128,1024]{1,0:T(8,128)(2,1)S(1)} %collective-permute-done.25.refs_4_), channel_id=1, source_target_pairs={{0,2},{1,3},{2,6},{3,7},{4,0},{5,1},{6,4},{7,5},{8,10},{9,11},{10,... | collective-permute-start | bytes 786440 | tf_op jit(solution)/shard_map/ppermute | solution.py:47
  104.1 4.2 %collective-permute-done.26.refs_5_ = bf16[128,1024]{1,0:T(8,128)(2,1)S(1)} collective-permute-done((bf16[128,1024]{1,0:T(8,128)(2,1)S(1)}, bf16[128,1024]{1,0:T(8,128)(2,1)S(1)}, u32[]{:S(2)}, u32[]{:S(2)}) %collective-permute-start.26) | collective-permute-done | bytes 262176 | tf_op jit(solution)/shard_map/ppermute | solution.py:31
  108.3 2.1 %collective-permute-done.27.refs_6_ = bf16[128,1024]{1,0:T(8,128)(2,1)S(1)} collective-permute-done((bf16[128,1024]{1,0:T(8,128)(2,1)S(1)}, bf16[128,1024]{1,0:T(8,128)(2,1)S(1)}, u32[]{:S(2)}, u32[]{:S(2)}) %collective-permute-start.27) | collective-permute-done | bytes 262176 | tf_op jit(solution)/shard_map/ppermute | solution.py:47
  110.4 0.5 collective-permute-start.28
  111.1 4.5 %logit_part.1 = (f32[128,512]{1,0:T(8,128)S(1)}, f32[128,128]{1,0:T(8,128)S(1)}) custom-call(f32[8,1024]{1,0:T(8,128)S(1)} %reshape.20.gain_ref, bf16[4096,512]{1,0:T(8,128)(2,1)} %own_ref.3, bf16[4096,512]{1,0:T(8,128)(2,1)} %copy-done.6, bf16[128,1024]{1,0:T(8,128)(2,1)S(1)} %get-tuple-element.64.refs_0_, ...), custom_call_target="tpu_custom_call" | custom-call | flops 939524096 | bytes 9175040 | tf_op jit(solution)/shard_map/logit_part/pallas_call | solution.py:431
  115.6 1.1 collective-permute-done.28.block_ref
  116.8 1.9 %vocab_stats.1 = f32[8,128]{1,0:T(8,128)S(1)} custom-call(s32[128,1]{1,0:T(8,128)S(1)} %copy.13.targets_ref, f32[8,1024]{1,0:T(8,128)S(1)} %reshape.20.gain_ref, f32[128,512]{1,0:T(8,128)S(1)} %get-tuple-element.60.logits_ref, f32[128,128]{1,0:T(8,128)S(1)} %get-tuple-element.61.squares_ref, bf16[128,1024]{1,0:T(8,128)(2,1)S(1)} %collective-permute-done.28.block_ref, ...), custom_call_target="tpu_custom_call" | custom-call | tf_op jit(solution)/shard_map/vocab_stats/pallas_call | solution.py:483
  118.7 0.6 collective-permute-start.29
  119.3 3.0 %collective-permute-done.29 = f32[3,128]{1,0:T(4,128)S(1)} collective-permute-done((f32[3,128]{1,0:T(4,128)S(1)}, f32[3,128]{1,0:T(4,128)S(1)}, u32[]{:S(2)}, u32[]{:S(2)}) %collective-permute-start.29) | collective-permute-done | bytes 1568 | tf_op jit(solution)/shard_map/ppermute | solution.py:31
  122.3 2.8 %collective-permute-start.30 = (f32[3,128]{1,0:T(4,128)S(1)}, f32[3,128]{1,0:T(4,128)S(1)}, u32[]{:S(2)}, u32[]{:S(2)}) collective-permute-start(f32[3,128]{1,0:T(4,128)S(1)} %pad_maximum_fusion.1), channel_id=1, source_target_pairs={{0,6},{1,7},{2,0},{3,1},{4,2},{5,3},{6,4},{7,5},{8,14},{9,15},{10,... | collective-permute-start | bytes 4616 | tf_op jit(solution)/shard_map/ppermute | solution.py:620
  125.1 0.6 collective-permute-start.32
  125.8 0.7 collective-permute-done.30
  126.4 3.2 %collective-permute-done.31 = f32[3,128]{1,0:T(4,128)S(1)} collective-permute-done((f32[3,128]{1,0:T(4,128)S(1)}, f32[3,128]{1,0:T(4,128)S(1)}, u32[]{:S(2)}, u32[]{:S(2)}) %collective-permute-start.31) | collective-permute-done | bytes 1568 | tf_op jit(solution)/shard_map/ppermute | solution.py:620
  129.6 0.9 collective-permute-done.32
  130.6 1.1 collective-permute-done.33
  131.8 0.7 select_reduce_fusion
  (68 shorter events, 2.5 us)
Async XLA Ops:
  0.6 4.4 %copy-start = (bf16[1024,256]{1,0:T(8,128)(2,1)S(1)}, bf16[1024,256]{1,0:T(8,128)(2,1)}, u32[]{:S(2)}) copy-start(bf16[1024,256]{1,0:T(8,128)(2,1)} %param.14) | copy-start | bytes 1572868
  0.6 1.1 copy-start.1
  1.7 0.7 copy-start.3
  2.4 15.8 %copy-start.2 = (bf16[4,256,256]{2,1,0:T(8,128)(2,1)S(1)}, bf16[4,256,256]{2,1,0:T(8,128)(2,1)}, u32[]{:S(2)}) copy-start(bf16[4,256,256]{2,1,0:T(8,128)(2,1)} %cache_own.1) | copy-start | bytes 1572868
  2.4 31.3 %copy-start.14 = (s32[4]{0:T(128)S(1)}, s32[4]{0:T(128)}, u32[]{:S(2)}) copy-start(s32[4]{0:T(128)} %param.20) | copy-start | bytes 52
  2.4 31.3 %copy-start.13 = (s32[512]{0:T(512)S(1)}, s32[512]{0:T(512)}, u32[]{:S(2)}) copy-start(s32[512]{0:T(512)} %param.21) | copy-start | bytes 6148
  2.4 38.7 %copy-start.11 = (f32[8192]{0:T(1024)S(1)}, f32[8192]{0:T(1024)}, u32[]{:S(2)}) copy-start(f32[8192]{0:T(1024)} %param.12) | copy-start | bytes 98308
  3.3 1.7 %collective-permute-start = (bf16[128,1024]{1,0:T(8,128)(2,1)S(1)}, bf16[128,1024]{1,0:T(8,128)(2,1)S(1)}, u32[]{:S(2)}, u32[]{:S(2)}) collective-permute-start(bf16[128,1024]{1,0:T(8,128)(2,1)S(1)} %get-tuple-element.34), channel_id=1, source_target_pairs={{0,8},{8,0},{1,9},{9,1},{2,10},{10,2},{3,11},{11,3},{4,12},{12,4},... | collective-permute-start | bytes 786440 | tf_op jit(solution)/shard_map/ppermute | solution.py:26
  3.8 1.6 %copy-start.7 = (bf16[4096,256]{1,0:T(8,128)(2,1)S(1)}, bf16[4096,256]{1,0:T(8,128)(2,1)}, u32[]{:S(2)}) copy-start(bf16[4096,256]{1,0:T(8,128)(2,1)} %q_own.3) | copy-start | bytes 6291460
  5.4 12.8 %collective-permute-start.3 = (bf16[4096,256]{1,0:T(8,128)(2,1)S(1)}, bf16[4096,256]{1,0:T(8,128)(2,1)S(1)}, u32[]{:S(2)}, u32[]{:S(2)}) collective-permute-start(bf16[4096,256]{1,0:T(8,128)(2,1)S(1)} %copy-done.7), channel_id=1, source_target_pairs={{0,8},{8,0},{1,9},{9,1},{2,10},{10,2},{3,11},{11,3},{4,12},{12,4},... | collective-permute-start | bytes 6291464 | tf_op jit(solution)/shard_map/ppermute | solution.py:26
  5.8 12.0 %collective-permute-start.1 = (bf16[128,1280]{1,0:T(8,128)(2,1)S(1)}, bf16[128,1280]{1,0:T(8,128)(2,1)S(1)}, u32[]{:S(2)}, u32[]{:S(2)}) collective-permute-start(bf16[128,1280]{1,0:T(8,128)(2,1)S(1)} %pad_maximum_fusion.refs_0_), channel_id=1, source_target_pairs={{0,2},{1,3},{2,6},{3,7},{4,0},{5,1},{6,4},{7,5},{8,10},{9,11},{10,... | collective-permute-start | bytes 983048 | tf_op jit(solution)/shard_map/ppermute | solution.py:47
  8.5 9.7 %collective-permute-start.2 = (bf16[128,1280]{1,0:T(8,128)(2,1)S(1)}, bf16[128,1280]{1,0:T(8,128)(2,1)S(1)}, u32[]{:S(2)}, u32[]{:S(2)}) collective-permute-start(bf16[128,1280]{1,0:T(8,128)(2,1)S(1)} %pad_maximum_fusion.refs_0_), channel_id=1, source_target_pairs={{0,1},{1,0},{2,3},{3,2},{4,5},{5,4},{6,7},{7,6},{8,9},{9,8},{10,11... | collective-permute-start | bytes 983048 | tf_op jit(solution)/shard_map/ppermute | solution.py:31
  18.2 1.4 %copy-start.8 = (bf16[4096,256]{1,0:T(8,128)(2,1)}, bf16[4096,256]{1,0:T(8,128)(2,1)S(1)}, u32[]{:S(2)}) copy-start(bf16[4096,256]{1,0:T(8,128)(2,1)S(1)} %collective-permute-done.3.q_other) | copy-start | bytes 6291460
  18.2 12.5 %collective-permute-start.6 = (bf16[256,4096]{1,0:T(8,128)(2,1)}, bf16[256,4096]{1,0:T(8,128)(2,1)}, u32[]{:S(2)}, u32[]{:S(2)}) collective-permute-start(bf16[256,4096]{1,0:T(8,128)(2,1)} %out_own.3), channel_id=1, source_target_pairs={{0,8},{8,0},{1,9},{9,1},{2,10},{10,2},{3,11},{11,3},{4,12},{12,4},... | collective-permute-start | bytes 6291464 | tf_op jit(solution)/shard_map/ppermute | solution.py:26
  18.2 12.5 %collective-permute-start.7 = (bf16[4,256,256]{2,1,0:T(8,128)(2,1)S(1)}, bf16[4,256,256]{2,1,0:T(8,128)(2,1)}, u32[]{:S(2)}, u32[]{:S(2)}) collective-permute-start(bf16[4,256,256]{2,1,0:T(8,128)(2,1)S(1)} %copy-done.2), channel_id=1, source_target_pairs={{0,8},{8,0},{1,9},{9,1},{2,10},{10,2},{3,11},{11,3},{4,12},{12,4},... | collective-permute-start | bytes 1572872 | tf_op jit(solution)/shard_map/ppermute | solution.py:26
  19.6 9.8 %collective-permute-start.4 = (bf16[128,1280]{1,0:T(8,128)(2,1)S(1)}, bf16[128,1280]{1,0:T(8,128)(2,1)S(1)}, u32[]{:S(2)}, u32[]{:S(2)}) collective-permute-start(bf16[128,1280]{1,0:T(8,128)(2,1)S(1)} %collective-permute-done.1.refs_2_), channel_id=1, source_target_pairs={{0,2},{1,3},{2,6},{3,7},{4,0},{5,1},{6,4},{7,5},{8,10},{9,11},{10,... | collective-permute-start | bytes 983048 | tf_op jit(solution)/shard_map/ppermute | solution.py:47
  22.1 8.6 %collective-permute-start.5 = (bf16[128,1280]{1,0:T(8,128)(2,1)S(1)}, bf16[128,1280]{1,0:T(8,128)(2,1)S(1)}, u32[]{:S(2)}, u32[]{:S(2)}) collective-permute-start(bf16[128,1280]{1,0:T(8,128)(2,1)S(1)} %collective-permute-done.1.refs_2_), channel_id=1, source_target_pairs={{0,1},{1,0},{2,3},{3,2},{4,5},{5,4},{6,7},{7,6},{8,9},{9,8},{10,11... | collective-permute-start | bytes 983048 | tf_op jit(solution)/shard_map/ppermute | solution.py:31
  30.7 7.7 %collective-permute-start.9 = (bf16[128,1280]{1,0:T(8,128)(2,1)S(1)}, bf16[128,1280]{1,0:T(8,128)(2,1)S(1)}, u32[]{:S(2)}, u32[]{:S(2)}) collective-permute-start(bf16[128,1280]{1,0:T(8,128)(2,1)S(1)} %collective-permute-done.4.refs_4_), channel_id=1, source_target_pairs={{0,1},{1,0},{2,3},{3,2},{4,5},{5,4},{6,7},{7,6},{8,9},{9,8},{10,11... | collective-permute-start | bytes 983048 | tf_op jit(solution)/shard_map/ppermute | solution.py:31
  32.2 8.4 %collective-permute-start.10 = (bf16[128,1280]{1,0:T(8,128)(2,1)S(1)}, bf16[128,1280]{1,0:T(8,128)(2,1)}, u32[]{:S(2)}, u32[]{:S(2)}) collective-permute-start(bf16[128,1280]{1,0:T(8,128)(2,1)S(1)} %collective-permute-done.4.refs_4_), channel_id=1, source_target_pairs={{0,2},{1,3},{2,6},{3,7},{4,0},{5,1},{6,4},{7,5},{8,10},{9,11},{10,... | collective-permute-start | bytes 983048 | tf_op jit(solution)/shard_map/ppermute | solution.py:47
  33.7 1.1 collective-permute-start.8
  34.0 1.4 %collective-permute-start.11 = (s32[1,128]{1,0:T(1,128)S(1)}, s32[1,128]{1,0:T(1,128)S(1)}, u32[]{:S(2)}, u32[]{:S(2)}) collective-permute-start(s32[1,128]{1,0:T(1,128)S(1)} %slice_bitcast_fusion), channel_id=1, source_target_pairs={{0,8},{8,0},{1,9},{9,1},{2,10},{10,2},{3,11},{11,3},{4,12},{12,4},... | collective-permute-start | bytes 1544 | tf_op jit(solution)/shard_map/ppermute | solution.py:26
  38.4 0.7 copy-start.9
  40.6 7.3 %collective-permute-start.12 = (bf16[128,1280]{1,0:T(8,128)(2,1)}, bf16[128,1280]{1,0:T(8,128)(2,1)S(1)}, u32[]{:S(2)}, u32[]{:S(2)}) collective-permute-start(bf16[128,1280]{1,0:T(8,128)(2,1)} %collective-permute-done.10.refs_6_), channel_id=1, source_target_pairs={{0,1},{1,0},{2,3},{3,2},{4,5},{5,4},{6,7},{7,6},{8,9},{9,8},{10,11... | collective-permute-start | bytes 983048 | tf_op jit(solution)/shard_map/ppermute | solution.py:31
  41.1 6.8 %copy-start.4 = (s32[8]{0:T(128)S(1)}, s32[8]{0:T(128)}, u32[]{:S(2)}) copy-start(s32[8]{0:T(128)} %lens_ref.3) | copy-start | bytes 100
  51.6 9.3 %collective-permute-start.16 = (bf16[128,1024]{1,0:T(8,128)(2,1)S(1)}, bf16[128,1024]{1,0:T(8,128)(2,1)S(1)}, u32[]{:S(2)}, u32[]{:S(2)}) collective-permute-start(bf16[128,1024]{1,0:T(8,128)(2,1)S(1)} %get-tuple-element.54), channel_id=1, source_target_pairs={{0,1},{1,0},{2,3},{3,2},{4,5},{5,4},{6,7},{7,6},{8,9},{9,8},{10,11... | collective-permute-start | bytes 786440 | tf_op jit(solution)/shard_map/ppermute | solution.py:31
  54.9 28.8 %dynamic-slice-start = ((f32[8192]{0:T(1024)}, s32[]{:T(128)}), f32[1024]{0:T(1024)S(1)}, s32[]{:S(2)}) async-start(f32[8192]{0:T(1024)} %param.17, s32[]{:T(128)} %select_n.142), calls=%async_computation | async-start | bytes 8704 | tf_op jit(solution)/shard_map/dynamic_slice | solution.py:580
  54.9 11.4 %collective-permute-start.15 = (bf16[128,1024]{1,0:T(8,128)(2,1)S(1)}, bf16[128,1024]{1,0:T(8,128)(2,1)S(1)}, u32[]{:S(2)}, u32[]{:S(2)}) collective-permute-start(bf16[128,1024]{1,0:T(8,128)(2,1)S(1)} %get-tuple-element.52), channel_id=1, source_target_pairs={{0,1},{1,0},{2,3},{3,2},{4,5},{5,4},{6,7},{7,6},{8,9},{9,8},{10,11... | collective-permute-start | bytes 786440 | tf_op jit(solution)/shard_map/ppermute | solution.py:31
  60.9 30.3 %copy-start.5 = (bf16[4096,512]{1,0:T(8,128)(2,1)S(1)}, bf16[4096,512]{1,0:T(8,128)(2,1)}, u32[]{:S(2)}) copy-start(bf16[4096,512]{1,0:T(8,128)(2,1)} %own_ref.3) | copy-start | bytes 12582916
  60.9 7.3 %collective-permute-start.17 = (bf16[128,1024]{1,0:T(8,128)(2,1)S(1)}, bf16[128,1024]{1,0:T(8,128)(2,1)S(1)}, u32[]{:S(2)}, u32[]{:S(2)}) collective-permute-start(bf16[128,1024]{1,0:T(8,128)(2,1)S(1)} %add_convert_fusion.2), channel_id=1, source_target_pairs={{0,2},{1,3},{2,6},{3,7},{4,0},{5,1},{6,4},{7,5},{8,10},{9,11},{10,... | collective-permute-start | bytes 786440 | tf_op jit(solution)/shard_map/ppermute | solution.py:47
  61.9 8.0 %collective-permute-start.14 = (bf16[128,1024]{1,0:T(8,128)(2,1)S(1)}, bf16[128,1024]{1,0:T(8,128)(2,1)S(1)}, u32[]{:S(2)}, u32[]{:S(2)}) collective-permute-start(bf16[128,1024]{1,0:T(8,128)(2,1)S(1)} %get-tuple-element.50), channel_id=1, source_target_pairs={{0,1},{1,0},{2,3},{3,2},{4,5},{5,4},{6,7},{7,6},{8,9},{9,8},{10,11... | collective-permute-start | bytes 786440 | tf_op jit(solution)/shard_map/ppermute | solution.py:31
  68.4 42.5 %copy-start.12 = (f32[8192]{0:T(1024)S(1)}, f32[8192]{0:T(1024)}, u32[]{:S(2)}) copy-start(f32[8192]{0:T(1024)} %param.17) | copy-start | bytes 98308
  68.4 7.8 %collective-permute-start.18 = (bf16[128,1024]{1,0:T(8,128)(2,1)S(1)}, bf16[128,1024]{1,0:T(8,128)(2,1)S(1)}, u32[]{:S(2)}, u32[]{:S(2)}) collective-permute-start(bf16[128,1024]{1,0:T(8,128)(2,1)S(1)} %add_convert_fusion.1), channel_id=1, source_target_pairs={{0,2},{1,3},{2,6},{3,7},{4,0},{5,1},{6,4},{7,5},{8,10},{9,11},{10,... | collective-permute-start | bytes 786440 | tf_op jit(solution)/shard_map/ppermute | solution.py:47
  68.8 7.6 %collective-permute-start.13 = (bf16[128,1024]{1,0:T(8,128)(2,1)S(1)}, bf16[128,1024]{1,0:T(8,128)(2,1)S(1)}, u32[]{:S(2)}, u32[]{:S(2)}) collective-permute-start(bf16[128,1024]{1,0:T(8,128)(2,1)S(1)} %get-tuple-element.48), channel_id=1, source_target_pairs={{0,1},{1,0},{2,3},{3,2},{4,5},{5,4},{6,7},{7,6},{8,9},{9,8},{10,11... | collective-permute-start | bytes 786440 | tf_op jit(solution)/shard_map/ppermute | solution.py:31
  76.3 7.3 %collective-permute-start.19 = (bf16[128,1024]{1,0:T(8,128)(2,1)S(1)}, bf16[128,1024]{1,0:T(8,128)(2,1)S(1)}, u32[]{:S(2)}, u32[]{:S(2)}) collective-permute-start(bf16[128,1024]{1,0:T(8,128)(2,1)S(1)} %add_convert_fusion), channel_id=1, source_target_pairs={{0,2},{1,3},{2,6},{3,7},{4,0},{5,1},{6,4},{7,5},{8,10},{9,11},{10,... | collective-permute-start | bytes 786440 | tf_op jit(solution)/shard_map/ppermute | solution.py:47
  83.9 7.3 %collective-permute-start.20 = (bf16[128,1024]{1,0:T(8,128)(2,1)S(1)}, bf16[128,1024]{1,0:T(8,128)(2,1)S(1)}, u32[]{:S(2)}, u32[]{:S(2)}) collective-permute-start(bf16[128,1024]{1,0:T(8,128)(2,1)S(1)} %get-tuple-element.64.refs_0_), channel_id=1, source_target_pairs={{0,2},{1,3},{2,6},{3,7},{4,0},{5,1},{6,4},{7,5},{8,10},{9,11},{10,... | collective-permute-start | bytes 786440 | tf_op jit(solution)/shard_map/ppermute | solution.py:47
  83.9 7.3 %collective-permute-start.21 = (bf16[128,1024]{1,0:T(8,128)(2,1)S(1)}, bf16[128,1024]{1,0:T(8,128)(2,1)S(1)}, u32[]{:S(2)}, u32[]{:S(2)}) collective-permute-start(bf16[128,1024]{1,0:T(8,128)(2,1)S(1)} %get-tuple-element.64.refs_0_), channel_id=1, source_target_pairs={{0,1},{1,0},{2,3},{3,2},{4,5},{5,4},{6,7},{7,6},{8,9},{9,8},{10,11... | collective-permute-start | bytes 786440 | tf_op jit(solution)/shard_map/ppermute | solution.py:31
  91.2 9.7 %collective-permute-start.23 = (bf16[4096,512]{1,0:T(8,128)(2,1)S(1)}, bf16[4096,512]{1,0:T(8,128)(2,1)S(1)}, u32[]{:S(2)}, u32[]{:S(2)}) collective-permute-start(bf16[4096,512]{1,0:T(8,128)(2,1)S(1)} %copy-done.5), channel_id=1, source_target_pairs={{0,8},{8,0},{1,9},{9,1},{2,10},{10,2},{3,11},{11,3},{4,12},{12,4},... | collective-permute-start | bytes 12582920 | tf_op jit(solution)/shard_map/ppermute | solution.py:26
  91.2 7.5 %collective-permute-start.22 = (bf16[128,1024]{1,0:T(8,128)(2,1)S(1)}, bf16[128,1024]{1,0:T(8,128)(2,1)S(1)}, u32[]{:S(2)}, u32[]{:S(2)}) collective-permute-start(bf16[128,1024]{1,0:T(8,128)(2,1)S(1)} %get-tuple-element.56), channel_id=1, source_target_pairs={{0,8},{8,0},{1,9},{9,1},{2,10},{10,2},{3,11},{11,3},{4,12},{12,4},... | collective-permute-start | bytes 786440 | tf_op jit(solution)/shard_map/ppermute | solution.py:26
  91.7 8.3 %collective-permute-start.24 = (bf16[128,1024]{1,0:T(8,128)(2,1)S(1)}, bf16[128,1024]{1,0:T(8,128)(2,1)S(1)}, u32[]{:S(2)}, u32[]{:S(2)}) collective-permute-start(bf16[128,1024]{1,0:T(8,128)(2,1)S(1)} %collective-permute-done.20.refs_2_), channel_id=1, source_target_pairs={{0,1},{1,0},{2,3},{3,2},{4,5},{5,4},{6,7},{7,6},{8,9},{9,8},{10,11... | collective-permute-start | bytes 786440 | tf_op jit(solution)/shard_map/ppermute | solution.py:31
  91.9 9.0 %collective-permute-start.25 = (bf16[128,1024]{1,0:T(8,128)(2,1)S(1)}, bf16[128,1024]{1,0:T(8,128)(2,1)S(1)}, u32[]{:S(2)}, u32[]{:S(2)}) collective-permute-start(bf16[128,1024]{1,0:T(8,128)(2,1)S(1)} %collective-permute-done.20.refs_2_), channel_id=1, source_target_pairs={{0,2},{1,3},{2,6},{3,7},{4,0},{5,1},{6,4},{7,5},{8,10},{9,11},{10,... | collective-permute-start | bytes 786440 | tf_op jit(solution)/shard_map/ppermute | solution.py:47
  100.9 9.5 %copy-start.6 = (bf16[4096,512]{1,0:T(8,128)(2,1)}, bf16[4096,512]{1,0:T(8,128)(2,1)S(1)}, u32[]{:S(2)}) copy-start(bf16[4096,512]{1,0:T(8,128)(2,1)S(1)} %collective-permute-done.23.other_ref) | copy-start | bytes 12582916
  100.9 7.4 %collective-permute-start.26 = (bf16[128,1024]{1,0:T(8,128)(2,1)S(1)}, bf16[128,1024]{1,0:T(8,128)(2,1)S(1)}, u32[]{:S(2)}, u32[]{:S(2)}) collective-permute-start(bf16[128,1024]{1,0:T(8,128)(2,1)S(1)} %collective-permute-done.25.refs_4_), channel_id=1, source_target_pairs={{0,1},{1,0},{2,3},{3,2},{4,5},{5,4},{6,7},{7,6},{8,9},{9,8},{10,11... | collective-permute-start | bytes 786440 | tf_op jit(solution)/shard_map/ppermute | solution.py:31
  102.6 7.7 %collective-permute-start.27 = (bf16[128,1024]{1,0:T(8,128)(2,1)S(1)}, bf16[128,1024]{1,0:T(8,128)(2,1)S(1)}, u32[]{:S(2)}, u32[]{:S(2)}) collective-permute-start(bf16[128,1024]{1,0:T(8,128)(2,1)S(1)} %collective-permute-done.25.refs_4_), channel_id=1, source_target_pairs={{0,2},{1,3},{2,6},{3,7},{4,0},{5,1},{6,4},{7,5},{8,10},{9,11},{10,... | collective-permute-start | bytes 786440 | tf_op jit(solution)/shard_map/ppermute | solution.py:47
  110.4 0.7 copy-start.10
  110.4 6.4 %collective-permute-start.28 = (bf16[128,1024]{1,0:T(8,128)(2,1)S(1)}, bf16[128,1024]{1,0:T(8,128)(2,1)S(1)}, u32[]{:S(2)}, u32[]{:S(2)}) collective-permute-start(bf16[128,1024]{1,0:T(8,128)(2,1)S(1)} %collective-permute-done.27.refs_6_), channel_id=1, source_target_pairs={{0,1},{1,0},{2,3},{3,2},{4,5},{5,4},{6,7},{7,6},{8,9},{9,8},{10,11... | collective-permute-start | bytes 786440 | tf_op jit(solution)/shard_map/ppermute | solution.py:31
  118.7 3.7 %collective-permute-start.29 = (f32[3,128]{1,0:T(4,128)S(1)}, f32[3,128]{1,0:T(4,128)S(1)}, u32[]{:S(2)}, u32[]{:S(2)}) collective-permute-start(f32[3,128]{1,0:T(4,128)S(1)} %slice.71), channel_id=1, source_target_pairs={{0,1},{1,0},{2,3},{3,2},{4,5},{5,4},{6,7},{7,6},{8,9},{9,8},{10,11... | collective-permute-start | bytes 4616 | tf_op jit(solution)/shard_map/ppermute | solution.py:31
  122.3 4.1 %collective-permute-start.30 = (f32[3,128]{1,0:T(4,128)S(1)}, f32[3,128]{1,0:T(4,128)S(1)}, u32[]{:S(2)}, u32[]{:S(2)}) collective-permute-start(f32[3,128]{1,0:T(4,128)S(1)} %pad_maximum_fusion.1), channel_id=1, source_target_pairs={{0,6},{1,7},{2,0},{3,1},{4,2},{5,3},{6,4},{7,5},{8,14},{9,15},{10,... | collective-permute-start | bytes 4616 | tf_op jit(solution)/shard_map/ppermute | solution.py:620
  125.1 4.5 %collective-permute-start.31 = (f32[3,128]{1,0:T(4,128)S(1)}, f32[3,128]{1,0:T(4,128)S(1)}, u32[]{:S(2)}, u32[]{:S(2)}) collective-permute-start(f32[3,128]{1,0:T(4,128)S(1)} %pad_maximum_fusion.1), channel_id=1, source_target_pairs={{0,4},{1,5},{2,6},{3,7},{4,0},{5,1},{6,2},{7,3},{8,12},{9,13},{10,... | collective-permute-start | bytes 4616 | tf_op jit(solution)/shard_map/ppermute | solution.py:620
  125.1 5.4 %collective-permute-start.32 = (f32[3,128]{1,0:T(4,128)S(1)}, f32[3,128]{1,0:T(4,128)S(1)}, u32[]{:S(2)}, u32[]{:S(2)}) collective-permute-start(f32[3,128]{1,0:T(4,128)S(1)} %pad_maximum_fusion.1), channel_id=1, source_target_pairs={{0,2},{1,3},{2,4},{3,5},{4,6},{5,7},{6,0},{7,1},{8,10},{9,11},{10,... | collective-permute-start | bytes 4616 | tf_op jit(solution)/shard_map/ppermute | solution.py:620
  130.6 1.2 collective-permute-start.33

commit v7 on v6

--- a/solution.py
+++ b/solution.py
@@ -11,7 +11,7 @@
 QH_DEV = 2
 GROUP = 16
 SIDE = 2
-SWAP_STEP = {"q": 0, "out": 1, "cache": 1, "ctx": 2, "targets": 2, "layer": 5, "vocab": 5}
+SWAP_STEP = {"q": 0, "out": 0, "cache": 1, "ctx": 2, "targets": 2, "layer": 5, "vocab": 5}
 
 
 EPS = 1e-05
@@ -613,20 +613,29 @@
         ]
 
     side = tensor_pos % SIDE
-    stats = join(in_order(stats, [swap_side(stats)], lambda c: side ^ c))
+    corner = [
+        ((1 - d) * tensor_count + (i ^ 1), d * tensor_count + i)
+        for d in range(2)
+        for i in range(tensor_count)
+    ]
+    near, far = swap_dp(stats), lax.ppermute(stats, ("dp", "tensor"), corner)
+    stats = [
+        join(in_order(part, [other], lambda c: side ^ c))
+        for part, other in ((stats, swap_side(stats)), (near, far))
+    ]
+    stats = jnp.stack(stats, axis=1)
     ring_count = tensor_count // SIDE
     ring_pos = tensor_pos // SIDE
     others = [
         lax.ppermute(
-            stats, "tensor", [(i, (i + SIDE * c) % tensor_count) for i in range(tensor_count)]
+            stats, "tensor", [(i, i ^ (SIDE * c)) for i in range(tensor_count)]
         )
         for c in range(1, ring_count)
     ]
     stats = join(
-        in_order(stats, others, lambda c: (ring_pos - c + ring_count) % ring_count)
-    )
-    logprob = (stats[2] - stats[0] - jnp.log(stats[1]))[None, :]
-    both_logprob = jnp.concatenate([logprob, swap_dp(logprob)], axis=1)
+        in_order(stats, others, lambda c: ring_pos ^ c)
+    )
+    both_logprob = stats[2] - stats[0] - jnp.log(stats[1])
     token_logprob = jnp.sum(jnp.where(pick > 0, both_logprob.reshape(-1, 1), 0.0), axis=0)
     return (layer_out, token_logprob)
 

time: 133 us -> 130 us (0.977)
  waiting for transfers between devices: 74.8 us -> 73 us
    ppermute x9, starting transfers between devices: 12.8 us -> 9.95 us  [ring_step(): return lax.ppermute(value, 'tensor', pairs)]
    ppermute x3 -> x4, waiting for transfers between devices: 4.74 us -> 2.06 us  [the longest x3 2.06 us: per_device(): lax.ppermute(stats, 'tensor', [(i, i ^ SIDE * c) for i in range(tensor_co...]
    ppermute x3 -> x4, starting transfers between devices: 3.42 us -> 4.46 us  [the longest x3 4.45 us: per_device(): lax.ppermute(stats, 'tensor', [(i, i ^ SIDE * c) for i in range(tensor_co...]
    unnamed x30 -> x32, local copies, waits for them, and re-layouts: 3.46 us -> 3.9 us
  transfers between devices with their start and end apart: 34 -> 35, of which waited for: 28 -> 26; matrix products, arithmetic and copies ran while one was open for 2% -> 2% of each run, Pallas kernels for 8% -> 9%
where the time goes in v7:
time: 130 us
  waiting for transfers between devices  73 us (56%)
  starting transfers between devices  30.5 us (23%)
  Pallas kernels  17.5 us (13%)
  local copies, waits for them, and re-layouts  4.97 us (4%)
  other arithmetic  1.58 us (1%)
  matrix products  1.35 us (1%)
    ppermute x9, waiting for transfers between devices, ring_step(): return lax.ppermute(value, 'tensor', pairs)  40 us
    ppermute x13, waiting for transfers between devices, swap_side(): return lax.ppermute(value, 'tensor', [(i, i ^ 1) for i in range(count)])  25.1 us
    ppermute x13, starting transfers between devices, swap_side(): return lax.ppermute(value, 'tensor', [(i, i ^ 1) for i in range(count)])  12.3 us
    ppermute x9, starting transfers between devices, ring_step(): return lax.ppermute(value, 'tensor', pairs)  9.95 us
    ppermute x9, waiting for transfers between devices, swap_dp(): return lax.ppermute(value, 'dp', [(0, 1), (1, 0)])  5.88 us
    pallas_call x1, Pallas kernels, logit_part(): pl.pallas_call(logit_kernel, out_shape=[jax.ShapeDtypeStruct((half, vocab...  4.54 us
    ppermute x3, starting transfers between devices, per_device(): lax.ppermute(stats, 'tensor', [(i, i ^ SIDE * c) for i in range(tensor_co...  4.45 us
    unnamed x32, local copies, waits for them, and re-layouts  3.9 us
  transfers between devices with their start and end apart: 35, of which 26 were waited for; matrix products, arithmetic and copies ran while one was open for 2% of the time, Pallas kernels for 9%

profile of v7, /device:TPU:0, one launch (start us, length us, event | category | flops | bytes accessed | tf_op | source)
XLA Modules:
  0.0 129.9 jit_solution(7242206676076109110)
XLA Ops:
  0.7 1.1 copy-done.1
  1.7 0.7 copy-done.3
  2.4 0.9 pack_rows.1
  3.3 0.5 collective-permute-start
  3.8 0.8 dynamic_slice.9
  5.4 0.4 collective-permute-start.3
  5.9 2.9 %collective-permute-start.1 = (bf16[128,1280]{1,0:T(8,128)(2,1)S(1)}, bf16[128,1280]{1,0:T(8,128)(2,1)S(1)}, u32[]{:S(2)}, u32[]{:S(2)}) collective-permute-start(bf16[128,1280]{1,0:T(8,128)(2,1)S(1)} %pad_maximum_fusion.refs_0_), channel_id=1, source_target_pairs={{0,2},{1,3},{2,6},{3,7},{4,0},{5,1},{6,4},{7,5},{8,10},{9,11},{10,... | collective-permute-start | bytes 983048 | tf_op jit(solution)/shard_map/ppermute | solution.py:47
  8.9 1.5 %collective-permute-start.2 = (bf16[128,1280]{1,0:T(8,128)(2,1)S(1)}, bf16[128,1280]{1,0:T(8,128)(2,1)S(1)}, u32[]{:S(2)}, u32[]{:S(2)}) collective-permute-start(bf16[128,1280]{1,0:T(8,128)(2,1)S(1)} %pad_maximum_fusion.refs_0_), channel_id=1, source_target_pairs={{0,1},{1,0},{2,3},{3,2},{4,5},{5,4},{6,7},{7,6},{8,9},{9,8},{10,11... | collective-permute-start | bytes 983048 | tf_op jit(solution)/shard_map/ppermute | solution.py:31
  10.4 7.5 %collective-permute-done.1.refs_2_ = bf16[128,1280]{1,0:T(8,128)(2,1)S(1)} collective-permute-done((bf16[128,1280]{1,0:T(8,128)(2,1)S(1)}, bf16[128,1280]{1,0:T(8,128)(2,1)S(1)}, u32[]{:S(2)}, u32[]{:S(2)}) %collective-permute-start.1) | collective-permute-done | bytes 327712 | tf_op jit(solution)/shard_map/ppermute | solution.py:47
  17.9 0.5 collective-permute-done.2.refs_1_
  18.5 1.3 copy-done.8
  19.7 2.6 %collective-permute-start.5 = (bf16[128,1280]{1,0:T(8,128)(2,1)S(1)}, bf16[128,1280]{1,0:T(8,128)(2,1)S(1)}, u32[]{:S(2)}, u32[]{:S(2)}) collective-permute-start(bf16[128,1280]{1,0:T(8,128)(2,1)S(1)} %collective-permute-done.1.refs_2_), channel_id=1, source_target_pairs={{0,2},{1,3},{2,6},{3,7},{4,0},{5,1},{6,4},{7,5},{8,10},{9,11},{10,... | collective-permute-start | bytes 983048 | tf_op jit(solution)/shard_map/ppermute | solution.py:47
  22.3 1.5 %collective-permute-start.6 = (bf16[128,1280]{1,0:T(8,128)(2,1)S(1)}, bf16[128,1280]{1,0:T(8,128)(2,1)S(1)}, u32[]{:S(2)}, u32[]{:S(2)}) collective-permute-start(bf16[128,1280]{1,0:T(8,128)(2,1)S(1)} %collective-permute-done.1.refs_2_), channel_id=1, source_target_pairs={{0,1},{1,0},{2,3},{3,2},{4,5},{5,4},{6,7},{7,6},{8,9},{9,8},{10,11... | collective-permute-start | bytes 983048 | tf_op jit(solution)/shard_map/ppermute | solution.py:31
  23.8 5.6 %collective-permute-done.5.refs_4_ = bf16[128,1280]{1,0:T(8,128)(2,1)S(1)} collective-permute-done((bf16[128,1280]{1,0:T(8,128)(2,1)S(1)}, bf16[128,1280]{1,0:T(8,128)(2,1)S(1)}, u32[]{:S(2)}, u32[]{:S(2)}) %collective-permute-start.5) | collective-permute-done | bytes 327712 | tf_op jit(solution)/shard_map/ppermute | solution.py:47
  29.5 1.4 %collective-permute-done.6.refs_3_ = bf16[128,1280]{1,0:T(8,128)(2,1)S(1)} collective-permute-done((bf16[128,1280]{1,0:T(8,128)(2,1)S(1)}, bf16[128,1280]{1,0:T(8,128)(2,1)S(1)}, u32[]{:S(2)}, u32[]{:S(2)}) %collective-permute-start.6) | collective-permute-done | bytes 327712 | tf_op jit(solution)/shard_map/ppermute | solution.py:31
  30.9 1.5 %collective-permute-start.9 = (bf16[128,1280]{1,0:T(8,128)(2,1)S(1)}, bf16[128,1280]{1,0:T(8,128)(2,1)S(1)}, u32[]{:S(2)}, u32[]{:S(2)}) collective-permute-start(bf16[128,1280]{1,0:T(8,128)(2,1)S(1)} %collective-permute-done.5.refs_4_), channel_id=1, source_target_pairs={{0,1},{1,0},{2,3},{3,2},{4,5},{5,4},{6,7},{7,6},{8,9},{9,8},{10,11... | collective-permute-start | bytes 983048 | tf_op jit(solution)/shard_map/ppermute | solution.py:31
  32.4 1.3 collective-permute-start.10
  33.9 0.6 collective-permute-start.11
  34.5 0.3 collective-permute-done.8
  34.9 0.4 collective-permute-done.11
  35.3 3.2 %collective-permute-done.9.refs_5_ = bf16[128,1280]{1,0:T(8,128)(2,1)S(1)} collective-permute-done((bf16[128,1280]{1,0:T(8,128)(2,1)S(1)}, bf16[128,1280]{1,0:T(8,128)(2,1)S(1)}, u32[]{:S(2)}, u32[]{:S(2)}) %collective-permute-start.9) | collective-permute-done | bytes 327712 | tf_op jit(solution)/shard_map/ppermute | solution.py:31
  38.5 0.7 copy-done.10
  39.3 1.5 %collective-permute-done.10.refs_6_ = bf16[128,1280]{1,0:T(8,128)(2,1)} collective-permute-done((bf16[128,1280]{1,0:T(8,128)(2,1)S(1)}, bf16[128,1280]{1,0:T(8,128)(2,1)}, u32[]{:S(2)}, u32[]{:S(2)}) %collective-permute-start.10) | collective-permute-done | bytes 327712 | tf_op jit(solution)/shard_map/ppermute | solution.py:47
  40.8 0.5 collective-permute-start.12
  41.3 3.8 %query_part.1 = (f32[128,256]{1,0:T(8,128)S(1)}, f32[128,256]{1,0:T(8,128)S(1)}, f32[128,128]{1,0:T(8,128)S(1)}) custom-call(f32[8,1024]{1,0:T(8,128)S(1)} %reshape.104.gain_ref, bf16[4096,256]{1,0:T(8,128)(2,1)} %q_own.3, bf16[4096,256]{1,0:T(8,128)(2,1)} %copy-done.8, bf16[128,1280]{1,0:T(8,128)(2,1)S(1)} %pad_maximum_fusion.refs_0_, ...), custom_call_target="tpu_custom_call" | custom-call | flops 469762048 | bytes 5505024 | tf_op jit(solution)/shard_map/query_part/pallas_call | solution.py:201
  45.2 2.9 %collective-permute-done.12.block_ref = bf16[128,1280]{1,0:T(8,128)(2,1)S(1)} collective-permute-done((bf16[128,1280]{1,0:T(8,128)(2,1)}, bf16[128,1280]{1,0:T(8,128)(2,1)S(1)}, u32[]{:S(2)}, u32[]{:S(2)}) %collective-permute-start.12) | collective-permute-done | bytes 327712 | tf_op jit(solution)/shard_map/ppermute | solution.py:31
  48.1 3.6 %attend.1 = (bf16[128,256]{1,0:T(8,128)(2,1)S(1)}, bf16[128,1024]{1,0:T(8,128)(2,1)S(1)}) custom-call(s32[8]{0:T(128)S(1)} %copy-done.4, s32[8]{0:T(128)S(1)} %pad_add_fusion.ctx_ref, f32[8,1024]{1,0:T(8,128)S(1)} %reshape.104.gain_ref, f32[128,256]{1,0:T(8,128)S(1)} %get-tuple-element.43.query_ref, f32[128,256]{1,0:T(8,128)S(1)} %get-tuple-element.44.kv_ref, ...), custom_call_target="tpu_custom_call" | custom-call | tf_op jit(solution)/shard_map/attend/pallas_call | solution.py:347
  51.7 0.6 collective-permute-start.16
  52.3 2.8 %out_products.1 = (bf16[128,1024]{1,0:T(8,128)(2,1)S(1)}, bf16[128,1024]{1,0:T(8,128)(2,1)S(1)}, bf16[128,1024]{1,0:T(8,128)(2,1)S(1)}, bf16[128,1024]{1,0:T(8,1...) custom-call(bf16[128,256]{1,0:T(8,128)(2,1)S(1)} %get-tuple-element.46.att, ...), custom_call_target="tpu_custom_call" | custom-call | flops 469762048 | bytes 5505024 | tf_op jit(solution)/shard_map/out_products/pallas_call | solution.py:385
  55.1 1.6 %collective-permute-start.15 = (bf16[128,1024]{1,0:T(8,128)(2,1)S(1)}, bf16[128,1024]{1,0:T(8,128)(2,1)S(1)}, u32[]{:S(2)}, u32[]{:S(2)}) collective-permute-start(bf16[128,1024]{1,0:T(8,128)(2,1)S(1)} %get-tuple-element.52), channel_id=1, source_target_pairs={{0,1},{1,0},{2,3},{3,2},{4,5},{5,4},{6,7},{7,6},{8,9},{9,8},{10,11... | collective-permute-start | bytes 786440 | tf_op jit(solution)/shard_map/ppermute | solution.py:31
  56.7 4.4 %collective-permute-done.16 = bf16[128,1024]{1,0:T(8,128)(2,1)S(1)} collective-permute-done((bf16[128,1024]{1,0:T(8,128)(2,1)S(1)}, bf16[128,1024]{1,0:T(8,128)(2,1)S(1)}, u32[]{:S(2)}, u32[]{:S(2)}) %collective-permute-start.16) | collective-permute-done | bytes 262176 | tf_op jit(solution)/shard_map/ppermute | solution.py:31
  61.1 0.5 collective-permute-start.17
  61.6 0.9 collective-permute-start.14
  62.6 4.1 %collective-permute-done.15 = bf16[128,1024]{1,0:T(8,128)(2,1)S(1)} collective-permute-done((bf16[128,1024]{1,0:T(8,128)(2,1)S(1)}, bf16[128,1024]{1,0:T(8,128)(2,1)S(1)}, u32[]{:S(2)}, u32[]{:S(2)}) %collective-permute-start.15) | collective-permute-done | bytes 262176 | tf_op jit(solution)/shard_map/ppermute | solution.py:31
  66.7 1.8 %collective-permute-done.17 = bf16[128,1024]{1,0:T(8,128)(2,1)S(1)} collective-permute-done((bf16[128,1024]{1,0:T(8,128)(2,1)S(1)}, bf16[128,1024]{1,0:T(8,128)(2,1)S(1)}, u32[]{:S(2)}, u32[]{:S(2)}) %collective-permute-start.17) | collective-permute-done | bytes 262176 | tf_op jit(solution)/shard_map/ppermute | solution.py:47
  68.6 0.5 collective-permute-start.13
  69.2 0.9 collective-permute-done.14
  70.0 6.4 %collective-permute-done.18 = bf16[128,1024]{1,0:T(8,128)(2,1)S(1)} collective-permute-done((bf16[128,1024]{1,0:T(8,128)(2,1)S(1)}, bf16[128,1024]{1,0:T(8,128)(2,1)S(1)}, u32[]{:S(2)}, u32[]{:S(2)}) %collective-permute-start.18) | collective-permute-done | bytes 262176 | tf_op jit(solution)/shard_map/ppermute | solution.py:47
  76.6 7.2 %collective-permute-done.19 = bf16[128,1024]{1,0:T(8,128)(2,1)S(1)} collective-permute-done((bf16[128,1024]{1,0:T(8,128)(2,1)S(1)}, bf16[128,1024]{1,0:T(8,128)(2,1)S(1)}, u32[]{:S(2)}, u32[]{:S(2)}) %collective-permute-start.19) | collective-permute-done | bytes 262176 | tf_op jit(solution)/shard_map/ppermute | solution.py:47
  84.1 0.5 collective-permute-start.21
  84.6 6.8 %collective-permute-done.20.refs_2_ = bf16[128,1024]{1,0:T(8,128)(2,1)S(1)} collective-permute-done((bf16[128,1024]{1,0:T(8,128)(2,1)S(1)}, bf16[128,1024]{1,0:T(8,128)(2,1)S(1)}, u32[]{:S(2)}, u32[]{:S(2)}) %collective-permute-start.20) | collective-permute-done | bytes 262176 | tf_op jit(solution)/shard_map/ppermute | solution.py:47
  91.4 0.5 collective-permute-start.22
  91.9 0.4 collective-permute-start.24
  92.3 1.8 %collective-permute-start.25 = (bf16[128,1024]{1,0:T(8,128)(2,1)S(1)}, bf16[128,1024]{1,0:T(8,128)(2,1)S(1)}, u32[]{:S(2)}, u32[]{:S(2)}) collective-permute-start(bf16[128,1024]{1,0:T(8,128)(2,1)S(1)} %collective-permute-done.20.refs_2_), channel_id=1, source_target_pairs={{0,2},{1,3},{2,6},{3,7},{4,0},{5,1},{6,4},{7,5},{8,10},{9,11},{10,... | collective-permute-start | bytes 786440 | tf_op jit(solution)/shard_map/ppermute | solution.py:47
  94.1 4.8 %collective-permute-done.22 = bf16[128,1024]{1,0:T(8,128)(2,1)S(1)} collective-permute-done((bf16[128,1024]{1,0:T(8,128)(2,1)S(1)}, bf16[128,1024]{1,0:T(8,128)(2,1)S(1)}, u32[]{:S(2)}, u32[]{:S(2)}) %collective-permute-start.22) | collective-permute-done | bytes 262176 | tf_op jit(solution)/shard_map/ppermute | solution.py:26
  98.9 1.1 convolution_convert_fusion
  100.2 1.0 collective-permute-done.25.refs_4_
  101.2 1.6 %collective-permute-start.26 = (bf16[128,1024]{1,0:T(8,128)(2,1)S(1)}, bf16[128,1024]{1,0:T(8,128)(2,1)S(1)}, u32[]{:S(2)}, u32[]{:S(2)}) collective-permute-start(bf16[128,1024]{1,0:T(8,128)(2,1)S(1)} %collective-permute-done.25.refs_4_), channel_id=1, source_target_pairs={{0,1},{1,0},{2,3},{3,2},{4,5},{5,4},{6,7},{7,6},{8,9},{9,8},{10,11... | collective-permute-start | bytes 786440 | tf_op jit(solution)/shard_map/ppermute | solution.py:31
  102.8 0.6 collective-permute-start.27
  103.5 5.0 %collective-permute-done.26.refs_5_ = bf16[128,1024]{1,0:T(8,128)(2,1)S(1)} collective-permute-done((bf16[128,1024]{1,0:T(8,128)(2,1)S(1)}, bf16[128,1024]{1,0:T(8,128)(2,1)S(1)}, u32[]{:S(2)}, u32[]{:S(2)}) %collective-permute-start.26) | collective-permute-done | bytes 262176 | tf_op jit(solution)/shard_map/ppermute | solution.py:31
  108.5 2.1 %collective-permute-done.27.refs_6_ = bf16[128,1024]{1,0:T(8,128)(2,1)S(1)} collective-permute-done((bf16[128,1024]{1,0:T(8,128)(2,1)S(1)}, bf16[128,1024]{1,0:T(8,128)(2,1)S(1)}, u32[]{:S(2)}, u32[]{:S(2)}) %collective-permute-start.27) | collective-permute-done | bytes 262176 | tf_op jit(solution)/shard_map/ppermute | solution.py:47
  110.6 0.5 collective-permute-start.28
  111.3 4.5 %logit_part.1 = (f32[128,512]{1,0:T(8,128)S(1)}, f32[128,128]{1,0:T(8,128)S(1)}) custom-call(f32[8,1024]{1,0:T(8,128)S(1)} %reshape.106.gain_ref, bf16[4096,512]{1,0:T(8,128)(2,1)} %own_ref.3, bf16[4096,512]{1,0:T(8,128)(2,1)} %copy-done.6, bf16[128,1024]{1,0:T(8,128)(2,1)S(1)} %get-tuple-element.66.refs_0_, ...), custom_call_target="tpu_custom_call" | custom-call | flops 939524096 | bytes 9175040 | tf_op jit(solution)/shard_map/logit_part/pallas_call | solution.py:431
  115.8 1.1 collective-permute-done.28.block_ref
  116.9 1.9 %vocab_stats.1 = f32[8,128]{1,0:T(8,128)S(1)} custom-call(s32[128,1]{1,0:T(8,128)S(1)} %copy.13.targets_ref, f32[8,1024]{1,0:T(8,128)S(1)} %reshape.106.gain_ref, f32[128,512]{1,0:T(8,128)S(1)} %get-tuple-element.60.logits_ref, f32[128,128]{1,0:T(8,128)S(1)} %get-tuple-element.61.squares_ref, bf16[128,1024]{1,0:T(8,128)(2,1)S(1)} %collective-permute-done.28.block_ref, ...), custom_call_target="tpu_custom_call" | custom-call | tf_op jit(solution)/shard_map/vocab_stats/pallas_call | solution.py:483
  118.8 0.6 collective-permute-start.29
  119.4 1.6 %collective-permute-start.31 = (f32[3,128]{1,0:T(4,128)S(1)}, f32[3,128]{1,0:T(4,128)S(1)}, u32[]{:S(2)}, u32[]{:S(2)}) collective-permute-start(f32[3,128]{1,0:T(4,128)S(1)} %slice.91), channel_id=1, source_target_pairs={{0,8},{8,0},{1,9},{9,1},{2,10},{10,2},{3,11},{11,3},{4,12},{12,4},... | collective-permute-start | bytes 4616 | tf_op jit(solution)/shard_map/ppermute | solution.py:26
  121.0 1.4 %collective-permute-done.29 = f32[3,128]{1,0:T(4,128)S(1)} collective-permute-done((f32[3,128]{1,0:T(4,128)S(1)}, f32[3,128]{1,0:T(4,128)S(1)}, u32[]{:S(2)}, u32[]{:S(2)}) %collective-permute-start.29) | collective-permute-done | bytes 1568 | tf_op jit(solution)/shard_map/ppermute | solution.py:31
  122.6 2.0 %collective-permute-start.32 = (f32[3,2,128]{2,0,1:T(4,128)S(1)}, f32[3,2,128]{2,0,1:T(4,128)S(1)}, u32[]{:S(2)}, u32[]{:S(2)}) collective-permute-start(f32[3,2,128]{2,0,1:T(4,128)S(1)} %pad_maximum_fusion.1), channel_id=1, source_target_pairs={{0,6},{1,7},{2,4},{3,5},{4,2},{5,3},{6,0},{7,1},{8,14},{9,15},{10,... | collective-permute-start | bytes 9224 | tf_op jit(solution)/shard_map/ppermute | solution.py:630
  124.6 0.6 collective-permute-start.33
  125.2 1.9 %collective-permute-start.34 = (f32[3,2,128]{2,0,1:T(4,128)S(1)}, f32[3,2,128]{2,0,1:T(4,128)S(1)}, u32[]{:S(2)}, u32[]{:S(2)}) collective-permute-start(f32[3,2,128]{2,0,1:T(4,128)S(1)} %pad_maximum_fusion.1), channel_id=1, source_target_pairs={{0,2},{1,3},{2,0},{3,1},{4,6},{5,7},{6,4},{7,5},{8,10},{9,11},{10,... | collective-permute-start | bytes 9224 | tf_op jit(solution)/shard_map/ppermute | solution.py:630
  127.0 1.0 collective-permute-done.32
  128.1 1.0 collective-permute-done.33
  129.2 0.7 select_reduce_fusion
  (75 shorter events, 2.4 us)
Async XLA Ops:
  0.6 4.4 %copy-start = (bf16[1024,256]{1,0:T(8,128)(2,1)S(1)}, bf16[1024,256]{1,0:T(8,128)(2,1)}, u32[]{:S(2)}) copy-start(bf16[1024,256]{1,0:T(8,128)(2,1)} %param.14) | copy-start | bytes 1572868
  0.6 1.1 copy-start.1
  1.7 0.7 copy-start.3
  2.4 16.0 %copy-start.2 = (bf16[4,256,256]{2,1,0:T(8,128)(2,1)S(1)}, bf16[4,256,256]{2,1,0:T(8,128)(2,1)}, u32[]{:S(2)}) copy-start(bf16[4,256,256]{2,1,0:T(8,128)(2,1)} %cache_own.1) | copy-start | bytes 1572868
  2.4 31.3 %copy-start.15 = (s32[4]{0:T(128)S(1)}, s32[4]{0:T(128)}, u32[]{:S(2)}) copy-start(s32[4]{0:T(128)} %param.20) | copy-start | bytes 52
  2.4 31.3 %copy-start.14 = (s32[512]{0:T(512)S(1)}, s32[512]{0:T(512)}, u32[]{:S(2)}) copy-start(s32[512]{0:T(512)} %param.21) | copy-start | bytes 6148
  2.4 38.9 %copy-start.12 = (f32[8192]{0:T(1024)S(1)}, f32[8192]{0:T(1024)}, u32[]{:S(2)}) copy-start(f32[8192]{0:T(1024)} %param.12) | copy-start | bytes 98308
  3.3 1.7 %collective-permute-start = (bf16[128,1024]{1,0:T(8,128)(2,1)S(1)}, bf16[128,1024]{1,0:T(8,128)(2,1)S(1)}, u32[]{:S(2)}, u32[]{:S(2)}) collective-permute-start(bf16[128,1024]{1,0:T(8,128)(2,1)S(1)} %get-tuple-element.34), channel_id=1, source_target_pairs={{0,8},{8,0},{1,9},{9,1},{2,10},{10,2},{3,11},{11,3},{4,12},{12,4},... | collective-permute-start | bytes 786440 | tf_op jit(solution)/shard_map/ppermute | solution.py:26
  3.8 1.6 %copy-start.7 = (bf16[4096,256]{1,0:T(8,128)(2,1)S(1)}, bf16[4096,256]{1,0:T(8,128)(2,1)}, u32[]{:S(2)}) copy-start(bf16[4096,256]{1,0:T(8,128)(2,1)} %q_own.3) | copy-start | bytes 6291460
  5.4 12.9 %collective-permute-start.3 = (bf16[4096,256]{1,0:T(8,128)(2,1)S(1)}, bf16[4096,256]{1,0:T(8,128)(2,1)S(1)}, u32[]{:S(2)}, u32[]{:S(2)}) collective-permute-start(bf16[4096,256]{1,0:T(8,128)(2,1)S(1)} %copy-done.7), channel_id=1, source_target_pairs={{0,8},{8,0},{1,9},{9,1},{2,10},{10,2},{3,11},{11,3},{4,12},{12,4},... | collective-permute-start | bytes 6291464 | tf_op jit(solution)/shard_map/ppermute | solution.py:26
  5.8 12.6 %collective-permute-start.4 = (bf16[256,4096]{1,0:T(8,128)(2,1)}, bf16[256,4096]{1,0:T(8,128)(2,1)S(1)}, u32[]{:S(2)}, u32[]{:S(2)}) collective-permute-start(bf16[256,4096]{1,0:T(8,128)(2,1)} %out_own.3), channel_id=1, source_target_pairs={{0,8},{8,0},{1,9},{9,1},{2,10},{10,2},{3,11},{11,3},{4,12},{12,4},... | collective-permute-start | bytes 6291464 | tf_op jit(solution)/shard_map/ppermute | solution.py:26
  5.9 12.0 %collective-permute-start.1 = (bf16[128,1280]{1,0:T(8,128)(2,1)S(1)}, bf16[128,1280]{1,0:T(8,128)(2,1)S(1)}, u32[]{:S(2)}, u32[]{:S(2)}) collective-permute-start(bf16[128,1280]{1,0:T(8,128)(2,1)S(1)} %pad_maximum_fusion.refs_0_), channel_id=1, source_target_pairs={{0,2},{1,3},{2,6},{3,7},{4,0},{5,1},{6,4},{7,5},{8,10},{9,11},{10,... | collective-permute-start | bytes 983048 | tf_op jit(solution)/shard_map/ppermute | solution.py:47
  8.9 9.5 %collective-permute-start.2 = (bf16[128,1280]{1,0:T(8,128)(2,1)S(1)}, bf16[128,1280]{1,0:T(8,128)(2,1)S(1)}, u32[]{:S(2)}, u32[]{:S(2)}) collective-permute-start(bf16[128,1280]{1,0:T(8,128)(2,1)S(1)} %pad_maximum_fusion.refs_0_), channel_id=1, source_target_pairs={{0,1},{1,0},{2,3},{3,2},{4,5},{5,4},{6,7},{7,6},{8,9},{9,8},{10,11... | collective-permute-start | bytes 983048 | tf_op jit(solution)/shard_map/ppermute | solution.py:31
  18.4 1.4 %copy-start.8 = (bf16[4096,256]{1,0:T(8,128)(2,1)}, bf16[4096,256]{1,0:T(8,128)(2,1)S(1)}, u32[]{:S(2)}) copy-start(bf16[4096,256]{1,0:T(8,128)(2,1)S(1)} %collective-permute-done.3.q_other) | copy-start | bytes 6291460
  18.4 3.9 %copy-start.9 = (bf16[256,4096]{1,0:T(8,128)(2,1)}, bf16[256,4096]{1,0:T(8,128)(2,1)S(1)}, u32[]{:S(2)}) copy-start(bf16[256,4096]{1,0:T(8,128)(2,1)S(1)} %collective-permute-done.4.out_other) | copy-start | bytes 6291460
  18.4 12.5 %collective-permute-start.7 = (bf16[4,256,256]{2,1,0:T(8,128)(2,1)S(1)}, bf16[4,256,256]{2,1,0:T(8,128)(2,1)}, u32[]{:S(2)}, u32[]{:S(2)}) collective-permute-start(bf16[4,256,256]{2,1,0:T(8,128)(2,1)S(1)} %copy-done.2), channel_id=1, source_target_pairs={{0,8},{8,0},{1,9},{9,1},{2,10},{10,2},{3,11},{11,3},{4,12},{12,4},... | collective-permute-start | bytes 1572872 | tf_op jit(solution)/shard_map/ppermute | solution.py:26
  19.7 9.7 %collective-permute-start.5 = (bf16[128,1280]{1,0:T(8,128)(2,1)S(1)}, bf16[128,1280]{1,0:T(8,128)(2,1)S(1)}, u32[]{:S(2)}, u32[]{:S(2)}) collective-permute-start(bf16[128,1280]{1,0:T(8,128)(2,1)S(1)} %collective-permute-done.1.refs_2_), channel_id=1, source_target_pairs={{0,2},{1,3},{2,6},{3,7},{4,0},{5,1},{6,4},{7,5},{8,10},{9,11},{10,... | collective-permute-start | bytes 983048 | tf_op jit(solution)/shard_map/ppermute | solution.py:47
  22.3 8.6 %collective-permute-start.6 = (bf16[128,1280]{1,0:T(8,128)(2,1)S(1)}, bf16[128,1280]{1,0:T(8,128)(2,1)S(1)}, u32[]{:S(2)}, u32[]{:S(2)}) collective-permute-start(bf16[128,1280]{1,0:T(8,128)(2,1)S(1)} %collective-permute-done.1.refs_2_), channel_id=1, source_target_pairs={{0,1},{1,0},{2,3},{3,2},{4,5},{5,4},{6,7},{7,6},{8,9},{9,8},{10,11... | collective-permute-start | bytes 983048 | tf_op jit(solution)/shard_map/ppermute | solution.py:31
  30.9 7.6 %collective-permute-start.9 = (bf16[128,1280]{1,0:T(8,128)(2,1)S(1)}, bf16[128,1280]{1,0:T(8,128)(2,1)S(1)}, u32[]{:S(2)}, u32[]{:S(2)}) collective-permute-start(bf16[128,1280]{1,0:T(8,128)(2,1)S(1)} %collective-permute-done.5.refs_4_), channel_id=1, source_target_pairs={{0,1},{1,0},{2,3},{3,2},{4,5},{5,4},{6,7},{7,6},{8,9},{9,8},{10,11... | collective-permute-start | bytes 983048 | tf_op jit(solution)/shard_map/ppermute | solution.py:31
  32.4 8.4 %collective-permute-start.10 = (bf16[128,1280]{1,0:T(8,128)(2,1)S(1)}, bf16[128,1280]{1,0:T(8,128)(2,1)}, u32[]{:S(2)}, u32[]{:S(2)}) collective-permute-start(bf16[128,1280]{1,0:T(8,128)(2,1)S(1)} %collective-permute-done.5.refs_4_), channel_id=1, source_target_pairs={{0,2},{1,3},{2,6},{3,7},{4,0},{5,1},{6,4},{7,5},{8,10},{9,11},{10,... | collective-permute-start | bytes 983048 | tf_op jit(solution)/shard_map/ppermute | solution.py:47
  33.7 1.1 collective-permute-start.8
  33.9 1.4 %collective-permute-start.11 = (s32[1,128]{1,0:T(1,128)S(1)}, s32[1,128]{1,0:T(1,128)S(1)}, u32[]{:S(2)}, u32[]{:S(2)}) collective-permute-start(s32[1,128]{1,0:T(1,128)S(1)} %slice_bitcast_fusion), channel_id=1, source_target_pairs={{0,8},{8,0},{1,9},{9,1},{2,10},{10,2},{3,11},{11,3},{4,12},{12,4},... | collective-permute-start | bytes 1544 | tf_op jit(solution)/shard_map/ppermute | solution.py:26
  38.5 0.7 copy-start.10
  40.8 7.3 %collective-permute-start.12 = (bf16[128,1280]{1,0:T(8,128)(2,1)}, bf16[128,1280]{1,0:T(8,128)(2,1)S(1)}, u32[]{:S(2)}, u32[]{:S(2)}) collective-permute-start(bf16[128,1280]{1,0:T(8,128)(2,1)} %collective-permute-done.10.refs_6_), channel_id=1, source_target_pairs={{0,1},{1,0},{2,3},{3,2},{4,5},{5,4},{6,7},{7,6},{8,9},{9,8},{10,11... | collective-permute-start | bytes 983048 | tf_op jit(solution)/shard_map/ppermute | solution.py:31
  41.3 6.8 %copy-start.4 = (s32[8]{0:T(128)S(1)}, s32[8]{0:T(128)}, u32[]{:S(2)}) copy-start(s32[8]{0:T(128)} %lens_ref.3) | copy-start | bytes 100
  51.7 9.3 %collective-permute-start.16 = (bf16[128,1024]{1,0:T(8,128)(2,1)S(1)}, bf16[128,1024]{1,0:T(8,128)(2,1)S(1)}, u32[]{:S(2)}, u32[]{:S(2)}) collective-permute-start(bf16[128,1024]{1,0:T(8,128)(2,1)S(1)} %get-tuple-element.54), channel_id=1, source_target_pairs={{0,1},{1,0},{2,3},{3,2},{4,5},{5,4},{6,7},{7,6},{8,9},{9,8},{10,11... | collective-permute-start | bytes 786440 | tf_op jit(solution)/shard_map/ppermute | solution.py:31
  55.1 28.8 %dynamic-slice-start = ((f32[8192]{0:T(1024)}, s32[]{:T(128)}), f32[1024]{0:T(1024)S(1)}, s32[]{:S(2)}) async-start(f32[8192]{0:T(1024)} %param.17, s32[]{:T(128)} %select_n.122), calls=%async_computation | async-start | bytes 8704 | tf_op jit(solution)/shard_map/dynamic_slice | solution.py:580
  55.1 11.6 %collective-permute-start.15 = (bf16[128,1024]{1,0:T(8,128)(2,1)S(1)}, bf16[128,1024]{1,0:T(8,128)(2,1)S(1)}, u32[]{:S(2)}, u32[]{:S(2)}) collective-permute-start(bf16[128,1024]{1,0:T(8,128)(2,1)S(1)} %get-tuple-element.52), channel_id=1, source_target_pairs={{0,1},{1,0},{2,3},{3,2},{4,5},{5,4},{6,7},{7,6},{8,9},{9,8},{10,11... | collective-permute-start | bytes 786440 | tf_op jit(solution)/shard_map/ppermute | solution.py:31
  61.0 30.3 %copy-start.5 = (bf16[4096,512]{1,0:T(8,128)(2,1)S(1)}, bf16[4096,512]{1,0:T(8,128)(2,1)}, u32[]{:S(2)}) copy-start(bf16[4096,512]{1,0:T(8,128)(2,1)} %own_ref.3) | copy-start | bytes 12582916
  61.1 7.3 %collective-permute-start.17 = (bf16[128,1024]{1,0:T(8,128)(2,1)S(1)}, bf16[128,1024]{1,0:T(8,128)(2,1)S(1)}, u32[]{:S(2)}, u32[]{:S(2)}) collective-permute-start(bf16[128,1024]{1,0:T(8,128)(2,1)S(1)} %add_convert_fusion.2), channel_id=1, source_target_pairs={{0,2},{1,3},{2,6},{3,7},{4,0},{5,1},{6,4},{7,5},{8,10},{9,11},{10,... | collective-permute-start | bytes 786440 | tf_op jit(solution)/shard_map/ppermute | solution.py:47
  61.6 8.4 %collective-permute-start.14 = (bf16[128,1024]{1,0:T(8,128)(2,1)S(1)}, bf16[128,1024]{1,0:T(8,128)(2,1)S(1)}, u32[]{:S(2)}, u32[]{:S(2)}) collective-permute-start(bf16[128,1024]{1,0:T(8,128)(2,1)S(1)} %get-tuple-element.50), channel_id=1, source_target_pairs={{0,1},{1,0},{2,3},{3,2},{4,5},{5,4},{6,7},{7,6},{8,9},{9,8},{10,11... | collective-permute-start | bytes 786440 | tf_op jit(solution)/shard_map/ppermute | solution.py:31
  68.6 42.5 %copy-start.13 = (f32[8192]{0:T(1024)S(1)}, f32[8192]{0:T(1024)}, u32[]{:S(2)}) copy-start(f32[8192]{0:T(1024)} %param.17) | copy-start | bytes 98308
  68.6 7.8 %collective-permute-start.18 = (bf16[128,1024]{1,0:T(8,128)(2,1)S(1)}, bf16[128,1024]{1,0:T(8,128)(2,1)S(1)}, u32[]{:S(2)}, u32[]{:S(2)}) collective-permute-start(bf16[128,1024]{1,0:T(8,128)(2,1)S(1)} %add_convert_fusion.1), channel_id=1, source_target_pairs={{0,2},{1,3},{2,6},{3,7},{4,0},{5,1},{6,4},{7,5},{8,10},{9,11},{10,... | collective-permute-start | bytes 786440 | tf_op jit(solution)/shard_map/ppermute | solution.py:47
  68.6 7.9 %collective-permute-start.13 = (bf16[128,1024]{1,0:T(8,128)(2,1)S(1)}, bf16[128,1024]{1,0:T(8,128)(2,1)S(1)}, u32[]{:S(2)}, u32[]{:S(2)}) collective-permute-start(bf16[128,1024]{1,0:T(8,128)(2,1)S(1)} %get-tuple-element.48), channel_id=1, source_target_pairs={{0,1},{1,0},{2,3},{3,2},{4,5},{5,4},{6,7},{7,6},{8,9},{9,8},{10,11... | collective-permute-start | bytes 786440 | tf_op jit(solution)/shard_map/ppermute | solution.py:31
  76.5 7.3 %collective-permute-start.19 = (bf16[128,1024]{1,0:T(8,128)(2,1)S(1)}, bf16[128,1024]{1,0:T(8,128)(2,1)S(1)}, u32[]{:S(2)}, u32[]{:S(2)}) collective-permute-start(bf16[128,1024]{1,0:T(8,128)(2,1)S(1)} %add_convert_fusion), channel_id=1, source_target_pairs={{0,2},{1,3},{2,6},{3,7},{4,0},{5,1},{6,4},{7,5},{8,10},{9,11},{10,... | collective-permute-start | bytes 786440 | tf_op jit(solution)/shard_map/ppermute | solution.py:47
  84.0 7.3 %collective-permute-start.20 = (bf16[128,1024]{1,0:T(8,128)(2,1)S(1)}, bf16[128,1024]{1,0:T(8,128)(2,1)S(1)}, u32[]{:S(2)}, u32[]{:S(2)}) collective-permute-start(bf16[128,1024]{1,0:T(8,128)(2,1)S(1)} %get-tuple-element.66.refs_0_), channel_id=1, source_target_pairs={{0,2},{1,3},{2,6},{3,7},{4,0},{5,1},{6,4},{7,5},{8,10},{9,11},{10,... | collective-permute-start | bytes 786440 | tf_op jit(solution)/shard_map/ppermute | solution.py:47
  84.1 7.3 %collective-permute-start.21 = (bf16[128,1024]{1,0:T(8,128)(2,1)S(1)}, bf16[128,1024]{1,0:T(8,128)(2,1)S(1)}, u32[]{:S(2)}, u32[]{:S(2)}) collective-permute-start(bf16[128,1024]{1,0:T(8,128)(2,1)S(1)} %get-tuple-element.66.refs_0_), channel_id=1, source_target_pairs={{0,1},{1,0},{2,3},{3,2},{4,5},{5,4},{6,7},{7,6},{8,9},{9,8},{10,11... | collective-permute-start | bytes 786440 | tf_op jit(solution)/shard_map/ppermute | solution.py:31
  91.4 9.8 %collective-permute-start.23 = (bf16[4096,512]{1,0:T(8,128)(2,1)S(1)}, bf16[4096,512]{1,0:T(8,128)(2,1)S(1)}, u32[]{:S(2)}, u32[]{:S(2)}) collective-permute-start(bf16[4096,512]{1,0:T(8,128)(2,1)S(1)} %copy-done.5), channel_id=1, source_target_pairs={{0,8},{8,0},{1,9},{9,1},{2,10},{10,2},{3,11},{11,3},{4,12},{12,4},... | collective-permute-start | bytes 12582920 | tf_op jit(solution)/shard_map/ppermute | solution.py:26
  91.4 7.5 %collective-permute-start.22 = (bf16[128,1024]{1,0:T(8,128)(2,1)S(1)}, bf16[128,1024]{1,0:T(8,128)(2,1)S(1)}, u32[]{:S(2)}, u32[]{:S(2)}) collective-permute-start(bf16[128,1024]{1,0:T(8,128)(2,1)S(1)} %get-tuple-element.56), channel_id=1, source_target_pairs={{0,8},{8,0},{1,9},{9,1},{2,10},{10,2},{3,11},{11,3},{4,12},{12,4},... | collective-permute-start | bytes 786440 | tf_op jit(solution)/shard_map/ppermute | solution.py:26
  91.9 8.3 %collective-permute-start.24 = (bf16[128,1024]{1,0:T(8,128)(2,1)S(1)}, bf16[128,1024]{1,0:T(8,128)(2,1)S(1)}, u32[]{:S(2)}, u32[]{:S(2)}) collective-permute-start(bf16[128,1024]{1,0:T(8,128)(2,1)S(1)} %collective-permute-done.20.refs_2_), channel_id=1, source_target_pairs={{0,1},{1,0},{2,3},{3,2},{4,5},{5,4},{6,7},{7,6},{8,9},{9,8},{10,11... | collective-permute-start | bytes 786440 | tf_op jit(solution)/shard_map/ppermute | solution.py:31
  92.3 8.9 %collective-permute-start.25 = (bf16[128,1024]{1,0:T(8,128)(2,1)S(1)}, bf16[128,1024]{1,0:T(8,128)(2,1)S(1)}, u32[]{:S(2)}, u32[]{:S(2)}) collective-permute-start(bf16[128,1024]{1,0:T(8,128)(2,1)S(1)} %collective-permute-done.20.refs_2_), channel_id=1, source_target_pairs={{0,2},{1,3},{2,6},{3,7},{4,0},{5,1},{6,4},{7,5},{8,10},{9,11},{10,... | collective-permute-start | bytes 786440 | tf_op jit(solution)/shard_map/ppermute | solution.py:47
  101.2 9.4 %copy-start.6 = (bf16[4096,512]{1,0:T(8,128)(2,1)}, bf16[4096,512]{1,0:T(8,128)(2,1)S(1)}, u32[]{:S(2)}) copy-start(bf16[4096,512]{1,0:T(8,128)(2,1)S(1)} %collective-permute-done.23.other_ref) | copy-start | bytes 12582916
  101.2 7.3 %collective-permute-start.26 = (bf16[128,1024]{1,0:T(8,128)(2,1)S(1)}, bf16[128,1024]{1,0:T(8,128)(2,1)S(1)}, u32[]{:S(2)}, u32[]{:S(2)}) collective-permute-start(bf16[128,1024]{1,0:T(8,128)(2,1)S(1)} %collective-permute-done.25.refs_4_), channel_id=1, source_target_pairs={{0,1},{1,0},{2,3},{3,2},{4,5},{5,4},{6,7},{7,6},{8,9},{9,8},{10,11... | collective-permute-start | bytes 786440 | tf_op jit(solution)/shard_map/ppermute | solution.py:31
  102.8 7.7 %collective-permute-start.27 = (bf16[128,1024]{1,0:T(8,128)(2,1)S(1)}, bf16[128,1024]{1,0:T(8,128)(2,1)S(1)}, u32[]{:S(2)}, u32[]{:S(2)}) collective-permute-start(bf16[128,1024]{1,0:T(8,128)(2,1)S(1)} %collective-permute-done.25.refs_4_), channel_id=1, source_target_pairs={{0,2},{1,3},{2,6},{3,7},{4,0},{5,1},{6,4},{7,5},{8,10},{9,11},{10,... | collective-permute-start | bytes 786440 | tf_op jit(solution)/shard_map/ppermute | solution.py:47
  110.6 0.7 copy-start.11
  110.6 6.4 %collective-permute-start.28 = (bf16[128,1024]{1,0:T(8,128)(2,1)S(1)}, bf16[128,1024]{1,0:T(8,128)(2,1)S(1)}, u32[]{:S(2)}, u32[]{:S(2)}) collective-permute-start(bf16[128,1024]{1,0:T(8,128)(2,1)S(1)} %collective-permute-done.27.refs_6_), channel_id=1, source_target_pairs={{0,1},{1,0},{2,3},{3,2},{4,5},{5,4},{6,7},{7,6},{8,9},{9,8},{10,11... | collective-permute-start | bytes 786440 | tf_op jit(solution)/shard_map/ppermute | solution.py:31
  118.8 3.7 %collective-permute-start.29 = (f32[3,128]{1,0:T(4,128)S(1)}, f32[3,128]{1,0:T(4,128)S(1)}, u32[]{:S(2)}, u32[]{:S(2)}) collective-permute-start(f32[3,128]{1,0:T(4,128)S(1)} %slice.91), channel_id=1, source_target_pairs={{0,1},{1,0},{2,3},{3,2},{4,5},{5,4},{6,7},{7,6},{8,9},{9,8},{10,11... | collective-permute-start | bytes 4616 | tf_op jit(solution)/shard_map/ppermute | solution.py:31
  119.4 3.1 %collective-permute-start.30 = (f32[3,128]{1,0:T(4,128)S(1)}, f32[3,128]{1,0:T(4,128)S(1)}, u32[]{:S(2)}, u32[]{:S(2)}) collective-permute-start(f32[3,128]{1,0:T(4,128)S(1)} %slice.91), channel_id=1, source_target_pairs={{9,0},{8,1},{11,2},{10,3},{13,4},{12,5},{15,6},{14,7},{1,8},{0,9},... | collective-permute-start | bytes 4616 | tf_op jit(solution)/shard_map/ppermute | solution.py:621
  119.4 3.1 %collective-permute-start.31 = (f32[3,128]{1,0:T(4,128)S(1)}, f32[3,128]{1,0:T(4,128)S(1)}, u32[]{:S(2)}, u32[]{:S(2)}) collective-permute-start(f32[3,128]{1,0:T(4,128)S(1)} %slice.91), channel_id=1, source_target_pairs={{0,8},{8,0},{1,9},{9,1},{2,10},{10,2},{3,11},{11,3},{4,12},{12,4},... | collective-permute-start | bytes 4616 | tf_op jit(solution)/shard_map/ppermute | solution.py:26
  122.6 5.5 %collective-permute-start.32 = (f32[3,2,128]{2,0,1:T(4,128)S(1)}, f32[3,2,128]{2,0,1:T(4,128)S(1)}, u32[]{:S(2)}, u32[]{:S(2)}) collective-permute-start(f32[3,2,128]{2,0,1:T(4,128)S(1)} %pad_maximum_fusion.1), channel_id=1, source_target_pairs={{0,6},{1,7},{2,4},{3,5},{4,2},{5,3},{6,0},{7,1},{8,14},{9,15},{10,... | collective-permute-start | bytes 9224 | tf_op jit(solution)/shard_map/ppermute | solution.py:630
  124.6 4.5 %collective-permute-start.33 = (f32[3,2,128]{2,0,1:T(4,128)S(1)}, f32[3,2,128]{2,0,1:T(4,128)S(1)}, u32[]{:S(2)}, u32[]{:S(2)}) collective-permute-start(f32[3,2,128]{2,0,1:T(4,128)S(1)} %pad_maximum_fusion.1), channel_id=1, source_target_pairs={{0,4},{1,5},{2,6},{3,7},{4,0},{5,1},{6,2},{7,3},{8,12},{9,13},{10,... | collective-permute-start | bytes 9224 | tf_op jit(solution)/shard_map/ppermute | solution.py:630
  125.2 3.9 %collective-permute-start.34 = (f32[3,2,128]{2,0,1:T(4,128)S(1)}, f32[3,2,128]{2,0,1:T(4,128)S(1)}, u32[]{:S(2)}, u32[]{:S(2)}) collective-permute-start(f32[3,2,128]{2,0,1:T(4,128)S(1)} %pad_maximum_fusion.1), channel_id=1, source_target_pairs={{0,2},{1,3},{2,0},{3,1},{4,6},{5,7},{6,4},{7,5},{8,10},{9,11},{10,... | collective-permute-start | bytes 9224 | tf_op jit(solution)/shard_map/ppermute | solution.py:630

commit v8 on v7

--- a/solution.py
+++ b/solution.py
@@ -11,7 +11,7 @@
 QH_DEV = 2
 GROUP = 16
 SIDE = 2
-SWAP_STEP = {"q": 0, "out": 0, "cache": 1, "ctx": 2, "targets": 2, "layer": 5, "vocab": 5}
+SWAP_STEP = {"q": 0, "out": 0, "cache": 1, "ctx": 2, "targets": 1, "layer": 5, "vocab": 5}
 
 
 EPS = 1e-05

time: 130 us -> 129 us (level)
  starting transfers between devices: 30.5 us -> 35.5 us
  waiting for transfers between devices: 73 us -> 68.2 us
  local copies, waits for them, and re-layouts: 4.97 us -> 3.48 us
    ppermute x13, waiting for transfers between devices: 25.1 us -> 21 us  [swap_side(): return lax.ppermute(value, 'tensor', [(i, i ^ 1) for i in range(count)])]
    ppermute x9, starting transfers between devices: 9.95 us -> 13.1 us  [ring_step(): return lax.ppermute(value, 'tensor', pairs)]
    ppermute x13, starting transfers between devices: 12.3 us -> 15 us  [swap_side(): return lax.ppermute(value, 'tensor', [(i, i ^ 1) for i in range(count)])]
    ppermute x9, waiting for transfers between devices: 40 us -> 37.6 us  [ring_step(): return lax.ppermute(value, 'tensor', pairs)]
    unnamed x32 -> x28, local copies, waits for them, and re-layouts: 3.9 us -> 2.55 us
where the time goes in v8:
time: 129 us
  waiting for transfers between devices  68.2 us (53%)
  starting transfers between devices  35.5 us (28%)
  Pallas kernels  17.5 us (14%)
  local copies, waits for them, and re-layouts  3.48 us (3%)
  other arithmetic  1.58 us (1%)
  matrix products  1.35 us (1%)
    ppermute x9, waiting for transfers between devices, ring_step(): return lax.ppermute(value, 'tensor', pairs)  37.6 us
    ppermute x13, waiting for transfers between devices, swap_side(): return lax.ppermute(value, 'tensor', [(i, i ^ 1) for i in range(count)])  21 us
    ppermute x13, starting transfers between devices, swap_side(): return lax.ppermute(value, 'tensor', [(i, i ^ 1) for i in range(count)])  15 us
    ppermute x9, starting transfers between devices, ring_step(): return lax.ppermute(value, 'tensor', pairs)  13.1 us
    ppermute x9, waiting for transfers between devices, swap_dp(): return lax.ppermute(value, 'dp', [(0, 1), (1, 0)])  6.58 us
    pallas_call x1, Pallas kernels, logit_part(): pl.pallas_call(logit_kernel, out_shape=[jax.ShapeDtypeStruct((half, vocab...  4.55 us
    ppermute x3, starting transfers between devices, per_device(): lax.ppermute(stats, 'tensor', [(i, i ^ SIDE * c) for i in range(tensor_co...  4.45 us
    pallas_call x1, Pallas kernels, query_part(): pl.pallas_call(functools.partial(query_kernel, shard), out_shape=[jax.Sha...  3.84 us
  transfers between devices with their start and end apart: 35, of which 26 were waited for; matrix products, arithmetic and copies ran while one was open for 2% of the time, Pallas kernels for 9%

profile of v8, /device:TPU:0, one launch (start us, length us, event | category | flops | bytes accessed | tf_op | source)
XLA Modules:
  0.0 128.6 jit_solution(16194148438927394561)
XLA Ops:
  0.7 1.1 copy-done.1
  1.7 0.7 copy-done.3
  2.4 0.9 pack_rows.1
  3.3 0.5 collective-permute-start
  3.8 0.7 dynamic_slice.9
  4.5 0.5 collective-permute-done
  5.3 0.4 collective-permute-start.3
  5.9 2.9 %collective-permute-start.1 = (bf16[128,1280]{1,0:T(8,128)(2,1)S(1)}, bf16[128,1280]{1,0:T(8,128)(2,1)S(1)}, u32[]{:S(2)}, u32[]{:S(2)}) collective-permute-start(bf16[128,1280]{1,0:T(8,128)(2,1)S(1)} %pad_maximum_fusion.refs_0_), channel_id=1, source_target_pairs={{0,2},{1,3},{2,6},{3,7},{4,0},{5,1},{6,4},{7,5},{8,10},{9,11},{10,... | collective-permute-start | bytes 983048 | tf_op jit(solution)/shard_map/ppermute | solution.py:47
  8.9 1.5 %collective-permute-start.2 = (bf16[128,1280]{1,0:T(8,128)(2,1)S(1)}, bf16[128,1280]{1,0:T(8,128)(2,1)S(1)}, u32[]{:S(2)}, u32[]{:S(2)}) collective-permute-start(bf16[128,1280]{1,0:T(8,128)(2,1)S(1)} %pad_maximum_fusion.refs_0_), channel_id=1, source_target_pairs={{0,1},{1,0},{2,3},{3,2},{4,5},{5,4},{6,7},{7,6},{8,9},{9,8},{10,11... | collective-permute-start | bytes 983048 | tf_op jit(solution)/shard_map/ppermute | solution.py:31
  10.4 7.5 %collective-permute-done.1.refs_2_ = bf16[128,1280]{1,0:T(8,128)(2,1)S(1)} collective-permute-done((bf16[128,1280]{1,0:T(8,128)(2,1)S(1)}, bf16[128,1280]{1,0:T(8,128)(2,1)S(1)}, u32[]{:S(2)}, u32[]{:S(2)}) %collective-permute-start.1) | collective-permute-done | bytes 327712 | tf_op jit(solution)/shard_map/ppermute | solution.py:47
  17.9 0.5 collective-permute-done.2.refs_1_
  18.3 2.6 %collective-permute-start.5 = (bf16[128,1280]{1,0:T(8,128)(2,1)S(1)}, bf16[128,1280]{1,0:T(8,128)(2,1)S(1)}, u32[]{:S(2)}, u32[]{:S(2)}) collective-permute-start(bf16[128,1280]{1,0:T(8,128)(2,1)S(1)} %collective-permute-done.1.refs_2_), channel_id=1, source_target_pairs={{0,2},{1,3},{2,6},{3,7},{4,0},{5,1},{6,4},{7,5},{8,10},{9,11},{10,... | collective-permute-start | bytes 983048 | tf_op jit(solution)/shard_map/ppermute | solution.py:47
  20.9 1.5 %collective-permute-start.6 = (bf16[128,1280]{1,0:T(8,128)(2,1)S(1)}, bf16[128,1280]{1,0:T(8,128)(2,1)S(1)}, u32[]{:S(2)}, u32[]{:S(2)}) collective-permute-start(bf16[128,1280]{1,0:T(8,128)(2,1)S(1)} %collective-permute-done.1.refs_2_), channel_id=1, source_target_pairs={{0,1},{1,0},{2,3},{3,2},{4,5},{5,4},{6,7},{7,6},{8,9},{9,8},{10,11... | collective-permute-start | bytes 983048 | tf_op jit(solution)/shard_map/ppermute | solution.py:31
  22.7 0.6 collective-permute-start.8
  23.2 1.1 collective-permute-done.8
  24.4 3.7 %collective-permute-done.5.refs_4_ = bf16[128,1280]{1,0:T(8,128)(2,1)S(1)} collective-permute-done((bf16[128,1280]{1,0:T(8,128)(2,1)S(1)}, bf16[128,1280]{1,0:T(8,128)(2,1)S(1)}, u32[]{:S(2)}, u32[]{:S(2)}) %collective-permute-start.5) | collective-permute-done | bytes 327712 | tf_op jit(solution)/shard_map/ppermute | solution.py:47
  28.1 1.2 collective-permute-done.6.refs_3_
  29.2 1.5 %collective-permute-start.10 = (bf16[128,1280]{1,0:T(8,128)(2,1)S(1)}, bf16[128,1280]{1,0:T(8,128)(2,1)S(1)}, u32[]{:S(2)}, u32[]{:S(2)}) collective-permute-start(bf16[128,1280]{1,0:T(8,128)(2,1)S(1)} %collective-permute-done.5.refs_4_), channel_id=1, source_target_pairs={{0,1},{1,0},{2,3},{3,2},{4,5},{5,4},{6,7},{7,6},{8,9},{9,8},{10,11... | collective-permute-start | bytes 983048 | tf_op jit(solution)/shard_map/ppermute | solution.py:31
  30.8 1.6 %collective-permute-start.11 = (bf16[128,1280]{1,0:T(8,128)(2,1)S(1)}, bf16[128,1280]{1,0:T(8,128)(2,1)}, u32[]{:S(2)}, u32[]{:S(2)}) collective-permute-start(bf16[128,1280]{1,0:T(8,128)(2,1)S(1)} %collective-permute-done.5.refs_4_), channel_id=1, source_target_pairs={{0,2},{1,3},{2,6},{3,7},{4,0},{5,1},{6,4},{7,5},{8,10},{9,11},{10,... | collective-permute-start | bytes 983048 | tf_op jit(solution)/shard_map/ppermute | solution.py:47
  32.3 1.1 collective-permute-done.9
  33.5 3.1 %collective-permute-done.10.refs_5_ = bf16[128,1280]{1,0:T(8,128)(2,1)S(1)} collective-permute-done((bf16[128,1280]{1,0:T(8,128)(2,1)S(1)}, bf16[128,1280]{1,0:T(8,128)(2,1)S(1)}, u32[]{:S(2)}, u32[]{:S(2)}) %collective-permute-start.10) | collective-permute-done | bytes 327712 | tf_op jit(solution)/shard_map/ppermute | solution.py:31
  36.6 0.8 copy-done.8
  37.4 1.5 %collective-permute-done.11.refs_6_ = bf16[128,1280]{1,0:T(8,128)(2,1)} collective-permute-done((bf16[128,1280]{1,0:T(8,128)(2,1)S(1)}, bf16[128,1280]{1,0:T(8,128)(2,1)}, u32[]{:S(2)}, u32[]{:S(2)}) %collective-permute-start.11) | collective-permute-done | bytes 327712 | tf_op jit(solution)/shard_map/ppermute | solution.py:47
  38.9 0.5 collective-permute-start.12
  39.4 3.8 %query_part.1 = (f32[128,256]{1,0:T(8,128)S(1)}, f32[128,256]{1,0:T(8,128)S(1)}, f32[128,128]{1,0:T(8,128)S(1)}) custom-call(f32[8,1024]{1,0:T(8,128)S(1)} %reshape.104.gain_ref, bf16[4096,256]{1,0:T(8,128)(2,1)} %q_own.3, bf16[4096,256]{1,0:T(8,128)(2,1)} %collective-permute-done.3.q_other, bf16[128,1280]{1,0:T(8,128)(2,1)S(1)} %pad_maximum_fusion.refs_0_, ...), custom_call_target="tpu_custom_call" | custom-call | flops 469762048 | bytes 5505024 | tf_op jit(solution)/shard_map/query_part/pallas_call | solution.py:201
  43.3 2.9 %collective-permute-done.12.block_ref = bf16[128,1280]{1,0:T(8,128)(2,1)S(1)} collective-permute-done((bf16[128,1280]{1,0:T(8,128)(2,1)}, bf16[128,1280]{1,0:T(8,128)(2,1)S(1)}, u32[]{:S(2)}, u32[]{:S(2)}) %collective-permute-start.12) | collective-permute-done | bytes 327712 | tf_op jit(solution)/shard_map/ppermute | solution.py:31
  46.2 3.6 %attend.1 = (bf16[128,256]{1,0:T(8,128)(2,1)S(1)}, bf16[128,1024]{1,0:T(8,128)(2,1)S(1)}) custom-call(s32[8]{0:T(128)S(1)} %copy-done.4, s32[8]{0:T(128)S(1)} %pad_add_fusion.ctx_ref, f32[8,1024]{1,0:T(8,128)S(1)} %reshape.104.gain_ref, f32[128,256]{1,0:T(8,128)S(1)} %get-tuple-element.43.query_ref, f32[128,256]{1,0:T(8,128)S(1)} %get-tuple-element.44.kv_ref, ...), custom_call_target="tpu_custom_call" | custom-call | tf_op jit(solution)/shard_map/attend/pallas_call | solution.py:347
  49.8 0.6 collective-permute-start.16
  50.4 2.8 %out_products.1 = (bf16[128,1024]{1,0:T(8,128)(2,1)S(1)}, bf16[128,1024]{1,0:T(8,128)(2,1)S(1)}, bf16[128,1024]{1,0:T(8,128)(2,1)S(1)}, bf16[128,1024]{1,0:T(8,1...) custom-call(bf16[128,256]{1,0:T(8,128)(2,1)S(1)} %get-tuple-element.46.att, ...), custom_call_target="tpu_custom_call" | custom-call | flops 469762048 | bytes 5505024 | tf_op jit(solution)/shard_map/out_products/pallas_call | solution.py:385
  53.2 1.6 %collective-permute-start.15 = (bf16[128,1024]{1,0:T(8,128)(2,1)S(1)}, bf16[128,1024]{1,0:T(8,128)(2,1)S(1)}, u32[]{:S(2)}, u32[]{:S(2)}) collective-permute-start(bf16[128,1024]{1,0:T(8,128)(2,1)S(1)} %get-tuple-element.52), channel_id=1, source_target_pairs={{0,1},{1,0},{2,3},{3,2},{4,5},{5,4},{6,7},{7,6},{8,9},{9,8},{10,11... | collective-permute-start | bytes 786440 | tf_op jit(solution)/shard_map/ppermute | solution.py:31
  54.8 3.9 %collective-permute-done.16 = bf16[128,1024]{1,0:T(8,128)(2,1)S(1)} collective-permute-done((bf16[128,1024]{1,0:T(8,128)(2,1)S(1)}, bf16[128,1024]{1,0:T(8,128)(2,1)S(1)}, u32[]{:S(2)}, u32[]{:S(2)}) %collective-permute-start.16) | collective-permute-done | bytes 262176 | tf_op jit(solution)/shard_map/ppermute | solution.py:31
  58.8 1.5 %collective-permute-start.17 = (bf16[128,1024]{1,0:T(8,128)(2,1)S(1)}, bf16[128,1024]{1,0:T(8,128)(2,1)S(1)}, u32[]{:S(2)}, u32[]{:S(2)}) collective-permute-start(bf16[128,1024]{1,0:T(8,128)(2,1)S(1)} %add_convert_fusion.2), channel_id=1, source_target_pairs={{0,2},{1,3},{2,6},{3,7},{4,0},{5,1},{6,4},{7,5},{8,10},{9,11},{10,... | collective-permute-start | bytes 786440 | tf_op jit(solution)/shard_map/ppermute | solution.py:47
  60.3 1.0 collective-permute-start.14
  61.2 2.7 %collective-permute-done.15 = bf16[128,1024]{1,0:T(8,128)(2,1)S(1)} collective-permute-done((bf16[128,1024]{1,0:T(8,128)(2,1)S(1)}, bf16[128,1024]{1,0:T(8,128)(2,1)S(1)}, u32[]{:S(2)}, u32[]{:S(2)}) %collective-permute-start.15) | collective-permute-done | bytes 262176 | tf_op jit(solution)/shard_map/ppermute | solution.py:31
  63.9 2.2 %collective-permute-done.17 = bf16[128,1024]{1,0:T(8,128)(2,1)S(1)} collective-permute-done((bf16[128,1024]{1,0:T(8,128)(2,1)S(1)}, bf16[128,1024]{1,0:T(8,128)(2,1)S(1)}, u32[]{:S(2)}, u32[]{:S(2)}) %collective-permute-start.17) | collective-permute-done | bytes 262176 | tf_op jit(solution)/shard_map/ppermute | solution.py:47
  66.2 0.7 collective-permute-start.18
  66.9 0.9 collective-permute-start.13
  67.8 6.3 %collective-permute-done.18 = bf16[128,1024]{1,0:T(8,128)(2,1)S(1)} collective-permute-done((bf16[128,1024]{1,0:T(8,128)(2,1)S(1)}, bf16[128,1024]{1,0:T(8,128)(2,1)S(1)}, u32[]{:S(2)}, u32[]{:S(2)}) %collective-permute-start.18) | collective-permute-done | bytes 262176 | tf_op jit(solution)/shard_map/ppermute | solution.py:47
  74.4 7.2 %collective-permute-done.19 = bf16[128,1024]{1,0:T(8,128)(2,1)S(1)} collective-permute-done((bf16[128,1024]{1,0:T(8,128)(2,1)S(1)}, bf16[128,1024]{1,0:T(8,128)(2,1)S(1)}, u32[]{:S(2)}, u32[]{:S(2)}) %collective-permute-start.19) | collective-permute-done | bytes 262176 | tf_op jit(solution)/shard_map/ppermute | solution.py:47
  81.9 1.3 collective-permute-start.21
  83.2 5.9 %collective-permute-done.20.refs_2_ = bf16[128,1024]{1,0:T(8,128)(2,1)S(1)} collective-permute-done((bf16[128,1024]{1,0:T(8,128)(2,1)S(1)}, bf16[128,1024]{1,0:T(8,128)(2,1)S(1)}, u32[]{:S(2)}, u32[]{:S(2)}) %collective-permute-start.20) | collective-permute-done | bytes 262176 | tf_op jit(solution)/shard_map/ppermute | solution.py:47
  89.1 0.5 collective-permute-start.22
  89.6 1.3 collective-permute-start.24
  90.9 1.9 %collective-permute-start.25 = (bf16[128,1024]{1,0:T(8,128)(2,1)S(1)}, bf16[128,1024]{1,0:T(8,128)(2,1)S(1)}, u32[]{:S(2)}, u32[]{:S(2)}) collective-permute-start(bf16[128,1024]{1,0:T(8,128)(2,1)S(1)} %collective-permute-done.20.refs_2_), channel_id=1, source_target_pairs={{0,2},{1,3},{2,6},{3,7},{4,0},{5,1},{6,4},{7,5},{8,10},{9,11},{10,... | collective-permute-start | bytes 786440 | tf_op jit(solution)/shard_map/ppermute | solution.py:47
  92.8 3.8 %collective-permute-done.22 = bf16[128,1024]{1,0:T(8,128)(2,1)S(1)} collective-permute-done((bf16[128,1024]{1,0:T(8,128)(2,1)S(1)}, bf16[128,1024]{1,0:T(8,128)(2,1)S(1)}, u32[]{:S(2)}, u32[]{:S(2)}) %collective-permute-start.22) | collective-permute-done | bytes 262176 | tf_op jit(solution)/shard_map/ppermute | solution.py:26
  96.6 1.1 convolution_convert_fusion
  97.9 1.9 %collective-permute-done.25.refs_4_ = bf16[128,1024]{1,0:T(8,128)(2,1)S(1)} collective-permute-done((bf16[128,1024]{1,0:T(8,128)(2,1)S(1)}, bf16[128,1024]{1,0:T(8,128)(2,1)S(1)}, u32[]{:S(2)}, u32[]{:S(2)}) %collective-permute-start.25) | collective-permute-done | bytes 262176 | tf_op jit(solution)/shard_map/ppermute | solution.py:47
  99.8 0.7 collective-permute-start.26
  100.6 1.6 %collective-permute-start.27 = (bf16[128,1024]{1,0:T(8,128)(2,1)S(1)}, bf16[128,1024]{1,0:T(8,128)(2,1)S(1)}, u32[]{:S(2)}, u32[]{:S(2)}) collective-permute-start(bf16[128,1024]{1,0:T(8,128)(2,1)S(1)} %collective-permute-done.25.refs_4_), channel_id=1, source_target_pairs={{0,2},{1,3},{2,6},{3,7},{4,0},{5,1},{6,4},{7,5},{8,10},{9,11},{10,... | collective-permute-start | bytes 786440 | tf_op jit(solution)/shard_map/ppermute | solution.py:47
  102.2 4.8 %collective-permute-done.26.refs_5_ = bf16[128,1024]{1,0:T(8,128)(2,1)S(1)} collective-permute-done((bf16[128,1024]{1,0:T(8,128)(2,1)S(1)}, bf16[128,1024]{1,0:T(8,128)(2,1)S(1)}, u32[]{:S(2)}, u32[]{:S(2)}) %collective-permute-start.26) | collective-permute-done | bytes 262176 | tf_op jit(solution)/shard_map/ppermute | solution.py:31
  106.9 1.4 %collective-permute-done.27.refs_6_ = bf16[128,1024]{1,0:T(8,128)(2,1)S(1)} collective-permute-done((bf16[128,1024]{1,0:T(8,128)(2,1)S(1)}, bf16[128,1024]{1,0:T(8,128)(2,1)S(1)}, u32[]{:S(2)}, u32[]{:S(2)}) %collective-permute-start.27) | collective-permute-done | bytes 262176 | tf_op jit(solution)/shard_map/ppermute | solution.py:47
  108.3 1.3 collective-permute-start.28
  109.7 4.5 %logit_part.1 = (f32[128,512]{1,0:T(8,128)S(1)}, f32[128,128]{1,0:T(8,128)S(1)}) custom-call(f32[8,1024]{1,0:T(8,128)S(1)} %reshape.106.gain_ref, bf16[4096,512]{1,0:T(8,128)(2,1)} %own_ref.3, bf16[4096,512]{1,0:T(8,128)(2,1)} %copy-done.6, bf16[128,1024]{1,0:T(8,128)(2,1)S(1)} %get-tuple-element.66.refs_0_, ...), custom_call_target="tpu_custom_call" | custom-call | flops 939524096 | bytes 9175040 | tf_op jit(solution)/shard_map/logit_part/pallas_call | solution.py:431
  114.7 1.9 %vocab_stats.1 = f32[8,128]{1,0:T(8,128)S(1)} custom-call(s32[128,1]{1,0:T(8,128)S(1)} %copy.13.targets_ref, f32[8,1024]{1,0:T(8,128)S(1)} %reshape.106.gain_ref, f32[128,512]{1,0:T(8,128)S(1)} %get-tuple-element.60.logits_ref, f32[128,128]{1,0:T(8,128)S(1)} %get-tuple-element.61.squares_ref, bf16[128,1024]{1,0:T(8,128)(2,1)S(1)} %collective-permute-done.28.block_ref, ...), custom_call_target="tpu_custom_call" | custom-call | tf_op jit(solution)/shard_map/vocab_stats/pallas_call | solution.py:483
  116.6 1.3 %collective-permute-start.29 = (f32[3,128]{1,0:T(4,128)S(1)}, f32[3,128]{1,0:T(4,128)S(1)}, u32[]{:S(2)}, u32[]{:S(2)}) collective-permute-start(f32[3,128]{1,0:T(4,128)S(1)} %slice.91), channel_id=1, source_target_pairs={{0,1},{1,0},{2,3},{3,2},{4,5},{5,4},{6,7},{7,6},{8,9},{9,8},{10,11... | collective-permute-start | bytes 4616 | tf_op jit(solution)/shard_map/ppermute | solution.py:31
  117.9 0.9 collective-permute-start.31
  118.8 1.4 %collective-permute-done.29 = f32[3,128]{1,0:T(4,128)S(1)} collective-permute-done((f32[3,128]{1,0:T(4,128)S(1)}, f32[3,128]{1,0:T(4,128)S(1)}, u32[]{:S(2)}, u32[]{:S(2)}) %collective-permute-start.29) | collective-permute-done | bytes 1568 | tf_op jit(solution)/shard_map/ppermute | solution.py:31
  120.2 0.7 collective-permute-done.30
  121.0 2.3 %collective-permute-start.32 = (f32[3,2,128]{2,0,1:T(4,128)S(1)}, f32[3,2,128]{2,0,1:T(4,128)S(1)}, u32[]{:S(2)}, u32[]{:S(2)}) collective-permute-start(f32[3,2,128]{2,0,1:T(4,128)S(1)} %pad_maximum_fusion.1), channel_id=1, source_target_pairs={{0,6},{1,7},{2,4},{3,5},{4,2},{5,3},{6,0},{7,1},{8,14},{9,15},{10,... | collective-permute-start | bytes 9224 | tf_op jit(solution)/shard_map/ppermute | solution.py:630
  123.3 0.6 collective-permute-start.33
  123.9 1.5 %collective-permute-start.34 = (f32[3,2,128]{2,0,1:T(4,128)S(1)}, f32[3,2,128]{2,0,1:T(4,128)S(1)}, u32[]{:S(2)}, u32[]{:S(2)}) collective-permute-start(f32[3,2,128]{2,0,1:T(4,128)S(1)} %pad_maximum_fusion.1), channel_id=1, source_target_pairs={{0,2},{1,3},{2,0},{3,1},{4,6},{5,7},{6,4},{7,5},{8,10},{9,11},{10,... | collective-permute-start | bytes 9224 | tf_op jit(solution)/shard_map/ppermute | solution.py:630
  125.4 1.0 collective-permute-done.32
  126.4 1.4 %collective-permute-done.33 = f32[3,2,128]{2,0,1:T(4,128)S(1)} collective-permute-done((f32[3,2,128]{2,0,1:T(4,128)S(1)}, f32[3,2,128]{2,0,1:T(4,128)S(1)}, u32[]{:S(2)}, u32[]{:S(2)}) %collective-permute-start.33) | collective-permute-done | bytes 3104 | tf_op jit(solution)/shard_map/ppermute | solution.py:630
  127.9 0.7 select_reduce_fusion
  (71 shorter events, 2.4 us)
Async XLA Ops:
  0.6 4.4 %copy-start = (bf16[1024,256]{1,0:T(8,128)(2,1)S(1)}, bf16[1024,256]{1,0:T(8,128)(2,1)}, u32[]{:S(2)}) copy-start(bf16[1024,256]{1,0:T(8,128)(2,1)} %param.14) | copy-start | bytes 1572868
  0.6 1.1 copy-start.1
  1.7 0.7 copy-start.3
  2.4 20.0 %copy-start.2 = (bf16[4,256,256]{2,1,0:T(8,128)(2,1)S(1)}, bf16[4,256,256]{2,1,0:T(8,128)(2,1)}, u32[]{:S(2)}) copy-start(bf16[4,256,256]{2,1,0:T(8,128)(2,1)} %cache_own.1) | copy-start | bytes 1572868
  2.4 20.0 %copy-start.12 = (s32[512]{0:T(512)S(1)}, s32[512]{0:T(512)}, u32[]{:S(2)}) copy-start(s32[512]{0:T(512)} %param.21) | copy-start | bytes 6148
  2.4 29.9 %copy-start.13 = (s32[4]{0:T(128)S(1)}, s32[4]{0:T(128)}, u32[]{:S(2)}) copy-start(s32[4]{0:T(128)} %param.20) | copy-start | bytes 52
  2.4 37.0 %copy-start.10 = (f32[8192]{0:T(1024)S(1)}, f32[8192]{0:T(1024)}, u32[]{:S(2)}) copy-start(f32[8192]{0:T(1024)} %param.12) | copy-start | bytes 98308
  3.3 1.7 %collective-permute-start = (bf16[128,1024]{1,0:T(8,128)(2,1)S(1)}, bf16[128,1024]{1,0:T(8,128)(2,1)S(1)}, u32[]{:S(2)}, u32[]{:S(2)}) collective-permute-start(bf16[128,1024]{1,0:T(8,128)(2,1)S(1)} %get-tuple-element.34), channel_id=1, source_target_pairs={{0,8},{8,0},{1,9},{9,1},{2,10},{10,2},{3,11},{11,3},{4,12},{12,4},... | collective-permute-start | bytes 786440 | tf_op jit(solution)/shard_map/ppermute | solution.py:26
  5.3 13.0 %collective-permute-start.3 = (bf16[4096,256]{1,0:T(8,128)(2,1)}, bf16[4096,256]{1,0:T(8,128)(2,1)}, u32[]{:S(2)}, u32[]{:S(2)}) collective-permute-start(bf16[4096,256]{1,0:T(8,128)(2,1)} %q_own.3), channel_id=1, source_target_pairs={{0,8},{8,0},{1,9},{9,1},{2,10},{10,2},{3,11},{11,3},{4,12},{12,4},... | collective-permute-start | bytes 6291464 | tf_op jit(solution)/shard_map/ppermute | solution.py:26
  5.8 12.6 %collective-permute-start.4 = (bf16[256,4096]{1,0:T(8,128)(2,1)}, bf16[256,4096]{1,0:T(8,128)(2,1)}, u32[]{:S(2)}, u32[]{:S(2)}) collective-permute-start(bf16[256,4096]{1,0:T(8,128)(2,1)} %out_own.3), channel_id=1, source_target_pairs={{0,8},{8,0},{1,9},{9,1},{2,10},{10,2},{3,11},{11,3},{4,12},{12,4},... | collective-permute-start | bytes 6291464 | tf_op jit(solution)/shard_map/ppermute | solution.py:26
  5.9 12.0 %collective-permute-start.1 = (bf16[128,1280]{1,0:T(8,128)(2,1)S(1)}, bf16[128,1280]{1,0:T(8,128)(2,1)S(1)}, u32[]{:S(2)}, u32[]{:S(2)}) collective-permute-start(bf16[128,1280]{1,0:T(8,128)(2,1)S(1)} %pad_maximum_fusion.refs_0_), channel_id=1, source_target_pairs={{0,2},{1,3},{2,6},{3,7},{4,0},{5,1},{6,4},{7,5},{8,10},{9,11},{10,... | collective-permute-start | bytes 983048 | tf_op jit(solution)/shard_map/ppermute | solution.py:47
  8.9 9.5 %collective-permute-start.2 = (bf16[128,1280]{1,0:T(8,128)(2,1)S(1)}, bf16[128,1280]{1,0:T(8,128)(2,1)S(1)}, u32[]{:S(2)}, u32[]{:S(2)}) collective-permute-start(bf16[128,1280]{1,0:T(8,128)(2,1)S(1)} %pad_maximum_fusion.refs_0_), channel_id=1, source_target_pairs={{0,1},{1,0},{2,3},{3,2},{4,5},{5,4},{6,7},{7,6},{8,9},{9,8},{10,11... | collective-permute-start | bytes 983048 | tf_op jit(solution)/shard_map/ppermute | solution.py:31
  18.3 9.8 %collective-permute-start.5 = (bf16[128,1280]{1,0:T(8,128)(2,1)S(1)}, bf16[128,1280]{1,0:T(8,128)(2,1)S(1)}, u32[]{:S(2)}, u32[]{:S(2)}) collective-permute-start(bf16[128,1280]{1,0:T(8,128)(2,1)S(1)} %collective-permute-done.1.refs_2_), channel_id=1, source_target_pairs={{0,2},{1,3},{2,6},{3,7},{4,0},{5,1},{6,4},{7,5},{8,10},{9,11},{10,... | collective-permute-start | bytes 983048 | tf_op jit(solution)/shard_map/ppermute | solution.py:47
  20.9 8.3 %collective-permute-start.6 = (bf16[128,1280]{1,0:T(8,128)(2,1)S(1)}, bf16[128,1280]{1,0:T(8,128)(2,1)S(1)}, u32[]{:S(2)}, u32[]{:S(2)}) collective-permute-start(bf16[128,1280]{1,0:T(8,128)(2,1)S(1)} %collective-permute-done.1.refs_2_), channel_id=1, source_target_pairs={{0,1},{1,0},{2,3},{3,2},{4,5},{5,4},{6,7},{7,6},{8,9},{9,8},{10,11... | collective-permute-start | bytes 983048 | tf_op jit(solution)/shard_map/ppermute | solution.py:31
  22.4 6.8 %collective-permute-start.7 = (bf16[4,256,256]{2,1,0:T(8,128)(2,1)S(1)}, bf16[4,256,256]{2,1,0:T(8,128)(2,1)S(1)}, u32[]{:S(2)}, u32[]{:S(2)}) collective-permute-start(bf16[4,256,256]{2,1,0:T(8,128)(2,1)S(1)} %copy-done.2), channel_id=1, source_target_pairs={{0,8},{8,0},{1,9},{9,1},{2,10},{10,2},{3,11},{11,3},{4,12},{12,4},... | collective-permute-start | bytes 1572872 | tf_op jit(solution)/shard_map/ppermute | solution.py:26
  22.7 1.7 %collective-permute-start.8 = (s32[1,128]{1,0:T(1,128)S(1)}, s32[1,128]{1,0:T(1,128)S(1)}, u32[]{:S(2)}, u32[]{:S(2)}) collective-permute-start(s32[1,128]{1,0:T(1,128)S(1)} %slice_bitcast_fusion), channel_id=1, source_target_pairs={{0,8},{8,0},{1,9},{9,1},{2,10},{10,2},{3,11},{11,3},{4,12},{12,4},... | collective-permute-start | bytes 1544 | tf_op jit(solution)/shard_map/ppermute | solution.py:26
  29.2 9.7 %copy-start.7 = (bf16[4,256,256]{2,1,0:T(8,128)(2,1)}, bf16[4,256,256]{2,1,0:T(8,128)(2,1)S(1)}, u32[]{:S(2)}) copy-start(bf16[4,256,256]{2,1,0:T(8,128)(2,1)S(1)} %collective-permute-done.7.cache_other) | copy-start | bytes 1572868
  29.2 7.4 %collective-permute-start.10 = (bf16[128,1280]{1,0:T(8,128)(2,1)S(1)}, bf16[128,1280]{1,0:T(8,128)(2,1)S(1)}, u32[]{:S(2)}, u32[]{:S(2)}) collective-permute-start(bf16[128,1280]{1,0:T(8,128)(2,1)S(1)} %collective-permute-done.5.refs_4_), channel_id=1, source_target_pairs={{0,1},{1,0},{2,3},{3,2},{4,5},{5,4},{6,7},{7,6},{8,9},{9,8},{10,11... | collective-permute-start | bytes 983048 | tf_op jit(solution)/shard_map/ppermute | solution.py:31
  30.8 8.1 %collective-permute-start.11 = (bf16[128,1280]{1,0:T(8,128)(2,1)S(1)}, bf16[128,1280]{1,0:T(8,128)(2,1)}, u32[]{:S(2)}, u32[]{:S(2)}) collective-permute-start(bf16[128,1280]{1,0:T(8,128)(2,1)S(1)} %collective-permute-done.5.refs_4_), channel_id=1, source_target_pairs={{0,2},{1,3},{2,6},{3,7},{4,0},{5,1},{6,4},{7,5},{8,10},{9,11},{10,... | collective-permute-start | bytes 983048 | tf_op jit(solution)/shard_map/ppermute | solution.py:47
  32.3 1.1 collective-permute-start.9
  36.6 0.8 copy-start.8
  38.9 7.3 %collective-permute-start.12 = (bf16[128,1280]{1,0:T(8,128)(2,1)}, bf16[128,1280]{1,0:T(8,128)(2,1)S(1)}, u32[]{:S(2)}, u32[]{:S(2)}) collective-permute-start(bf16[128,1280]{1,0:T(8,128)(2,1)} %collective-permute-done.11.refs_6_), channel_id=1, source_target_pairs={{0,1},{1,0},{2,3},{3,2},{4,5},{5,4},{6,7},{7,6},{8,9},{9,8},{10,11... | collective-permute-start | bytes 983048 | tf_op jit(solution)/shard_map/ppermute | solution.py:31
  39.4 6.8 %copy-start.4 = (s32[8]{0:T(128)S(1)}, s32[8]{0:T(128)}, u32[]{:S(2)}) copy-start(s32[8]{0:T(128)} %lens_ref.3) | copy-start | bytes 100
  49.8 8.9 %collective-permute-start.16 = (bf16[128,1024]{1,0:T(8,128)(2,1)S(1)}, bf16[128,1024]{1,0:T(8,128)(2,1)S(1)}, u32[]{:S(2)}, u32[]{:S(2)}) collective-permute-start(bf16[128,1024]{1,0:T(8,128)(2,1)S(1)} %get-tuple-element.54), channel_id=1, source_target_pairs={{0,1},{1,0},{2,3},{3,2},{4,5},{5,4},{6,7},{7,6},{8,9},{9,8},{10,11... | collective-permute-start | bytes 786440 | tf_op jit(solution)/shard_map/ppermute | solution.py:31
  53.2 28.4 %dynamic-slice-start = ((f32[8192]{0:T(1024)}, s32[]{:T(128)}), f32[1024]{0:T(1024)S(1)}, s32[]{:S(2)}) async-start(f32[8192]{0:T(1024)} %param.17, s32[]{:T(128)} %select_n.122), calls=%async_computation | async-start | bytes 8704 | tf_op jit(solution)/shard_map/dynamic_slice | solution.py:580
  53.2 10.7 %collective-permute-start.15 = (bf16[128,1024]{1,0:T(8,128)(2,1)S(1)}, bf16[128,1024]{1,0:T(8,128)(2,1)S(1)}, u32[]{:S(2)}, u32[]{:S(2)}) collective-permute-start(bf16[128,1024]{1,0:T(8,128)(2,1)S(1)} %get-tuple-element.52), channel_id=1, source_target_pairs={{0,1},{1,0},{2,3},{3,2},{4,5},{5,4},{6,7},{7,6},{8,9},{9,8},{10,11... | collective-permute-start | bytes 786440 | tf_op jit(solution)/shard_map/ppermute | solution.py:31
  58.7 30.4 %copy-start.5 = (bf16[4096,512]{1,0:T(8,128)(2,1)S(1)}, bf16[4096,512]{1,0:T(8,128)(2,1)}, u32[]{:S(2)}) copy-start(bf16[4096,512]{1,0:T(8,128)(2,1)} %own_ref.3) | copy-start | bytes 12582916
  58.8 7.3 %collective-permute-start.17 = (bf16[128,1024]{1,0:T(8,128)(2,1)S(1)}, bf16[128,1024]{1,0:T(8,128)(2,1)S(1)}, u32[]{:S(2)}, u32[]{:S(2)}) collective-permute-start(bf16[128,1024]{1,0:T(8,128)(2,1)S(1)} %add_convert_fusion.2), channel_id=1, source_target_pairs={{0,2},{1,3},{2,6},{3,7},{4,0},{5,1},{6,4},{7,5},{8,10},{9,11},{10,... | collective-permute-start | bytes 786440 | tf_op jit(solution)/shard_map/ppermute | solution.py:47
  60.3 7.5 %collective-permute-start.14 = (bf16[128,1024]{1,0:T(8,128)(2,1)S(1)}, bf16[128,1024]{1,0:T(8,128)(2,1)S(1)}, u32[]{:S(2)}, u32[]{:S(2)}) collective-permute-start(bf16[128,1024]{1,0:T(8,128)(2,1)S(1)} %get-tuple-element.50), channel_id=1, source_target_pairs={{0,1},{1,0},{2,3},{3,2},{4,5},{5,4},{6,7},{7,6},{8,9},{9,8},{10,11... | collective-permute-start | bytes 786440 | tf_op jit(solution)/shard_map/ppermute | solution.py:31
  66.2 43.4 %copy-start.11 = (f32[8192]{0:T(1024)S(1)}, f32[8192]{0:T(1024)}, u32[]{:S(2)}) copy-start(f32[8192]{0:T(1024)} %param.17) | copy-start | bytes 98308
  66.2 7.9 %collective-permute-start.18 = (bf16[128,1024]{1,0:T(8,128)(2,1)S(1)}, bf16[128,1024]{1,0:T(8,128)(2,1)S(1)}, u32[]{:S(2)}, u32[]{:S(2)}) collective-permute-start(bf16[128,1024]{1,0:T(8,128)(2,1)S(1)} %add_convert_fusion.1), channel_id=1, source_target_pairs={{0,2},{1,3},{2,6},{3,7},{4,0},{5,1},{6,4},{7,5},{8,10},{9,11},{10,... | collective-permute-start | bytes 786440 | tf_op jit(solution)/shard_map/ppermute | solution.py:47
  66.9 7.5 %collective-permute-start.13 = (bf16[128,1024]{1,0:T(8,128)(2,1)S(1)}, bf16[128,1024]{1,0:T(8,128)(2,1)S(1)}, u32[]{:S(2)}, u32[]{:S(2)}) collective-permute-start(bf16[128,1024]{1,0:T(8,128)(2,1)S(1)} %get-tuple-element.48), channel_id=1, source_target_pairs={{0,1},{1,0},{2,3},{3,2},{4,5},{5,4},{6,7},{7,6},{8,9},{9,8},{10,11... | collective-permute-start | bytes 786440 | tf_op jit(solution)/shard_map/ppermute | solution.py:31
  74.2 7.3 %collective-permute-start.19 = (bf16[128,1024]{1,0:T(8,128)(2,1)S(1)}, bf16[128,1024]{1,0:T(8,128)(2,1)S(1)}, u32[]{:S(2)}, u32[]{:S(2)}) collective-permute-start(bf16[128,1024]{1,0:T(8,128)(2,1)S(1)} %add_convert_fusion), channel_id=1, source_target_pairs={{0,2},{1,3},{2,6},{3,7},{4,0},{5,1},{6,4},{7,5},{8,10},{9,11},{10,... | collective-permute-start | bytes 786440 | tf_op jit(solution)/shard_map/ppermute | solution.py:47
  81.8 7.3 %collective-permute-start.20 = (bf16[128,1024]{1,0:T(8,128)(2,1)S(1)}, bf16[128,1024]{1,0:T(8,128)(2,1)S(1)}, u32[]{:S(2)}, u32[]{:S(2)}) collective-permute-start(bf16[128,1024]{1,0:T(8,128)(2,1)S(1)} %get-tuple-element.66.refs_0_), channel_id=1, source_target_pairs={{0,2},{1,3},{2,6},{3,7},{4,0},{5,1},{6,4},{7,5},{8,10},{9,11},{10,... | collective-permute-start | bytes 786440 | tf_op jit(solution)/shard_map/ppermute | solution.py:47
  81.9 7.2 %collective-permute-start.21 = (bf16[128,1024]{1,0:T(8,128)(2,1)S(1)}, bf16[128,1024]{1,0:T(8,128)(2,1)S(1)}, u32[]{:S(2)}, u32[]{:S(2)}) collective-permute-start(bf16[128,1024]{1,0:T(8,128)(2,1)S(1)} %get-tuple-element.66.refs_0_), channel_id=1, source_target_pairs={{0,1},{1,0},{2,3},{3,2},{4,5},{5,4},{6,7},{7,6},{8,9},{9,8},{10,11... | collective-permute-start | bytes 786440 | tf_op jit(solution)/shard_map/ppermute | solution.py:31
  89.1 10.7 %collective-permute-start.23 = (bf16[4096,512]{1,0:T(8,128)(2,1)S(1)}, bf16[4096,512]{1,0:T(8,128)(2,1)S(1)}, u32[]{:S(2)}, u32[]{:S(2)}) collective-permute-start(bf16[4096,512]{1,0:T(8,128)(2,1)S(1)} %copy-done.5), channel_id=1, source_target_pairs={{0,8},{8,0},{1,9},{9,1},{2,10},{10,2},{3,11},{11,3},{4,12},{12,4},... | collective-permute-start | bytes 12582920 | tf_op jit(solution)/shard_map/ppermute | solution.py:26
  89.1 7.5 %collective-permute-start.22 = (bf16[128,1024]{1,0:T(8,128)(2,1)S(1)}, bf16[128,1024]{1,0:T(8,128)(2,1)S(1)}, u32[]{:S(2)}, u32[]{:S(2)}) collective-permute-start(bf16[128,1024]{1,0:T(8,128)(2,1)S(1)} %get-tuple-element.56), channel_id=1, source_target_pairs={{0,8},{8,0},{1,9},{9,1},{2,10},{10,2},{3,11},{11,3},{4,12},{12,4},... | collective-permute-start | bytes 786440 | tf_op jit(solution)/shard_map/ppermute | solution.py:26
  89.6 8.3 %collective-permute-start.24 = (bf16[128,1024]{1,0:T(8,128)(2,1)S(1)}, bf16[128,1024]{1,0:T(8,128)(2,1)S(1)}, u32[]{:S(2)}, u32[]{:S(2)}) collective-permute-start(bf16[128,1024]{1,0:T(8,128)(2,1)S(1)} %collective-permute-done.20.refs_2_), channel_id=1, source_target_pairs={{0,1},{1,0},{2,3},{3,2},{4,5},{5,4},{6,7},{7,6},{8,9},{9,8},{10,11... | collective-permute-start | bytes 786440 | tf_op jit(solution)/shard_map/ppermute | solution.py:31
  90.9 8.9 %collective-permute-start.25 = (bf16[128,1024]{1,0:T(8,128)(2,1)S(1)}, bf16[128,1024]{1,0:T(8,128)(2,1)S(1)}, u32[]{:S(2)}, u32[]{:S(2)}) collective-permute-start(bf16[128,1024]{1,0:T(8,128)(2,1)S(1)} %collective-permute-done.20.refs_2_), channel_id=1, source_target_pairs={{0,2},{1,3},{2,6},{3,7},{4,0},{5,1},{6,4},{7,5},{8,10},{9,11},{10,... | collective-permute-start | bytes 786440 | tf_op jit(solution)/shard_map/ppermute | solution.py:47
  99.8 8.5 %copy-start.6 = (bf16[4096,512]{1,0:T(8,128)(2,1)}, bf16[4096,512]{1,0:T(8,128)(2,1)S(1)}, u32[]{:S(2)}) copy-start(bf16[4096,512]{1,0:T(8,128)(2,1)S(1)} %collective-permute-done.23.other_ref) | copy-start | bytes 12582916
  99.8 7.1 %collective-permute-start.26 = (bf16[128,1024]{1,0:T(8,128)(2,1)S(1)}, bf16[128,1024]{1,0:T(8,128)(2,1)S(1)}, u32[]{:S(2)}, u32[]{:S(2)}) collective-permute-start(bf16[128,1024]{1,0:T(8,128)(2,1)S(1)} %collective-permute-done.25.refs_4_), channel_id=1, source_target_pairs={{0,1},{1,0},{2,3},{3,2},{4,5},{5,4},{6,7},{7,6},{8,9},{9,8},{10,11... | collective-permute-start | bytes 786440 | tf_op jit(solution)/shard_map/ppermute | solution.py:31
  100.6 7.7 %collective-permute-start.27 = (bf16[128,1024]{1,0:T(8,128)(2,1)S(1)}, bf16[128,1024]{1,0:T(8,128)(2,1)S(1)}, u32[]{:S(2)}, u32[]{:S(2)}) collective-permute-start(bf16[128,1024]{1,0:T(8,128)(2,1)S(1)} %collective-permute-done.25.refs_4_), channel_id=1, source_target_pairs={{0,2},{1,3},{2,6},{3,7},{4,0},{5,1},{6,4},{7,5},{8,10},{9,11},{10,... | collective-permute-start | bytes 786440 | tf_op jit(solution)/shard_map/ppermute | solution.py:47
  108.3 1.4 %copy-start.9 = (bf16[128,1024]{1,0:T(8,128)(2,1)}, bf16[128,1024]{1,0:T(8,128)(2,1)S(1)}, u32[]{:S(2)}) copy-start(bf16[128,1024]{1,0:T(8,128)(2,1)S(1)} %collective-permute-done.27.refs_6_) | copy-start | bytes 786436
  108.3 6.4 %collective-permute-start.28 = (bf16[128,1024]{1,0:T(8,128)(2,1)S(1)}, bf16[128,1024]{1,0:T(8,128)(2,1)S(1)}, u32[]{:S(2)}, u32[]{:S(2)}) collective-permute-start(bf16[128,1024]{1,0:T(8,128)(2,1)S(1)} %collective-permute-done.27.refs_6_), channel_id=1, source_target_pairs={{0,1},{1,0},{2,3},{3,2},{4,5},{5,4},{6,7},{7,6},{8,9},{9,8},{10,11... | collective-permute-start | bytes 786440 | tf_op jit(solution)/shard_map/ppermute | solution.py:31
  116.6 3.7 %collective-permute-start.29 = (f32[3,128]{1,0:T(4,128)S(1)}, f32[3,128]{1,0:T(4,128)S(1)}, u32[]{:S(2)}, u32[]{:S(2)}) collective-permute-start(f32[3,128]{1,0:T(4,128)S(1)} %slice.91), channel_id=1, source_target_pairs={{0,1},{1,0},{2,3},{3,2},{4,5},{5,4},{6,7},{7,6},{8,9},{9,8},{10,11... | collective-permute-start | bytes 4616 | tf_op jit(solution)/shard_map/ppermute | solution.py:31
  117.9 3.0 %collective-permute-start.30 = (f32[3,128]{1,0:T(4,128)S(1)}, f32[3,128]{1,0:T(4,128)S(1)}, u32[]{:S(2)}, u32[]{:S(2)}) collective-permute-start(f32[3,128]{1,0:T(4,128)S(1)} %slice.91), channel_id=1, source_target_pairs={{9,0},{8,1},{11,2},{10,3},{13,4},{12,5},{15,6},{14,7},{1,8},{0,9},... | collective-permute-start | bytes 4616 | tf_op jit(solution)/shard_map/ppermute | solution.py:621
  117.9 3.0 %collective-permute-start.31 = (f32[3,128]{1,0:T(4,128)S(1)}, f32[3,128]{1,0:T(4,128)S(1)}, u32[]{:S(2)}, u32[]{:S(2)}) collective-permute-start(f32[3,128]{1,0:T(4,128)S(1)} %slice.91), channel_id=1, source_target_pairs={{0,8},{8,0},{1,9},{9,1},{2,10},{10,2},{3,11},{11,3},{4,12},{12,4},... | collective-permute-start | bytes 4616 | tf_op jit(solution)/shard_map/ppermute | solution.py:26
  121.0 5.5 %collective-permute-start.32 = (f32[3,2,128]{2,0,1:T(4,128)S(1)}, f32[3,2,128]{2,0,1:T(4,128)S(1)}, u32[]{:S(2)}, u32[]{:S(2)}) collective-permute-start(f32[3,2,128]{2,0,1:T(4,128)S(1)} %pad_maximum_fusion.1), channel_id=1, source_target_pairs={{0,6},{1,7},{2,4},{3,5},{4,2},{5,3},{6,0},{7,1},{8,14},{9,15},{10,... | collective-permute-start | bytes 9224 | tf_op jit(solution)/shard_map/ppermute | solution.py:630
  123.3 4.5 %collective-permute-start.33 = (f32[3,2,128]{2,0,1:T(4,128)S(1)}, f32[3,2,128]{2,0,1:T(4,128)S(1)}, u32[]{:S(2)}, u32[]{:S(2)}) collective-permute-start(f32[3,2,128]{2,0,1:T(4,128)S(1)} %pad_maximum_fusion.1), channel_id=1, source_target_pairs={{0,4},{1,5},{2,6},{3,7},{4,0},{5,1},{6,2},{7,3},{8,12},{9,13},{10,... | collective-permute-start | bytes 9224 | tf_op jit(solution)/shard_map/ppermute | solution.py:630
  123.9 3.9 %collective-permute-start.34 = (f32[3,2,128]{2,0,1:T(4,128)S(1)}, f32[3,2,128]{2,0,1:T(4,128)S(1)}, u32[]{:S(2)}, u32[]{:S(2)}) collective-permute-start(f32[3,2,128]{2,0,1:T(4,128)S(1)} %pad_maximum_fusion.1), channel_id=1, source_target_pairs={{0,2},{1,3},{2,0},{3,1},{4,6},{5,7},{6,4},{7,5},{8,10},{9,11},{10,... | collective-permute-start | bytes 9224 | tf_op jit(solution)/shard_map/ppermute | solution.py:630
